TPU v7x, 32 devices: a whole 2x2x4 slice. The times are simulated.
32 devices in a mesh: parts: 2 (over x), dp: 16 (over z, y, core).
Axes of the slice: x: 2, y: 2, z: 4, core: 2. Of those that a mesh axis runs over, the one named last changes fastest.
Arguments:
- layer_input: bfloat16 [32768, 4096], P(('parts', 'dp')), parts along dimension 0, may hold values from -60 to 60
- out_grads: bfloat16 [32768, 2, 1024], P(('parts', 'dp')), parts along dimension 0, may hold values from -60 to 60, as said below
- in_proj: bfloat16 [2, 64, 4096], replicated, may hold values from -0.09375 to 0.09375
- out_proj: bfloat16 [2, 64, 1024], replicated, may hold values from -0.1875 to 0.1875
- queries: bfloat16 [256, 8192], P(('parts', 'dp')), parts along dimension 0, may hold values from -6 to 6
Outputs:
- scores: float32 [256, 128], P(('parts', 'dp')), parts along dimension 0
There are 2 independent parts, one for each index of `parts`. A program takes and returns all parts, laid end to end along the dimension named above; an argument that names none is the same for every part. Nothing has to cross between parts.
Inputs may be any that keep to these rules, and one draw needn't show every extreme that they name: `out_grads`: output gradients at each token.
All inputs are finite; a program needn't handle non-finite values.
Results may differ from a plain program's by a relative error of at most 0.0054.
Values may be sent and summed in bfloat16 or wider, within the bound.
No kernel may reach another device: no remote copies, remote signals or barrier semaphores. Data moves between devices by JAX's collectives and lax.ppermute only.
A program may use at most 64 MiB of HBM per device.

v0:
```python
import jax
import jax.numpy as jnp
from jax import lax
from jax.sharding import PartitionSpec as P

R = 64
LEN = 128


damping_ratio = 0.1


def damped_inverse(covariance):
    order_dim = covariance.shape[-1]
    identity = jnp.eye(order_dim, dtype=covariance.dtype)
    trace_sum = jnp.trace(covariance, axis1=1, axis2=2)
    damped = covariance + (damping_ratio * trace_sum / order_dim)[:, None, None] * identity
    factor = jnp.linalg.cholesky(damped)
    return jax.vmap(lambda lower: jax.scipy.linalg.cho_solve((lower, True), identity))(factor)


def row_products(left_rows, right_rows):
    return lax.dot_general(
        left_rows, right_rows, (((1,), (1,)), ((), ())), preferred_element_type=jnp.float32
    )


def per_device(layer_input, out_grads, in_proj, out_proj, queries):
    local_tokens = layer_input.shape[0]
    in_flat = in_proj.reshape(2 * R, in_proj.shape[2])
    projected_in = row_products(layer_input, in_flat).astype(jnp.bfloat16)
    projected_in = projected_in.reshape(local_tokens, 2, R)
    projected_out = jnp.einsum(
        "tmk,mrk->tmr", out_grads, out_proj, preferred_element_type=jnp.float32
    ).astype(jnp.bfloat16)
    local_in = jnp.einsum(
        "tmr,tms->mrs", projected_in, projected_in, preferred_element_type=jnp.float32
    )
    local_out = jnp.einsum(
        "tmr,tms->mrs", projected_out, projected_out, preferred_element_type=jnp.float32
    )
    cov_in, cov_out = lax.psum((local_in, local_out), "dp")
    total_tokens = local_tokens * lax.axis_size("dp")
    inv_in = damped_inverse(cov_in / total_tokens)
    inv_out = damped_inverse(cov_out / total_tokens)
    seq_count = local_tokens // LEN
    moments = (
        jnp.einsum(
            "slmo,slmc->smoc",
            projected_out.reshape(seq_count, LEN, 2, R),
            projected_in.reshape(seq_count, LEN, 2, R),
            preferred_element_type=jnp.float32,
        )
        / LEN
    )
    left_side = jnp.einsum("moa,smac->smoc", inv_out, moments, precision=lax.Precision.HIGHEST)
    precond = jnp.einsum("smoa,mac->smoc", left_side, inv_in, precision=lax.Precision.HIGHEST)
    precond = precond.astype(jnp.bfloat16).reshape(seq_count, 2 * R * R)
    return row_products(precond, lax.all_gather(queries, "dp", axis=0, tiled=True))


def solution(mesh):
    return jax.shard_map(
        per_device,
        mesh=mesh,
        in_specs=(
            P(("parts", "dp"), None),
            P(("parts", "dp"), None, None),
            P(),
            P(),
            P(("parts", "dp"), None),
        ),
        out_specs=P(("parts", "dp"), None),
        check_vma=False,
    )
```

profile of v0, /device:TPU:0, one launch (start us, length us, event | category | flops | bytes accessed | tf_op | source)
XLA Modules:
  0.0 165.7 jit_solution(9201504189107347552)
XLA Ops:
  6.5 0.0 copy-start
  6.5 0.0 all-reduce.3.cloned.1.call-start
  6.5 1.2 copy-done
  7.8 0.0 copy-start.1
  7.8 0.0 copy-start.2
  7.8 6.4 %convolution_convert_fusion.1 = bf16[1024,128]{0,1:T(8,128)(2,1)S(1)} fusion(bf16[1024,4096]{1,0:T(8,128)(2,1)} %param.8, bf16[128,4096]{1,0:T(8,128)(2,1)S(1)} %bitcast.65), kind=kOutput, calls=%fused_computation.6 | convolution fusion | flops 1073872896 | bytes 9699328 | tf_op jit(solution)/shard_map/dot_general | solution.py:23
  14.2 0.8 fusion.23
  15.0 0.0 copy-done.1
  15.0 0.0 copy-done.2
  15.0 1.4 fusion.2
  16.5 0.8 fusion.9
  17.3 0.0 all-reduce.3.cloned.1.call-update
  17.3 0.0 all-gather.2.cloned.1.call-start
  17.4 0.7 all-gather.2.cloned.1.call-update
  18.1 0.1 copy.23
  18.2 0.1 copy.47
  18.3 0.3 convolution_multiply_fusion
  18.6 88.7 %all-reduce.3.cloned.1.call-done = (f32[2,64,64]{1,2,0:T(8,128)}, f32[2,64,64]{1,2,0:T(8,128)}) async-done(((f32[2,64,64]{1,2,0:T(8,128)}, f32[2,64,64]{1,2,0:T(8,128)}), (f32[2,64,64]{1,2,0:T(8,128)}, f32[2,64,64]{1,2,0:T(8,128)})) %all-reduce.3.cloned.1.call-update) | async-done | bytes 65552 | tf_op jit(solution)/shard_map/psum | solution.py:42
  107.2 1.0 select_reduce_fusion.2
  108.2 1.0 multiply_add_fusion
  109.2 0.1 copy.22
  109.3 11.7 %custom-call.10 = f32[2,64,64]{2,1,0:T(8,128)S(1)} custom-call(f32[2,64,64]{2,1,0:T(8,128)S(1)} %fusion.19), custom_call_target="Cholesky" | custom-call | tf_op jit(solution)/shard_map/jit(cholesky)/cholesky | solution.py:18
  121.0 0.1 copy.29
  121.1 11.7 %custom-call.12 = f32[2,64,64]{2,1,0:T(8,128)S(1)} custom-call(f32[2,64,64]{2,1,0:T(8,128)S(1)} %fusion.15), custom_call_target="Cholesky" | custom-call | tf_op jit(solution)/shard_map/jit(cholesky)/cholesky | solution.py:18
  132.9 0.1 compare_reduce_fusion
  133.0 0.1 compare_reduce_fusion.1
  133.2 0.1 select_bitcast_fusion
  133.2 9.8 %custom-call.13 = f32[2,1,64,64]{2,3,1,0:T(8,128)S(1)} custom-call(f32[2,1,64,64]{3,2,1,0:T(8,128)S(1)} %get-tuple-element.15), custom_call_target="InvertDiagBlocksLowerTriangular" | custom-call | tf_op jit(solution)/shard_map/vmap(jit(_cho_solve))/triangular_solve | solution.py:19
  143.1 9.8 %custom-call.11 = f32[2,1,64,64]{2,3,1,0:T(8,128)S(1)} custom-call(f32[2,1,64,64]{3,2,1,0:T(8,128)S(1)} %get-tuple-element.16), custom_call_target="InvertDiagBlocksLowerTriangular" | custom-call | tf_op jit(solution)/shard_map/vmap(jit(_cho_solve))/triangular_solve | solution.py:19
  152.9 0.3 fusion.13
  153.2 0.2 convolution_bitcast_fusion.1
  153.4 0.3 fusion.17
  153.7 0.3 convolution_bitcast_fusion.2
  154.0 1.0 convolution_bitcast_fusion
  155.0 0.6 fusion.5
  155.6 0.2 copy.35
  155.8 0.3 reshape.40
  156.0 0.0 all-gather.2.cloned.1.call-done
  156.1 2.8 %fusion.24 = f32[8,128]{1,0:T(8,128)} fusion(bf16[8,8192]{1,0:T(8,128)(2,1)S(1)} %reshape.40, bf16[128,8192]{1,0:T(8,128)(2,1)} %all-gather.2.cloned.1.call-done), kind=kOutput, calls=%fused_computation.45 | convolution fusion | flops 16777216 | bytes 2232320 | tf_op jit(solution)/shard_map/dot_general | solution.py:23
  (8 shorter events, 0.1 us)
Async XLA Ops:
  6.5 1.2 copy-start
  6.5 100.7 %all-reduce.3.cloned.1.call-start = ((), (), s32[]{:S(2)}) async-start(), calls=%async_computation.1 | async-start | bytes 262144 | tf_op jit(solution)/shard_map/psum | solution.py:42
  7.8 7.3 %copy-start.1 = (bf16[1024,2,1024]{2,1,0:T(2,128)(2,1)S(1)}, bf16[1024,2,1024]{2,1,0:T(2,128)(2,1)}, u32[]{:S(2)}) copy-start(bf16[1024,2,1024]{2,1,0:T(2,128)(2,1)} %param.9) | copy-start | bytes 12582916
  7.8 7.3 %copy-start.2 = (bf16[2,64,1024]{2,1,0:T(8,128)(2,1)S(1)}, bf16[2,64,1024]{2,1,0:T(8,128)(2,1)}, u32[]{:S(2)}) copy-start(bf16[2,64,1024]{2,1,0:T(8,128)(2,1)} %param.11) | copy-start | bytes 786436
  17.3 138.7 %all-gather.2.cloned.1.call-start = ((), (), s32[]{:S(2)}) async-start(), calls=%async_computation | async-start | bytes 2228224 | tf_op jit(solution)/shard_map/all_gather | solution.py:59
Sparse Core Ops, SparseCore 0:
  17.4 89.7 all-reduce.2
  109.4 43.4 all-gather.1
where the time goes:
time: 167 us; the launch traced here: 166 us
  waiting for transfers between devices  89.4 us (54%)
  other arithmetic  45.5 us (27%)
  matrix products  15.3 us (9%)
  between operations  13.5 us (8%)
  local copies, waits for them, and re-layouts  1.97 us (1%)
    psum x1, waiting for transfers between devices, per_device(): cov_in, cov_out = lax.psum((local_in, local_out), 'dp')  88.7 us
    another operation x6, other arithmetic, damped_inverse(): factor = jnp.linalg.cholesky(damped)  23.8 us
    another operation x4, other arithmetic, damped_inverse(): jax.scipy.linalg.cho_solve((lower, True), identity)  19.8 us
    dot_general x2, matrix products, row_products(): lax.dot_general(left_rows, right_rows, (((1,), (1,)), ((), ())), preferre...  9.24 us
  transfers between devices with their start and end apart: 2, of which 1 were waited for; matrix products, arithmetic and copies ran while one was open for 30% of the time, Pallas kernels for 0%

commit v1 on v0

v1 whole, which is shorter than its diff:
```python
import functools

import jax
import jax.numpy as jnp
from jax import lax
from jax.experimental import pallas as pl
from jax.experimental.pallas import tpu as pltpu
from jax.sharding import Mesh, PartitionSpec as P

R = 64
LEN = 128
PAIR = 2 * R
DAMPING = 0.1
STEP = 512

F32 = jnp.float32
BF16 = jnp.bfloat16
MIB = 1024 * 1024


def dot(a, b, dims, precision=None):
    return lax.dot_general(a, b, (dims, ((), ())), precision=precision, preferred_element_type=F32)


NN = ((1,), (0,))
NT = ((1,), (1,))
TN = ((0,), (0,))


def statistics_kernel(core_ref, x_ref, w_ref, outs_ref, keep_cov, send_cov, keep_mom, send_mom, total):
    step = pl.program_id(0)
    term = dot(x_ref[...], w_ref[...], NT)

    @pl.when(step == 0)
    def _():
        total[...] = term

    @pl.when(step > 0)
    def _():
        total[...] += term

    @pl.when(step == pl.num_programs(0) - 1)
    def _():
        first = core_ref[0] == 0
        acts = total[...].astype(BF16)
        outs = outs_ref[...]
        low = lax.broadcasted_iota(jnp.int32, (R, PAIR), 1) < R
        cov_in = dot(acts, acts, TN)
        cov_out = dot(outs, outs, NT)
        cov0 = jnp.where(low, cov_in[:R], pltpu.roll(cov_out[:R], R, 1))
        cov1 = jnp.where(low, pltpu.roll(cov_in[R:], R, 1), cov_out[R:])
        keep_cov[...] = jnp.where(first, cov0, cov1)
        send_cov[...] = jnp.where(first, cov1, cov0)
        for pair in range(acts.shape[0] // LEN // 2):
            blocks = []
            for seq in (2 * pair, 2 * pair + 1):
                rows = slice(seq * LEN, (seq + 1) * LEN)
                blocks.append(dot(outs[:, rows], acts[rows], NN) * (1.0 / LEN))
            mom0 = jnp.where(low, blocks[0][:R], pltpu.roll(blocks[1][:R], R, 1))
            mom1 = jnp.where(low, pltpu.roll(blocks[0][R:], R, 1), blocks[1][R:])
            lanes = slice(pair * PAIR, (pair + 1) * PAIR)
            keep_mom[:, lanes] = jnp.where(first, mom0, mom1)
            send_mom[:, lanes] = jnp.where(first, mom1, mom0)


def statistics(core, layer_input, in_flat, outs):
    tokens, width = layer_input.shape
    seqs = tokens // LEN
    cov = jax.ShapeDtypeStruct((R, PAIR), F32)
    mom = jax.ShapeDtypeStruct((R, seqs * R), F32)
    whole = lambda shape: pl.BlockSpec(shape, lambda k: (0, 0))
    return pl.pallas_call(
        statistics_kernel,
        grid=(width // STEP,),
        in_specs=[
            pl.BlockSpec(memory_space=pltpu.SMEM),
            pl.BlockSpec((tokens, STEP), lambda k: (0, k)),
            pl.BlockSpec((PAIR, STEP), lambda k: (0, k)),
            whole(outs.shape),
        ],
        out_specs=[whole(cov.shape), whole(cov.shape), whole(mom.shape), whole(mom.shape)],
        out_shape=[cov, cov, mom, mom],
        scratch_shapes=[pltpu.VMEM((tokens, PAIR), F32)],
        compiler_params=pltpu.CompilerParams(vmem_limit_bytes=16 * MIB),
        cost_estimate=pl.CostEstimate(
            flops=2 * tokens * width * PAIR, bytes_accessed=2 * tokens * width, transcendentals=0
        ),
        name="statistics",
    )(core, layer_input, in_flat, outs)


def invert_pair(work):
    row = lax.broadcasted_iota(jnp.int32, (R, PAIR), 0)
    lane = lax.broadcasted_iota(jnp.int32, (R, PAIR), 1)
    low = lane < R
    column = jnp.where(low, lane, lane - R)
    for k in range(R):
        col = jnp.where(low, work[:, k : k + 1], work[:, R + k : R + k + 1])
        here = column[:1] == k
        pivot = jnp.where(here, 1.0, work[k : k + 1]) / col[k : k + 1]
        col = jnp.where(row == k, -1.0, col)
        work = jnp.where((row == k) | (column == k), 0.0, work) - col * pivot
    return work


def precondition_kernel(total_tokens, cov_ref, keep_ref, recv_ref, out_ref, inv_ref, flat_ref):
    row = lax.broadcasted_iota(jnp.int32, (R, PAIR), 0)
    lane = lax.broadcasted_iota(jnp.int32, (R, PAIR), 1)
    low = lane < R
    column = jnp.where(low, lane, lane - R)
    cov = cov_ref[...] / total_tokens
    diagonal = jnp.where(row == column, cov, 0.0)
    trace_in = jnp.sum(jnp.where(low, diagonal, 0.0), keepdims=True)
    trace_out = jnp.sum(jnp.where(low, 0.0, diagonal), keepdims=True)
    shift = jnp.where(low, trace_in, trace_out) * (DAMPING / R)
    inv = invert_pair(cov + jnp.where(row == column, shift, 0.0))
    inv_ref[...] = inv
    half = R // 2
    left = jnp.concatenate(
        [inv_ref[pl.ds(0, half, stride=2), :], inv_ref[pl.ds(1, half, stride=2), :]], axis=0
    )
    left = pltpu.roll(left, R, 1)[:, :R]
    moments = jnp.concatenate([keep_ref[...], recv_ref[...]], axis=1)
    mixed = dot(left, moments, NN, lax.Precision.HIGHEST)
    pairs = moments.shape[1] // PAIR
    stack = jnp.concatenate(
        [
            jnp.concatenate(
                [mixed[:half, j * PAIR : (j + 1) * PAIR], mixed[half:, j * PAIR : (j + 1) * PAIR]], axis=1
            )
            for j in range(pairs)
        ],
        axis=0,
    )
    zero = jnp.zeros((R, PAIR), F32)
    at_low = jnp.where(low, inv, 0.0)
    at_high = pltpu.roll(at_low, R, 1)
    right = jnp.concatenate(
        [
            jnp.concatenate([at_low, zero], axis=1),
            jnp.concatenate([zero, at_low], axis=1),
            jnp.concatenate([at_high, zero], axis=1),
            jnp.concatenate([zero, at_high], axis=1),
        ],
        axis=0,
    )
    done = dot(stack, right, NN, lax.Precision.HIGHEST)
    for j in range(pairs):
        rows = done[j * half : (j + 1) * half]
        flat_ref[(2 * j) * half : (2 * j + 1) * half, :] = rows[:, :PAIR]
        flat_ref[(2 * j + 1) * half : (2 * j + 2) * half, :] = rows[:, PAIR:]
    for k in range(half):
        out_ref[:, k * PAIR : (k + 1) * PAIR] = flat_ref[pl.ds(k, 2 * pairs, stride=half), :].astype(BF16)


def precondition(cov, keep_mom, recv_mom, total_tokens):
    seqs = 2 * keep_mom.shape[1] // R
    return pl.pallas_call(
        functools.partial(precondition_kernel, total_tokens),
        in_specs=[pl.BlockSpec(memory_space=pltpu.VMEM)] * 3,
        out_specs=pl.BlockSpec(memory_space=pltpu.VMEM),
        out_shape=jax.ShapeDtypeStruct((seqs, R * R), BF16),
        scratch_shapes=[pltpu.VMEM((R, PAIR), F32), pltpu.VMEM((seqs * R // 2, PAIR), F32)],
        compiler_params=pltpu.CompilerParams(vmem_limit_bytes=16 * MIB),
        name="precondition",
    )(cov, keep_mom, recv_mom)


def scores_kernel(core_ref, flat_ref, mine_ref, other_ref, out_ref):
    first = core_ref[0] == 0
    flat = flat_ref[...]
    mine = dot(mine_ref[...], flat, NT)
    other = dot(other_ref[...], flat, NT)
    low = jnp.where(first, mine, other)
    high = jnp.where(first, other, mine)
    groups = []
    for at in range(0, mine.shape[0], 8):
        groups += [low[at : at + 8], high[at : at + 8]]
    out_ref[...] = jnp.concatenate(groups, axis=0).T


def score(core, flat, mine, other):
    queries = mine.shape[0] + other.shape[0]
    return pl.pallas_call(
        scores_kernel,
        in_specs=[pl.BlockSpec(memory_space=pltpu.SMEM)] + [pl.BlockSpec(memory_space=pltpu.VMEM)] * 3,
        out_specs=pl.BlockSpec(memory_space=pltpu.VMEM),
        out_shape=jax.ShapeDtypeStruct((flat.shape[0], queries), F32),
        compiler_params=pltpu.CompilerParams(vmem_limit_bytes=32 * MIB),
        name="scores",
    )(core, flat, mine, other)


def per_device(layer_input, out_grads, in_proj, out_proj, queries):
    local_tokens = layer_input.shape[0]
    chips = lax.axis_size("chip")
    core = lax.axis_index("core").astype(jnp.int32)
    core_arg = core.reshape(1)
    swap = [(0, 1), (1, 0)]
    entries = R * R
    column = lax.all_gather(queries, "chip", axis=0, tiled=True)
    outs = jnp.einsum("mrk,tmk->mrt", out_proj, out_grads, preferred_element_type=F32).astype(BF16)
    keep_cov, send_cov, keep_mom, send_mom = statistics(
        core_arg, layer_input, in_proj.reshape(PAIR, in_proj.shape[2]), outs.reshape(PAIR, local_tokens)
    )
    cov = keep_cov + lax.ppermute(send_cov, "core", swap)
    recv_mom = lax.ppermute(send_mom, "core", swap)
    distance = 1
    while distance < chips:
        cov = cov + lax.ppermute(cov, "chip", [(i, i ^ distance) for i in range(chips)])
        distance *= 2
    flat = precondition(cov, keep_mom, recv_mom, local_tokens * chips * 2)
    mine = lax.dynamic_slice(column, (0, core * entries), (column.shape[0], entries))
    theirs = lax.dynamic_slice(column, (0, (1 - core) * entries), (column.shape[0], entries))
    other = lax.ppermute(theirs, "core", swap)
    partial = score(core_arg, flat, mine, other)
    seqs = local_tokens // LEN
    return partial[:seqs] + lax.ppermute(partial[seqs:], "core", swap)


def solution(mesh):
    parts, dp = mesh.devices.shape
    grid = Mesh(mesh.devices.reshape(parts, dp // 2, 2), ("parts", "chip", "core"))
    split = ("parts", "chip", "core")
    return jax.shard_map(
        per_device,
        mesh=grid,
        in_specs=(P(split, None), P(split, None, None), P(), P(), P(split, None)),
        out_specs=P(split, None),
        check_vma=False,
    )
```

time: 167 us -> 96.2 us (0.58)
  other arithmetic: 45.5 us -> 0.62 us
  waiting for transfers between devices: 89.4 us -> 58.9 us
  Pallas kernels: 0 us -> 12.2 us
  matrix products: 15.3 us -> 3.63 us
  local copies, waits for them, and re-layouts: 1.97 us -> 4.66 us
  starting transfers between devices: 0.04 us -> 2.53 us
    psum x1 -> x0, waiting for transfers between devices: 88.7 us -> none  [per_device(): cov_in, cov_out = lax.psum((local_in, local_out), 'dp')]
    all_gather x1, waiting for transfers between devices: 0.02 us -> 45.1 us  [per_device(): column = lax.all_gather(queries, 'chip', axis=0, tiled=True)]
    another operation x10 -> x0, other arithmetic: 43.5 us -> none  [the longest x6 23.8 us: damped_inverse(): factor = jnp.linalg.cholesky(damped)]
    ppermute x0 -> x7, waiting for transfers between devices: none -> 13.1 us  [the longest x3 11.2 us: per_device(): lax.ppermute(cov, 'chip', [(i, i ^ distance) for i in range(chips)])]
    pallas_call x0 -> x3, Pallas kernels: none -> 12.2 us  [the longest x1 6.6 us: precondition(): pl.pallas_call(functools.partial(precondition_kernel, total_tokens), in_s...]
    dot_general x8 -> x1, matrix products: 14.2 us -> 3.63 us  [per_device(): jnp.einsum('mrk,tmk->mrt', out_proj, out_grads, preferred_element_type=F32)]
    ppermute x0 -> x7, starting transfers between devices: none -> 2.52 us  [the longest x3 1.78 us: per_device(): lax.ppermute(cov, 'chip', [(i, i ^ distance) for i in range(chips)])]
    unnamed x7 -> x6, local copies, waits for them, and re-layouts: 1.28 us -> 3.38 us
  transfers between devices with their start and end apart: 2 -> 8, of which waited for: 1 -> 6; matrix products, arithmetic and copies ran while one was open for 30% -> 4% of each run, Pallas kernels for 0% -> 12%
where the time goes in v1:
time: 96.2 us; the launch traced here: 96 us
  waiting for transfers between devices  58.9 us (61%)
  between operations  13.5 us (14%)
  Pallas kernels  12.2 us (13%)
  local copies, waits for them, and re-layouts  4.66 us (5%)
  matrix products  3.63 us (4%)
  starting transfers between devices  2.53 us (3%)
    all_gather x1, waiting for transfers between devices, per_device(): column = lax.all_gather(queries, 'chip', axis=0, tiled=True)  45.1 us
    ppermute x3, waiting for transfers between devices, per_device(): lax.ppermute(cov, 'chip', [(i, i ^ distance) for i in range(chips)])  11.2 us
    pallas_call x1, Pallas kernels, precondition(): pl.pallas_call(functools.partial(precondition_kernel, total_tokens), in_s...  6.6 us
    pallas_call x1, Pallas kernels, statistics(): pl.pallas_call(statistics_kernel, grid=(width // STEP,), in_specs=[pl.Blo...  5.11 us
    dot_general x1, matrix products, per_device(): jnp.einsum('mrk,tmk->mrt', out_proj, out_grads, preferred_element_type=F32)  3.63 us
    unnamed x6, local copies, waits for them, and re-layouts  3.38 us
  transfers between devices with their start and end apart: 8, of which 6 were waited for; matrix products, arithmetic and copies ran while one was open for 4% of the time, Pallas kernels for 12%

profile of v1, /device:TPU:0, one launch (start us, length us, event | category | flops | bytes accessed | tf_op | source)
XLA Modules:
  0.0 96.0 jit_solution(15019136509565542191)
XLA Ops:
  6.5 0.0 copy-start
  6.5 0.0 copy-start.2
  6.5 0.0 all-gather.2.cloned.1.call-start
  6.5 0.7 all-gather.2.cloned.1.call-update
  7.3 45.1 %all-gather.2.cloned.1.call-done = bf16[64,8192]{1,0:T(8,128)(2,1)} async-done(((bf16[8,8192]{1,0:T(8,128)(2,1)}), bf16[64,8192]{1,0:T(8,128)(2,1)}) %all-gather.2.cloned.1.call-update) | async-done | bytes 1048592 | tf_op jit(solution)/shard_map/all_gather | solution.py:201
  52.4 1.3 %constant_dynamic-slice_fusion = (bf16[64,4096]{1,0:T(8,128)(2,1)S(1)}, bf16[64,4096]{1,0:T(8,128)(2,1)S(1)}) fusion(bf16[64,8192]{1,0:T(8,128)(2,1)} %all-gather.2.cloned.1.call-done, s32[]{:T(128)S(6)} %select_n.7, s32[]{:T(128)S(6)} %select_n.6), kind=kLoop, calls=%fused_computation.4 | loop fusion | bytes 2097160 | tf_op jit(solution)/shard_map/dynamic_slice | solution.py:214
  53.7 0.1 collective-permute-start.5
  53.7 0.0 copy-done
  53.7 3.6 %fusion.2 = bf16[2,64,1024]{2,1,0:T(8,128)(2,1)S(1)} fusion(bf16[2,64,1024]{2,1,0:T(8,128)(2,1)S(1)} %copy-done, bf16[1024,2,1024]{2,1,0:T(2,128)(2,1)} %param.6), kind=kOutput, calls=%fused_computation.2 | convolution fusion | flops 268566528 | bytes 4718592 | tf_op jit(solution)/shard_map/mrk,tmk->mrt/dot_general | solution.py:202
  57.4 0.0 copy-done.2
  57.4 0.0 copy-start.1
  57.4 3.4 %copy-done.1 = bf16[1024,4096]{1,0:T(8,128)(2,1)S(1)} copy-done((bf16[1024,4096]{1,0:T(8,128)(2,1)S(1)}, bf16[1024,4096]{1,0:T(8,128)(2,1)}, u32[]{:S(2)}) %copy-start.1) | copy-done | bytes 8388632
  60.8 5.1 %statistics.1 = (f32[64,128]{1,0:T(8,128)S(1)}, f32[64,128]{1,0:T(8,128)S(1)}, f32[64,512]{1,0:T(8,128)S(1)}, f32[64,512]{1,0:T(8,128)S(1)}) custom-call(s32[1]{0:T(128)} %bitcast.core_ref, bf16[1024,4096]{1,0:T(8,128)(2,1)S(1)} %copy-done.1, bf16[128,4096]{1,0:T(8,128)(2,1)S(1)} %bitcast.4, bf16[128,1024]{1,0:T(8,128)(2,1)S(1)} %bitcast.5), custom_call_target="tpu_custom_call" | custom-call | flops 1073741824 | bytes 8388608 | tf_op jit(solution)/shard_map/statistics/pallas_call | solution.py:72
  65.9 0.6 collective-permute-start
  66.4 0.1 collective-permute-start.4
  66.5 0.8 collective-permute-done
  67.3 0.6 collective-permute-start.1
  67.9 3.4 %collective-permute-done.1 = f32[64,128]{1,0:T(8,128)S(1)} collective-permute-done((f32[64,128]{1,0:T(8,128)S(1)}, f32[64,128]{1,0:T(8,128)S(1)}, u32[]{:S(2)}, u32[]{:S(2)}) %collective-permute-start.1) | collective-permute-done | bytes 32800 | tf_op jit(solution)/shard_map/ppermute | solution.py:210
  71.2 0.5 collective-permute-start.2
  71.7 3.4 %collective-permute-done.2 = f32[64,128]{1,0:T(8,128)S(1)} collective-permute-done((f32[64,128]{1,0:T(8,128)S(1)}, f32[64,128]{1,0:T(8,128)S(1)}, u32[]{:S(2)}, u32[]{:S(2)}) %collective-permute-start.2) | collective-permute-done | bytes 32800 | tf_op jit(solution)/shard_map/ppermute | solution.py:210
  75.1 0.7 collective-permute-start.3
  75.8 4.4 %collective-permute-done.3 = f32[64,128]{1,0:T(8,128)S(1)} collective-permute-done((f32[64,128]{1,0:T(8,128)S(1)}, f32[64,128]{1,0:T(8,128)S(1)}, u32[]{:S(2)}, u32[]{:S(2)}) %collective-permute-start.3) | collective-permute-done | bytes 32800 | tf_op jit(solution)/shard_map/ppermute | solution.py:210
  80.3 0.0 collective-permute-done.4.recv_ref
  80.3 6.6 %precondition.1.flat_ref = bf16[16,4096]{1,0:T(8,128)(2,1)S(1)} custom-call(f32[64,128]{1,0:T(8,128)S(1)} %add.24.cov_ref, f32[64,512]{1,0:T(8,128)S(1)} %get-tuple-element.11.keep_ref, f32[64,512]{1,0:T(8,128)S(1)} %collective-permute-done.4.recv_ref), custom_call_target="tpu_custom_call" | custom-call | tf_op jit(solution)/shard_map/precondition/pallas_call | solution.py:158
  86.9 0.0 collective-permute-done.5.other_ref
  86.9 0.5 scores.1
  87.4 0.0 collective-permute-start.6
  87.4 1.2 %collective-permute-done.6 = f32[8,128]{1,0:T(8,128)S(1)} collective-permute-done((f32[8,128]{1,0:T(8,128)S(1)}, f32[8,128]{1,0:T(8,128)S(1)}, u32[]{:S(2)}, u32[]{:S(2)}) %collective-permute-start.6) | collective-permute-done | bytes 4128 | tf_op jit(solution)/shard_map/ppermute | solution.py:218
  88.6 0.6 slice_add_fusion
  (5 shorter events, 0.0 us)
Async XLA Ops:
  6.5 47.2 %copy-start = (bf16[2,64,1024]{2,1,0:T(8,128)(2,1)S(1)}, bf16[2,64,1024]{2,1,0:T(8,128)(2,1)}, u32[]{:S(2)}) copy-start(bf16[2,64,1024]{2,1,0:T(8,128)(2,1)} %param.8) | copy-start | bytes 786436
  6.5 50.8 %copy-start.2 = (bf16[2,64,4096]{2,1,0:T(8,128)(2,1)S(1)}, bf16[2,64,4096]{2,1,0:T(8,128)(2,1)}, u32[]{:S(2)}) copy-start(bf16[2,64,4096]{2,1,0:T(8,128)(2,1)} %param.7) | copy-start | bytes 3145732
  6.5 45.8 %all-gather.2.cloned.1.call-start = ((), (), s32[]{:S(2)}) async-start(), calls=%async_computation | async-start | bytes 1179648 | tf_op jit(solution)/shard_map/all_gather | solution.py:201
  53.7 33.2 %collective-permute-start.5 = (bf16[64,4096]{1,0:T(8,128)(2,1)S(1)}, bf16[64,4096]{1,0:T(8,128)(2,1)S(1)}, u32[]{:S(2)}, u32[]{:S(2)}) collective-permute-start(bf16[64,4096]{1,0:T(8,128)(2,1)S(1)} %get-tuple-element.13), channel_id=1, source_target_pairs={{0,1},{1,0},{2,3},{3,2},{4,5},{5,4},{6,7},{7,6},{8,9},{9,8},{10,11... | collective-permute-start | bytes 1572872 | tf_op jit(solution)/shard_map/ppermute | solution.py:215
  57.4 3.4 %copy-start.1 = (bf16[1024,4096]{1,0:T(8,128)(2,1)S(1)}, bf16[1024,4096]{1,0:T(8,128)(2,1)}, u32[]{:S(2)}) copy-start(bf16[1024,4096]{1,0:T(8,128)(2,1)} %x_ref.1) | copy-start | bytes 25165828
  65.9 1.4 %collective-permute-start = (f32[64,128]{1,0:T(8,128)S(1)}, f32[64,128]{1,0:T(8,128)S(1)}, u32[]{:S(2)}, u32[]{:S(2)}) collective-permute-start(f32[64,128]{1,0:T(8,128)S(1)} %get-tuple-element.10), channel_id=1, source_target_pairs={{0,1},{1,0},{2,3},{3,2},{4,5},{5,4},{6,7},{7,6},{8,9},{9,8},{10,11... | collective-permute-start | bytes 98312 | tf_op jit(solution)/shard_map/ppermute | solution.py:206
  66.4 13.8 %collective-permute-start.4 = (f32[64,512]{1,0:T(8,128)S(1)}, f32[64,512]{1,0:T(8,128)S(1)}, u32[]{:S(2)}, u32[]{:S(2)}) collective-permute-start(f32[64,512]{1,0:T(8,128)S(1)} %get-tuple-element.12), channel_id=1, source_target_pairs={{0,1},{1,0},{2,3},{3,2},{4,5},{5,4},{6,7},{7,6},{8,9},{9,8},{10,11... | collective-permute-start | bytes 393224 | tf_op jit(solution)/shard_map/ppermute | solution.py:207
  67.3 3.9 %collective-permute-start.1 = (f32[64,128]{1,0:T(8,128)S(1)}, f32[64,128]{1,0:T(8,128)S(1)}, u32[]{:S(2)}, u32[]{:S(2)}) collective-permute-start(f32[64,128]{1,0:T(8,128)S(1)} %add.21), channel_id=1, source_target_pairs={{0,2},{2,0},{4,6},{6,4},{8,10},{10,8},{12,14},{14,12},{1,3},{3,1},... | collective-permute-start | bytes 98312 | tf_op jit(solution)/shard_map/ppermute | solution.py:210
  71.2 3.9 %collective-permute-start.2 = (f32[64,128]{1,0:T(8,128)S(1)}, f32[64,128]{1,0:T(8,128)S(1)}, u32[]{:S(2)}, u32[]{:S(2)}) collective-permute-start(f32[64,128]{1,0:T(8,128)S(1)} %add.22), channel_id=1, source_target_pairs={{0,4},{2,6},{4,0},{6,2},{8,12},{10,14},{12,8},{14,10},{1,5},{3,7},... | collective-permute-start | bytes 98312 | tf_op jit(solution)/shard_map/ppermute | solution.py:210
  75.1 5.1 %collective-permute-start.3 = (f32[64,128]{1,0:T(8,128)S(1)}, f32[64,128]{1,0:T(8,128)S(1)}, u32[]{:S(2)}, u32[]{:S(2)}) collective-permute-start(f32[64,128]{1,0:T(8,128)S(1)} %add.23), channel_id=1, source_target_pairs={{0,8},{2,10},{4,12},{6,14},{8,0},{10,2},{12,4},{14,6},{1,9},{3,11}... | collective-permute-start | bytes 98312 | tf_op jit(solution)/shard_map/ppermute | solution.py:210
  87.4 1.2 %collective-permute-start.6 = (f32[8,128]{1,0:T(8,128)S(1)}, f32[8,128]{1,0:T(8,128)S(1)}, u32[]{:S(2)}, u32[]{:S(2)}) collective-permute-start(f32[8,128]{1,0:T(8,128)S(1)} %slice.9), channel_id=1, source_target_pairs={{0,1},{1,0},{2,3},{3,2},{4,5},{5,4},{6,7},{7,6},{8,9},{9,8},{10,11... | collective-permute-start | bytes 12296 | tf_op jit(solution)/shard_map/ppermute | solution.py:218
Sparse Core Ops, SparseCore 0:
  9.5 42.8 all-gather.1

commit v2 on v0

v2 whole, which is shorter than its diff:
```python
import functools

import jax
import jax.numpy as jnp
from jax import lax
from jax.experimental import pallas as pl
from jax.experimental.pallas import tpu as pltpu
from jax.sharding import PartitionSpec as P

R = 64
LEN = 128
PAIR = 2 * R
DAMPING = 0.1
STEP = 512
BLOCK = 4
GROUP = 4

F32 = jnp.float32
BF16 = jnp.bfloat16
MIB = 1024 * 1024


def dot(a, b, dims, precision=None):
    return lax.dot_general(a, b, (dims, ((), ())), precision=precision, preferred_element_type=F32)


NN = ((1,), (0,))
NT = ((1,), (1,))
TN = ((0,), (0,))


def statistics_kernel(
    core_ref, x_hbm, w_hbm, outs_ref, keep_cov, send_cov, keep_mom, send_mom, x_buf, w_buf, total, x_sem, w_sem
):
    chunks = x_buf.shape[0]

    def x_copy(k):
        columns = pl.ds(pl.multiple_of(k * STEP, STEP), STEP)
        return pltpu.make_async_copy(x_hbm.at[:, columns], x_buf.at[k], x_sem.at[k])

    def w_copy(k):
        columns = pl.ds(pl.multiple_of(k * STEP, STEP), STEP)
        return pltpu.make_async_copy(w_hbm.at[:, columns], w_buf.at[k], w_sem.at[k])

    for k in range(chunks):
        w_copy(k).start()
        x_copy(k).start()
    total[...] = jnp.zeros_like(total)

    @pl.loop(0, chunks)
    def _(k):
        w_copy(k).wait()
        x_copy(k).wait()
        total[...] += dot(x_buf[k], w_buf[k], NT)

    first = core_ref[0] == 0
    acts = total[...].astype(BF16)
    outs = outs_ref[...]
    low = lax.broadcasted_iota(jnp.int32, (R, PAIR), 1) < R
    cov_in = dot(acts, acts, TN)
    cov_out = dot(outs, outs, NT)
    cov0 = jnp.where(low, cov_in[:R], pltpu.roll(cov_out[:R], R, 1))
    cov1 = jnp.where(low, pltpu.roll(cov_in[R:], R, 1), cov_out[R:])
    keep_cov[...] = jnp.where(first, cov0, cov1)
    send_cov[...] = jnp.where(first, cov1, cov0)
    for pair in range(acts.shape[0] // LEN // 2):
        blocks = []
        for seq in (2 * pair, 2 * pair + 1):
            rows = slice(seq * LEN, (seq + 1) * LEN)
            blocks.append(dot(outs[:, rows], acts[rows], NN) * (1.0 / LEN))
        mom0 = jnp.where(low, blocks[0][:R], pltpu.roll(blocks[1][:R], R, 1))
        mom1 = jnp.where(low, pltpu.roll(blocks[0][R:], R, 1), blocks[1][R:])
        lanes = slice(pair * PAIR, (pair + 1) * PAIR)
        keep_mom[:, lanes] = jnp.where(first, mom0, mom1)
        send_mom[:, lanes] = jnp.where(first, mom1, mom0)


def statistics(core, layer_input, in_flat, outs):
    tokens, width = layer_input.shape
    seqs = tokens // LEN
    chunks = width // STEP
    cov = jax.ShapeDtypeStruct((R, PAIR), F32)
    mom = jax.ShapeDtypeStruct((R, seqs * R), F32)
    vmem = pl.BlockSpec(memory_space=pltpu.VMEM)
    return pl.pallas_call(
        statistics_kernel,
        in_specs=[
            pl.BlockSpec(memory_space=pltpu.SMEM),
            pl.BlockSpec(memory_space=pl.ANY),
            pl.BlockSpec(memory_space=pl.ANY),
            vmem,
        ],
        out_specs=[vmem] * 4,
        out_shape=[cov, cov, mom, mom],
        scratch_shapes=[
            pltpu.VMEM((chunks, tokens, STEP), BF16),
            pltpu.VMEM((chunks, PAIR, STEP), BF16),
            pltpu.VMEM((tokens, PAIR), F32),
            pltpu.SemaphoreType.DMA((chunks,)),
            pltpu.SemaphoreType.DMA((chunks,)),
        ],
        compiler_params=pltpu.CompilerParams(vmem_limit_bytes=48 * MIB),
        cost_estimate=pl.CostEstimate(
            flops=2 * tokens * width * PAIR, bytes_accessed=2 * tokens * width, transcendentals=0
        ),
        name="statistics",
    )(core, layer_input, in_flat, outs)


def solve_block(p, rows):
    det = 1.0 / (p[0][0] * p[1][1] - p[0][1] * p[0][1])
    a, b, c = p[1][1] * det, -p[0][1] * det, p[0][0] * det
    t = [[a * p[0][j] + b * p[1][j], b * p[0][j] + c * p[1][j]] for j in (2, 3)]
    s22 = p[2][2] - p[0][2] * t[0][0] - p[1][2] * t[0][1]
    s23 = p[2][3] - p[0][2] * t[1][0] - p[1][2] * t[1][1]
    s33 = p[3][3] - p[0][3] * t[1][0] - p[1][3] * t[1][1]
    det = 1.0 / (s22 * s33 - s23 * s23)
    y0 = a * rows[0] + b * rows[1]
    y1 = b * rows[0] + c * rows[1]
    z2 = rows[2] - p[0][2] * y0 - p[1][2] * y1
    z3 = rows[3] - p[0][3] * y0 - p[1][3] * y1
    x2 = (s33 * z2 - s23 * z3) * det
    x3 = (s22 * z3 - s23 * z2) * det
    return [y0 - t[0][0] * x2 - t[1][0] * x3, y1 - t[0][1] * x2 - t[1][1] * x3, x2, x3]


def invert_pair(matrix):
    lane = lax.broadcasted_iota(jnp.int32, (8, PAIR), 1)
    row = lax.broadcasted_iota(jnp.int32, (8, PAIR), 0)
    column = lane % R
    base = lane - column
    work = [matrix[8 * g : 8 * g + 8] for g in range(R // 8)]
    for k in range(0, R, BLOCK):
        cols = [[jnp.take_along_axis(part, base + (k + j), axis=1) for j in range(BLOCK)] for part in work]
        home, at = k // 8, k % 8
        inside = (column >= k) & (column < k + BLOCK)
        pivots = [[cols[home][j][at + i : at + i + 1] for j in range(BLOCK)] for i in range(BLOCK)]
        rows = [
            jnp.where(
                inside[:1], jnp.where(column[:1] == k + i, 1.0, 0.0), work[home][at + i : at + i + 1]
            )
            for i in range(BLOCK)
        ]
        solved = solve_block(pivots, rows)
        for g in range(R // 8):
            part = jnp.where(inside, 0.0, work[g])
            col = cols[g]
            if g == home:
                block_row = (row >= at) & (row < at + BLOCK)
                part = jnp.where(block_row, 0.0, part)
                col = [
                    jnp.where(block_row, jnp.where(row == at + j, -1.0, 0.0), col[j]) for j in range(BLOCK)
                ]
            work[g] = part - (col[0] * solved[0] + col[1] * solved[1]) - (col[2] * solved[2] + col[3] * solved[3])
    return jnp.concatenate(work, axis=0)


def inverse_kernel(total_tokens, cov_ref, inv_ref):
    row = lax.broadcasted_iota(jnp.int32, (R, PAIR), 0)
    lane = lax.broadcasted_iota(jnp.int32, (R, PAIR), 1)
    low = lane < R
    column = jnp.where(low, lane, lane - R)
    cov = cov_ref[...]
    diagonal = jnp.where(row == column, cov, 0.0)
    trace_in = jnp.sum(jnp.where(low, diagonal, 0.0), keepdims=True)
    trace_out = jnp.sum(jnp.where(low, 0.0, diagonal), keepdims=True)
    scale = R / jnp.where(low, trace_in, trace_out)
    inv_ref[...] = invert_pair(cov * scale + jnp.where(row == column, DAMPING, 0.0)) * (scale * total_tokens)


def inverse(cov, total_tokens):
    vmem = pl.BlockSpec(memory_space=pltpu.VMEM)
    return pl.pallas_call(
        functools.partial(inverse_kernel, total_tokens),
        in_specs=[vmem],
        out_specs=vmem,
        out_shape=jax.ShapeDtypeStruct(cov.shape, F32),
        cost_estimate=pl.CostEstimate(flops=4 * 10**9, bytes_accessed=2**16, transcendentals=0),
        name="inverse",
    )(cov)


def scores_kernel(count, place_ref, inv_ref, *refs):
    moment_refs, shard_refs, (out_ref, flat_ref, part_ref) = refs[:count], refs[count:-3], refs[-3:]
    place = place_ref[0]
    upper = (place >> 1) & 1 == 1
    low = lax.broadcasted_iota(jnp.int32, (R, PAIR), 1) < R
    inv = inv_ref[...]
    tiles = R // 4
    even = [inv_ref[pl.ds(start, tiles, stride=2), :] for start in (0, R // 2)]
    odd = [inv_ref[pl.ds(start + 1, tiles, stride=2), :] for start in (0, R // 2)]
    left = jnp.concatenate([jnp.where(upper, even[1], even[0]), jnp.where(upper, odd[1], odd[0])], axis=0)
    left = pltpu.roll(left, R, 1)[:, :R]
    moments = jnp.concatenate([ref[...] for ref in moment_refs], axis=1)
    mixed = dot(left, moments, NN, lax.Precision.HIGHEST)
    pairs = moments.shape[1] // PAIR
    stack = jnp.concatenate(
        [
            jnp.concatenate(
                [mixed[:tiles, j * PAIR : (j + 1) * PAIR], mixed[tiles:, j * PAIR : (j + 1) * PAIR]], axis=1
            )
            for j in range(pairs)
        ],
        axis=0,
    )
    zero = jnp.zeros((R, PAIR), F32)
    at_low = jnp.where(low, inv, 0.0)
    at_high = pltpu.roll(at_low, R, 1)
    right = jnp.concatenate(
        [
            jnp.concatenate([at_low, zero], axis=1),
            jnp.concatenate([zero, at_low], axis=1),
            jnp.concatenate([at_high, zero], axis=1),
            jnp.concatenate([zero, at_high], axis=1),
        ],
        axis=0,
    )
    done = dot(stack, right, NN, lax.Precision.HIGHEST)
    for j in range(pairs):
        rows = done[j * tiles : (j + 1) * tiles]
        flat_ref[(2 * j) * tiles : (2 * j + 1) * tiles, :] = rows[:, :PAIR]
        flat_ref[(2 * j + 1) * tiles : (2 * j + 2) * tiles, :] = rows[:, PAIR:]
    flat = jnp.concatenate(
        [flat_ref[pl.ds(k, 2 * pairs, stride=tiles), :].astype(BF16) for k in range(tiles)], axis=1
    )
    part = dot(jnp.concatenate([ref[...] for ref in shard_refs], axis=0), flat, NT)
    group = part_ref.shape[1]
    for distance in range(part_ref.shape[0]):
        part_ref[place ^ distance] = part[distance * group : (distance + 1) * group]
    out_ref[...] = part_ref[...].reshape(part.shape).T


def score(place, inv, moments, shards, group):
    seqs = sum(part.shape[1] for part in moments) // R
    queries = sum(shard.shape[0] for shard in shards)
    vmem = pl.BlockSpec(memory_space=pltpu.VMEM)
    return pl.pallas_call(
        functools.partial(scores_kernel, len(moments)),
        in_specs=[pl.BlockSpec(memory_space=pltpu.SMEM), vmem] + [vmem] * (len(moments) + len(shards)),
        out_specs=vmem,
        out_shape=jax.ShapeDtypeStruct((seqs, queries), F32),
        scratch_shapes=[
            pltpu.VMEM((seqs * R // 4, PAIR), F32),
            pltpu.VMEM((queries // group, group, seqs), F32),
        ],
        compiler_params=pltpu.CompilerParams(vmem_limit_bytes=32 * MIB),
        name="scores",
    )(place, inv, *moments, *shards)


def exchange(value, distance):
    return lax.ppermute(value, "dp", [(i, i ^ distance) for i in range(lax.axis_size("dp"))])


def per_device(layer_input, out_grads, in_proj, out_proj, queries):
    local_tokens = layer_input.shape[0]
    local_queries = queries.shape[0]
    devices = lax.axis_size("dp")
    place = lax.axis_index("dp").astype(jnp.int32)
    module = place & 1
    quarter = queries.shape[1] // GROUP

    def block_for(distance):
        target = place ^ distance
        block = ((target & 1) << 1) | ((target >> 1) & 1)
        return lax.dynamic_slice_in_dim(queries, block * quarter, quarter, 1)

    shard = jnp.concatenate(
        [block_for(0)] + [exchange(block_for(distance), distance) for distance in range(1, GROUP)], axis=0
    )
    outs = jnp.einsum("tmk,mrk->tmr", out_grads, out_proj, preferred_element_type=F32).astype(BF16)
    outs = outs.reshape(local_tokens, PAIR).T
    shard, outs = lax.optimization_barrier((shard, outs))
    shards = [shard] + [exchange(shard, distance) for distance in range(GROUP, devices, GROUP)]
    keep_cov, send_cov, keep_mom, send_mom = statistics(
        module.reshape(1), layer_input, in_proj.reshape(PAIR, in_proj.shape[2]), outs
    )
    cov = keep_cov + exchange(send_cov, 1)
    recv_mom = exchange(send_mom, 1)
    cov = cov + exchange(cov, 2)
    moments = [keep_mom, recv_mom, exchange(keep_mom, 2), exchange(recv_mom, 2)]
    cov, shards = lax.optimization_barrier((cov, shards))
    cov = cov + sum(exchange(cov, distance) for distance in range(GROUP, devices, GROUP))
    partial = score(place.reshape(1), inverse(cov, local_tokens * devices), moments, shards, local_queries)
    seqs = local_tokens // LEN
    result = partial[:seqs]
    for distance in range(1, GROUP):
        result = result + exchange(partial[distance * seqs : (distance + 1) * seqs], distance)
    return result


def solution(mesh):
    return jax.shard_map(
        per_device,
        mesh=mesh,
        in_specs=(
            P(("parts", "dp"), None),
            P(("parts", "dp"), None, None),
            P(),
            P(),
            P(("parts", "dp"), None),
        ),
        out_specs=P(("parts", "dp"), None),
        check_vma=False,
    )
```

time: 167 us -> 43.8 us (0.26)
  waiting for transfers between devices: 89.4 us -> 7.99 us
  other arithmetic: 45.5 us -> 1.23 us
  starting transfers between devices: 0.04 us -> 18.4 us
  between operations: 13.5 us -> 0.11 us
  matrix products: 15.3 us -> 3.62 us
  Pallas kernels: 0 us -> 10.5 us
    psum x1 -> x0, waiting for transfers between devices: 88.7 us -> none  [per_device(): cov_in, cov_out = lax.psum((local_in, local_out), 'dp')]
    another operation x10 -> x0, other arithmetic: 43.5 us -> none  [the longest x6 23.8 us: damped_inverse(): factor = jnp.linalg.cholesky(damped)]
    ppermute x0 -> x17, starting transfers between devices: none -> 18.4 us  [exchange(): lax.ppermute(value, 'dp', [(i, i ^ distance) for i in range(lax.axis_size...]
    dot_general x8 -> x1, matrix products: 14.2 us -> 3.62 us  [per_device(): jnp.einsum('tmk,mrk->tmr', out_grads, out_proj, preferred_element_type=F32)]
    pallas_call x0 -> x3, Pallas kernels: none -> 10.5 us  [the longest x1 5.31 us: statistics(): pl.pallas_call(statistics_kernel, in_specs=[pl.BlockSpec(memory_space=plt...]
    ppermute x0 -> x17, waiting for transfers between devices: none -> 7.99 us  [exchange(): lax.ppermute(value, 'dp', [(i, i ^ distance) for i in range(lax.axis_size...]
  transfers between devices with their start and end apart: 2 -> 17, of which waited for: 1 -> 6; matrix products, arithmetic and copies ran while one was open for 30% -> 10% of each run, Pallas kernels for 0% -> 21%
where the time goes in v2:
time: 43.8 us; the launch traced here: 43.5 us
  starting transfers between devices  18.4 us (42%)
  Pallas kernels  10.5 us (24%)
  waiting for transfers between devices  7.99 us (18%)
  matrix products  3.62 us (8%)
  local copies, waits for them, and re-layouts  1.69 us (4%)
  other arithmetic  1.23 us (3%)
    ppermute x17, starting transfers between devices, exchange(): lax.ppermute(value, 'dp', [(i, i ^ distance) for i in range(lax.axis_size...  18.4 us
    ppermute x17, waiting for transfers between devices, exchange(): lax.ppermute(value, 'dp', [(i, i ^ distance) for i in range(lax.axis_size...  7.99 us
    pallas_call x1, Pallas kernels, statistics(): pl.pallas_call(statistics_kernel, in_specs=[pl.BlockSpec(memory_space=plt...  5.31 us
    pallas_call x1, Pallas kernels, inverse(): pl.pallas_call(functools.partial(inverse_kernel, total_tokens), in_specs=...  3.89 us
    dot_general x1, matrix products, per_device(): jnp.einsum('tmk,mrk->tmr', out_grads, out_proj, preferred_element_type=F32)  3.62 us
    pallas_call x1, Pallas kernels, score(): pl.pallas_call(functools.partial(scores_kernel, len(moments)), in_specs=[...  1.3 us
    dynamic_slice x1, local copies, waits for them, and re-layouts, block_for(): return lax.dynamic_slice_in_dim(queries, block * quarter, quarter, 1)  0.92 us
  transfers between devices with their start and end apart: 17, of which 6 were waited for; matrix products, arithmetic and copies ran while one was open for 10% of the time, Pallas kernels for 21%

profile of v2, /device:TPU:0, one launch (start us, length us, event | category | flops | bytes accessed | tf_op | source)
XLA Modules:
  0.0 43.5 jit_solution(2982666761504941524)
XLA Ops:
  0.0 0.0 copy-start
  0.0 0.0 copy-start.1
  0.0 0.9 %constant_dynamic-slice_fusion.3 = (bf16[8,2048]{1,0:T(8,128)(2,1)S(1)}, bf16[8,2048]{1,0:T(8,128)(2,1)S(1)}, bf16[8,2048]{1,0:T(8,128)(2,1)S(1)}, bf16[8,2048]{1,0:T(8,128)(2,1)S(1)}) fusion(bf16[8,8192]{1,0:T(8,128)(2,1)} %param.9, s32[]{:T(128)S(6)} %select_n.12, s32[]{:T(128)S(6)} %select_n.13, s32[]{:T(128)S(6)} %select_n.15, s32[]{:T(128)S(6)} %select_n.14), kind=kLoop, calls=%fused_computation.11 | loop fusion | bytes 262160 | tf_op jit(solution)/shard_map/dynamic_slice | solution.py:266
  0.9 0.5 %collective-permute-start = (bf16[8,2048]{1,0:T(8,128)(2,1)S(1)}, bf16[8,2048]{1,0:T(8,128)(2,1)S(1)}, u32[]{:S(2)}, u32[]{:S(2)}) collective-permute-start(bf16[8,2048]{1,0:T(8,128)(2,1)S(1)} %get-tuple-element.28), channel_id=1, source_target_pairs={{0,1},{1,0},{2,3},{3,2},{4,5},{5,4},{6,7},{7,6},{8,9},{9,8},{10,11... | collective-permute-start | bytes 98312 | tf_op jit(solution)/shard_map/ppermute | solution.py:252
  1.4 2.6 %collective-permute-start.1 = (bf16[8,2048]{1,0:T(8,128)(2,1)S(1)}, bf16[8,2048]{1,0:T(8,128)(2,1)S(1)}, u32[]{:S(2)}, u32[]{:S(2)}) collective-permute-start(bf16[8,2048]{1,0:T(8,128)(2,1)S(1)} %get-tuple-element.30), channel_id=1, source_target_pairs={{0,2},{1,3},{2,0},{3,1},{4,6},{5,7},{6,4},{7,5},{8,10},{9,11},{10,... | collective-permute-start | bytes 98312 | tf_op jit(solution)/shard_map/ppermute | solution.py:252
  4.0 0.1 collective-permute-start.2
  4.1 0.0 copy-done
  4.1 3.6 %fusion.2 = bf16[2,64,1024]{2,1,0:T(8,128)(2,1)S(1)} fusion(bf16[2,64,1024]{2,1,0:T(8,128)(2,1)S(1)} %copy-done, bf16[1024,2,1024]{2,1,0:T(2,128)(2,1)} %param.6), kind=kOutput, calls=%fused_computation.2 | convolution fusion | flops 268566528 | bytes 4718592 | tf_op jit(solution)/shard_map/tmk,mrk->tmr/dot_general | solution.py:271
  7.7 0.0 collective-permute-done
  7.8 0.0 collective-permute-done.1
  7.8 0.0 collective-permute-done.2
  7.8 1.8 %collective-permute-start.5 = (bf16[32,2048]{1,0:T(8,128)(2,1)S(1)}, bf16[32,2048]{1,0:T(8,128)(2,1)S(1)}, u32[]{:S(2)}, u32[]{:S(2)}) collective-permute-start(bf16[32,2048]{1,0:T(8,128)(2,1)S(1)} %pad_maximum_fusion.refs_4_), channel_id=1, source_target_pairs={{0,4},{1,5},{2,6},{3,7},{4,0},{5,1},{6,2},{7,3},{8,12},{9,13},{10,... | collective-permute-start | bytes 393224 | tf_op jit(solution)/shard_map/ppermute | solution.py:252
  9.6 2.6 %collective-permute-start.6 = (bf16[32,2048]{1,0:T(8,128)(2,1)S(1)}, bf16[32,2048]{1,0:T(8,128)(2,1)S(1)}, u32[]{:S(2)}, u32[]{:S(2)}) collective-permute-start(bf16[32,2048]{1,0:T(8,128)(2,1)S(1)} %pad_maximum_fusion.refs_4_), channel_id=1, source_target_pairs={{0,8},{1,9},{2,10},{3,11},{4,12},{5,13},{6,14},{7,15},{8,0},{9,1},... | collective-permute-start | bytes 393224 | tf_op jit(solution)/shard_map/ppermute | solution.py:252
  12.2 0.0 collective-permute-start.7
  12.2 0.0 copy-done.1
  12.2 5.3 %statistics.1 = (f32[64,128]{1,0:T(8,128)S(1)}, f32[64,128]{1,0:T(8,128)S(1)}, f32[64,512]{1,0:T(8,128)S(1)}, f32[64,512]{1,0:T(8,128)S(1)}) custom-call(s32[1]{0:T(128)} %bitcast.1.core_ref, bf16[1024,4096]{1,0:T(8,128)(2,1)} %x_hbm.1, bf16[128,4096]{1,0:T(8,128)(2,1)S(1)} %bitcast.9, bf16[128,1024]{1,0:T(8,128)(2,1)S(1)} %bitcast.10), custom_call_target="tpu_custom_call" | custom-call | flops 1073741824 | bytes 8388608 | tf_op jit(solution)/shard_map/statistics/pallas_call | solution.py:85
  17.6 0.1 collective-permute-start.11
  17.6 0.5 %collective-permute-start.3 = (f32[64,128]{1,0:T(8,128)S(1)}, f32[64,128]{1,0:T(8,128)S(1)}, u32[]{:S(2)}, u32[]{:S(2)}) collective-permute-start(f32[64,128]{1,0:T(8,128)S(1)} %get-tuple-element.18), channel_id=1, source_target_pairs={{0,1},{1,0},{2,3},{3,2},{4,5},{5,4},{6,7},{7,6},{8,9},{9,8},{10,11... | collective-permute-start | bytes 98312 | tf_op jit(solution)/shard_map/ppermute | solution.py:252
  18.1 0.9 %collective-permute-done.3 = f32[64,128]{1,0:T(8,128)S(1)} collective-permute-done((f32[64,128]{1,0:T(8,128)S(1)}, f32[64,128]{1,0:T(8,128)S(1)}, u32[]{:S(2)}, u32[]{:S(2)}) %collective-permute-start.3) | collective-permute-done | bytes 32800 | tf_op jit(solution)/shard_map/ppermute | solution.py:252
  19.0 1.7 %collective-permute-start.4 = (f32[64,128]{1,0:T(8,128)S(1)}, f32[64,128]{1,0:T(8,128)S(1)}, u32[]{:S(2)}, u32[]{:S(2)}) collective-permute-start(f32[64,128]{1,0:T(8,128)S(1)} %add.40), channel_id=1, source_target_pairs={{0,2},{1,3},{2,0},{3,1},{4,6},{5,7},{6,4},{7,5},{8,10},{9,11},{10,... | collective-permute-start | bytes 98312 | tf_op jit(solution)/shard_map/ppermute | solution.py:252
  20.8 2.2 %collective-permute-done.4 = f32[64,128]{1,0:T(8,128)S(1)} collective-permute-done((f32[64,128]{1,0:T(8,128)S(1)}, f32[64,128]{1,0:T(8,128)S(1)}, u32[]{:S(2)}, u32[]{:S(2)}) %collective-permute-start.4) | collective-permute-done | bytes 32800 | tf_op jit(solution)/shard_map/ppermute | solution.py:252
  23.0 0.0 collective-permute-done.5.refs_5_
  23.0 0.0 collective-permute-done.6.refs_6_
  23.0 0.0 collective-permute-done.7.refs_7_
  23.0 3.9 %collective-permute-start.10 = (f32[64,128]{1,0:T(8,128)S(1)}, f32[64,128]{1,0:T(8,128)S(1)}, u32[]{:S(2)}, u32[]{:S(2)}) collective-permute-start(f32[64,128]{1,0:T(8,128)S(1)} %add.41), channel_id=1, source_target_pairs={{0,12},{1,13},{2,14},{3,15},{4,8},{5,9},{6,10},{7,11},{8,4},{9,5},... | collective-permute-start | bytes 98312 | tf_op jit(solution)/shard_map/ppermute | solution.py:252
  26.9 0.0 collective-permute-start.8
  26.9 0.6 %collective-permute-start.9 = (f32[64,128]{1,0:T(8,128)S(1)}, f32[64,128]{1,0:T(8,128)S(1)}, u32[]{:S(2)}, u32[]{:S(2)}) collective-permute-start(f32[64,128]{1,0:T(8,128)S(1)} %add.41), channel_id=1, source_target_pairs={{0,8},{1,9},{2,10},{3,11},{4,12},{5,13},{6,14},{7,15},{8,0},{9,1},... | collective-permute-start | bytes 98312 | tf_op jit(solution)/shard_map/ppermute | solution.py:252
  27.5 1.7 %collective-permute-start.12 = (f32[64,512]{1,0:T(8,128)S(1)}, f32[64,512]{1,0:T(8,128)S(1)}, u32[]{:S(2)}, u32[]{:S(2)}) collective-permute-start(f32[64,512]{1,0:T(8,128)S(1)} %get-tuple-element.21.refs_0_), channel_id=1, source_target_pairs={{0,2},{1,3},{2,0},{3,1},{4,6},{5,7},{6,4},{7,5},{8,10},{9,11},{10,... | collective-permute-start | bytes 393224 | tf_op jit(solution)/shard_map/ppermute | solution.py:252
  29.2 0.0 collective-permute-done.11.refs_1_
  29.2 0.4 collective-permute-start.13
  29.5 0.0 collective-permute-done.10
  29.5 1.2 %collective-permute-done.8 = f32[64,128]{1,0:T(8,128)S(1)} collective-permute-done((f32[64,128]{1,0:T(8,128)S(1)}, f32[64,128]{1,0:T(8,128)S(1)}, u32[]{:S(2)}, u32[]{:S(2)}) %collective-permute-start.8) | collective-permute-done | bytes 32800 | tf_op jit(solution)/shard_map/ppermute | solution.py:252
  30.8 0.9 %collective-permute-done.9 = f32[64,128]{1,0:T(8,128)S(1)} collective-permute-done((f32[64,128]{1,0:T(8,128)S(1)}, f32[64,128]{1,0:T(8,128)S(1)}, u32[]{:S(2)}, u32[]{:S(2)}) %collective-permute-start.9) | collective-permute-done | bytes 32800 | tf_op jit(solution)/shard_map/ppermute | solution.py:252
  31.7 0.6 %add_add_fusion.cov_ref = f32[64,128]{1,0:T(8,128)} fusion(f32[64,128]{1,0:T(8,128)S(1)} %add.41, f32[64,128]{1,0:T(8,128)S(1)} %collective-permute-done.10, f32[64,128]{1,0:T(8,128)S(1)} %collective-permute-done.8, f32[64,128]{1,0:T(8,128)S(1)} %collective-permute-done.9), kind=kLoop, calls=%fused_computation.4 | loop fusion | flops 24576 | bytes 163840 | tf_op jit(solution)/shard_map/add | solution.py:283
  32.3 3.9 %inverse.1.inv_ref = f32[64,128]{1,0:T(8,128)} custom-call(f32[64,128]{1,0:T(8,128)} %add_add_fusion.cov_ref), custom_call_target="tpu_custom_call" | custom-call | flops 4000000000 | bytes 65536 | tf_op jit(solution)/shard_map/inverse/pallas_call | solution.py:173
  36.2 0.0 collective-permute-done.12.refs_2_
  36.2 0.0 collective-permute-done.13.refs_3_
  36.2 0.0 copy-start.2
  36.2 0.8 %copy-done.2 = f32[64,128]{1,0:T(8,128)S(1)} copy-done((f32[64,128]{1,0:T(8,128)S(1)}, f32[64,128]{1,0:T(8,128)}, u32[]{:S(2)}) %copy-start.2) | copy-done | bytes 32792
  37.0 1.3 %scores.1 = f32[32,128]{1,0:T(8,128)S(1)} custom-call(s32[1]{0:T(128)} %bitcast.place_ref, f32[64,128]{1,0:T(8,128)S(1)} %copy-done.2, f32[64,512]{1,0:T(8,128)S(1)} %get-tuple-element.21.refs_0_, f32[64,512]{1,0:T(8,128)S(1)} %collective-permute-done.11.refs_1_, f32[64,512]{1,0:T(8,128)S(1)} %collective-permute-done.12.refs_2_, ...), custom_call_target="tpu_custom_call" | custom-call | tf_op jit(solution)/shard_map/scores/pallas_call | solution.py:237
  38.3 0.1 collective-permute-start.14
  38.3 1.6 %collective-permute-start.15 = (f32[8,128]{1,0:T(8,128)S(1)}, f32[8,128]{1,0:T(8,128)S(1)}, u32[]{:S(2)}, u32[]{:S(2)}) collective-permute-start(f32[8,128]{1,0:T(8,128)S(1)} %get-tuple-element.33), channel_id=1, source_target_pairs={{0,2},{1,3},{2,0},{3,1},{4,6},{5,7},{6,4},{7,5},{8,10},{9,11},{10,... | collective-permute-start | bytes 12296 | tf_op jit(solution)/shard_map/ppermute | solution.py:252
  39.9 0.3 collective-permute-start.16
  40.2 0.0 collective-permute-done.14
  40.2 1.8 %collective-permute-done.15 = f32[8,128]{1,0:T(8,128)S(1)} collective-permute-done((f32[8,128]{1,0:T(8,128)S(1)}, f32[8,128]{1,0:T(8,128)S(1)}, u32[]{:S(2)}, u32[]{:S(2)}) %collective-permute-start.15) | collective-permute-done | bytes 4128 | tf_op jit(solution)/shard_map/ppermute | solution.py:252
  42.0 0.9 %collective-permute-done.16 = f32[8,128]{1,0:T(8,128)S(1)} collective-permute-done((f32[8,128]{1,0:T(8,128)S(1)}, f32[8,128]{1,0:T(8,128)S(1)}, u32[]{:S(2)}, u32[]{:S(2)}) %collective-permute-start.16) | collective-permute-done | bytes 4128 | tf_op jit(solution)/shard_map/ppermute | solution.py:252
  42.9 0.6 %fusion.6 = f32[8,128]{1,0:T(8,128)} fusion(f32[8,128]{1,0:T(8,128)S(1)} %collective-permute-done.16, f32[8,128]{1,0:T(8,128)S(1)} %collective-permute-done.15, f32[8,128]{1,0:T(8,128)S(1)} %collective-permute-done.14, f32[32,128]{1,0:T(8,128)S(1)} %scores.1), kind=kLoop, calls=%fused_computation.7 | loop fusion | flops 3072 | bytes 20480 | tf_op jit(solution)/shard_map/add | solution.py:288
  (4 shorter events, 0.0 us)
Async XLA Ops:
  0.0 4.1 %copy-start = (bf16[2,64,1024]{2,1,0:T(8,128)(2,1)S(1)}, bf16[2,64,1024]{2,1,0:T(8,128)(2,1)}, u32[]{:S(2)}) copy-start(bf16[2,64,1024]{2,1,0:T(8,128)(2,1)} %param.8) | copy-start | bytes 786436
  0.0 12.2 %copy-start.1 = (bf16[2,64,4096]{2,1,0:T(8,128)(2,1)S(1)}, bf16[2,64,4096]{2,1,0:T(8,128)(2,1)}, u32[]{:S(2)}) copy-start(bf16[2,64,4096]{2,1,0:T(8,128)(2,1)} %param.7) | copy-start | bytes 3145732
  0.9 6.8 %collective-permute-start = (bf16[8,2048]{1,0:T(8,128)(2,1)S(1)}, bf16[8,2048]{1,0:T(8,128)(2,1)S(1)}, u32[]{:S(2)}, u32[]{:S(2)}) collective-permute-start(bf16[8,2048]{1,0:T(8,128)(2,1)S(1)} %get-tuple-element.28), channel_id=1, source_target_pairs={{0,1},{1,0},{2,3},{3,2},{4,5},{5,4},{6,7},{7,6},{8,9},{9,8},{10,11... | collective-permute-start | bytes 98312 | tf_op jit(solution)/shard_map/ppermute | solution.py:252
  1.4 6.3 %collective-permute-start.1 = (bf16[8,2048]{1,0:T(8,128)(2,1)S(1)}, bf16[8,2048]{1,0:T(8,128)(2,1)S(1)}, u32[]{:S(2)}, u32[]{:S(2)}) collective-permute-start(bf16[8,2048]{1,0:T(8,128)(2,1)S(1)} %get-tuple-element.30), channel_id=1, source_target_pairs={{0,2},{1,3},{2,0},{3,1},{4,6},{5,7},{6,4},{7,5},{8,10},{9,11},{10,... | collective-permute-start | bytes 98312 | tf_op jit(solution)/shard_map/ppermute | solution.py:252
  4.0 3.7 %collective-permute-start.2 = (bf16[8,2048]{1,0:T(8,128)(2,1)S(1)}, bf16[8,2048]{1,0:T(8,128)(2,1)S(1)}, u32[]{:S(2)}, u32[]{:S(2)}) collective-permute-start(bf16[8,2048]{1,0:T(8,128)(2,1)S(1)} %get-tuple-element.29), channel_id=1, source_target_pairs={{0,3},{1,2},{2,1},{3,0},{4,7},{5,6},{6,5},{7,4},{8,11},{9,10},{10,... | collective-permute-start | bytes 98312 | tf_op jit(solution)/shard_map/ppermute | solution.py:252
  7.8 15.2 %collective-permute-start.5 = (bf16[32,2048]{1,0:T(8,128)(2,1)S(1)}, bf16[32,2048]{1,0:T(8,128)(2,1)S(1)}, u32[]{:S(2)}, u32[]{:S(2)}) collective-permute-start(bf16[32,2048]{1,0:T(8,128)(2,1)S(1)} %pad_maximum_fusion.refs_4_), channel_id=1, source_target_pairs={{0,4},{1,5},{2,6},{3,7},{4,0},{5,1},{6,2},{7,3},{8,12},{9,13},{10,... | collective-permute-start | bytes 393224 | tf_op jit(solution)/shard_map/ppermute | solution.py:252
  9.6 13.3 %collective-permute-start.6 = (bf16[32,2048]{1,0:T(8,128)(2,1)S(1)}, bf16[32,2048]{1,0:T(8,128)(2,1)S(1)}, u32[]{:S(2)}, u32[]{:S(2)}) collective-permute-start(bf16[32,2048]{1,0:T(8,128)(2,1)S(1)} %pad_maximum_fusion.refs_4_), channel_id=1, source_target_pairs={{0,8},{1,9},{2,10},{3,11},{4,12},{5,13},{6,14},{7,15},{8,0},{9,1},... | collective-permute-start | bytes 393224 | tf_op jit(solution)/shard_map/ppermute | solution.py:252
  12.2 10.7 %collective-permute-start.7 = (bf16[32,2048]{1,0:T(8,128)(2,1)S(1)}, bf16[32,2048]{1,0:T(8,128)(2,1)S(1)}, u32[]{:S(2)}, u32[]{:S(2)}) collective-permute-start(bf16[32,2048]{1,0:T(8,128)(2,1)S(1)} %pad_maximum_fusion.refs_4_), channel_id=1, source_target_pairs={{0,12},{1,13},{2,14},{3,15},{4,8},{5,9},{6,10},{7,11},{8,4},{9,5},... | collective-permute-start | bytes 393224 | tf_op jit(solution)/shard_map/ppermute | solution.py:252
  17.6 11.6 %collective-permute-start.11 = (f32[64,512]{1,0:T(8,128)S(1)}, f32[64,512]{1,0:T(8,128)S(1)}, u32[]{:S(2)}, u32[]{:S(2)}) collective-permute-start(f32[64,512]{1,0:T(8,128)S(1)} %get-tuple-element.22), channel_id=1, source_target_pairs={{0,1},{1,0},{2,3},{3,2},{4,5},{5,4},{6,7},{7,6},{8,9},{9,8},{10,11... | collective-permute-start | bytes 393224 | tf_op jit(solution)/shard_map/ppermute | solution.py:252
  17.6 1.4 %collective-permute-start.3 = (f32[64,128]{1,0:T(8,128)S(1)}, f32[64,128]{1,0:T(8,128)S(1)}, u32[]{:S(2)}, u32[]{:S(2)}) collective-permute-start(f32[64,128]{1,0:T(8,128)S(1)} %get-tuple-element.18), channel_id=1, source_target_pairs={{0,1},{1,0},{2,3},{3,2},{4,5},{5,4},{6,7},{7,6},{8,9},{9,8},{10,11... | collective-permute-start | bytes 98312 | tf_op jit(solution)/shard_map/ppermute | solution.py:252
  19.0 3.9 %collective-permute-start.4 = (f32[64,128]{1,0:T(8,128)S(1)}, f32[64,128]{1,0:T(8,128)S(1)}, u32[]{:S(2)}, u32[]{:S(2)}) collective-permute-start(f32[64,128]{1,0:T(8,128)S(1)} %add.40), channel_id=1, source_target_pairs={{0,2},{1,3},{2,0},{3,1},{4,6},{5,7},{6,4},{7,5},{8,10},{9,11},{10,... | collective-permute-start | bytes 98312 | tf_op jit(solution)/shard_map/ppermute | solution.py:252
  23.0 6.6 %collective-permute-start.10 = (f32[64,128]{1,0:T(8,128)S(1)}, f32[64,128]{1,0:T(8,128)S(1)}, u32[]{:S(2)}, u32[]{:S(2)}) collective-permute-start(f32[64,128]{1,0:T(8,128)S(1)} %add.41), channel_id=1, source_target_pairs={{0,12},{1,13},{2,14},{3,15},{4,8},{5,9},{6,10},{7,11},{8,4},{9,5},... | collective-permute-start | bytes 98312 | tf_op jit(solution)/shard_map/ppermute | solution.py:252
  26.9 3.9 %collective-permute-start.8 = (f32[64,128]{1,0:T(8,128)S(1)}, f32[64,128]{1,0:T(8,128)S(1)}, u32[]{:S(2)}, u32[]{:S(2)}) collective-permute-start(f32[64,128]{1,0:T(8,128)S(1)} %add.41), channel_id=1, source_target_pairs={{0,4},{1,5},{2,6},{3,7},{4,0},{5,1},{6,2},{7,3},{8,12},{9,13},{10,... | collective-permute-start | bytes 98312 | tf_op jit(solution)/shard_map/ppermute | solution.py:252
  26.9 4.8 %collective-permute-start.9 = (f32[64,128]{1,0:T(8,128)S(1)}, f32[64,128]{1,0:T(8,128)S(1)}, u32[]{:S(2)}, u32[]{:S(2)}) collective-permute-start(f32[64,128]{1,0:T(8,128)S(1)} %add.41), channel_id=1, source_target_pairs={{0,8},{1,9},{2,10},{3,11},{4,12},{5,13},{6,14},{7,15},{8,0},{9,1},... | collective-permute-start | bytes 98312 | tf_op jit(solution)/shard_map/ppermute | solution.py:252
  27.5 8.7 %collective-permute-start.12 = (f32[64,512]{1,0:T(8,128)S(1)}, f32[64,512]{1,0:T(8,128)S(1)}, u32[]{:S(2)}, u32[]{:S(2)}) collective-permute-start(f32[64,512]{1,0:T(8,128)S(1)} %get-tuple-element.21.refs_0_), channel_id=1, source_target_pairs={{0,2},{1,3},{2,0},{3,1},{4,6},{5,7},{6,4},{7,5},{8,10},{9,11},{10,... | collective-permute-start | bytes 393224 | tf_op jit(solution)/shard_map/ppermute | solution.py:252
  29.2 7.0 %collective-permute-start.13 = (f32[64,512]{1,0:T(8,128)S(1)}, f32[64,512]{1,0:T(8,128)S(1)}, u32[]{:S(2)}, u32[]{:S(2)}) collective-permute-start(f32[64,512]{1,0:T(8,128)S(1)} %collective-permute-done.11.refs_1_), channel_id=1, source_target_pairs={{0,2},{1,3},{2,0},{3,1},{4,6},{5,7},{6,4},{7,5},{8,10},{9,11},{10,... | collective-permute-start | bytes 393224 | tf_op jit(solution)/shard_map/ppermute | solution.py:252
  36.2 0.8 %copy-start.2 = (f32[64,128]{1,0:T(8,128)S(1)}, f32[64,128]{1,0:T(8,128)}, u32[]{:S(2)}) copy-start(f32[64,128]{1,0:T(8,128)} %inverse.1.inv_ref) | copy-start | bytes 98308
  38.3 1.9 %collective-permute-start.14 = (f32[8,128]{1,0:T(8,128)S(1)}, f32[8,128]{1,0:T(8,128)S(1)}, u32[]{:S(2)}, u32[]{:S(2)}) collective-permute-start(f32[8,128]{1,0:T(8,128)S(1)} %get-tuple-element.31), channel_id=1, source_target_pairs={{0,1},{1,0},{2,3},{3,2},{4,5},{5,4},{6,7},{7,6},{8,9},{9,8},{10,11... | collective-permute-start | bytes 12296 | tf_op jit(solution)/shard_map/ppermute | solution.py:252
  38.3 3.7 %collective-permute-start.15 = (f32[8,128]{1,0:T(8,128)S(1)}, f32[8,128]{1,0:T(8,128)S(1)}, u32[]{:S(2)}, u32[]{:S(2)}) collective-permute-start(f32[8,128]{1,0:T(8,128)S(1)} %get-tuple-element.33), channel_id=1, source_target_pairs={{0,2},{1,3},{2,0},{3,1},{4,6},{5,7},{6,4},{7,5},{8,10},{9,11},{10,... | collective-permute-start | bytes 12296 | tf_op jit(solution)/shard_map/ppermute | solution.py:252
  39.9 3.0 %collective-permute-start.16 = (f32[8,128]{1,0:T(8,128)S(1)}, f32[8,128]{1,0:T(8,128)S(1)}, u32[]{:S(2)}, u32[]{:S(2)}) collective-permute-start(f32[8,128]{1,0:T(8,128)S(1)} %get-tuple-element.32), channel_id=1, source_target_pairs={{0,3},{1,2},{2,1},{3,0},{4,7},{5,6},{6,5},{7,4},{8,11},{9,10},{10,... | collective-permute-start | bytes 12296 | tf_op jit(solution)/shard_map/ppermute | solution.py:252

commit v3 on v2

v3 whole, which is shorter than its diff:
```python
import functools

import jax
import jax.numpy as jnp
from jax import lax
from jax.experimental import pallas as pl
from jax.experimental.pallas import tpu as pltpu
from jax.sharding import Mesh, PartitionSpec as P

R = 64
LEN = 128
PAIR = 2 * R
DAMPING = 0.1
STEP = 512
BLOCK = 4
GROUP = 4

F32 = jnp.float32
BF16 = jnp.bfloat16
MIB = 1024 * 1024


def dot(a, b, dims, precision=None):
    return lax.dot_general(a, b, (dims, ((), ())), precision=precision, preferred_element_type=F32)


NN = ((1,), (0,))
NT = ((1,), (1,))
TN = ((0,), (0,))


def statistics_kernel(
    x_hbm, g_hbm, w_hbm, v_hbm, cov_ref, mom_ref, x_buf, g_buf, w_buf, v_buf, total, both, x_sem, g_sem, w_sem, v_sem
):
    chunks, tokens, step = x_buf.shape
    seqs = tokens // LEN

    def x_copy(k):
        return pltpu.make_async_copy(x_hbm.at[:, k * step : (k + 1) * step], x_buf.at[k], x_sem.at[k])

    def w_copy(k):
        return pltpu.make_async_copy(w_hbm.at[:, k * step : (k + 1) * step], w_buf.at[k], w_sem.at[k])

    def g_copy(seq):
        return pltpu.make_async_copy(
            g_hbm.at[pl.ds(seq * LEN, LEN)], g_buf.at[pl.ds(seq * LEN, LEN)], g_sem.at[seq]
        )

    v_copy = pltpu.make_async_copy(v_hbm, v_buf, v_sem)
    v_copy.start()
    for seq in range(seqs):
        g_copy(seq).start()
    for k in range(chunks):
        w_copy(k).start()
        x_copy(k).start()
    v_copy.wait()

    @pl.loop(0, seqs)
    def _(seq):
        g_copy(seq).wait()
        rows = pl.ds(pl.multiple_of(seq * LEN, LEN), LEN)
        outs = [dot(g_buf[rows, m, :], v_buf[m], NT) for m in range(2)]
        both[rows, PAIR:] = jnp.concatenate(outs, axis=1).astype(BF16)

    for k in range(chunks):
        w_copy(k).wait()
        x_copy(k).wait()
        term = dot(x_buf[k], w_buf[k], NT)
        if k == 0:
            total[...] = term
        elif k < chunks - 1:
            total[...] += term
        else:
            both[:, :PAIR] = (total[...] + term).astype(BF16)

    low = lax.broadcasted_iota(jnp.int32, (R, PAIR), 1) < R
    products = []
    for seq in range(seqs):
        part = both[seq * LEN : (seq + 1) * LEN, :]
        products.append(dot(part, part, TN))
    for pair in range(seqs // 2):
        blocks = [products[2 * pair + i][PAIR:, :PAIR] * (1.0 / LEN) for i in range(2)]
        lanes = slice(pair * PAIR, (pair + 1) * PAIR)
        mom_ref[0, :, lanes] = jnp.where(low, blocks[0][:R], pltpu.roll(blocks[1][:R], R, 1))
        mom_ref[1, :, lanes] = jnp.where(low, pltpu.roll(blocks[0][R:], R, 1), blocks[1][R:])
    mom_ref[2] = mom_ref[0]
    mom_ref[3] = mom_ref[1]
    cov_in = sum(product[:PAIR, :PAIR] for product in products)
    cov_out = sum(product[PAIR:, PAIR:] for product in products)
    cov0 = jnp.where(low, cov_in[:R], pltpu.roll(cov_out[:R], R, 1))
    cov1 = jnp.where(low, pltpu.roll(cov_in[R:], R, 1), cov_out[R:])
    for group in range(GROUP):
        cov_ref[group] = (cov0, cov1)[group & 1]


def statistics(layer_input, out_grads, in_flat, out_proj):
    tokens, width = layer_input.shape
    seqs = tokens // LEN
    chunks = width // STEP
    vmem = pl.BlockSpec(memory_space=pltpu.VMEM)
    return pl.pallas_call(
        statistics_kernel,
        in_specs=[pl.BlockSpec(memory_space=pl.ANY)] * 4,
        out_specs=[vmem, vmem],
        out_shape=[
            jax.ShapeDtypeStruct((GROUP, R, PAIR), F32),
            jax.ShapeDtypeStruct((GROUP, R, seqs * R), F32),
        ],
        scratch_shapes=[
            pltpu.VMEM((chunks, tokens, STEP), BF16),
            pltpu.VMEM(out_grads.shape, BF16),
            pltpu.VMEM((chunks, PAIR, STEP), BF16),
            pltpu.VMEM(out_proj.shape, BF16),
            pltpu.VMEM((tokens, PAIR), F32),
            pltpu.VMEM((tokens, 2 * PAIR), BF16),
            pltpu.SemaphoreType.DMA((chunks,)),
            pltpu.SemaphoreType.DMA((seqs,)),
            pltpu.SemaphoreType.DMA((chunks,)),
            pltpu.SemaphoreType.DMA,
        ],
        compiler_params=pltpu.CompilerParams(vmem_limit_bytes=48 * MIB),
        cost_estimate=pl.CostEstimate(
            flops=3 * tokens * width * PAIR, bytes_accessed=3 * tokens * width, transcendentals=0
        ),
        name="statistics",
    )(layer_input, out_grads, in_flat, out_proj)


def solve_block(p, rows):
    det = 1.0 / (p[0][0] * p[1][1] - p[0][1] * p[0][1])
    a, b, c = p[1][1] * det, -p[0][1] * det, p[0][0] * det
    t = [[a * p[0][j] + b * p[1][j], b * p[0][j] + c * p[1][j]] for j in (2, 3)]
    s22 = p[2][2] - p[0][2] * t[0][0] - p[1][2] * t[0][1]
    s23 = p[2][3] - p[0][2] * t[1][0] - p[1][2] * t[1][1]
    s33 = p[3][3] - p[0][3] * t[1][0] - p[1][3] * t[1][1]
    det = 1.0 / (s22 * s33 - s23 * s23)
    y0 = a * rows[0] + b * rows[1]
    y1 = b * rows[0] + c * rows[1]
    z2 = rows[2] - p[0][2] * y0 - p[1][2] * y1
    z3 = rows[3] - p[0][3] * y0 - p[1][3] * y1
    x2 = (s33 * z2 - s23 * z3) * det
    x3 = (s22 * z3 - s23 * z2) * det
    return [y0 - t[0][0] * x2 - t[1][0] * x3, y1 - t[0][1] * x2 - t[1][1] * x3, x2, x3]


def invert_pair(matrix):
    lane = lax.broadcasted_iota(jnp.int32, (8, PAIR), 1)
    row = lax.broadcasted_iota(jnp.int32, (8, PAIR), 0)
    column = lane % R
    base = lane - column
    work = [matrix[8 * g : 8 * g + 8] for g in range(R // 8)]
    for k in range(0, R, BLOCK):
        cols = [[jnp.take_along_axis(part, base + (k + j), axis=1) for j in range(BLOCK)] for part in work]
        home, at = k // 8, k % 8
        inside = (column >= k) & (column < k + BLOCK)
        pivots = [[cols[home][j][at + i : at + i + 1] for j in range(BLOCK)] for i in range(BLOCK)]
        rows = [
            jnp.where(
                inside[:1], jnp.where(column[:1] == k + i, 1.0, 0.0), work[home][at + i : at + i + 1]
            )
            for i in range(BLOCK)
        ]
        solved = solve_block(pivots, rows)
        for g in range(R // 8):
            part = jnp.where(inside, 0.0, work[g])
            col = cols[g]
            if g == home:
                block_row = (row >= at) & (row < at + BLOCK)
                part = jnp.where(block_row, 0.0, part)
                col = [
                    jnp.where(block_row, jnp.where(row == at + j, -1.0, 0.0), col[j]) for j in range(BLOCK)
                ]
            work[g] = part - (col[0] * solved[0] + col[1] * solved[1]) - (col[2] * solved[2] + col[3] * solved[3])
    return jnp.concatenate(work, axis=0)


def inverse_kernel(total_tokens, cov_ref, inv_ref):
    row = lax.broadcasted_iota(jnp.int32, (R, PAIR), 0)
    lane = lax.broadcasted_iota(jnp.int32, (R, PAIR), 1)
    low = lane < R
    column = jnp.where(low, lane, lane - R)
    cov = jnp.sum(cov_ref[...], axis=0)
    diagonal = jnp.where(row == column, cov, 0.0)
    trace_in = jnp.sum(jnp.where(low, diagonal, 0.0), keepdims=True)
    trace_out = jnp.sum(jnp.where(low, 0.0, diagonal), keepdims=True)
    scale = R / jnp.where(low, trace_in, trace_out)
    inv_ref[...] = invert_pair(cov * scale + jnp.where(row == column, DAMPING, 0.0)) * (scale * total_tokens)


def inverse(cov, total_tokens):
    vmem = pl.BlockSpec(memory_space=pltpu.VMEM)
    return pl.pallas_call(
        functools.partial(inverse_kernel, total_tokens),
        in_specs=[vmem],
        out_specs=vmem,
        out_shape=jax.ShapeDtypeStruct(cov.shape[1:], F32),
        compiler_params=pltpu.CompilerParams(vmem_limit_bytes=16 * MIB),
        cost_estimate=pl.CostEstimate(flops=4 * 10**9, bytes_accessed=2**16, transcendentals=0),
        name="inverse",
    )(cov)


def scores_kernel(upper_ref, inv_ref, moments_ref, queries_ref, out_ref, flat_ref):
    upper = upper_ref[0] == 1
    low = lax.broadcasted_iota(jnp.int32, (R, PAIR), 1) < R
    inv = inv_ref[...]
    tiles = R // 4
    even = [inv_ref[pl.ds(start, tiles, stride=2), :] for start in (0, R // 2)]
    odd = [inv_ref[pl.ds(start + 1, tiles, stride=2), :] for start in (0, R // 2)]
    left = jnp.concatenate([jnp.where(upper, even[1], even[0]), jnp.where(upper, odd[1], odd[0])], axis=0)
    left = pltpu.roll(left, R, 1)[:, :R]
    moments = jnp.concatenate([moments_ref[group] for group in range(GROUP)], axis=1)
    mixed = dot(left, moments, NN, lax.Precision.HIGHEST)
    pairs = moments.shape[1] // PAIR
    stack = jnp.concatenate(
        [
            jnp.concatenate(
                [mixed[:tiles, j * PAIR : (j + 1) * PAIR], mixed[tiles:, j * PAIR : (j + 1) * PAIR]], axis=1
            )
            for j in range(pairs)
        ],
        axis=0,
    )
    zero = jnp.zeros((R, PAIR), F32)
    at_low = jnp.where(low, inv, 0.0)
    at_high = pltpu.roll(at_low, R, 1)
    right = jnp.concatenate(
        [
            jnp.concatenate([at_low, zero], axis=1),
            jnp.concatenate([zero, at_low], axis=1),
            jnp.concatenate([at_high, zero], axis=1),
            jnp.concatenate([zero, at_high], axis=1),
        ],
        axis=0,
    )
    done = dot(stack, right, NN, lax.Precision.HIGHEST)
    for j in range(pairs):
        rows = done[j * tiles : (j + 1) * tiles]
        flat_ref[(2 * j) * tiles : (2 * j + 1) * tiles, :] = rows[:, :PAIR]
        flat_ref[(2 * j + 1) * tiles : (2 * j + 2) * tiles, :] = rows[:, PAIR:]
    flat = jnp.concatenate(
        [flat_ref[pl.ds(k, 2 * pairs, stride=tiles), :].astype(BF16) for k in range(tiles)], axis=1
    )
    out_ref[...] = dot(flat, queries_ref[...], NT)


def score(upper, inv, moments, queries):
    seqs = GROUP * moments.shape[2] // R
    vmem = pl.BlockSpec(memory_space=pltpu.VMEM)
    return pl.pallas_call(
        scores_kernel,
        in_specs=[pl.BlockSpec(memory_space=pltpu.SMEM), vmem, vmem, vmem],
        out_specs=vmem,
        out_shape=jax.ShapeDtypeStruct((seqs, queries.shape[0]), F32),
        scratch_shapes=[pltpu.VMEM((seqs * R // 4, PAIR), F32)],
        compiler_params=pltpu.CompilerParams(vmem_limit_bytes=16 * MIB),
        name="scores",
    )(upper, inv, moments, queries)


def swap(value, axis):
    return lax.all_to_all(value, axis, 0, 0, tiled=False)


def per_device(layer_input, out_grads, in_proj, out_proj, queries):
    local_tokens = layer_input.shape[0]
    local_queries = queries.shape[0]
    slabs = lax.axis_size("slab")
    upper = (lax.axis_index("group").astype(jnp.int32) >> 1).reshape(1)
    quarter = queries.shape[1] // GROUP
    blocks = [queries[:, block * quarter : (block + 1) * quarter] for block in (0, 2, 1, 3)]
    shard = swap(jnp.stack(blocks), "group").reshape(GROUP * local_queries, quarter)
    every = swap(jnp.broadcast_to(shard, (slabs,) + shard.shape), "slab")
    every = every.reshape(slabs * GROUP * local_queries, quarter)
    cov, moments = statistics(
        layer_input, out_grads, in_proj.reshape(PAIR, in_proj.shape[2]), out_proj
    )
    cov = jnp.sum(swap(cov, "group"), axis=0)
    moments = swap(moments, "group")
    cov = swap(jnp.broadcast_to(cov, (slabs,) + cov.shape), "slab")
    partial = score(upper, inverse(cov, local_tokens * slabs * GROUP), moments, every)
    return jnp.sum(swap(partial.reshape(GROUP, local_tokens // LEN, partial.shape[1]), "group"), axis=0)


def solution(mesh):
    parts, devices = mesh.devices.shape
    grid = Mesh(mesh.devices.reshape(parts, devices // GROUP, GROUP), ("parts", "slab", "group"))
    split = ("parts", "slab", "group")
    return jax.shard_map(
        per_device,
        mesh=grid,
        in_specs=(P(split, None), P(split, None, None), P(), P(), P(split, None)),
        out_specs=P(split, None),
        check_vma=False,
    )
```

time: 43.8 us -> 87.7 us (2.00)
  blocking collectives: 0 us -> 28.5 us
  waiting for transfers between devices: 7.99 us -> 20.5 us
  Pallas kernels: 10.5 us -> 20.5 us
  starting transfers between devices: 18.4 us -> 11 us
  matrix products: 3.62 us -> 0 us
  local copies, waits for them, and re-layouts: 1.69 us -> 5.23 us
    all_to_all x0 -> x3, blocking collectives: none -> 28.5 us  [swap(): return lax.all_to_all(value, axis, 0, 0, tiled=False)]
    all_to_all x0 -> x3, waiting for transfers between devices: none -> 20.5 us  [swap(): return lax.all_to_all(value, axis, 0, 0, tiled=False)]
    ppermute x17 -> x0, starting transfers between devices: 18.4 us -> none  [exchange(): lax.ppermute(value, 'dp', [(i, i ^ distance) for i in range(lax.axis_size...]
    pallas_call x2, Pallas kernels: 6.61 us -> 18.1 us  [the longest x1 17 us: statistics(): pl.pallas_call(statistics_kernel, in_specs=[pl.BlockSpec(memory_space=pl....]
    all_to_all x0 -> x3, starting transfers between devices: none -> 11 us  [swap(): return lax.all_to_all(value, axis, 0, 0, tiled=False)]
    ppermute x17 -> x0, waiting for transfers between devices: 7.99 us -> none  [exchange(): lax.ppermute(value, 'dp', [(i, i ^ distance) for i in range(lax.axis_size...]
    dot_general x1 -> x0, matrix products: 3.62 us -> none  [per_device(): jnp.einsum('tmk,mrk->tmr', out_grads, out_proj, preferred_element_type=F32)]
    unnamed x6 -> x8, local copies, waits for them, and re-layouts: 0.76 us -> 4.36 us
  transfers between devices with their start and end apart: 17 -> 3, of which waited for: 6 -> 3; matrix products, arithmetic and copies ran while one was open for 10% -> 1% of each run, Pallas kernels for 21% -> 3%
where the time goes in v3:
time: 87.7 us; the launch traced here: 87.1 us
  blocking collectives  28.5 us (32%)
  Pallas kernels  20.5 us (23%)
  waiting for transfers between devices  20.5 us (23%)
  starting transfers between devices  11 us (13%)
  local copies, waits for them, and re-layouts  5.23 us (6%)
  other arithmetic  1.28 us (1%)
    all_to_all x3, blocking collectives, swap(): return lax.all_to_all(value, axis, 0, 0, tiled=False)  28.5 us
    all_to_all x3, waiting for transfers between devices, swap(): return lax.all_to_all(value, axis, 0, 0, tiled=False)  20.5 us
    pallas_call x1, Pallas kernels, statistics(): pl.pallas_call(statistics_kernel, in_specs=[pl.BlockSpec(memory_space=pl....  17 us
    all_to_all x3, starting transfers between devices, swap(): return lax.all_to_all(value, axis, 0, 0, tiled=False)  11 us
    unnamed x8, local copies, waits for them, and re-layouts  4.36 us
    pallas_call x1, Pallas kernels, inverse(): pl.pallas_call(functools.partial(inverse_kernel, total_tokens), in_specs=...  2.41 us
  transfers between devices with their start and end apart: 3, of which 3 were waited for; matrix products, arithmetic and copies ran while one was open for 1% of the time, Pallas kernels for 3%

profile of v3, /device:TPU:0, one launch (start us, length us, event | category | flops | bytes accessed | tf_op | source)
XLA Modules:
  0.0 87.1 jit_solution(985655105764513682)
XLA Ops:
  0.0 0.0 copy-start
  0.0 2.2 %copy-done = bf16[1024,2,1024]{2,1,0:T(2,128)(2,1)S(1)} copy-done((bf16[1024,2,1024]{2,1,0:T(2,128)(2,1)S(1)}, bf16[1024,2,1024]{2,1,0:T(2,128)(2,1)}, u32[]{:S(2)}) %copy-start) | copy-done | bytes 4194328
  2.2 0.0 copy-start.1
  2.2 1.2 %copy-done.1 = bf16[2,64,4096]{2,1,0:T(8,128)(2,1)S(1)} copy-done((bf16[2,64,4096]{2,1,0:T(8,128)(2,1)S(1)}, bf16[2,64,4096]{2,1,0:T(8,128)(2,1)}, u32[]{:S(2)}) %copy-start.1) | copy-done | bytes 1048600
  3.4 0.0 copy-start.2
  3.4 0.9 %copy-done.2 = bf16[2,64,1024]{2,1,0:T(8,128)(2,1)S(1)} copy-done((bf16[2,64,1024]{2,1,0:T(8,128)(2,1)S(1)}, bf16[2,64,1024]{2,1,0:T(8,128)(2,1)}, u32[]{:S(2)}) %copy-start.2) | copy-done | bytes 262168
  4.4 0.0 copy-start.3
  4.4 17.0 %statistics.1 = (f32[4,64,128]{2,1,0:T(8,128)}, f32[4,64,512]{2,1,0:T(8,128)S(1)}) custom-call(bf16[1024,4096]{1,0:T(8,128)(2,1)} %x_hbm.1, bf16[1024,2,1024]{2,1,0:T(2,128)(2,1)S(1)} %copy-done, bf16[128,4096]{1,0:T(8,128)(2,1)S(1)} %bitcast.14, bf16[2,64,1024]{2,1,0:T(8,128)(2,1)S(1)} %copy-done.2), custom_call_target="tpu_custom_call" | custom-call | flops 1610612736 | bytes 12582912 | tf_op jit(solution)/shard_map/statistics/pallas_call | solution.py:101
  21.3 4.2 %all-to-all-start = ((f32[4,64,128]{2,1,0:T(8,128)}), f32[4,64,128]{2,1,0:T(8,128)S(1)}, u32[]{:S(2)}, u32[]{:S(2)}) async-start(f32[4,64,128]{2,1,0:T(8,128)} %get-tuple-element.7), calls=%async_computation | async-start | bytes 262144 | tf_op jit(solution)/shard_map/all_to_all | solution.py:262
  25.6 0.0 copy-done.3
  25.6 0.7 pad_maximum_fusion
  26.3 3.9 %all-to-all-done = f32[4,64,128]{2,1,0:T(8,128)S(1)} async-done(((f32[4,64,128]{2,1,0:T(8,128)}), f32[4,64,128]{2,1,0:T(8,128)S(1)}, u32[]{:S(2)}, u32[]{:S(2)}) %all-to-all-start) | async-done | bytes 131104 | tf_op jit(solution)/shard_map/all_to_all | solution.py:262
  30.2 3.3 %all-to-all-start.3 = ((bf16[4,8,2048]{2,1,0:T(8,128)(2,1)}), bf16[4,8,2048]{2,1,0:T(8,128)(2,1)S(1)}, u32[]{:S(2)}, u32[]{:S(2)}) async-start(bf16[4,8,2048]{2,1,0:T(8,128)(2,1)} %pad_maximum_fusion), calls=%async_computation.3 | async-start | bytes 262144 | tf_op jit(solution)/shard_map/all_to_all | solution.py:262
  33.6 4.6 %all-to-all-done.3 = bf16[4,8,2048]{2,1,0:T(8,128)(2,1)S(1)} async-done(((bf16[4,8,2048]{2,1,0:T(8,128)(2,1)}), bf16[4,8,2048]{2,1,0:T(8,128)(2,1)S(1)}, u32[]{:S(2)}, u32[]{:S(2)}) %all-to-all-start.3) | async-done | bytes 131104 | tf_op jit(solution)/shard_map/all_to_all | solution.py:262
  38.2 11.1 %all_to_all.30.cov_ref = f32[4,64,128]{2,1,0:T(8,128)S(1)} all-to-all(f32[4,64,128]{2,1,0:T(8,128)S(1)} %broadcast_in_dim.6), channel_id=1, replica_groups=mesh['parts'=2,'slab'=4,'group'=4] {'slab'}, dimensions={0} | all-to-all | bytes 262144 | tf_op jit(solution)/shard_map/all_to_all | solution.py:262
  49.2 11.2 %all_to_all.31.moments_ref = f32[4,64,512]{2,1,0:T(8,128)S(1)} all-to-all(f32[4,64,512]{2,1,0:T(8,128)S(1)} %get-tuple-element.8), channel_id=1, replica_groups=mesh['parts'=2,'slab'=4,'group'=4] {'group'}, dimensions={0} | all-to-all | bytes 1048576 | tf_op jit(solution)/shard_map/all_to_all | solution.py:262
  60.5 0.8 broadcast_in_dim.7
  61.3 3.5 %all-to-all-start.4 = ((bf16[4,32,2048]{2,1,0:T(8,128)(2,1)}), bf16[4,32,2048]{2,1,0:T(8,128)(2,1)S(1)}, u32[]{:S(2)}, u32[]{:S(2)}) async-start(bf16[4,32,2048]{2,1,0:T(8,128)(2,1)} %broadcast_in_dim.7), calls=%async_computation.4 | async-start | bytes 1048576 | tf_op jit(solution)/shard_map/all_to_all | solution.py:262
  64.8 2.4 %inverse.1.inv_ref = f32[64,128]{1,0:T(8,128)S(1)} custom-call(f32[4,64,128]{2,1,0:T(8,128)S(1)} %all_to_all.30.cov_ref), custom_call_target="tpu_custom_call" | custom-call | flops 4000000000 | bytes 65536 | tf_op jit(solution)/shard_map/inverse/pallas_call | solution.py:192
  67.2 12.0 %all-to-all-done.4 = bf16[4,32,2048]{2,1,0:T(8,128)(2,1)S(1)} async-done(((bf16[4,32,2048]{2,1,0:T(8,128)(2,1)}), bf16[4,32,2048]{2,1,0:T(8,128)(2,1)S(1)}, u32[]{:S(2)}, u32[]{:S(2)}) %all-to-all-start.4) | async-done | bytes 524320 | tf_op jit(solution)/shard_map/all_to_all | solution.py:262
  79.2 1.1 %scores.1 = f32[32,128]{1,0:T(8,128)S(1)} custom-call(s32[1]{0:T(128)} %bitcast.upper_ref, f32[64,128]{1,0:T(8,128)S(1)} %inverse.1.inv_ref, f32[4,64,512]{2,1,0:T(8,128)S(1)} %all_to_all.31.moments_ref, bf16[128,2048]{1,0:T(8,128)(2,1)S(1)} %bitcast.13), custom_call_target="tpu_custom_call" | custom-call | tf_op jit(solution)/shard_map/scores/pallas_call | solution.py:250
  80.3 6.2 %all_to_all.32 = f32[4,8,128]{2,1,0:T(8,128)S(1)} all-to-all(f32[4,8,128]{2,1,0:T(8,128)S(1)} %bitcast.15), channel_id=1, replica_groups=mesh['parts'=2,'slab'=4,'group'=4] {'group'}, dimensions={0} | all-to-all | bytes 32768 | tf_op jit(solution)/shard_map/all_to_all | solution.py:262
  86.5 0.6 reduce_sum.19
  (3 shorter events, 0.0 us)
Async XLA Ops:
  0.0 2.2 %copy-start = (bf16[1024,2,1024]{2,1,0:T(2,128)(2,1)S(1)}, bf16[1024,2,1024]{2,1,0:T(2,128)(2,1)}, u32[]{:S(2)}) copy-start(bf16[1024,2,1024]{2,1,0:T(2,128)(2,1)} %g_hbm.1) | copy-start | bytes 12582916
  2.2 1.2 %copy-start.1 = (bf16[2,64,4096]{2,1,0:T(8,128)(2,1)S(1)}, bf16[2,64,4096]{2,1,0:T(8,128)(2,1)}, u32[]{:S(2)}) copy-start(bf16[2,64,4096]{2,1,0:T(8,128)(2,1)} %param.7) | copy-start | bytes 3145732
  3.4 0.9 %copy-start.2 = (bf16[2,64,1024]{2,1,0:T(8,128)(2,1)S(1)}, bf16[2,64,1024]{2,1,0:T(8,128)(2,1)}, u32[]{:S(2)}) copy-start(bf16[2,64,1024]{2,1,0:T(8,128)(2,1)} %v_hbm.1) | copy-start | bytes 786436
  4.4 21.2 %copy-start.3 = (bf16[8,8192]{1,0:T(8,128)(2,1)S(1)}, bf16[8,8192]{1,0:T(8,128)(2,1)}, u32[]{:S(2)}) copy-start(bf16[8,8192]{1,0:T(8,128)(2,1)} %param.9) | copy-start | bytes 393220
  21.3 8.9 %all-to-all-start = ((f32[4,64,128]{2,1,0:T(8,128)}), f32[4,64,128]{2,1,0:T(8,128)S(1)}, u32[]{:S(2)}, u32[]{:S(2)}) async-start(f32[4,64,128]{2,1,0:T(8,128)} %get-tuple-element.7), calls=%async_computation | async-start | bytes 262144 | tf_op jit(solution)/shard_map/all_to_all | solution.py:262
  30.2 7.9 %all-to-all-start.3 = ((bf16[4,8,2048]{2,1,0:T(8,128)(2,1)}), bf16[4,8,2048]{2,1,0:T(8,128)(2,1)S(1)}, u32[]{:S(2)}, u32[]{:S(2)}) async-start(bf16[4,8,2048]{2,1,0:T(8,128)(2,1)} %pad_maximum_fusion), calls=%async_computation.3 | async-start | bytes 262144 | tf_op jit(solution)/shard_map/all_to_all | solution.py:262
  61.3 17.8 %all-to-all-start.4 = ((bf16[4,32,2048]{2,1,0:T(8,128)(2,1)}), bf16[4,32,2048]{2,1,0:T(8,128)(2,1)S(1)}, u32[]{:S(2)}, u32[]{:S(2)}) async-start(bf16[4,32,2048]{2,1,0:T(8,128)(2,1)} %broadcast_in_dim.7), calls=%async_computation.4 | async-start | bytes 1048576 | tf_op jit(solution)/shard_map/all_to_all | solution.py:262

commit v4 on v2

v4 whole, which is shorter than its diff:
```python
import functools

import jax
import jax.numpy as jnp
from jax import lax
from jax.experimental import pallas as pl
from jax.experimental.pallas import tpu as pltpu
from jax.sharding import PartitionSpec as P

R = 64
LEN = 128
PAIR = 2 * R
DAMPING = 0.1
STEP = 512
BLOCK = 4
GROUP = 4

F32 = jnp.float32
BF16 = jnp.bfloat16
MIB = 1024 * 1024


def dot(a, b, dims, precision=None):
    return lax.dot_general(a, b, (dims, ((), ())), precision=precision, preferred_element_type=F32)


NN = ((1,), (0,))
NT = ((1,), (1,))
TN = ((0,), (0,))


def project_kernel(x_hbm, w_hbm, acts_ref, x_buf, w_buf, total, x_sem, w_sem):
    chunks, _, step = x_buf.shape

    def x_copy(k):
        return pltpu.make_async_copy(x_hbm.at[:, k * step : (k + 1) * step], x_buf.at[k], x_sem.at[k])

    def w_copy(k):
        return pltpu.make_async_copy(w_hbm.at[:, k * step : (k + 1) * step], w_buf.at[k], w_sem.at[k])

    for k in range(chunks):
        w_copy(k).start()
        x_copy(k).start()
    for k in range(chunks):
        w_copy(k).wait()
        x_copy(k).wait()
        term = dot(x_buf[k], w_buf[k], NT)
        if k == 0:
            total[...] = term
        elif k < chunks - 1:
            total[...] += term
        else:
            acts_ref[...] = (total[...] + term).astype(BF16)


def project(layer_input, in_flat):
    tokens, width = layer_input.shape
    chunks = width // STEP
    return pl.pallas_call(
        project_kernel,
        in_specs=[pl.BlockSpec(memory_space=pl.ANY)] * 2,
        out_specs=pl.BlockSpec(memory_space=pltpu.VMEM),
        out_shape=jax.ShapeDtypeStruct((tokens, PAIR), BF16),
        scratch_shapes=[
            pltpu.VMEM((chunks, tokens, STEP), BF16),
            pltpu.VMEM((chunks, PAIR, STEP), BF16),
            pltpu.VMEM((tokens, PAIR), F32),
            pltpu.SemaphoreType.DMA((chunks,)),
            pltpu.SemaphoreType.DMA((chunks,)),
        ],
        compiler_params=pltpu.CompilerParams(vmem_limit_bytes=48 * MIB),
        cost_estimate=pl.CostEstimate(
            flops=4 * tokens * width * PAIR, bytes_accessed=2 * tokens * width, transcendentals=0
        ),
        name="project",
    )(layer_input, in_flat)


def statistics_kernel(core_ref, acts_ref, outs_ref, keep_cov, send_cov, keep_mom, send_mom):
    first = core_ref[0] == 0
    acts = acts_ref[...]
    outs = outs_ref[...]
    low = lax.broadcasted_iota(jnp.int32, (R, PAIR), 1) < R
    cov_in = dot(acts, acts, TN)
    cov_out = dot(outs, outs, NT)
    cov0 = jnp.where(low, cov_in[:R], pltpu.roll(cov_out[:R], R, 1))
    cov1 = jnp.where(low, pltpu.roll(cov_in[R:], R, 1), cov_out[R:])
    keep_cov[...] = jnp.where(first, cov0, cov1)
    send_cov[...] = jnp.where(first, cov1, cov0)
    for pair in range(acts.shape[0] // LEN // 2):
        blocks = []
        for seq in (2 * pair, 2 * pair + 1):
            rows = slice(seq * LEN, (seq + 1) * LEN)
            blocks.append(dot(outs[:, rows], acts[rows], NN) * (1.0 / LEN))
        mom0 = jnp.where(low, blocks[0][:R], pltpu.roll(blocks[1][:R], R, 1))
        mom1 = jnp.where(low, pltpu.roll(blocks[0][R:], R, 1), blocks[1][R:])
        lanes = slice(pair * PAIR, (pair + 1) * PAIR)
        keep_mom[:, lanes] = jnp.where(first, mom0, mom1)
        send_mom[:, lanes] = jnp.where(first, mom1, mom0)


def statistics(core, acts, outs):
    seqs = acts.shape[0] // LEN
    cov = jax.ShapeDtypeStruct((R, PAIR), F32)
    mom = jax.ShapeDtypeStruct((R, seqs * R), F32)
    vmem = pl.BlockSpec(memory_space=pltpu.VMEM)
    return pl.pallas_call(
        statistics_kernel,
        in_specs=[pl.BlockSpec(memory_space=pltpu.SMEM), vmem, vmem],
        out_specs=[vmem] * 4,
        out_shape=[cov, cov, mom, mom],
        compiler_params=pltpu.CompilerParams(vmem_limit_bytes=16 * MIB),
        name="statistics",
    )(core, acts, outs)


def solve_block(p, rows):
    det = 1.0 / (p[0][0] * p[1][1] - p[0][1] * p[0][1])
    a, b, c = p[1][1] * det, -p[0][1] * det, p[0][0] * det
    t = [[a * p[0][j] + b * p[1][j], b * p[0][j] + c * p[1][j]] for j in (2, 3)]
    s22 = p[2][2] - p[0][2] * t[0][0] - p[1][2] * t[0][1]
    s23 = p[2][3] - p[0][2] * t[1][0] - p[1][2] * t[1][1]
    s33 = p[3][3] - p[0][3] * t[1][0] - p[1][3] * t[1][1]
    det = 1.0 / (s22 * s33 - s23 * s23)
    y0 = a * rows[0] + b * rows[1]
    y1 = b * rows[0] + c * rows[1]
    z2 = rows[2] - p[0][2] * y0 - p[1][2] * y1
    z3 = rows[3] - p[0][3] * y0 - p[1][3] * y1
    x2 = (s33 * z2 - s23 * z3) * det
    x3 = (s22 * z3 - s23 * z2) * det
    return [y0 - t[0][0] * x2 - t[1][0] * x3, y1 - t[0][1] * x2 - t[1][1] * x3, x2, x3]


def invert_pair(matrix):
    lane = lax.broadcasted_iota(jnp.int32, (8, PAIR), 1)
    row = lax.broadcasted_iota(jnp.int32, (8, PAIR), 0)
    column = lane % R
    base = lane - column
    work = [matrix[8 * g : 8 * g + 8] for g in range(R // 8)]
    for k in range(0, R, BLOCK):
        cols = [[jnp.take_along_axis(part, base + (k + j), axis=1) for j in range(BLOCK)] for part in work]
        home, at = k // 8, k % 8
        inside = (column >= k) & (column < k + BLOCK)
        pivots = [[cols[home][j][at + i : at + i + 1] for j in range(BLOCK)] for i in range(BLOCK)]
        rows = [
            jnp.where(
                inside[:1], jnp.where(column[:1] == k + i, 1.0, 0.0), work[home][at + i : at + i + 1]
            )
            for i in range(BLOCK)
        ]
        solved = solve_block(pivots, rows)
        for g in range(R // 8):
            part = jnp.where(inside, 0.0, work[g])
            col = cols[g]
            if g == home:
                block_row = (row >= at) & (row < at + BLOCK)
                part = jnp.where(block_row, 0.0, part)
                col = [
                    jnp.where(block_row, jnp.where(row == at + j, -1.0, 0.0), col[j]) for j in range(BLOCK)
                ]
            work[g] = part - (col[0] * solved[0] + col[1] * solved[1]) - (col[2] * solved[2] + col[3] * solved[3])
    return jnp.concatenate(work, axis=0)


def inverse_kernel(total_tokens, *refs):
    cov_refs, inv_ref = refs[:-1], refs[-1]
    row = lax.broadcasted_iota(jnp.int32, (R, PAIR), 0)
    lane = lax.broadcasted_iota(jnp.int32, (R, PAIR), 1)
    low = lane < R
    column = jnp.where(low, lane, lane - R)
    cov = sum(ref[...] for ref in cov_refs)
    diagonal = jnp.where(row == column, cov, 0.0)
    trace_in = jnp.sum(jnp.where(low, diagonal, 0.0), keepdims=True)
    trace_out = jnp.sum(jnp.where(low, 0.0, diagonal), keepdims=True)
    scale = R / jnp.where(low, trace_in, trace_out)
    inv_ref[...] = invert_pair(cov * scale + jnp.where(row == column, DAMPING, 0.0)) * (scale * total_tokens)


def inverse(covs, total_tokens):
    vmem = pl.BlockSpec(memory_space=pltpu.VMEM)
    return pl.pallas_call(
        functools.partial(inverse_kernel, total_tokens),
        in_specs=[vmem] * len(covs),
        out_specs=vmem,
        out_shape=jax.ShapeDtypeStruct(covs[0].shape, F32),
        compiler_params=pltpu.CompilerParams(vmem_limit_bytes=16 * MIB),
        name="inverse",
    )(*covs)


def scores_kernel(order, place_ref, inv_ref, keep_ref, recv_ref, *refs):
    query_refs, (out_ref, flat_ref, part_ref) = refs[:-3], refs[-3:]
    place = place_ref[0]
    low = lax.broadcasted_iota(jnp.int32, (R, PAIR), 1) < R
    inv = inv_ref[...]
    tiles = R // 2
    left = jnp.concatenate([inv_ref[pl.ds(start, tiles, stride=2), :] for start in range(2)], axis=0)
    left = pltpu.roll(left, R, 1)[:, :R]
    moments = jnp.concatenate([keep_ref[...], recv_ref[...]], axis=1)
    mixed = dot(left, moments, NN, lax.Precision.HIGHEST)
    pairs = moments.shape[1] // PAIR
    stack = jnp.concatenate(
        [
            jnp.concatenate(
                [mixed[:tiles, j * PAIR : (j + 1) * PAIR], mixed[tiles:, j * PAIR : (j + 1) * PAIR]], axis=1
            )
            for j in range(pairs)
        ],
        axis=0,
    )
    zero = jnp.zeros((R, PAIR), F32)
    at_low = jnp.where(low, inv, 0.0)
    at_high = pltpu.roll(at_low, R, 1)
    right = jnp.concatenate(
        [
            jnp.concatenate([at_low, zero], axis=1),
            jnp.concatenate([zero, at_low], axis=1),
            jnp.concatenate([at_high, zero], axis=1),
            jnp.concatenate([zero, at_high], axis=1),
        ],
        axis=0,
    )
    done = dot(stack, right, NN, lax.Precision.HIGHEST)
    for j in range(pairs):
        rows = done[j * tiles : (j + 1) * tiles]
        flat_ref[(2 * j) * tiles : (2 * j + 1) * tiles, :] = rows[:, :PAIR]
        flat_ref[(2 * j + 1) * tiles : (2 * j + 2) * tiles, :] = rows[:, PAIR:]
    flat = jnp.concatenate(
        [flat_ref[pl.ds(k, 2 * pairs, stride=tiles), :].astype(BF16) for k in range(tiles)], axis=1
    )
    part = dot(jnp.concatenate([ref[...] for ref in query_refs], axis=0), flat, NT)
    group = part_ref.shape[1]
    for at, distance in enumerate(order):
        part_ref[place ^ distance] = part[at * group : (at + 1) * group]
    out_ref[...] = part_ref[...].reshape(part.shape).T


def score(place, inv, moments, queries, order):
    seqs = sum(part.shape[1] for part in moments) // R
    count = sum(part.shape[0] for part in queries)
    vmem = pl.BlockSpec(memory_space=pltpu.VMEM)
    return pl.pallas_call(
        functools.partial(scores_kernel, order),
        in_specs=[pl.BlockSpec(memory_space=pltpu.SMEM)] + [vmem] * (1 + len(moments) + len(queries)),
        out_specs=vmem,
        out_shape=jax.ShapeDtypeStruct((seqs, count), F32),
        scratch_shapes=[
            pltpu.VMEM((seqs * R // 2, PAIR), F32),
            pltpu.VMEM((len(order), count // len(order), seqs), F32),
        ],
        compiler_params=pltpu.CompilerParams(vmem_limit_bytes=16 * MIB),
        name="scores",
    )(place, inv, *moments, *queries)


def exchange(value, distance):
    return lax.ppermute(value, "dp", [(i, i ^ distance) for i in range(lax.axis_size("dp"))])


def halves(values, upper):
    picked = []
    for value in values:
        low, high = jnp.split(value, 2, axis=1)
        picked.append((jnp.where(upper, high, low), jnp.where(upper, low, high)))
    return [jnp.concatenate(side, axis=0) for side in zip(*picked)]


def per_device(layer_input, out_grads, in_proj, out_proj, queries):
    local_tokens = layer_input.shape[0]
    devices = lax.axis_size("dp")
    slabs = devices // GROUP
    place = lax.axis_index("dp").astype(jnp.int32)
    module = place & 1
    column = [queries] + [exchange(queries, slab * GROUP) for slab in range(1, slabs)]
    acts = project(layer_input, in_proj.reshape(PAIR, in_proj.shape[2]))
    acts, out_grads, column[1] = lax.optimization_barrier((acts, out_grads, column[1]))
    near, send_near = halves(column[:2], module == 1)
    outs = jnp.einsum("tmk,mrk->tmr", out_grads, out_proj, preferred_element_type=F32).astype(BF16)
    outs = outs.reshape(local_tokens, PAIR).T
    near = jnp.concatenate([near, exchange(send_near, 1)], axis=0)
    acts, outs, near, column[2] = lax.optimization_barrier((acts, outs, near, column[2]))
    keep_cov, send_cov, keep_mom, send_mom = statistics(module.reshape(1), acts, outs)
    cov = keep_cov + exchange(send_cov, 1)
    moments = [keep_mom, exchange(send_mom, 1)]
    cov, column[3] = lax.optimization_barrier((cov, column[3]))
    cov = cov + exchange(cov, 2)
    far, send_far = halves(column[2:], module == 1)
    far = jnp.concatenate([far, exchange(send_far, 1)], axis=0)
    cov, moments, far = lax.optimization_barrier((cov, moments, far))
    across = exchange(near, 2)
    cov = cov + exchange(cov, GROUP)
    cov, across = lax.optimization_barrier((cov, across))
    distance = 2 * GROUP
    while distance < devices:
        last = exchange(cov, distance)
        if 2 * distance < devices:
            cov = cov + last
        distance *= 2
    inv = inverse([cov, last], local_tokens * devices)
    gathered = [near, across, far, exchange(far, 2)]
    order = [
        slab * GROUP + 2 * over + core
        for part in (range(2), range(2, slabs))
        for over in range(2)
        for core in range(2)
        for slab in part
    ]
    partial = score(place.reshape(1), inv, moments, gathered, order)
    seqs = local_tokens // LEN
    return partial[:seqs] + exchange(partial[seqs:], 1)


def solution(mesh):
    return jax.shard_map(
        per_device,
        mesh=mesh,
        in_specs=(
            P(("parts", "dp"), None),
            P(("parts", "dp"), None, None),
            P(),
            P(),
            P(("parts", "dp"), None),
        ),
        out_specs=P(("parts", "dp"), None),
        check_vma=False,
    )
```

time: 43.8 us -> 39.7 us (0.906)
  starting transfers between devices: 18.4 us -> 12.6 us
  waiting for transfers between devices: 7.99 us -> 11.7 us
  matrix products: 3.62 us -> 1.44 us
  local copies, waits for them, and re-layouts: 1.69 us -> 1.23 us
    pallas_call x1 -> x2, Pallas kernels: 1.3 us -> 7.91 us  [the longest x1 6.35 us: project(): pl.pallas_call(project_kernel, in_specs=[pl.BlockSpec(memory_space=pl.ANY...]
    ppermute x17 -> x13, starting transfers between devices: 18.4 us -> 12.6 us  [exchange(): lax.ppermute(value, 'dp', [(i, i ^ distance) for i in range(lax.axis_size...]
    pallas_call x1, Pallas kernels: 5.31 us -> 0.47 us  [statistics(): pl.pallas_call(statistics_kernel, in_specs=[pl.BlockSpec(memory_space=plt...]
    ppermute x17 -> x13, waiting for transfers between devices: 7.99 us -> 11.7 us  [exchange(): lax.ppermute(value, 'dp', [(i, i ^ distance) for i in range(lax.axis_size...]
    dot_general x1, matrix products: 3.62 us -> 1.44 us  [per_device(): jnp.einsum('tmk,mrk->tmr', out_grads, out_proj, preferred_element_type=F32)]
    pallas_call x1, Pallas kernels: 3.89 us -> 2.41 us  [inverse(): pl.pallas_call(functools.partial(inverse_kernel, total_tokens), in_specs=...]
    select_n x0 -> x4, other arithmetic: none -> 0.96 us  [halves(): picked.append((jnp.where(upper, high, low), jnp.where(upper, low, high)))]
    dynamic_slice x1 -> x0, local copies, waits for them, and re-layouts: 0.92 us -> none  [block_for(): return lax.dynamic_slice_in_dim(queries, block * quarter, quarter, 1)]
  transfers between devices with their start and end apart: 17 -> 13, of which waited for: 6 -> 7; matrix products, arithmetic and copies ran while one was open for 10% -> 6% of each run, Pallas kernels for 21% -> 23%
where the time goes in v4:
time: 39.7 us; the launch traced here: 39.6 us
  starting transfers between devices  12.6 us (32%)
  waiting for transfers between devices  11.7 us (29%)
  Pallas kernels  10.8 us (27%)
  other arithmetic  1.64 us (4%)
  matrix products  1.44 us (4%)
  local copies, waits for them, and re-layouts  1.23 us (3%)
    ppermute x13, starting transfers between devices, exchange(): lax.ppermute(value, 'dp', [(i, i ^ distance) for i in range(lax.axis_size...  12.6 us
    ppermute x13, waiting for transfers between devices, exchange(): lax.ppermute(value, 'dp', [(i, i ^ distance) for i in range(lax.axis_size...  11.7 us
    pallas_call x1, Pallas kernels, project(): pl.pallas_call(project_kernel, in_specs=[pl.BlockSpec(memory_space=pl.ANY...  6.35 us
    pallas_call x1, Pallas kernels, inverse(): pl.pallas_call(functools.partial(inverse_kernel, total_tokens), in_specs=...  2.41 us
    pallas_call x1, Pallas kernels, score(): pl.pallas_call(functools.partial(scores_kernel, order), in_specs=[pl.Bloc...  1.56 us
    dot_general x1, matrix products, per_device(): jnp.einsum('tmk,mrk->tmr', out_grads, out_proj, preferred_element_type=F32)  1.44 us
    unnamed x6, local copies, waits for them, and re-layouts  1.23 us
    select_n x4, other arithmetic, halves(): picked.append((jnp.where(upper, high, low), jnp.where(upper, low, high)))  0.96 us
  transfers between devices with their start and end apart: 13, of which 7 were waited for; matrix products, arithmetic and copies ran while one was open for 6% of the time, Pallas kernels for 23%

profile of v4, /device:TPU:0, one launch (start us, length us, event | category | flops | bytes accessed | tf_op | source)
XLA Modules:
  0.0 39.6 jit_solution(1901971246889525245)
XLA Ops:
  0.0 0.0 copy-start
  0.0 3.0 %collective-permute-start = (bf16[8,8192]{1,0:T(8,128)(2,1)}, bf16[8,8192]{1,0:T(8,128)(2,1)S(1)}, u32[]{:S(2)}, u32[]{:S(2)}) collective-permute-start(bf16[8,8192]{1,0:T(8,128)(2,1)} %param.9), channel_id=1, source_target_pairs={{0,4},{1,5},{2,6},{3,7},{4,0},{5,1},{6,2},{7,3},{8,12},{9,13},{10,... | collective-permute-start | bytes 393224 | tf_op jit(solution)/shard_map/ppermute | solution.py:257
  3.0 2.6 %collective-permute-start.2 = (bf16[8,8192]{1,0:T(8,128)(2,1)}, bf16[8,8192]{1,0:T(8,128)(2,1)S(1)}, u32[]{:S(2)}, u32[]{:S(2)}) collective-permute-start(bf16[8,8192]{1,0:T(8,128)(2,1)} %param.9), channel_id=1, source_target_pairs={{0,8},{1,9},{2,10},{3,11},{4,12},{5,13},{6,14},{7,15},{8,0},{9,1},... | collective-permute-start | bytes 393224 | tf_op jit(solution)/shard_map/ppermute | solution.py:257
  5.6 0.0 collective-permute-start.4
  5.6 0.9 %broadcast_select_fusion.7 = (bf16[8,4096]{1,0:T(8,128)(2,1)S(1)}, bf16[8,4096]{1,0:T(8,128)(2,1)S(1)}) fusion(pred[]{:T(512)S(6)} %eq.4, bf16[8,8192]{1,0:T(8,128)(2,1)} %param.9), kind=kLoop, calls=%fused_computation.14 | loop fusion | flops 65536 | bytes 262145 | tf_op jit(solution)/shard_map/jit(_where)/select_n | solution.py:264
  6.5 0.0 copy-start.1
  6.6 1.2 %copy-done.1 = bf16[2,64,4096]{2,1,0:T(8,128)(2,1)S(1)} copy-done((bf16[2,64,4096]{2,1,0:T(8,128)(2,1)S(1)}, bf16[2,64,4096]{2,1,0:T(8,128)(2,1)}, u32[]{:S(2)}) %copy-start.1) | copy-done | bytes 1048600
  7.8 0.0 copy-start.2
  7.8 6.4 %project.1.acts_ref = bf16[1024,128]{1,0:T(8,128)(2,1)S(1)} custom-call(bf16[1024,4096]{1,0:T(8,128)(2,1)} %x_hbm.1, bf16[128,4096]{1,0:T(8,128)(2,1)S(1)} %bitcast.9), custom_call_target="tpu_custom_call" | custom-call | flops 2147483648 | bytes 8388608 | tf_op jit(solution)/shard_map/project/pallas_call | solution.py:59
  14.1 0.0 collective-permute-done
  14.2 0.1 collective-permute-start.1
  14.3 0.0 copy-done
  14.3 0.0 copy-done.2
  14.3 1.4 %fusion.2 = bf16[2,1024,64]{1,2,0:T(8,128)(2,1)S(1)} fusion(bf16[2,64,1024]{2,1,0:T(8,128)(2,1)S(1)} %copy-done, bf16[1024,2,1024]{2,1,0:T(2,128)(2,1)S(1)} %copy-done.2), kind=kOutput, calls=%fused_computation.2 | convolution fusion | flops 268566528 | bytes 4718592 | tf_op jit(solution)/shard_map/tmk,mrk->tmr/dot_general | solution.py:278
  15.7 0.0 collective-permute-done.1
  15.8 0.4 %collective-permute-done.2 = bf16[8,8192]{1,0:T(8,128)(2,1)S(1)} collective-permute-done((bf16[8,8192]{1,0:T(8,128)(2,1)}, bf16[8,8192]{1,0:T(8,128)(2,1)S(1)}, u32[]{:S(2)}, u32[]{:S(2)}) %collective-permute-start.2) | collective-permute-done | bytes 131104 | tf_op jit(solution)/shard_map/ppermute | solution.py:257
  16.2 0.5 %statistics.1 = (f32[64,128]{1,0:T(8,128)S(1)}, f32[64,128]{1,0:T(8,128)S(1)}, f32[64,512]{1,0:T(8,128)S(1)}, f32[64,512]{1,0:T(8,128)S(1)}) custom-call(s32[1]{0:T(128)} %bitcast.1.core_ref, bf16[1024,128]{1,0:T(8,128)(2,1)S(1)} %project.1.acts_ref, bf16[128,1024]{1,0:T(8,128)(2,1)S(1)} %bitcast.10), custom_call_target="tpu_custom_call" | custom-call | tf_op jit(solution)/shard_map/statistics/pallas_call | solution.py:107
  16.7 0.2 collective-permute-start.3
  16.8 1.1 %collective-permute-done.3 = f32[64,128]{1,0:T(8,128)S(1)} collective-permute-done((f32[64,128]{1,0:T(8,128)S(1)}, f32[64,128]{1,0:T(8,128)S(1)}, u32[]{:S(2)}, u32[]{:S(2)}) %collective-permute-start.3) | collective-permute-done | bytes 32800 | tf_op jit(solution)/shard_map/ppermute | solution.py:257
  17.9 0.0 collective-permute-done.4
  18.0 0.2 collective-permute-start.7
  18.2 1.6 %collective-permute-start.5 = (f32[64,128]{1,0:T(8,128)S(1)}, f32[64,128]{1,0:T(8,128)S(1)}, u32[]{:S(2)}, u32[]{:S(2)}) collective-permute-start(f32[64,128]{1,0:T(8,128)S(1)} %add.12), channel_id=1, source_target_pairs={{0,2},{1,3},{2,0},{3,1},{4,6},{5,7},{6,4},{7,5},{8,10},{9,11},{10,... | collective-permute-start | bytes 98312 | tf_op jit(solution)/shard_map/ppermute | solution.py:257
  19.8 0.0 collective-permute-start.6
  19.8 0.5 %collective-permute-start.9 = (bf16[32,4096]{1,0:T(8,128)(2,1)S(1)}, bf16[32,4096]{1,0:T(8,128)(2,1)S(1)}, u32[]{:S(2)}, u32[]{:S(2)}) collective-permute-start(bf16[32,4096]{1,0:T(8,128)(2,1)S(1)} %pad_maximum_fusion.refs_0_), channel_id=1, source_target_pairs={{0,2},{1,3},{2,0},{3,1},{4,6},{5,7},{6,4},{7,5},{8,10},{9,11},{10,... | collective-permute-start | bytes 786440 | tf_op jit(solution)/shard_map/ppermute | solution.py:257
  20.3 1.8 %collective-permute-done.5 = f32[64,128]{1,0:T(8,128)S(1)} collective-permute-done((f32[64,128]{1,0:T(8,128)S(1)}, f32[64,128]{1,0:T(8,128)S(1)}, u32[]{:S(2)}, u32[]{:S(2)}) %collective-permute-start.5) | collective-permute-done | bytes 32800 | tf_op jit(solution)/shard_map/ppermute | solution.py:257
  22.1 0.0 collective-permute-done.7
  22.2 0.0 collective-permute-done.6.recv_ref
  22.2 2.0 %collective-permute-start.11 = (bf16[32,4096]{1,0:T(8,128)(2,1)S(1)}, bf16[32,4096]{1,0:T(8,128)(2,1)S(1)}, u32[]{:S(2)}, u32[]{:S(2)}) collective-permute-start(bf16[32,4096]{1,0:T(8,128)(2,1)S(1)} %pad_maximum_fusion.1.refs_2_), channel_id=1, source_target_pairs={{0,2},{1,3},{2,0},{3,1},{4,6},{5,7},{6,4},{7,5},{8,10},{9,11},{10,... | collective-permute-start | bytes 786440 | tf_op jit(solution)/shard_map/ppermute | solution.py:257
  24.2 0.6 %collective-permute-start.8 = (f32[64,128]{1,0:T(8,128)S(1)}, f32[64,128]{1,0:T(8,128)S(1)}, u32[]{:S(2)}, u32[]{:S(2)}) collective-permute-start(f32[64,128]{1,0:T(8,128)S(1)} %add.13), channel_id=1, source_target_pairs={{0,4},{1,5},{2,6},{3,7},{4,0},{5,1},{6,2},{7,3},{8,12},{9,13},{10,... | collective-permute-start | bytes 98312 | tf_op jit(solution)/shard_map/ppermute | solution.py:257
  24.8 3.3 %collective-permute-done.8 = f32[64,128]{1,0:T(8,128)S(1)} collective-permute-done((f32[64,128]{1,0:T(8,128)S(1)}, f32[64,128]{1,0:T(8,128)S(1)}, u32[]{:S(2)}, u32[]{:S(2)}) %collective-permute-start.8) | collective-permute-done | bytes 32800 | tf_op jit(solution)/shard_map/ppermute | solution.py:257
  28.1 0.8 %collective-permute-done.9.refs_1_ = bf16[32,4096]{1,0:T(8,128)(2,1)S(1)} collective-permute-done((bf16[32,4096]{1,0:T(8,128)(2,1)S(1)}, bf16[32,4096]{1,0:T(8,128)(2,1)S(1)}, u32[]{:S(2)}, u32[]{:S(2)}) %collective-permute-start.9) | collective-permute-done | bytes 262176 | tf_op jit(solution)/shard_map/ppermute | solution.py:257
  28.9 1.7 %collective-permute-start.10 = (f32[64,128]{1,0:T(8,128)S(1)}, f32[64,128]{1,0:T(8,128)S(1)}, u32[]{:S(2)}, u32[]{:S(2)}) collective-permute-start(f32[64,128]{1,0:T(8,128)S(1)} %add.14.refs_0_), channel_id=1, source_target_pairs={{0,8},{1,9},{2,10},{3,11},{4,12},{5,13},{6,14},{7,15},{8,0},{9,1},... | collective-permute-start | bytes 98312 | tf_op jit(solution)/shard_map/ppermute | solution.py:257
  30.6 3.1 %collective-permute-done.10.refs_1_ = f32[64,128]{1,0:T(8,128)S(1)} collective-permute-done((f32[64,128]{1,0:T(8,128)S(1)}, f32[64,128]{1,0:T(8,128)S(1)}, u32[]{:S(2)}, u32[]{:S(2)}) %collective-permute-start.10) | collective-permute-done | bytes 32800 | tf_op jit(solution)/shard_map/ppermute | solution.py:257
  33.8 2.4 %inverse.1.inv_ref = f32[64,128]{1,0:T(8,128)S(1)} custom-call(f32[64,128]{1,0:T(8,128)S(1)} %add.14.refs_0_, f32[64,128]{1,0:T(8,128)S(1)} %collective-permute-done.10.refs_1_), custom_call_target="tpu_custom_call" | custom-call | tf_op jit(solution)/shard_map/inverse/pallas_call | solution.py:181
  36.2 0.0 collective-permute-done.11.refs_3_
  36.2 1.6 %scores.1 = f32[16,128]{1,0:T(8,128)S(1)} custom-call(s32[1]{0:T(128)} %bitcast.place_ref, f32[64,128]{1,0:T(8,128)S(1)} %inverse.1.inv_ref, f32[64,512]{1,0:T(8,128)S(1)} %get-tuple-element.39.keep_ref, f32[64,512]{1,0:T(8,128)S(1)} %collective-permute-done.6.recv_ref, bf16[32,4096]{1,0:T(8,128)(2,1)S(1)} %pad_maximum_fusion.refs_0_, ...), custom_call_target="tpu_custom_call" | custom-call | tf_op jit(solution)/shard_map/scores/pallas_call | solution.py:242
  37.7 0.0 collective-permute-start.12
  37.8 1.2 %collective-permute-done.12 = f32[8,128]{1,0:T(8,128)S(1)} collective-permute-done((f32[8,128]{1,0:T(8,128)S(1)}, f32[8,128]{1,0:T(8,128)S(1)}, u32[]{:S(2)}, u32[]{:S(2)}) %collective-permute-start.12) | collective-permute-done | bytes 4128 | tf_op jit(solution)/shard_map/ppermute | solution.py:257
  39.0 0.6 %slice_add_fusion = f32[8,128]{1,0:T(8,128)} fusion(f32[8,128]{1,0:T(8,128)S(1)} %collective-permute-done.12, f32[16,128]{1,0:T(8,128)S(1)} %scores.1), kind=kLoop, calls=%fused_computation.15 | loop fusion | flops 1024 | bytes 12288 | tf_op jit(solution)/shard_map/add | solution.py:310
  (11 shorter events, 0.1 us)
Async XLA Ops:
  0.0 14.3 %copy-start = (bf16[2,64,1024]{2,1,0:T(8,128)(2,1)S(1)}, bf16[2,64,1024]{2,1,0:T(8,128)(2,1)}, u32[]{:S(2)}) copy-start(bf16[2,64,1024]{2,1,0:T(8,128)(2,1)} %param.8) | copy-start | bytes 786436
  0.0 14.1 %collective-permute-start = (bf16[8,8192]{1,0:T(8,128)(2,1)}, bf16[8,8192]{1,0:T(8,128)(2,1)S(1)}, u32[]{:S(2)}, u32[]{:S(2)}) collective-permute-start(bf16[8,8192]{1,0:T(8,128)(2,1)} %param.9), channel_id=1, source_target_pairs={{0,4},{1,5},{2,6},{3,7},{4,0},{5,1},{6,2},{7,3},{8,12},{9,13},{10,... | collective-permute-start | bytes 393224 | tf_op jit(solution)/shard_map/ppermute | solution.py:257
  3.0 13.2 %collective-permute-start.2 = (bf16[8,8192]{1,0:T(8,128)(2,1)}, bf16[8,8192]{1,0:T(8,128)(2,1)S(1)}, u32[]{:S(2)}, u32[]{:S(2)}) collective-permute-start(bf16[8,8192]{1,0:T(8,128)(2,1)} %param.9), channel_id=1, source_target_pairs={{0,8},{1,9},{2,10},{3,11},{4,12},{5,13},{6,14},{7,15},{8,0},{9,1},... | collective-permute-start | bytes 393224 | tf_op jit(solution)/shard_map/ppermute | solution.py:257
  5.6 12.3 %collective-permute-start.4 = (bf16[8,8192]{1,0:T(8,128)(2,1)}, bf16[8,8192]{1,0:T(8,128)(2,1)S(1)}, u32[]{:S(2)}, u32[]{:S(2)}) collective-permute-start(bf16[8,8192]{1,0:T(8,128)(2,1)} %param.9), channel_id=1, source_target_pairs={{0,12},{1,13},{2,14},{3,15},{4,8},{5,9},{6,10},{7,11},{8,4},{9,5},... | collective-permute-start | bytes 393224 | tf_op jit(solution)/shard_map/ppermute | solution.py:257
  6.5 1.2 %copy-start.1 = (bf16[2,64,4096]{2,1,0:T(8,128)(2,1)S(1)}, bf16[2,64,4096]{2,1,0:T(8,128)(2,1)}, u32[]{:S(2)}) copy-start(bf16[2,64,4096]{2,1,0:T(8,128)(2,1)} %param.7) | copy-start | bytes 3145732
  7.8 6.5 %copy-start.2 = (bf16[1024,2,1024]{2,1,0:T(2,128)(2,1)S(1)}, bf16[1024,2,1024]{2,1,0:T(2,128)(2,1)}, u32[]{:S(2)}) copy-start(bf16[1024,2,1024]{2,1,0:T(2,128)(2,1)} %param.6) | copy-start | bytes 12582916
  14.2 1.5 %collective-permute-start.1 = (bf16[16,4096]{1,0:T(8,128)(2,1)S(1)}, bf16[16,4096]{1,0:T(8,128)(2,1)S(1)}, u32[]{:S(2)}, u32[]{:S(2)}) collective-permute-start(bf16[16,4096]{1,0:T(8,128)(2,1)S(1)} %pad_maximum_fusion.2), channel_id=1, source_target_pairs={{0,1},{1,0},{2,3},{3,2},{4,5},{5,4},{6,7},{7,6},{8,9},{9,8},{10,11... | collective-permute-start | bytes 393224 | tf_op jit(solution)/shard_map/ppermute | solution.py:257
  16.7 1.3 %collective-permute-start.3 = (f32[64,128]{1,0:T(8,128)S(1)}, f32[64,128]{1,0:T(8,128)S(1)}, u32[]{:S(2)}, u32[]{:S(2)}) collective-permute-start(f32[64,128]{1,0:T(8,128)S(1)} %get-tuple-element.30), channel_id=1, source_target_pairs={{0,1},{1,0},{2,3},{3,2},{4,5},{5,4},{6,7},{7,6},{8,9},{9,8},{10,11... | collective-permute-start | bytes 98312 | tf_op jit(solution)/shard_map/ppermute | solution.py:257
  18.0 4.2 %collective-permute-start.7 = (bf16[16,4096]{1,0:T(8,128)(2,1)S(1)}, bf16[16,4096]{1,0:T(8,128)(2,1)S(1)}, u32[]{:S(2)}, u32[]{:S(2)}) collective-permute-start(bf16[16,4096]{1,0:T(8,128)(2,1)S(1)} %pad_maximum_fusion.3), channel_id=1, source_target_pairs={{0,1},{1,0},{2,3},{3,2},{4,5},{5,4},{6,7},{7,6},{8,9},{9,8},{10,11... | collective-permute-start | bytes 393224 | tf_op jit(solution)/shard_map/ppermute | solution.py:257
  18.2 3.9 %collective-permute-start.5 = (f32[64,128]{1,0:T(8,128)S(1)}, f32[64,128]{1,0:T(8,128)S(1)}, u32[]{:S(2)}, u32[]{:S(2)}) collective-permute-start(f32[64,128]{1,0:T(8,128)S(1)} %add.12), channel_id=1, source_target_pairs={{0,2},{1,3},{2,0},{3,1},{4,6},{5,7},{6,4},{7,5},{8,10},{9,11},{10,... | collective-permute-start | bytes 98312 | tf_op jit(solution)/shard_map/ppermute | solution.py:257
  19.8 2.3 %collective-permute-start.6 = (f32[64,512]{1,0:T(8,128)S(1)}, f32[64,512]{1,0:T(8,128)S(1)}, u32[]{:S(2)}, u32[]{:S(2)}) collective-permute-start(f32[64,512]{1,0:T(8,128)S(1)} %get-tuple-element.33), channel_id=1, source_target_pairs={{0,1},{1,0},{2,3},{3,2},{4,5},{5,4},{6,7},{7,6},{8,9},{9,8},{10,11... | collective-permute-start | bytes 393224 | tf_op jit(solution)/shard_map/ppermute | solution.py:257
  19.8 9.1 %collective-permute-start.9 = (bf16[32,4096]{1,0:T(8,128)(2,1)S(1)}, bf16[32,4096]{1,0:T(8,128)(2,1)S(1)}, u32[]{:S(2)}, u32[]{:S(2)}) collective-permute-start(bf16[32,4096]{1,0:T(8,128)(2,1)S(1)} %pad_maximum_fusion.refs_0_), channel_id=1, source_target_pairs={{0,2},{1,3},{2,0},{3,1},{4,6},{5,7},{6,4},{7,5},{8,10},{9,11},{10,... | collective-permute-start | bytes 786440 | tf_op jit(solution)/shard_map/ppermute | solution.py:257
  22.2 14.0 %collective-permute-start.11 = (bf16[32,4096]{1,0:T(8,128)(2,1)S(1)}, bf16[32,4096]{1,0:T(8,128)(2,1)S(1)}, u32[]{:S(2)}, u32[]{:S(2)}) collective-permute-start(bf16[32,4096]{1,0:T(8,128)(2,1)S(1)} %pad_maximum_fusion.1.refs_2_), channel_id=1, source_target_pairs={{0,2},{1,3},{2,0},{3,1},{4,6},{5,7},{6,4},{7,5},{8,10},{9,11},{10,... | collective-permute-start | bytes 786440 | tf_op jit(solution)/shard_map/ppermute | solution.py:257
  24.2 3.9 %collective-permute-start.8 = (f32[64,128]{1,0:T(8,128)S(1)}, f32[64,128]{1,0:T(8,128)S(1)}, u32[]{:S(2)}, u32[]{:S(2)}) collective-permute-start(f32[64,128]{1,0:T(8,128)S(1)} %add.13), channel_id=1, source_target_pairs={{0,4},{1,5},{2,6},{3,7},{4,0},{5,1},{6,2},{7,3},{8,12},{9,13},{10,... | collective-permute-start | bytes 98312 | tf_op jit(solution)/shard_map/ppermute | solution.py:257
  28.9 4.8 %collective-permute-start.10 = (f32[64,128]{1,0:T(8,128)S(1)}, f32[64,128]{1,0:T(8,128)S(1)}, u32[]{:S(2)}, u32[]{:S(2)}) collective-permute-start(f32[64,128]{1,0:T(8,128)S(1)} %add.14.refs_0_), channel_id=1, source_target_pairs={{0,8},{1,9},{2,10},{3,11},{4,12},{5,13},{6,14},{7,15},{8,0},{9,1},... | collective-permute-start | bytes 98312 | tf_op jit(solution)/shard_map/ppermute | solution.py:257
  37.7 1.2 %collective-permute-start.12 = (f32[8,128]{1,0:T(8,128)S(1)}, f32[8,128]{1,0:T(8,128)S(1)}, u32[]{:S(2)}, u32[]{:S(2)}) collective-permute-start(f32[8,128]{1,0:T(8,128)S(1)} %slice.9), channel_id=1, source_target_pairs={{0,1},{1,0},{2,3},{3,2},{4,5},{5,4},{6,7},{7,6},{8,9},{9,8},{10,11... | collective-permute-start | bytes 12296 | tf_op jit(solution)/shard_map/ppermute | solution.py:257

commit v5 on v4

--- a/solution.py
+++ b/solution.py
@@ -11,7 +11,7 @@
 LEN = 128
 PAIR = 2 * R
 DAMPING = 0.1
-STEP = 512
+ROWS = 256
 BLOCK = 4
 GROUP = 4
 
@@ -26,49 +26,48 @@
 
 NN = ((1,), (0,))
 NT = ((1,), (1,))
-TN = ((0,), (0,))
-
-
-def project_kernel(x_hbm, w_hbm, acts_ref, x_buf, w_buf, total, x_sem, w_sem):
-    chunks, _, step = x_buf.shape
-
-    def x_copy(k):
-        return pltpu.make_async_copy(x_hbm.at[:, k * step : (k + 1) * step], x_buf.at[k], x_sem.at[k])
-
-    def w_copy(k):
-        return pltpu.make_async_copy(w_hbm.at[:, k * step : (k + 1) * step], w_buf.at[k], w_sem.at[k])
-
-    for k in range(chunks):
-        w_copy(k).start()
-        x_copy(k).start()
-    for k in range(chunks):
-        w_copy(k).wait()
-        x_copy(k).wait()
-        term = dot(x_buf[k], w_buf[k], NT)
-        if k == 0:
-            total[...] = term
-        elif k < chunks - 1:
-            total[...] += term
-        else:
-            acts_ref[...] = (total[...] + term).astype(BF16)
+
+
+def stage_kernel(core_ref, source_ref, all_ref, keep_ref, send_ref):
+    first = core_ref[0] == 0
+    values = source_ref[...]
+    half = values.shape[1] // 2
+    low, high = values[:, :half], values[:, half:]
+    all_ref[...] = values
+    keep_ref[...] = jnp.where(first, low, high)
+    send_ref[...] = jnp.where(first, high, low)
+
+
+def stage(core, queries):
+    rows, entries = queries.shape
+    vmem = pl.BlockSpec(memory_space=pltpu.VMEM)
+    half = jax.ShapeDtypeStruct((rows, entries // 2), BF16)
+    return pl.pallas_call(
+        stage_kernel,
+        in_specs=[pl.BlockSpec(memory_space=pltpu.SMEM), vmem],
+        out_specs=[vmem] * 3,
+        out_shape=[jax.ShapeDtypeStruct(queries.shape, BF16), half, half],
+        compiler_params=pltpu.CompilerParams(vmem_limit_bytes=16 * MIB),
+        cost_estimate=pl.CostEstimate(flops=8 * 10**9, bytes_accessed=2**18, transcendentals=0),
+        name="stage",
+    )(core, queries)
+
+
+def project_kernel(x_ref, w_ref, acts_ref):
+    tokens = x_ref.shape[0]
+    for at in range(0, tokens, ROWS):
+        acts_ref[:, at : at + ROWS] = dot(w_ref[...], x_ref[at : at + ROWS], NT).astype(BF16)
 
 
 def project(layer_input, in_flat):
     tokens, width = layer_input.shape
-    chunks = width // STEP
+    vmem = pl.BlockSpec(memory_space=pltpu.VMEM)
     return pl.pallas_call(
         project_kernel,
-        in_specs=[pl.BlockSpec(memory_space=pl.ANY)] * 2,
-        out_specs=pl.BlockSpec(memory_space=pltpu.VMEM),
-        out_shape=jax.ShapeDtypeStruct((tokens, PAIR), BF16),
-        scratch_shapes=[
-            pltpu.VMEM((chunks, tokens, STEP), BF16),
-            pltpu.VMEM((chunks, PAIR, STEP), BF16),
-            pltpu.VMEM((tokens, PAIR), F32),
-            pltpu.SemaphoreType.DMA((chunks,)),
-            pltpu.SemaphoreType.DMA((chunks,)),
-        ],
-        compiler_params=pltpu.CompilerParams(vmem_limit_bytes=48 * MIB),
+        in_specs=[vmem, vmem],
+        out_specs=vmem,
+        out_shape=jax.ShapeDtypeStruct((PAIR, tokens), BF16),
+        compiler_params=pltpu.CompilerParams(vmem_limit_bytes=24 * MIB),
         cost_estimate=pl.CostEstimate(
             flops=4 * tokens * width * PAIR, bytes_accessed=2 * tokens * width, transcendentals=0
         ),
@@ -81,17 +80,17 @@
     acts = acts_ref[...]
     outs = outs_ref[...]
     low = lax.broadcasted_iota(jnp.int32, (R, PAIR), 1) < R
-    cov_in = dot(acts, acts, TN)
+    cov_in = dot(acts, acts, NT)
     cov_out = dot(outs, outs, NT)
     cov0 = jnp.where(low, cov_in[:R], pltpu.roll(cov_out[:R], R, 1))
     cov1 = jnp.where(low, pltpu.roll(cov_in[R:], R, 1), cov_out[R:])
     keep_cov[...] = jnp.where(first, cov0, cov1)
     send_cov[...] = jnp.where(first, cov1, cov0)
-    for pair in range(acts.shape[0] // LEN // 2):
+    for pair in range(acts.shape[1] // LEN // 2):
         blocks = []
         for seq in (2 * pair, 2 * pair + 1):
-            rows = slice(seq * LEN, (seq + 1) * LEN)
-            blocks.append(dot(outs[:, rows], acts[rows], NN) * (1.0 / LEN))
+            tokens = slice(seq * LEN, (seq + 1) * LEN)
+            blocks.append(dot(outs[:, tokens], acts[:, tokens], NT) * (1.0 / LEN))
         mom0 = jnp.where(low, blocks[0][:R], pltpu.roll(blocks[1][:R], R, 1))
         mom1 = jnp.where(low, pltpu.roll(blocks[0][R:], R, 1), blocks[1][R:])
         lanes = slice(pair * PAIR, (pair + 1) * PAIR)
@@ -100,7 +99,7 @@
 
 
 def statistics(core, acts, outs):
-    seqs = acts.shape[0] // LEN
+    seqs = acts.shape[1] // LEN
     cov = jax.ShapeDtypeStruct((R, PAIR), F32)
     mom = jax.ShapeDtypeStruct((R, seqs * R), F32)
     vmem = pl.BlockSpec(memory_space=pltpu.VMEM)
@@ -257,12 +256,9 @@
     return lax.ppermute(value, "dp", [(i, i ^ distance) for i in range(lax.axis_size("dp"))])
 
 
-def halves(values, upper):
-    picked = []
-    for value in values:
-        low, high = jnp.split(value, 2, axis=1)
-        picked.append((jnp.where(upper, high, low), jnp.where(upper, low, high)))
-    return [jnp.concatenate(side, axis=0) for side in zip(*picked)]
+def halves(value, upper):
+    low, high = jnp.split(value, 2, axis=1)
+    return jnp.where(upper, high, low), jnp.where(upper, low, high)
 
 
 def per_device(layer_input, out_grads, in_proj, out_proj, queries):
@@ -271,31 +267,35 @@
     slabs = devices // GROUP
     place = lax.axis_index("dp").astype(jnp.int32)
     module = place & 1
-    column = [queries] + [exchange(queries, slab * GROUP) for slab in range(1, slabs)]
+    own, near, send_near = stage(module.reshape(1), queries)
+    column = [own] + [exchange(own, slab * GROUP) for slab in range(1, slabs)]
     acts = project(layer_input, in_proj.reshape(PAIR, in_proj.shape[2]))
     acts, out_grads, column[1] = lax.optimization_barrier((acts, out_grads, column[1]))
-    near, send_near = halves(column[:2], module == 1)
+    keep, send = halves(column[1], module == 1)
+    near = jnp.concatenate([near, keep], axis=0)
+    send_near = jnp.concatenate([send_near, send], axis=0)
     outs = jnp.einsum("tmk,mrk->tmr", out_grads, out_proj, preferred_element_type=F32).astype(BF16)
     outs = outs.reshape(local_tokens, PAIR).T
     near = jnp.concatenate([near, exchange(send_near, 1)], axis=0)
-    acts, outs, near, column[2] = lax.optimization_barrier((acts, outs, near, column[2]))
+    acts, outs, near = lax.optimization_barrier((acts, outs, near))
     keep_cov, send_cov, keep_mom, send_mom = statistics(module.reshape(1), acts, outs)
     cov = keep_cov + exchange(send_cov, 1)
     moments = [keep_mom, exchange(send_mom, 1)]
-    cov, column[3] = lax.optimization_barrier((cov, column[3]))
+    cov, column[2] = lax.optimization_barrier((cov, column[2]))
     cov = cov + exchange(cov, 2)
-    far, send_far = halves(column[2:], module == 1)
+    far, send_far = zip(*(halves(value, module == 1) for value in column[2:]))
+    far, send_far = jnp.concatenate(far, axis=0), jnp.concatenate(send_far, axis=0)
     far = jnp.concatenate([far, exchange(send_far, 1)], axis=0)
     cov, moments, far = lax.optimization_barrier((cov, moments, far))
     across = exchange(near, 2)
     cov = cov + exchange(cov, GROUP)
-    cov, across = lax.optimization_barrier((cov, across))
     distance = 2 * GROUP
     while distance < devices:
         last = exchange(cov, distance)
         if 2 * distance < devices:
             cov = cov + last
         distance *= 2
+    cov, last, across = lax.optimization_barrier((cov, last, across))
     inv = inverse([cov, last], local_tokens * devices)
     gathered = [near, across, far, exchange(far, 2)]
     order = [

time: 39.7 us -> 37.8 us (0.952)
  waiting for transfers between devices: 11.7 us -> 8.06 us
  Pallas kernels: 10.8 us -> 7.39 us
  local copies, waits for them, and re-layouts: 1.23 us -> 4.35 us
  starting transfers between devices: 12.6 us -> 15.6 us
  other arithmetic: 1.64 us -> 0.72 us
    ppermute x13, waiting for transfers between devices: 11.7 us -> 8.06 us  [exchange(): lax.ppermute(value, 'dp', [(i, i ^ distance) for i in range(lax.axis_size...]
    pallas_call x1 -> x2, Pallas kernels: 6.35 us -> 2.9 us  [the longest x1 2.89 us: project(): pl.pallas_call(project_kernel, in_specs=[vmem, vmem], out_specs=vmem, out...]
    unnamed x6 -> x10, local copies, waits for them, and re-layouts: 1.23 us -> 4.34 us
    ppermute x13, starting transfers between devices: 12.6 us -> 15.6 us  [exchange(): lax.ppermute(value, 'dp', [(i, i ^ distance) for i in range(lax.axis_size...]
    select_n x4 -> x3, other arithmetic: 0.96 us -> 0.04 us  [halves(): return (jnp.where(upper, high, low), jnp.where(upper, low, high))]
  transfers between devices with their start and end apart: 13 -> 13, of which waited for: 7 -> 6; matrix products, arithmetic and copies ran while one was open for 6% -> 4% of each run, Pallas kernels for 23% -> 15%
where the time goes in v5:
time: 37.8 us; the launch traced here: 37.7 us
  starting transfers between devices  15.6 us (41%)
  waiting for transfers between devices  8.06 us (21%)
  Pallas kernels  7.39 us (20%)
  local copies, waits for them, and re-layouts  4.35 us (12%)
  matrix products  1.44 us (4%)
  other arithmetic  0.72 us (2%)
    ppermute x13, starting transfers between devices, exchange(): lax.ppermute(value, 'dp', [(i, i ^ distance) for i in range(lax.axis_size...  15.6 us
    ppermute x13, waiting for transfers between devices, exchange(): lax.ppermute(value, 'dp', [(i, i ^ distance) for i in range(lax.axis_size...  8.06 us
    unnamed x10, local copies, waits for them, and re-layouts  4.34 us
    pallas_call x1, Pallas kernels, project(): pl.pallas_call(project_kernel, in_specs=[vmem, vmem], out_specs=vmem, out...  2.89 us
    pallas_call x1, Pallas kernels, inverse(): pl.pallas_call(functools.partial(inverse_kernel, total_tokens), in_specs=...  2.41 us
    pallas_call x1, Pallas kernels, score(): pl.pallas_call(functools.partial(scores_kernel, order), in_specs=[pl.Bloc...  1.56 us
    dot_general x1, matrix products, per_device(): jnp.einsum('tmk,mrk->tmr', out_grads, out_proj, preferred_element_type=F32)  1.44 us
  transfers between devices with their start and end apart: 13, of which 6 were waited for; matrix products, arithmetic and copies ran while one was open for 4% of the time, Pallas kernels for 15%

profile of v5, /device:TPU:0, one launch (start us, length us, event | category | flops | bytes accessed | tf_op | source)
XLA Modules:
  0.0 37.7 jit_solution(9102262192127930385)
XLA Ops:
  0.0 0.0 copy-start
  0.0 0.0 copy-start.3
  0.0 0.9 %copy-done.3 = bf16[8,8192]{1,0:T(8,128)(2,1)S(1)} copy-done((bf16[8,8192]{1,0:T(8,128)(2,1)S(1)}, bf16[8,8192]{1,0:T(8,128)(2,1)}, u32[]{:S(2)}) %copy-start.3) | copy-done | bytes 131096
  1.0 0.0 copy-start.2
  1.0 3.1 %collective-permute-start = (bf16[8,8192]{1,0:T(8,128)(2,1)S(1)}, bf16[8,8192]{1,0:T(8,128)(2,1)S(1)}, u32[]{:S(2)}, u32[]{:S(2)}) collective-permute-start(bf16[8,8192]{1,0:T(8,128)(2,1)S(1)} %get-tuple-element.27), channel_id=1, source_target_pairs={{0,4},{1,5},{2,6},{3,7},{4,0},{5,1},{6,2},{7,3},{8,12},{9,13},{10,... | collective-permute-start | bytes 393224 | tf_op jit(solution)/shard_map/ppermute | solution.py:256
  4.1 2.6 %collective-permute-start.3 = (bf16[8,8192]{1,0:T(8,128)(2,1)S(1)}, bf16[8,8192]{1,0:T(8,128)(2,1)S(1)}, u32[]{:S(2)}, u32[]{:S(2)}) collective-permute-start(bf16[8,8192]{1,0:T(8,128)(2,1)S(1)} %get-tuple-element.27), channel_id=1, source_target_pairs={{0,8},{1,9},{2,10},{3,11},{4,12},{5,13},{6,14},{7,15},{8,0},{9,1},... | collective-permute-start | bytes 393224 | tf_op jit(solution)/shard_map/ppermute | solution.py:256
  6.7 0.0 collective-permute-start.6
  6.7 0.0 copy-done.2
  6.7 0.0 copy-start.1
  6.7 3.4 %copy-done.1 = bf16[1024,4096]{1,0:T(8,128)(2,1)S(1)} copy-done((bf16[1024,4096]{1,0:T(8,128)(2,1)S(1)}, bf16[1024,4096]{1,0:T(8,128)(2,1)}, u32[]{:S(2)}) %copy-start.1) | copy-done | bytes 8388632
  10.0 0.0 copy-start.4
  10.0 2.9 %project.1.acts_ref = bf16[128,1024]{1,0:T(8,128)(2,1)S(1)} custom-call(bf16[1024,4096]{1,0:T(8,128)(2,1)S(1)} %copy-done.1, bf16[128,4096]{1,0:T(8,128)(2,1)S(1)} %bitcast.9), custom_call_target="tpu_custom_call" | custom-call | flops 2147483648 | bytes 8388608 | tf_op jit(solution)/shard_map/project/pallas_call | solution.py:65
  12.9 0.0 collective-permute-done
  13.0 0.1 collective-permute-start.1
  13.1 0.0 copy-done
  13.1 0.0 copy-done.4
  13.1 1.4 %fusion.2 = bf16[2,1024,64]{1,2,0:T(8,128)(2,1)S(1)} fusion(bf16[2,64,1024]{2,1,0:T(8,128)(2,1)S(1)} %copy-done, bf16[1024,2,1024]{2,1,0:T(2,128)(2,1)S(1)} %copy-done.4), kind=kOutput, calls=%fused_computation.2 | convolution fusion | flops 268566528 | bytes 4718592 | tf_op jit(solution)/shard_map/tmk,mrk->tmr/dot_general | solution.py:277
  14.5 0.0 collective-permute-done.1
  14.6 0.5 %statistics.1 = (f32[64,128]{1,0:T(8,128)S(1)}, f32[64,128]{1,0:T(8,128)S(1)}, f32[64,512]{1,0:T(8,128)S(1)}, f32[64,512]{1,0:T(8,128)S(1)}) custom-call(s32[1]{0:T(128)} %bitcast.1.core_ref, bf16[128,1024]{1,0:T(8,128)(2,1)S(1)} %project.1.acts_ref, bf16[128,1024]{1,0:T(8,128)(2,1)S(1)} %bitcast.10), custom_call_target="tpu_custom_call" | custom-call | tf_op jit(solution)/shard_map/statistics/pallas_call | solution.py:106
  15.1 0.5 %collective-permute-start.2 = (f32[64,128]{1,0:T(8,128)S(1)}, f32[64,128]{1,0:T(8,128)S(1)}, u32[]{:S(2)}, u32[]{:S(2)}) collective-permute-start(f32[64,128]{1,0:T(8,128)S(1)} %get-tuple-element.36), channel_id=1, source_target_pairs={{0,1},{1,0},{2,3},{3,2},{4,5},{5,4},{6,7},{7,6},{8,9},{9,8},{10,11... | collective-permute-start | bytes 98312 | tf_op jit(solution)/shard_map/ppermute | solution.py:256
  15.6 0.0 collective-permute-done.6
  15.7 0.8 %collective-permute-done.2 = f32[64,128]{1,0:T(8,128)S(1)} collective-permute-done((f32[64,128]{1,0:T(8,128)S(1)}, f32[64,128]{1,0:T(8,128)S(1)}, u32[]{:S(2)}, u32[]{:S(2)}) %collective-permute-start.2) | collective-permute-done | bytes 32800 | tf_op jit(solution)/shard_map/ppermute | solution.py:256
  16.5 0.5 %collective-permute-done.3 = bf16[8,8192]{1,0:T(8,128)(2,1)S(1)} collective-permute-done((bf16[8,8192]{1,0:T(8,128)(2,1)S(1)}, bf16[8,8192]{1,0:T(8,128)(2,1)S(1)}, u32[]{:S(2)}, u32[]{:S(2)}) %collective-permute-start.3) | collective-permute-done | bytes 131104 | tf_op jit(solution)/shard_map/ppermute | solution.py:256
  17.0 0.1 collective-permute-start.7
  17.1 1.6 %collective-permute-start.4 = (f32[64,128]{1,0:T(8,128)S(1)}, f32[64,128]{1,0:T(8,128)S(1)}, u32[]{:S(2)}, u32[]{:S(2)}) collective-permute-start(f32[64,128]{1,0:T(8,128)S(1)} %add.12), channel_id=1, source_target_pairs={{0,2},{1,3},{2,0},{3,1},{4,6},{5,7},{6,4},{7,5},{8,10},{9,11},{10,... | collective-permute-start | bytes 98312 | tf_op jit(solution)/shard_map/ppermute | solution.py:256
  18.7 0.1 collective-permute-start.5
  18.9 0.5 %collective-permute-start.10 = (bf16[32,4096]{1,0:T(8,128)(2,1)S(1)}, bf16[32,4096]{1,0:T(8,128)(2,1)S(1)}, u32[]{:S(2)}, u32[]{:S(2)}) collective-permute-start(bf16[32,4096]{1,0:T(8,128)(2,1)S(1)} %pad_maximum_fusion.refs_0_), channel_id=1, source_target_pairs={{0,2},{1,3},{2,0},{3,1},{4,6},{5,7},{6,4},{7,5},{8,10},{9,11},{10,... | collective-permute-start | bytes 786440 | tf_op jit(solution)/shard_map/ppermute | solution.py:256
  19.4 1.7 %collective-permute-done.4 = f32[64,128]{1,0:T(8,128)S(1)} collective-permute-done((f32[64,128]{1,0:T(8,128)S(1)}, f32[64,128]{1,0:T(8,128)S(1)}, u32[]{:S(2)}, u32[]{:S(2)}) %collective-permute-start.4) | collective-permute-done | bytes 32800 | tf_op jit(solution)/shard_map/ppermute | solution.py:256
  21.1 0.0 collective-permute-done.7
  21.1 0.0 collective-permute-done.5.recv_ref
  21.1 1.9 %collective-permute-start.11 = (bf16[32,4096]{1,0:T(8,128)(2,1)S(1)}, bf16[32,4096]{1,0:T(8,128)(2,1)S(1)}, u32[]{:S(2)}, u32[]{:S(2)}) collective-permute-start(bf16[32,4096]{1,0:T(8,128)(2,1)S(1)} %pad_maximum_fusion.1.refs_2_), channel_id=1, source_target_pairs={{0,2},{1,3},{2,0},{3,1},{4,6},{5,7},{6,4},{7,5},{8,10},{9,11},{10,... | collective-permute-start | bytes 786440 | tf_op jit(solution)/shard_map/ppermute | solution.py:256
  23.1 2.0 %collective-permute-start.8 = (f32[64,128]{1,0:T(8,128)S(1)}, f32[64,128]{1,0:T(8,128)S(1)}, u32[]{:S(2)}, u32[]{:S(2)}) collective-permute-start(f32[64,128]{1,0:T(8,128)S(1)} %add.13), channel_id=1, source_target_pairs={{0,4},{1,5},{2,6},{3,7},{4,0},{5,1},{6,2},{7,3},{8,12},{9,13},{10,... | collective-permute-start | bytes 98312 | tf_op jit(solution)/shard_map/ppermute | solution.py:256
  25.1 2.0 %collective-permute-done.8 = f32[64,128]{1,0:T(8,128)S(1)} collective-permute-done((f32[64,128]{1,0:T(8,128)S(1)}, f32[64,128]{1,0:T(8,128)S(1)}, u32[]{:S(2)}, u32[]{:S(2)}) %collective-permute-start.8) | collective-permute-done | bytes 32800 | tf_op jit(solution)/shard_map/ppermute | solution.py:256
  27.0 3.0 %collective-permute-start.9 = (f32[64,128]{1,0:T(8,128)S(1)}, f32[64,128]{1,0:T(8,128)S(1)}, u32[]{:S(2)}, u32[]{:S(2)}) collective-permute-start(f32[64,128]{1,0:T(8,128)S(1)} %add.14.refs_0_), channel_id=1, source_target_pairs={{0,8},{1,9},{2,10},{3,11},{4,12},{5,13},{6,14},{7,15},{8,0},{9,1},... | collective-permute-start | bytes 98312 | tf_op jit(solution)/shard_map/ppermute | solution.py:256
  30.0 1.9 %collective-permute-done.9.refs_1_ = f32[64,128]{1,0:T(8,128)S(1)} collective-permute-done((f32[64,128]{1,0:T(8,128)S(1)}, f32[64,128]{1,0:T(8,128)S(1)}, u32[]{:S(2)}, u32[]{:S(2)}) %collective-permute-start.9) | collective-permute-done | bytes 32800 | tf_op jit(solution)/shard_map/ppermute | solution.py:256
  31.9 0.0 collective-permute-done.10.refs_1_
  31.9 2.4 %inverse.1.inv_ref = f32[64,128]{1,0:T(8,128)S(1)} custom-call(f32[64,128]{1,0:T(8,128)S(1)} %add.14.refs_0_, f32[64,128]{1,0:T(8,128)S(1)} %collective-permute-done.9.refs_1_), custom_call_target="tpu_custom_call" | custom-call | tf_op jit(solution)/shard_map/inverse/pallas_call | solution.py:180
  34.3 0.0 collective-permute-done.11.refs_3_
  34.3 1.6 %scores.1 = f32[16,128]{1,0:T(8,128)S(1)} custom-call(s32[1]{0:T(128)} %bitcast.place_ref, f32[64,128]{1,0:T(8,128)S(1)} %inverse.1.inv_ref, f32[64,512]{1,0:T(8,128)S(1)} %get-tuple-element.45.keep_ref, f32[64,512]{1,0:T(8,128)S(1)} %collective-permute-done.5.recv_ref, bf16[32,4096]{1,0:T(8,128)(2,1)S(1)} %pad_maximum_fusion.refs_0_, ...), custom_call_target="tpu_custom_call" | custom-call | tf_op jit(solution)/shard_map/scores/pallas_call | solution.py:241
  35.9 0.0 collective-permute-start.12
  35.9 1.2 %collective-permute-done.12 = f32[8,128]{1,0:T(8,128)S(1)} collective-permute-done((f32[8,128]{1,0:T(8,128)S(1)}, f32[8,128]{1,0:T(8,128)S(1)}, u32[]{:S(2)}, u32[]{:S(2)}) %collective-permute-start.12) | collective-permute-done | bytes 4128 | tf_op jit(solution)/shard_map/ppermute | solution.py:256
  37.1 0.6 %slice_add_fusion = f32[8,128]{1,0:T(8,128)} fusion(f32[8,128]{1,0:T(8,128)S(1)} %collective-permute-done.12, f32[16,128]{1,0:T(8,128)S(1)} %scores.1), kind=kLoop, calls=%fused_computation.13 | loop fusion | flops 1024 | bytes 12288 | tf_op jit(solution)/shard_map/add | solution.py:310
  (12 shorter events, 0.1 us)
Async XLA Ops:
  0.0 13.1 %copy-start = (bf16[2,64,1024]{2,1,0:T(8,128)(2,1)S(1)}, bf16[2,64,1024]{2,1,0:T(8,128)(2,1)}, u32[]{:S(2)}) copy-start(bf16[2,64,1024]{2,1,0:T(8,128)(2,1)} %param.8) | copy-start | bytes 786436
  0.0 0.9 %copy-start.3 = (bf16[8,8192]{1,0:T(8,128)(2,1)S(1)}, bf16[8,8192]{1,0:T(8,128)(2,1)}, u32[]{:S(2)}) copy-start(bf16[8,8192]{1,0:T(8,128)(2,1)} %source_ref.1) | copy-start | bytes 393220
  1.0 5.7 %copy-start.2 = (bf16[2,64,4096]{2,1,0:T(8,128)(2,1)S(1)}, bf16[2,64,4096]{2,1,0:T(8,128)(2,1)}, u32[]{:S(2)}) copy-start(bf16[2,64,4096]{2,1,0:T(8,128)(2,1)} %param.7) | copy-start | bytes 3145732
  1.0 12.0 %collective-permute-start = (bf16[8,8192]{1,0:T(8,128)(2,1)S(1)}, bf16[8,8192]{1,0:T(8,128)(2,1)S(1)}, u32[]{:S(2)}, u32[]{:S(2)}) collective-permute-start(bf16[8,8192]{1,0:T(8,128)(2,1)S(1)} %get-tuple-element.27), channel_id=1, source_target_pairs={{0,4},{1,5},{2,6},{3,7},{4,0},{5,1},{6,2},{7,3},{8,12},{9,13},{10,... | collective-permute-start | bytes 393224 | tf_op jit(solution)/shard_map/ppermute | solution.py:256
  4.1 12.9 %collective-permute-start.3 = (bf16[8,8192]{1,0:T(8,128)(2,1)S(1)}, bf16[8,8192]{1,0:T(8,128)(2,1)S(1)}, u32[]{:S(2)}, u32[]{:S(2)}) collective-permute-start(bf16[8,8192]{1,0:T(8,128)(2,1)S(1)} %get-tuple-element.27), channel_id=1, source_target_pairs={{0,8},{1,9},{2,10},{3,11},{4,12},{5,13},{6,14},{7,15},{8,0},{9,1},... | collective-permute-start | bytes 393224 | tf_op jit(solution)/shard_map/ppermute | solution.py:256
  6.7 9.0 %collective-permute-start.6 = (bf16[8,8192]{1,0:T(8,128)(2,1)S(1)}, bf16[8,8192]{1,0:T(8,128)(2,1)S(1)}, u32[]{:S(2)}, u32[]{:S(2)}) collective-permute-start(bf16[8,8192]{1,0:T(8,128)(2,1)S(1)} %get-tuple-element.27), channel_id=1, source_target_pairs={{0,12},{1,13},{2,14},{3,15},{4,8},{5,9},{6,10},{7,11},{8,4},{9,5},... | collective-permute-start | bytes 393224 | tf_op jit(solution)/shard_map/ppermute | solution.py:256
  6.7 3.4 %copy-start.1 = (bf16[1024,4096]{1,0:T(8,128)(2,1)S(1)}, bf16[1024,4096]{1,0:T(8,128)(2,1)}, u32[]{:S(2)}) copy-start(bf16[1024,4096]{1,0:T(8,128)(2,1)} %x_ref.1) | copy-start | bytes 25165828
  10.0 3.0 %copy-start.4 = (bf16[1024,2,1024]{2,1,0:T(2,128)(2,1)S(1)}, bf16[1024,2,1024]{2,1,0:T(2,128)(2,1)}, u32[]{:S(2)}) copy-start(bf16[1024,2,1024]{2,1,0:T(2,128)(2,1)} %param.6) | copy-start | bytes 12582916
  13.0 1.5 %collective-permute-start.1 = (bf16[16,4096]{1,0:T(8,128)(2,1)S(1)}, bf16[16,4096]{1,0:T(8,128)(2,1)S(1)}, u32[]{:S(2)}, u32[]{:S(2)}) collective-permute-start(bf16[16,4096]{1,0:T(8,128)(2,1)S(1)} %pad_maximum_fusion.2), channel_id=1, source_target_pairs={{0,1},{1,0},{2,3},{3,2},{4,5},{5,4},{6,7},{7,6},{8,9},{9,8},{10,11... | collective-permute-start | bytes 393224 | tf_op jit(solution)/shard_map/ppermute | solution.py:256
  15.1 1.4 %collective-permute-start.2 = (f32[64,128]{1,0:T(8,128)S(1)}, f32[64,128]{1,0:T(8,128)S(1)}, u32[]{:S(2)}, u32[]{:S(2)}) collective-permute-start(f32[64,128]{1,0:T(8,128)S(1)} %get-tuple-element.36), channel_id=1, source_target_pairs={{0,1},{1,0},{2,3},{3,2},{4,5},{5,4},{6,7},{7,6},{8,9},{9,8},{10,11... | collective-permute-start | bytes 98312 | tf_op jit(solution)/shard_map/ppermute | solution.py:256
  17.0 4.1 %collective-permute-start.7 = (bf16[16,4096]{1,0:T(8,128)(2,1)S(1)}, bf16[16,4096]{1,0:T(8,128)(2,1)S(1)}, u32[]{:S(2)}, u32[]{:S(2)}) collective-permute-start(bf16[16,4096]{1,0:T(8,128)(2,1)S(1)} %pad_maximum_fusion.3), channel_id=1, source_target_pairs={{0,1},{1,0},{2,3},{3,2},{4,5},{5,4},{6,7},{7,6},{8,9},{9,8},{10,11... | collective-permute-start | bytes 393224 | tf_op jit(solution)/shard_map/ppermute | solution.py:256
  17.1 4.0 %collective-permute-start.4 = (f32[64,128]{1,0:T(8,128)S(1)}, f32[64,128]{1,0:T(8,128)S(1)}, u32[]{:S(2)}, u32[]{:S(2)}) collective-permute-start(f32[64,128]{1,0:T(8,128)S(1)} %add.12), channel_id=1, source_target_pairs={{0,2},{1,3},{2,0},{3,1},{4,6},{5,7},{6,4},{7,5},{8,10},{9,11},{10,... | collective-permute-start | bytes 98312 | tf_op jit(solution)/shard_map/ppermute | solution.py:256
  18.7 2.4 %collective-permute-start.5 = (f32[64,512]{1,0:T(8,128)S(1)}, f32[64,512]{1,0:T(8,128)S(1)}, u32[]{:S(2)}, u32[]{:S(2)}) collective-permute-start(f32[64,512]{1,0:T(8,128)S(1)} %get-tuple-element.39), channel_id=1, source_target_pairs={{0,1},{1,0},{2,3},{3,2},{4,5},{5,4},{6,7},{7,6},{8,9},{9,8},{10,11... | collective-permute-start | bytes 393224 | tf_op jit(solution)/shard_map/ppermute | solution.py:256
  18.9 13.0 %collective-permute-start.10 = (bf16[32,4096]{1,0:T(8,128)(2,1)S(1)}, bf16[32,4096]{1,0:T(8,128)(2,1)S(1)}, u32[]{:S(2)}, u32[]{:S(2)}) collective-permute-start(bf16[32,4096]{1,0:T(8,128)(2,1)S(1)} %pad_maximum_fusion.refs_0_), channel_id=1, source_target_pairs={{0,2},{1,3},{2,0},{3,1},{4,6},{5,7},{6,4},{7,5},{8,10},{9,11},{10,... | collective-permute-start | bytes 786440 | tf_op jit(solution)/shard_map/ppermute | solution.py:256
  21.1 13.2 %collective-permute-start.11 = (bf16[32,4096]{1,0:T(8,128)(2,1)S(1)}, bf16[32,4096]{1,0:T(8,128)(2,1)S(1)}, u32[]{:S(2)}, u32[]{:S(2)}) collective-permute-start(bf16[32,4096]{1,0:T(8,128)(2,1)S(1)} %pad_maximum_fusion.1.refs_2_), channel_id=1, source_target_pairs={{0,2},{1,3},{2,0},{3,1},{4,6},{5,7},{6,4},{7,5},{8,10},{9,11},{10,... | collective-permute-start | bytes 786440 | tf_op jit(solution)/shard_map/ppermute | solution.py:256
  23.1 3.9 %collective-permute-start.8 = (f32[64,128]{1,0:T(8,128)S(1)}, f32[64,128]{1,0:T(8,128)S(1)}, u32[]{:S(2)}, u32[]{:S(2)}) collective-permute-start(f32[64,128]{1,0:T(8,128)S(1)} %add.13), channel_id=1, source_target_pairs={{0,4},{1,5},{2,6},{3,7},{4,0},{5,1},{6,2},{7,3},{8,12},{9,13},{10,... | collective-permute-start | bytes 98312 | tf_op jit(solution)/shard_map/ppermute | solution.py:256
  27.0 4.9 %collective-permute-start.9 = (f32[64,128]{1,0:T(8,128)S(1)}, f32[64,128]{1,0:T(8,128)S(1)}, u32[]{:S(2)}, u32[]{:S(2)}) collective-permute-start(f32[64,128]{1,0:T(8,128)S(1)} %add.14.refs_0_), channel_id=1, source_target_pairs={{0,8},{1,9},{2,10},{3,11},{4,12},{5,13},{6,14},{7,15},{8,0},{9,1},... | collective-permute-start | bytes 98312 | tf_op jit(solution)/shard_map/ppermute | solution.py:256
  35.9 1.2 %collective-permute-start.12 = (f32[8,128]{1,0:T(8,128)S(1)}, f32[8,128]{1,0:T(8,128)S(1)}, u32[]{:S(2)}, u32[]{:S(2)}) collective-permute-start(f32[8,128]{1,0:T(8,128)S(1)} %slice.9), channel_id=1, source_target_pairs={{0,1},{1,0},{2,3},{3,2},{4,5},{5,4},{6,7},{7,6},{8,9},{9,8},{10,11... | collective-permute-start | bytes 12296 | tf_op jit(solution)/shard_map/ppermute | solution.py:256

commit v6 on v5

--- a/solution.py
+++ b/solution.py
@@ -12,6 +12,7 @@
 PAIR = 2 * R
 DAMPING = 0.1
 ROWS = 256
+STAGE = 8 * 10**10
 BLOCK = 4
 GROUP = 4
 
@@ -28,29 +29,19 @@
 NT = ((1,), (1,))
 
 
-def stage_kernel(core_ref, source_ref, all_ref, keep_ref, send_ref):
-    first = core_ref[0] == 0
-    values = source_ref[...]
-    half = values.shape[1] // 2
-    low, high = values[:, :half], values[:, half:]
-    all_ref[...] = values
-    keep_ref[...] = jnp.where(first, low, high)
-    send_ref[...] = jnp.where(first, high, low)
-
-
-def stage(core, queries):
-    rows, entries = queries.shape
-    vmem = pl.BlockSpec(memory_space=pltpu.VMEM)
-    half = jax.ShapeDtypeStruct((rows, entries // 2), BF16)
-    return pl.pallas_call(
-        stage_kernel,
-        in_specs=[pl.BlockSpec(memory_space=pltpu.SMEM), vmem],
-        out_specs=[vmem] * 3,
-        out_shape=[jax.ShapeDtypeStruct(queries.shape, BF16), half, half],
-        compiler_params=pltpu.CompilerParams(vmem_limit_bytes=16 * MIB),
-        cost_estimate=pl.CostEstimate(flops=8 * 10**9, bytes_accessed=2**18, transcendentals=0),
-        name="stage",
-    )(core, queries)
+def place_kernel(out_ref):
+    out_ref[0] = lax.axis_index("dp")
+
+
+def own_place():
+    return pl.pallas_call(
+        place_kernel,
+        out_specs=pl.BlockSpec(memory_space=pltpu.SMEM),
+        out_shape=jax.ShapeDtypeStruct((1,), jnp.int32),
+        compiler_params=pltpu.CompilerParams(vmem_limit_bytes=MIB),
+        cost_estimate=pl.CostEstimate(flops=STAGE, bytes_accessed=8, transcendentals=0),
+        name="own_place",
+    )()
 
 
 def project_kernel(x_ref, w_ref, acts_ref):
@@ -75,8 +66,8 @@
     )(layer_input, in_flat)
 
 
-def statistics_kernel(core_ref, acts_ref, outs_ref, keep_cov, send_cov, keep_mom, send_mom):
-    first = core_ref[0] == 0
+def statistics_kernel(place_ref, acts_ref, outs_ref, keep_cov, send_cov, keep_mom, send_mom):
+    first = place_ref[0] & 1 == 0
     acts = acts_ref[...]
     outs = outs_ref[...]
     low = lax.broadcasted_iota(jnp.int32, (R, PAIR), 1) < R
@@ -98,7 +89,7 @@
         send_mom[:, lanes] = jnp.where(first, mom1, mom0)
 
 
-def statistics(core, acts, outs):
+def statistics(place, acts, outs):
     seqs = acts.shape[1] // LEN
     cov = jax.ShapeDtypeStruct((R, PAIR), F32)
     mom = jax.ShapeDtypeStruct((R, seqs * R), F32)
@@ -110,7 +101,7 @@
         out_shape=[cov, cov, mom, mom],
         compiler_params=pltpu.CompilerParams(vmem_limit_bytes=16 * MIB),
         name="statistics",
-    )(core, acts, outs)
+    )(place, acts, outs)
 
 
 def solve_block(p, rows):
@@ -265,47 +256,48 @@
     local_tokens = layer_input.shape[0]
     devices = lax.axis_size("dp")
     slabs = devices // GROUP
-    place = lax.axis_index("dp").astype(jnp.int32)
-    module = place & 1
-    own, near, send_near = stage(module.reshape(1), queries)
-    column = [own] + [exchange(own, slab * GROUP) for slab in range(1, slabs)]
+    place = own_place()
+    place, queries = lax.optimization_barrier((place, queries))
+    near_slabs, far_slabs = [0, 2], [1, 3] + list(range(4, slabs))
+    column = {slab: exchange(queries, slab * GROUP) for slab in [2, 3, 1] + list(range(4, slabs))}
+    column[0] = queries
     acts = project(layer_input, in_proj.reshape(PAIR, in_proj.shape[2]))
-    acts, out_grads, column[1] = lax.optimization_barrier((acts, out_grads, column[1]))
-    keep, send = halves(column[1], module == 1)
-    near = jnp.concatenate([near, keep], axis=0)
-    send_near = jnp.concatenate([send_near, send], axis=0)
+    acts, out_grads, column[0] = lax.optimization_barrier((acts, out_grads, column[0]))
+    upper = place[0] & 1 == 1
+
+    def fold(picked):
+        keep, send = zip(*(halves(column[slab], upper) for slab in picked))
+        keep, send = jnp.concatenate(keep, axis=0), jnp.concatenate(send, axis=0)
+        return jnp.concatenate([keep, exchange(send, 1)], axis=0)
+
     outs = jnp.einsum("tmk,mrk->tmr", out_grads, out_proj, preferred_element_type=F32).astype(BF16)
     outs = outs.reshape(local_tokens, PAIR).T
-    near = jnp.concatenate([near, exchange(send_near, 1)], axis=0)
-    acts, outs, near = lax.optimization_barrier((acts, outs, near))
-    keep_cov, send_cov, keep_mom, send_mom = statistics(module.reshape(1), acts, outs)
+    keep_cov, send_cov, keep_mom, send_mom = statistics(place, acts, outs)
     cov = keep_cov + exchange(send_cov, 1)
     moments = [keep_mom, exchange(send_mom, 1)]
-    cov, column[2] = lax.optimization_barrier((cov, column[2]))
+    cov, column[3] = lax.optimization_barrier((cov, column[3]))
     cov = cov + exchange(cov, 2)
-    far, send_far = zip(*(halves(value, module == 1) for value in column[2:]))
-    far, send_far = jnp.concatenate(far, axis=0), jnp.concatenate(send_far, axis=0)
-    far = jnp.concatenate([far, exchange(send_far, 1)], axis=0)
-    cov, moments, far = lax.optimization_barrier((cov, moments, far))
+    far = fold(far_slabs)
+    cov, far = lax.optimization_barrier((cov, far))
+    cov = cov + exchange(cov, GROUP)
+    near = fold(near_slabs)
     across = exchange(near, 2)
-    cov = cov + exchange(cov, GROUP)
     distance = 2 * GROUP
     while distance < devices:
         last = exchange(cov, distance)
         if 2 * distance < devices:
             cov = cov + last
         distance *= 2
-    cov, last, across = lax.optimization_barrier((cov, last, across))
     inv = inverse([cov, last], local_tokens * devices)
     gathered = [near, across, far, exchange(far, 2)]
     order = [
         slab * GROUP + 2 * over + core
-        for part in (range(2), range(2, slabs))
+        for part in (near_slabs, far_slabs)
         for over in range(2)
         for core in range(2)
         for slab in part
     ]
-    partial = score(place.reshape(1), inv, moments, gathered, order)
+    partial = score(place, inv, moments, gathered, order)
     seqs = local_tokens // LEN
     return partial[:seqs] + exchange(partial[seqs:], 1)
 

time: 37.8 us -> 36.8 us (0.974)
  waiting for transfers between devices: 8.06 us -> 12.4 us
  starting transfers between devices: 15.6 us -> 11.6 us
  local copies, waits for them, and re-layouts: 4.35 us -> 0.43 us
  Pallas kernels: 7.39 us -> 9.19 us
  between operations: 0.16 us -> 0.82 us
    ppermute x13, waiting for transfers between devices: 8.06 us -> 12.4 us  [exchange(): lax.ppermute(value, 'dp', [(i, i ^ distance) for i in range(lax.axis_size...]
    ppermute x13, starting transfers between devices: 15.6 us -> 11.6 us  [exchange(): lax.ppermute(value, 'dp', [(i, i ^ distance) for i in range(lax.axis_size...]
    unnamed x10, local copies, waits for them, and re-layouts: 4.34 us -> 0.42 us
    pallas_call x1, Pallas kernels: 0.51 us -> 1.16 us  [statistics(): pl.pallas_call(statistics_kernel, in_specs=[pl.BlockSpec(memory_space=plt...]
    pallas_call x1, Pallas kernels: 1.56 us -> 2.21 us  [score(): pl.pallas_call(functools.partial(scores_kernel, order), in_specs=[pl.Bloc...]
    pallas_call x1, Pallas kernels: 0.02 us -> 0.52 us  [own_place(): pl.pallas_call(place_kernel, out_specs=pl.BlockSpec(memory_space=pltpu.SM...]
  transfers between devices with their start and end apart: 13 -> 13, of which waited for: 6 -> 8; matrix products, arithmetic and copies ran while one was open for 4% -> 4% of each run, Pallas kernels for 15% -> 18%
where the time goes in v6:
time: 36.8 us; the launch traced here: 36.6 us
  waiting for transfers between devices  12.4 us (34%)
  starting transfers between devices  11.6 us (32%)
  Pallas kernels  9.19 us (25%)
  matrix products  1.44 us (4%)
  between operations  0.82 us (2%)
  other arithmetic  0.74 us (2%)
  local copies, waits for them, and re-layouts  0.43 us (1%)
    ppermute x13, waiting for transfers between devices, exchange(): lax.ppermute(value, 'dp', [(i, i ^ distance) for i in range(lax.axis_size...  12.4 us
    ppermute x13, starting transfers between devices, exchange(): lax.ppermute(value, 'dp', [(i, i ^ distance) for i in range(lax.axis_size...  11.6 us
    pallas_call x1, Pallas kernels, project(): pl.pallas_call(project_kernel, in_specs=[vmem, vmem], out_specs=vmem, out...  2.89 us
    pallas_call x1, Pallas kernels, inverse(): pl.pallas_call(functools.partial(inverse_kernel, total_tokens), in_specs=...  2.41 us
    pallas_call x1, Pallas kernels, score(): pl.pallas_call(functools.partial(scores_kernel, order), in_specs=[pl.Bloc...  2.21 us
    dot_general x1, matrix products, per_device(): jnp.einsum('tmk,mrk->tmr', out_grads, out_proj, preferred_element_type=F32)  1.44 us
    pallas_call x1, Pallas kernels, statistics(): pl.pallas_call(statistics_kernel, in_specs=[pl.BlockSpec(memory_space=plt...  1.16 us
  transfers between devices with their start and end apart: 13, of which 8 were waited for; matrix products, arithmetic and copies ran while one was open for 4% of the time, Pallas kernels for 18%

profile of v6, /device:TPU:0, one launch (start us, length us, event | category | flops | bytes accessed | tf_op | source)
XLA Modules:
  0.0 36.6 jit_solution(9525789614196069041)
XLA Ops:
  0.0 0.0 copy-start
  0.0 0.0 copy-start.3
  0.0 0.0 copy-start.1
  0.0 0.0 copy-start.2
  0.0 0.5 %own_place.1.place_ref = s32[1]{0:T(128)} custom-call(), custom_call_target="tpu_custom_call" | custom-call | flops 80000000000 | bytes 8 | tf_op jit(solution)/shard_map/own_place/pallas_call | solution.py:37
  0.5 0.4 %copy-done.3 = bf16[8,8192]{1,0:T(8,128)(2,1)S(1)} copy-done((bf16[8,8192]{1,0:T(8,128)(2,1)S(1)}, bf16[8,8192]{1,0:T(8,128)(2,1)}, u32[]{:S(2)}) %copy-start.3) | copy-done | bytes 131096
  1.0 5.0 %collective-permute-start.1 = (bf16[8,8192]{1,0:T(8,128)(2,1)S(1)}, bf16[8,8192]{1,0:T(8,128)(2,1)S(1)}, u32[]{:S(2)}, u32[]{:S(2)}) collective-permute-start(bf16[8,8192]{1,0:T(8,128)(2,1)S(1)} %copy-done.3), channel_id=1, source_target_pairs={{0,12},{1,13},{2,14},{3,15},{4,8},{5,9},{6,10},{7,11},{8,4},{9,5},... | collective-permute-start | bytes 393224 | tf_op jit(solution)/shard_map/ppermute | solution.py:247
  6.0 0.0 collective-permute-start.3
  6.0 0.6 %collective-permute-start.8 = (bf16[8,8192]{1,0:T(8,128)(2,1)S(1)}, bf16[8,8192]{1,0:T(8,128)(2,1)S(1)}, u32[]{:S(2)}, u32[]{:S(2)}) collective-permute-start(bf16[8,8192]{1,0:T(8,128)(2,1)S(1)} %copy-done.3), channel_id=1, source_target_pairs={{0,8},{1,9},{2,10},{3,11},{4,12},{5,13},{6,14},{7,15},{8,0},{9,1},... | collective-permute-start | bytes 393224 | tf_op jit(solution)/shard_map/ppermute | solution.py:247
  6.6 0.0 copy-done.1
  6.6 0.0 copy-done.2
  6.6 0.0 copy-start.4
  6.6 2.9 %project.1.acts_ref = bf16[128,1024]{1,0:T(8,128)(2,1)S(1)} custom-call(bf16[1024,4096]{1,0:T(8,128)(2,1)S(1)} %copy-done.1, bf16[128,4096]{1,0:T(8,128)(2,1)S(1)} %bitcast.8), custom_call_target="tpu_custom_call" | custom-call | flops 2147483648 | bytes 8388608 | tf_op jit(solution)/shard_map/project/pallas_call | solution.py:56
  9.5 0.0 copy-done
  9.5 0.0 copy-done.4
  9.5 1.4 %fusion.2 = bf16[2,1024,64]{1,2,0:T(8,128)(2,1)S(1)} fusion(bf16[2,64,1024]{2,1,0:T(8,128)(2,1)S(1)} %copy-done, bf16[1024,2,1024]{2,1,0:T(2,128)(2,1)S(1)} %copy-done.4), kind=kOutput, calls=%fused_computation.2 | convolution fusion | flops 268566528 | bytes 4718592 | tf_op jit(solution)/shard_map/tmk,mrk->tmr/dot_general | solution.py:273
  10.9 1.2 %statistics.1 = (f32[64,128]{1,0:T(8,128)S(1)}, f32[64,128]{1,0:T(8,128)S(1)}, f32[64,512]{1,0:T(8,128)S(1)}, f32[64,512]{1,0:T(8,128)S(1)}) custom-call(s32[1]{0:T(128)} %own_place.1.place_ref, bf16[128,1024]{1,0:T(8,128)(2,1)S(1)} %project.1.acts_ref, bf16[128,1024]{1,0:T(8,128)(2,1)S(1)} %bitcast.9), custom_call_target="tpu_custom_call" | custom-call | tf_op jit(solution)/shard_map/statistics/pallas_call | solution.py:97
  12.1 0.1 collective-permute-start
  12.9 0.5 %collective-permute-done = f32[64,128]{1,0:T(8,128)S(1)} collective-permute-done((f32[64,128]{1,0:T(8,128)S(1)}, f32[64,128]{1,0:T(8,128)S(1)}, u32[]{:S(2)}, u32[]{:S(2)}) %collective-permute-start) | collective-permute-done | bytes 32800 | tf_op jit(solution)/shard_map/ppermute | solution.py:247
  13.4 0.0 collective-permute-done.1
  13.4 1.8 %collective-permute-start.2 = (f32[64,128]{1,0:T(8,128)S(1)}, f32[64,128]{1,0:T(8,128)S(1)}, u32[]{:S(2)}, u32[]{:S(2)}) collective-permute-start(f32[64,128]{1,0:T(8,128)S(1)} %add.12), channel_id=1, source_target_pairs={{0,2},{1,3},{2,0},{3,1},{4,6},{5,7},{6,4},{7,5},{8,10},{9,11},{10,... | collective-permute-start | bytes 98312 | tf_op jit(solution)/shard_map/ppermute | solution.py:247
  15.2 0.0 collective-permute-done.3
  15.3 0.1 collective-permute-start.4
  15.3 1.7 %collective-permute-done.8 = bf16[8,8192]{1,0:T(8,128)(2,1)S(1)} collective-permute-done((bf16[8,8192]{1,0:T(8,128)(2,1)S(1)}, bf16[8,8192]{1,0:T(8,128)(2,1)S(1)}, u32[]{:S(2)}, u32[]{:S(2)}) %collective-permute-start.8) | collective-permute-done | bytes 131104 | tf_op jit(solution)/shard_map/ppermute | solution.py:247
  17.1 0.1 collective-permute-start.9
  17.2 0.2 collective-permute-done.2
  17.4 0.0 collective-permute-done.4
  17.4 1.1 %collective-permute-done.9 = bf16[16,4096]{1,0:T(8,128)(2,1)S(1)} collective-permute-done((bf16[16,4096]{1,0:T(8,128)(2,1)S(1)}, bf16[16,4096]{1,0:T(8,128)(2,1)S(1)}, u32[]{:S(2)}, u32[]{:S(2)}) %collective-permute-start.9) | collective-permute-done | bytes 131104 | tf_op jit(solution)/shard_map/ppermute | solution.py:247
  18.5 1.6 %collective-permute-start.10 = (bf16[32,4096]{1,0:T(8,128)(2,1)S(1)}, bf16[32,4096]{1,0:T(8,128)(2,1)S(1)}, u32[]{:S(2)}, u32[]{:S(2)}) collective-permute-start(bf16[32,4096]{1,0:T(8,128)(2,1)S(1)} %pad_maximum_fusion.1.refs_0_), channel_id=1, source_target_pairs={{0,2},{1,3},{2,0},{3,1},{4,6},{5,7},{6,4},{7,5},{8,10},{9,11},{10,... | collective-permute-start | bytes 786440 | tf_op jit(solution)/shard_map/ppermute | solution.py:247
  20.1 0.5 %collective-permute-start.11 = (bf16[32,4096]{1,0:T(8,128)(2,1)S(1)}, bf16[32,4096]{1,0:T(8,128)(2,1)S(1)}, u32[]{:S(2)}, u32[]{:S(2)}) collective-permute-start(bf16[32,4096]{1,0:T(8,128)(2,1)S(1)} %pad_maximum_fusion.refs_2_), channel_id=1, source_target_pairs={{0,2},{1,3},{2,0},{3,1},{4,6},{5,7},{6,4},{7,5},{8,10},{9,11},{10,... | collective-permute-start | bytes 786440 | tf_op jit(solution)/shard_map/ppermute | solution.py:247
  20.6 0.0 collective-permute-start.7
  20.6 0.4 %collective-permute-start.5 = (f32[64,128]{1,0:T(8,128)S(1)}, f32[64,128]{1,0:T(8,128)S(1)}, u32[]{:S(2)}, u32[]{:S(2)}) collective-permute-start(f32[64,128]{1,0:T(8,128)S(1)} %add.13), channel_id=1, source_target_pairs={{0,4},{1,5},{2,6},{3,7},{4,0},{5,1},{6,2},{7,3},{8,12},{9,13},{10,... | collective-permute-start | bytes 98312 | tf_op jit(solution)/shard_map/ppermute | solution.py:247
  21.0 3.5 %collective-permute-done.5 = f32[64,128]{1,0:T(8,128)S(1)} collective-permute-done((f32[64,128]{1,0:T(8,128)S(1)}, f32[64,128]{1,0:T(8,128)S(1)}, u32[]{:S(2)}, u32[]{:S(2)}) %collective-permute-start.5) | collective-permute-done | bytes 32800 | tf_op jit(solution)/shard_map/ppermute | solution.py:247
  24.6 1.4 %collective-permute-start.6 = (f32[64,128]{1,0:T(8,128)S(1)}, f32[64,128]{1,0:T(8,128)S(1)}, u32[]{:S(2)}, u32[]{:S(2)}) collective-permute-start(f32[64,128]{1,0:T(8,128)S(1)} %add.14.refs_0_), channel_id=1, source_target_pairs={{0,8},{1,9},{2,10},{3,11},{4,12},{5,13},{6,14},{7,15},{8,0},{9,1},... | collective-permute-start | bytes 98312 | tf_op jit(solution)/shard_map/ppermute | solution.py:247
  26.0 3.6 %collective-permute-done.6.refs_1_ = f32[64,128]{1,0:T(8,128)S(1)} collective-permute-done((f32[64,128]{1,0:T(8,128)S(1)}, f32[64,128]{1,0:T(8,128)S(1)}, u32[]{:S(2)}, u32[]{:S(2)}) %collective-permute-start.6) | collective-permute-done | bytes 32800 | tf_op jit(solution)/shard_map/ppermute | solution.py:247
  29.5 2.4 %inverse.1.inv_ref = f32[64,128]{1,0:T(8,128)S(1)} custom-call(f32[64,128]{1,0:T(8,128)S(1)} %add.14.refs_0_, f32[64,128]{1,0:T(8,128)S(1)} %collective-permute-done.6.refs_1_), custom_call_target="tpu_custom_call" | custom-call | tf_op jit(solution)/shard_map/inverse/pallas_call | solution.py:171
  31.9 0.0 collective-permute-done.7.recv_ref
  32.0 0.0 collective-permute-done.10.refs_1_
  32.0 0.6 %collective-permute-done.11.refs_3_ = bf16[32,4096]{1,0:T(8,128)(2,1)S(1)} collective-permute-done((bf16[32,4096]{1,0:T(8,128)(2,1)S(1)}, bf16[32,4096]{1,0:T(8,128)(2,1)S(1)}, u32[]{:S(2)}, u32[]{:S(2)}) %collective-permute-start.11) | collective-permute-done | bytes 262176 | tf_op jit(solution)/shard_map/ppermute | solution.py:247
  32.6 2.2 %scores.1 = f32[16,128]{1,0:T(8,128)S(1)} custom-call(s32[1]{0:T(128)} %own_place.1.place_ref, f32[64,128]{1,0:T(8,128)S(1)} %inverse.1.inv_ref, f32[64,512]{1,0:T(8,128)S(1)} %get-tuple-element.27.keep_ref, f32[64,512]{1,0:T(8,128)S(1)} %collective-permute-done.7.recv_ref, bf16[32,4096]{1,0:T(8,128)(2,1)S(1)} %pad_maximum_fusion.1.refs_0_, ...), custom_call_target="tpu_custom_call" | custom-call | tf_op jit(solution)/shard_map/scores/pallas_call | solution.py:232
  34.8 0.0 collective-permute-start.12
  34.9 1.2 %collective-permute-done.12 = f32[8,128]{1,0:T(8,128)S(1)} collective-permute-done((f32[8,128]{1,0:T(8,128)S(1)}, f32[8,128]{1,0:T(8,128)S(1)}, u32[]{:S(2)}, u32[]{:S(2)}) %collective-permute-start.12) | collective-permute-done | bytes 4128 | tf_op jit(solution)/shard_map/ppermute | solution.py:247
  36.0 0.6 %slice_add_fusion = f32[8,128]{1,0:T(8,128)} fusion(f32[8,128]{1,0:T(8,128)S(1)} %collective-permute-done.12, f32[16,128]{1,0:T(8,128)S(1)} %scores.1), kind=kLoop, calls=%fused_computation.15 | loop fusion | flops 1024 | bytes 12288 | tf_op jit(solution)/shard_map/add | solution.py:302
  (12 shorter events, 0.1 us)
Async XLA Ops:
  0.0 9.5 %copy-start = (bf16[2,64,1024]{2,1,0:T(8,128)(2,1)S(1)}, bf16[2,64,1024]{2,1,0:T(8,128)(2,1)}, u32[]{:S(2)}) copy-start(bf16[2,64,1024]{2,1,0:T(8,128)(2,1)} %param.8) | copy-start | bytes 786436
  0.0 0.9 %copy-start.3 = (bf16[8,8192]{1,0:T(8,128)(2,1)S(1)}, bf16[8,8192]{1,0:T(8,128)(2,1)}, u32[]{:S(2)}) copy-start(bf16[8,8192]{1,0:T(8,128)(2,1)} %param.9) | copy-start | bytes 393220
  0.0 6.6 %copy-start.1 = (bf16[1024,4096]{1,0:T(8,128)(2,1)S(1)}, bf16[1024,4096]{1,0:T(8,128)(2,1)}, u32[]{:S(2)}) copy-start(bf16[1024,4096]{1,0:T(8,128)(2,1)} %x_ref.1) | copy-start | bytes 25165828
  0.0 6.6 %copy-start.2 = (bf16[2,64,4096]{2,1,0:T(8,128)(2,1)S(1)}, bf16[2,64,4096]{2,1,0:T(8,128)(2,1)}, u32[]{:S(2)}) copy-start(bf16[2,64,4096]{2,1,0:T(8,128)(2,1)} %param.7) | copy-start | bytes 3145732
  1.0 12.4 %collective-permute-start.1 = (bf16[8,8192]{1,0:T(8,128)(2,1)S(1)}, bf16[8,8192]{1,0:T(8,128)(2,1)S(1)}, u32[]{:S(2)}, u32[]{:S(2)}) collective-permute-start(bf16[8,8192]{1,0:T(8,128)(2,1)S(1)} %copy-done.3), channel_id=1, source_target_pairs={{0,12},{1,13},{2,14},{3,15},{4,8},{5,9},{6,10},{7,11},{8,4},{9,5},... | collective-permute-start | bytes 393224 | tf_op jit(solution)/shard_map/ppermute | solution.py:247
  6.0 9.2 %collective-permute-start.3 = (bf16[8,8192]{1,0:T(8,128)(2,1)S(1)}, bf16[8,8192]{1,0:T(8,128)(2,1)S(1)}, u32[]{:S(2)}, u32[]{:S(2)}) collective-permute-start(bf16[8,8192]{1,0:T(8,128)(2,1)S(1)} %copy-done.3), channel_id=1, source_target_pairs={{0,4},{1,5},{2,6},{3,7},{4,0},{5,1},{6,2},{7,3},{8,12},{9,13},{10,... | collective-permute-start | bytes 393224 | tf_op jit(solution)/shard_map/ppermute | solution.py:247
  6.0 11.1 %collective-permute-start.8 = (bf16[8,8192]{1,0:T(8,128)(2,1)S(1)}, bf16[8,8192]{1,0:T(8,128)(2,1)S(1)}, u32[]{:S(2)}, u32[]{:S(2)}) collective-permute-start(bf16[8,8192]{1,0:T(8,128)(2,1)S(1)} %copy-done.3), channel_id=1, source_target_pairs={{0,8},{1,9},{2,10},{3,11},{4,12},{5,13},{6,14},{7,15},{8,0},{9,1},... | collective-permute-start | bytes 393224 | tf_op jit(solution)/shard_map/ppermute | solution.py:247
  6.6 2.9 %copy-start.4 = (bf16[1024,2,1024]{2,1,0:T(2,128)(2,1)S(1)}, bf16[1024,2,1024]{2,1,0:T(2,128)(2,1)}, u32[]{:S(2)}) copy-start(bf16[1024,2,1024]{2,1,0:T(2,128)(2,1)} %param.6) | copy-start | bytes 12582916
  12.1 1.3 %collective-permute-start = (f32[64,128]{1,0:T(8,128)S(1)}, f32[64,128]{1,0:T(8,128)S(1)}, u32[]{:S(2)}, u32[]{:S(2)}) collective-permute-start(f32[64,128]{1,0:T(8,128)S(1)} %get-tuple-element.23), channel_id=1, source_target_pairs={{0,1},{1,0},{2,3},{3,2},{4,5},{5,4},{6,7},{7,6},{8,9},{9,8},{10,11... | collective-permute-start | bytes 98312 | tf_op jit(solution)/shard_map/ppermute | solution.py:247
  13.4 4.0 %collective-permute-start.2 = (f32[64,128]{1,0:T(8,128)S(1)}, f32[64,128]{1,0:T(8,128)S(1)}, u32[]{:S(2)}, u32[]{:S(2)}) collective-permute-start(f32[64,128]{1,0:T(8,128)S(1)} %add.12), channel_id=1, source_target_pairs={{0,2},{1,3},{2,0},{3,1},{4,6},{5,7},{6,4},{7,5},{8,10},{9,11},{10,... | collective-permute-start | bytes 98312 | tf_op jit(solution)/shard_map/ppermute | solution.py:247
  15.3 2.1 %collective-permute-start.4 = (bf16[16,4096]{1,0:T(8,128)(2,1)S(1)}, bf16[16,4096]{1,0:T(8,128)(2,1)S(1)}, u32[]{:S(2)}, u32[]{:S(2)}) collective-permute-start(bf16[16,4096]{1,0:T(8,128)(2,1)S(1)} %pad_maximum_fusion.2), channel_id=1, source_target_pairs={{0,1},{1,0},{2,3},{3,2},{4,5},{5,4},{6,7},{7,6},{8,9},{9,8},{10,11... | collective-permute-start | bytes 393224 | tf_op jit(solution)/shard_map/ppermute | solution.py:247
  17.1 1.4 %collective-permute-start.9 = (bf16[16,4096]{1,0:T(8,128)(2,1)S(1)}, bf16[16,4096]{1,0:T(8,128)(2,1)S(1)}, u32[]{:S(2)}, u32[]{:S(2)}) collective-permute-start(bf16[16,4096]{1,0:T(8,128)(2,1)S(1)} %pad_maximum_fusion.3), channel_id=1, source_target_pairs={{0,1},{1,0},{2,3},{3,2},{4,5},{5,4},{6,7},{7,6},{8,9},{9,8},{10,11... | collective-permute-start | bytes 393224 | tf_op jit(solution)/shard_map/ppermute | solution.py:247
  18.5 13.4 %collective-permute-start.10 = (bf16[32,4096]{1,0:T(8,128)(2,1)S(1)}, bf16[32,4096]{1,0:T(8,128)(2,1)S(1)}, u32[]{:S(2)}, u32[]{:S(2)}) collective-permute-start(bf16[32,4096]{1,0:T(8,128)(2,1)S(1)} %pad_maximum_fusion.1.refs_0_), channel_id=1, source_target_pairs={{0,2},{1,3},{2,0},{3,1},{4,6},{5,7},{6,4},{7,5},{8,10},{9,11},{10,... | collective-permute-start | bytes 786440 | tf_op jit(solution)/shard_map/ppermute | solution.py:247
  20.1 12.4 %collective-permute-start.11 = (bf16[32,4096]{1,0:T(8,128)(2,1)S(1)}, bf16[32,4096]{1,0:T(8,128)(2,1)S(1)}, u32[]{:S(2)}, u32[]{:S(2)}) collective-permute-start(bf16[32,4096]{1,0:T(8,128)(2,1)S(1)} %pad_maximum_fusion.refs_2_), channel_id=1, source_target_pairs={{0,2},{1,3},{2,0},{3,1},{4,6},{5,7},{6,4},{7,5},{8,10},{9,11},{10,... | collective-permute-start | bytes 786440 | tf_op jit(solution)/shard_map/ppermute | solution.py:247
  20.6 11.3 %collective-permute-start.7 = (f32[64,512]{1,0:T(8,128)S(1)}, f32[64,512]{1,0:T(8,128)S(1)}, u32[]{:S(2)}, u32[]{:S(2)}) collective-permute-start(f32[64,512]{1,0:T(8,128)S(1)} %get-tuple-element.28), channel_id=1, source_target_pairs={{0,1},{1,0},{2,3},{3,2},{4,5},{5,4},{6,7},{7,6},{8,9},{9,8},{10,11... | collective-permute-start | bytes 393224 | tf_op jit(solution)/shard_map/ppermute | solution.py:247
  20.6 3.9 %collective-permute-start.5 = (f32[64,128]{1,0:T(8,128)S(1)}, f32[64,128]{1,0:T(8,128)S(1)}, u32[]{:S(2)}, u32[]{:S(2)}) collective-permute-start(f32[64,128]{1,0:T(8,128)S(1)} %add.13), channel_id=1, source_target_pairs={{0,4},{1,5},{2,6},{3,7},{4,0},{5,1},{6,2},{7,3},{8,12},{9,13},{10,... | collective-permute-start | bytes 98312 | tf_op jit(solution)/shard_map/ppermute | solution.py:247
  24.6 5.0 %collective-permute-start.6 = (f32[64,128]{1,0:T(8,128)S(1)}, f32[64,128]{1,0:T(8,128)S(1)}, u32[]{:S(2)}, u32[]{:S(2)}) collective-permute-start(f32[64,128]{1,0:T(8,128)S(1)} %add.14.refs_0_), channel_id=1, source_target_pairs={{0,8},{1,9},{2,10},{3,11},{4,12},{5,13},{6,14},{7,15},{8,0},{9,1},... | collective-permute-start | bytes 98312 | tf_op jit(solution)/shard_map/ppermute | solution.py:247
  34.8 1.2 %collective-permute-start.12 = (f32[8,128]{1,0:T(8,128)S(1)}, f32[8,128]{1,0:T(8,128)S(1)}, u32[]{:S(2)}, u32[]{:S(2)}) collective-permute-start(f32[8,128]{1,0:T(8,128)S(1)} %slice.9), channel_id=1, source_target_pairs={{0,1},{1,0},{2,3},{3,2},{4,5},{5,4},{6,7},{7,6},{8,9},{9,8},{10,11... | collective-permute-start | bytes 12296 | tf_op jit(solution)/shard_map/ppermute | solution.py:247

commit v7 on v6

--- a/solution.py
+++ b/solution.py
@@ -29,33 +29,34 @@
 NT = ((1,), (1,))
 
 
-def place_kernel(out_ref):
-    out_ref[0] = lax.axis_index("dp")
-
-
-def own_place():
-    return pl.pallas_call(
-        place_kernel,
-        out_specs=pl.BlockSpec(memory_space=pltpu.SMEM),
-        out_shape=jax.ShapeDtypeStruct((1,), jnp.int32),
+def token_kernel(out_ref):
+    out_ref[...] = jnp.zeros_like(out_ref)
+
+
+def first_token():
+    return pl.pallas_call(
+        token_kernel,
+        out_specs=pl.BlockSpec(memory_space=pltpu.VMEM),
+        out_shape=jax.ShapeDtypeStruct((8, 128), F32),
         compiler_params=pltpu.CompilerParams(vmem_limit_bytes=MIB),
         cost_estimate=pl.CostEstimate(flops=STAGE, bytes_accessed=8, transcendentals=0),
-        name="own_place",
+        name="first_token",
     )()
 
 
-def project_kernel(x_ref, w_ref, acts_ref):
+def project_kernel(token_ref, x_ref, w_ref, acts_ref):
+    del token_ref
     tokens = x_ref.shape[0]
     for at in range(0, tokens, ROWS):
         acts_ref[:, at : at + ROWS] = dot(w_ref[...], x_ref[at : at + ROWS], NT).astype(BF16)
 
 
-def project(layer_input, in_flat):
+def project(token, layer_input, in_flat):
     tokens, width = layer_input.shape
     vmem = pl.BlockSpec(memory_space=pltpu.VMEM)
     return pl.pallas_call(
         project_kernel,
-        in_specs=[vmem, vmem],
+        in_specs=[pl.BlockSpec(memory_space=pl.ANY), vmem, vmem],
         out_specs=vmem,
         out_shape=jax.ShapeDtypeStruct((PAIR, tokens), BF16),
         compiler_params=pltpu.CompilerParams(vmem_limit_bytes=24 * MIB),
@@ -63,7 +64,34 @@
             flops=4 * tokens * width * PAIR, bytes_accessed=2 * tokens * width, transcendentals=0
         ),
         name="project",
-    )(layer_input, in_flat)
+    )(token, layer_input, in_flat)
+
+
+def fold_pair(pair):
+    row = lax.broadcasted_iota(jnp.int32, (R, PAIR), 0)
+    lane = lax.broadcasted_iota(jnp.int32, (R, PAIR), 1)
+    turned = pltpu.roll(pair, R, 1)
+    mixed = jnp.where(lane >= row, pair, turned)
+    diagonal = jnp.sum(jnp.where(lane == row, turned, 0.0), axis=0, keepdims=True)
+    half = R // 2
+    folded = jnp.where(lane[:half] < R, mixed[:half], pltpu.roll(mixed[half:], R, 1))
+    return jnp.concatenate([folded, jnp.broadcast_to(diagonal, (8, PAIR))], axis=0)
+
+
+def unfold_pair(folded):
+    row = lax.broadcasted_iota(jnp.int32, (R, PAIR), 0)
+    lane = lax.broadcasted_iota(jnp.int32, (R, PAIR), 1)
+    low = lane < R
+    column = jnp.where(low, lane, lane - R)
+    half = R // 2
+    turned = pltpu.roll(folded, R, 1)
+    wide = low[:half]
+    mixed = jnp.concatenate(
+        [jnp.where(wide, folded[:half], turned[:half]), jnp.where(wide, turned[:half], folded[:half])], axis=0
+    )
+    flipped = jnp.concatenate([mixed, mixed], axis=0).T[:R]
+    pair = jnp.where((column >= row) == low, mixed, flipped)
+    return jnp.where((column == row) & (lane >= R), turned[half : half + 1], pair)
 
 
 def statistics_kernel(place_ref, acts_ref, outs_ref, keep_cov, send_cov, keep_mom, send_mom):
@@ -75,6 +103,7 @@
     cov_out = dot(outs, outs, NT)
     cov0 = jnp.where(low, cov_in[:R], pltpu.roll(cov_out[:R], R, 1))
     cov1 = jnp.where(low, pltpu.roll(cov_in[R:], R, 1), cov_out[R:])
+    cov0, cov1 = fold_pair(cov0), fold_pair(cov1)
     keep_cov[...] = jnp.where(first, cov0, cov1)
     send_cov[...] = jnp.where(first, cov1, cov0)
     for pair in range(acts.shape[1] // LEN // 2):
@@ -91,7 +120,7 @@
 
 def statistics(place, acts, outs):
     seqs = acts.shape[1] // LEN
-    cov = jax.ShapeDtypeStruct((R, PAIR), F32)
+    cov = jax.ShapeDtypeStruct((R // 2 + 8, PAIR), F32)
     mom = jax.ShapeDtypeStruct((R, seqs * R), F32)
     vmem = pl.BlockSpec(memory_space=pltpu.VMEM)
     return pl.pallas_call(
@@ -158,7 +187,7 @@
     lane = lax.broadcasted_iota(jnp.int32, (R, PAIR), 1)
     low = lane < R
     column = jnp.where(low, lane, lane - R)
-    cov = sum(ref[...] for ref in cov_refs)
+    cov = unfold_pair(sum(ref[...] for ref in cov_refs))
     diagonal = jnp.where(row == column, cov, 0.0)
     trace_in = jnp.sum(jnp.where(low, diagonal, 0.0), keepdims=True)
     trace_out = jnp.sum(jnp.where(low, 0.0, diagonal), keepdims=True)
@@ -172,7 +201,7 @@
         functools.partial(inverse_kernel, total_tokens),
         in_specs=[vmem] * len(covs),
         out_specs=vmem,
-        out_shape=jax.ShapeDtypeStruct(covs[0].shape, F32),
+        out_shape=jax.ShapeDtypeStruct((R, PAIR), F32),
         compiler_params=pltpu.CompilerParams(vmem_limit_bytes=16 * MIB),
         name="inverse",
     )(*covs)
@@ -256,14 +285,14 @@
     local_tokens = layer_input.shape[0]
     devices = lax.axis_size("dp")
     slabs = devices // GROUP
-    place = own_place()
-    place, queries = lax.optimization_barrier((place, queries))
+    place = lax.axis_index("dp").astype(jnp.int32)
+    token, queries = lax.optimization_barrier((first_token(), queries))
     near_slabs, far_slabs = [0, 2], [1, 3] + list(range(4, slabs))
     column = {slab: exchange(queries, slab * GROUP) for slab in [2, 3, 1] + list(range(4, slabs))}
     column[0] = queries
-    acts = project(layer_input, in_proj.reshape(PAIR, in_proj.shape[2]))
+    acts = project(token, layer_input, in_proj.reshape(PAIR, in_proj.shape[2]))
     acts, out_grads, column[0] = lax.optimization_barrier((acts, out_grads, column[0]))
-    upper = place[0] & 1 == 1
+    upper = place & 1 == 1
 
     def fold(picked):
         keep, send = zip(*(halves(column[slab], upper) for slab in picked))
@@ -272,7 +301,7 @@
 
     outs = jnp.einsum("tmk,mrk->tmr", out_grads, out_proj, preferred_element_type=F32).astype(BF16)
     outs = outs.reshape(local_tokens, PAIR).T
-    keep_cov, send_cov, keep_mom, send_mom = statistics(place, acts, outs)
+    keep_cov, send_cov, keep_mom, send_mom = statistics(place.reshape(1), acts, outs)
     cov = keep_cov + exchange(send_cov, 1)
     moments = [keep_mom, exchange(send_mom, 1)]
     cov, column[3] = lax.optimization_barrier((cov, column[3]))
@@ -297,7 +326,7 @@
         for core in range(2)
         for slab in part
     ]
-    partial = score(place, inv, moments, gathered, order)
+    partial = score(place.reshape(1), inv, moments, gathered, order)
     seqs = local_tokens // LEN
     return partial[:seqs] + exchange(partial[seqs:], 1)
 

time: 36.8 us -> 37.5 us (1.019)
  local copies, waits for them, and re-layouts: 0.43 us -> 4.34 us
  waiting for transfers between devices: 12.4 us -> 8.87 us
  starting transfers between devices: 11.6 us -> 14.1 us
  Pallas kernels: 9.19 us -> 7.65 us
  between operations: 0.82 us -> 0.19 us
    unnamed x10, local copies, waits for them, and re-layouts: 0.42 us -> 4.33 us
    ppermute x13, waiting for transfers between devices: 12.4 us -> 8.87 us  [exchange(): lax.ppermute(value, 'dp', [(i, i ^ distance) for i in range(lax.axis_size...]
    ppermute x13, starting transfers between devices: 11.6 us -> 14.1 us  [exchange(): lax.ppermute(value, 'dp', [(i, i ^ distance) for i in range(lax.axis_size...]
    pallas_call x1, Pallas kernels: 2.21 us -> 1.56 us  [score(): pl.pallas_call(functools.partial(scores_kernel, order), in_specs=[pl.Bloc...]
    pallas_call x1, Pallas kernels: 1.16 us -> 0.54 us  [statistics(): pl.pallas_call(statistics_kernel, in_specs=[pl.BlockSpec(memory_space=plt...]
    pallas_call x2, Pallas kernels: 3.42 us -> 2.89 us  [the longest x1 2.89 us: project(): pl.pallas_call(project_kernel, in_specs=[pl.BlockSpec(memory_space=pl.ANY...]
  transfers between devices with their start and end apart: 13 -> 13, of which waited for: 8 -> 6; matrix products, arithmetic and copies ran while one was open for 4% -> 4% of each run, Pallas kernels for 18% -> 16%
where the time goes in v7:
time: 37.5 us; the launch traced here: 37.3 us
  starting transfers between devices  14.1 us (38%)
  waiting for transfers between devices  8.87 us (24%)
  Pallas kernels  7.65 us (20%)
  local copies, waits for them, and re-layouts  4.34 us (12%)
  matrix products  1.44 us (4%)
  other arithmetic  0.73 us (2%)
    ppermute x13, starting transfers between devices, exchange(): lax.ppermute(value, 'dp', [(i, i ^ distance) for i in range(lax.axis_size...  14.1 us
    ppermute x13, waiting for transfers between devices, exchange(): lax.ppermute(value, 'dp', [(i, i ^ distance) for i in range(lax.axis_size...  8.87 us
    unnamed x10, local copies, waits for them, and re-layouts  4.33 us
    pallas_call x1, Pallas kernels, project(): pl.pallas_call(project_kernel, in_specs=[pl.BlockSpec(memory_space=pl.ANY...  2.89 us
    pallas_call x1, Pallas kernels, inverse(): pl.pallas_call(functools.partial(inverse_kernel, total_tokens), in_specs=...  2.65 us
    pallas_call x1, Pallas kernels, score(): pl.pallas_call(functools.partial(scores_kernel, order), in_specs=[pl.Bloc...  1.56 us
    dot_general x1, matrix products, per_device(): jnp.einsum('tmk,mrk->tmr', out_grads, out_proj, preferred_element_type=F32)  1.44 us
  transfers between devices with their start and end apart: 13, of which 6 were waited for; matrix products, arithmetic and copies ran while one was open for 4% of the time, Pallas kernels for 16%

profile of v7, /device:TPU:0, one launch (start us, length us, event | category | flops | bytes accessed | tf_op | source)
XLA Modules:
  0.0 37.3 jit_solution(10258279651723002195)
XLA Ops:
  0.0 0.0 copy-start
  0.0 0.0 copy-start.3
  0.0 0.0 copy-start.2
  0.0 0.9 %copy-done.3 = bf16[8,8192]{1,0:T(8,128)(2,1)S(1)} copy-done((bf16[8,8192]{1,0:T(8,128)(2,1)S(1)}, bf16[8,8192]{1,0:T(8,128)(2,1)}, u32[]{:S(2)}) %copy-start.3) | copy-done | bytes 131096
  1.0 5.0 %collective-permute-start.1 = (bf16[8,8192]{1,0:T(8,128)(2,1)S(1)}, bf16[8,8192]{1,0:T(8,128)(2,1)S(1)}, u32[]{:S(2)}, u32[]{:S(2)}) collective-permute-start(bf16[8,8192]{1,0:T(8,128)(2,1)S(1)} %copy-done.3), channel_id=1, source_target_pairs={{0,12},{1,13},{2,14},{3,15},{4,8},{5,9},{6,10},{7,11},{8,4},{9,5},... | collective-permute-start | bytes 393224 | tf_op jit(solution)/shard_map/ppermute | solution.py:276
  6.0 0.0 collective-permute-start.3
  6.0 0.6 %collective-permute-start.8 = (bf16[8,8192]{1,0:T(8,128)(2,1)S(1)}, bf16[8,8192]{1,0:T(8,128)(2,1)S(1)}, u32[]{:S(2)}, u32[]{:S(2)}) collective-permute-start(bf16[8,8192]{1,0:T(8,128)(2,1)S(1)} %copy-done.3), channel_id=1, source_target_pairs={{0,8},{1,9},{2,10},{3,11},{4,12},{5,13},{6,14},{7,15},{8,0},{9,1},... | collective-permute-start | bytes 393224 | tf_op jit(solution)/shard_map/ppermute | solution.py:276
  6.6 0.0 copy-done.2
  6.6 0.0 copy-start.1
  6.6 3.4 %copy-done.1 = bf16[1024,4096]{1,0:T(8,128)(2,1)S(1)} copy-done((bf16[1024,4096]{1,0:T(8,128)(2,1)S(1)}, bf16[1024,4096]{1,0:T(8,128)(2,1)}, u32[]{:S(2)}) %copy-start.1) | copy-done | bytes 8388632
  10.0 0.0 copy-start.4
  10.0 2.9 %project.1.acts_ref = bf16[128,1024]{1,0:T(8,128)(2,1)S(1)} custom-call(f32[8,128]{1,0:T(8,128)S(1)} %first_token.1.token_ref, bf16[1024,4096]{1,0:T(8,128)(2,1)S(1)} %copy-done.1, bf16[128,4096]{1,0:T(8,128)(2,1)S(1)} %bitcast.8), custom_call_target="tpu_custom_call" | custom-call | flops 2147483648 | bytes 8388608 | tf_op jit(solution)/shard_map/project/pallas_call | solution.py:57
  12.9 0.0 copy-done
  12.9 0.0 copy-done.4
  12.9 1.4 %fusion.2 = bf16[2,1024,64]{1,2,0:T(8,128)(2,1)S(1)} fusion(bf16[2,64,1024]{2,1,0:T(8,128)(2,1)S(1)} %copy-done, bf16[1024,2,1024]{2,1,0:T(2,128)(2,1)S(1)} %copy-done.4), kind=kOutput, calls=%fused_computation.2 | convolution fusion | flops 268566528 | bytes 4718592 | tf_op jit(solution)/shard_map/tmk,mrk->tmr/dot_general | solution.py:302
  14.3 0.5 %statistics.1 = (f32[40,128]{1,0:T(8,128)S(1)}, f32[40,128]{1,0:T(8,128)S(1)}, f32[64,512]{1,0:T(8,128)S(1)}, f32[64,512]{1,0:T(8,128)S(1)}) custom-call(s32[1]{0:T(128)} %bitcast.place_ref, bf16[128,1024]{1,0:T(8,128)(2,1)S(1)} %project.1.acts_ref, bf16[128,1024]{1,0:T(8,128)(2,1)S(1)} %bitcast.9), custom_call_target="tpu_custom_call" | custom-call | tf_op jit(solution)/shard_map/statistics/pallas_call | solution.py:126
  14.9 0.1 collective-permute-start
  15.0 1.1 %collective-permute-done = f32[40,128]{1,0:T(8,128)S(1)} collective-permute-done((f32[40,128]{1,0:T(8,128)S(1)}, f32[40,128]{1,0:T(8,128)S(1)}, u32[]{:S(2)}, u32[]{:S(2)}) %collective-permute-start) | collective-permute-done | bytes 20512 | tf_op jit(solution)/shard_map/ppermute | solution.py:276
  16.1 0.0 collective-permute-done.1
  16.1 1.8 %collective-permute-start.2 = (f32[40,128]{1,0:T(8,128)S(1)}, f32[40,128]{1,0:T(8,128)S(1)}, u32[]{:S(2)}, u32[]{:S(2)}) collective-permute-start(f32[40,128]{1,0:T(8,128)S(1)} %add.12), channel_id=1, source_target_pairs={{0,2},{1,3},{2,0},{3,1},{4,6},{5,7},{6,4},{7,5},{8,10},{9,11},{10,... | collective-permute-start | bytes 61448 | tf_op jit(solution)/shard_map/ppermute | solution.py:276
  17.9 0.0 collective-permute-done.3
  18.0 0.1 collective-permute-start.4
  18.1 0.0 collective-permute-done.8
  18.1 0.5 %collective-permute-start.9 = (bf16[16,4096]{1,0:T(8,128)(2,1)S(1)}, bf16[16,4096]{1,0:T(8,128)(2,1)S(1)}, u32[]{:S(2)}, u32[]{:S(2)}) collective-permute-start(bf16[16,4096]{1,0:T(8,128)(2,1)S(1)} %pad_maximum_fusion.3), channel_id=1, source_target_pairs={{0,1},{1,0},{2,3},{3,2},{4,5},{5,4},{6,7},{7,6},{8,9},{9,8},{10,11... | collective-permute-start | bytes 393224 | tf_op jit(solution)/shard_map/ppermute | solution.py:276
  18.7 1.3 %collective-permute-done.2 = f32[40,128]{1,0:T(8,128)S(1)} collective-permute-done((f32[40,128]{1,0:T(8,128)S(1)}, f32[40,128]{1,0:T(8,128)S(1)}, u32[]{:S(2)}, u32[]{:S(2)}) %collective-permute-start.2) | collective-permute-done | bytes 20512 | tf_op jit(solution)/shard_map/ppermute | solution.py:276
  20.0 0.0 collective-permute-done.4
  20.0 0.0 collective-permute-done.9
  20.1 1.8 %collective-permute-start.10 = (bf16[32,4096]{1,0:T(8,128)(2,1)S(1)}, bf16[32,4096]{1,0:T(8,128)(2,1)S(1)}, u32[]{:S(2)}, u32[]{:S(2)}) collective-permute-start(bf16[32,4096]{1,0:T(8,128)(2,1)S(1)} %pad_maximum_fusion.1.refs_0_), channel_id=1, source_target_pairs={{0,2},{1,3},{2,0},{3,1},{4,6},{5,7},{6,4},{7,5},{8,10},{9,11},{10,... | collective-permute-start | bytes 786440 | tf_op jit(solution)/shard_map/ppermute | solution.py:276
  21.9 0.3 collective-permute-start.11
  22.1 0.0 collective-permute-start.7
  22.1 1.5 %collective-permute-start.5 = (f32[40,128]{1,0:T(8,128)S(1)}, f32[40,128]{1,0:T(8,128)S(1)}, u32[]{:S(2)}, u32[]{:S(2)}) collective-permute-start(f32[40,128]{1,0:T(8,128)S(1)} %add.13), channel_id=1, source_target_pairs={{0,4},{1,5},{2,6},{3,7},{4,0},{5,1},{6,2},{7,3},{8,12},{9,13},{10,... | collective-permute-start | bytes 61448 | tf_op jit(solution)/shard_map/ppermute | solution.py:276
  23.6 2.3 %collective-permute-done.5 = f32[40,128]{1,0:T(8,128)S(1)} collective-permute-done((f32[40,128]{1,0:T(8,128)S(1)}, f32[40,128]{1,0:T(8,128)S(1)}, u32[]{:S(2)}, u32[]{:S(2)}) %collective-permute-start.5) | collective-permute-done | bytes 20512 | tf_op jit(solution)/shard_map/ppermute | solution.py:276
  25.9 2.4 %collective-permute-start.6 = (f32[40,128]{1,0:T(8,128)S(1)}, f32[40,128]{1,0:T(8,128)S(1)}, u32[]{:S(2)}, u32[]{:S(2)}) collective-permute-start(f32[40,128]{1,0:T(8,128)S(1)} %add.14.refs_0_), channel_id=1, source_target_pairs={{0,8},{1,9},{2,10},{3,11},{4,12},{5,13},{6,14},{7,15},{8,0},{9,1},... | collective-permute-start | bytes 61448 | tf_op jit(solution)/shard_map/ppermute | solution.py:276
  28.3 2.4 %collective-permute-done.6.refs_1_ = f32[40,128]{1,0:T(8,128)S(1)} collective-permute-done((f32[40,128]{1,0:T(8,128)S(1)}, f32[40,128]{1,0:T(8,128)S(1)}, u32[]{:S(2)}, u32[]{:S(2)}) %collective-permute-start.6) | collective-permute-done | bytes 20512 | tf_op jit(solution)/shard_map/ppermute | solution.py:276
  30.7 2.6 %inverse.1.inv_ref = f32[64,128]{1,0:T(8,128)S(1)} custom-call(f32[40,128]{1,0:T(8,128)S(1)} %add.14.refs_0_, f32[40,128]{1,0:T(8,128)S(1)} %collective-permute-done.6.refs_1_), custom_call_target="tpu_custom_call" | custom-call | tf_op jit(solution)/shard_map/inverse/pallas_call | solution.py:200
  33.4 0.0 collective-permute-done.7.recv_ref
  33.4 0.0 collective-permute-done.10.refs_1_
  33.4 0.6 %collective-permute-done.11.refs_3_ = bf16[32,4096]{1,0:T(8,128)(2,1)S(1)} collective-permute-done((bf16[32,4096]{1,0:T(8,128)(2,1)S(1)}, bf16[32,4096]{1,0:T(8,128)(2,1)S(1)}, u32[]{:S(2)}, u32[]{:S(2)}) %collective-permute-start.11) | collective-permute-done | bytes 262176 | tf_op jit(solution)/shard_map/ppermute | solution.py:276
  33.9 1.6 %scores.1 = f32[16,128]{1,0:T(8,128)S(1)} custom-call(s32[1]{0:T(128)} %bitcast.place_ref, f32[64,128]{1,0:T(8,128)S(1)} %inverse.1.inv_ref, f32[64,512]{1,0:T(8,128)S(1)} %get-tuple-element.27.keep_ref, f32[64,512]{1,0:T(8,128)S(1)} %collective-permute-done.7.recv_ref, bf16[32,4096]{1,0:T(8,128)(2,1)S(1)} %pad_maximum_fusion.1.refs_0_, ...), custom_call_target="tpu_custom_call" | custom-call | tf_op jit(solution)/shard_map/scores/pallas_call | solution.py:261
  35.5 0.0 collective-permute-start.12
  35.6 1.2 %collective-permute-done.12 = f32[8,128]{1,0:T(8,128)S(1)} collective-permute-done((f32[8,128]{1,0:T(8,128)S(1)}, f32[8,128]{1,0:T(8,128)S(1)}, u32[]{:S(2)}, u32[]{:S(2)}) %collective-permute-start.12) | collective-permute-done | bytes 4128 | tf_op jit(solution)/shard_map/ppermute | solution.py:276
  36.7 0.6 %slice_add_fusion = f32[8,128]{1,0:T(8,128)} fusion(f32[8,128]{1,0:T(8,128)S(1)} %collective-permute-done.12, f32[16,128]{1,0:T(8,128)S(1)} %scores.1), kind=kLoop, calls=%fused_computation.15 | loop fusion | flops 1024 | bytes 12288 | tf_op jit(solution)/shard_map/add | solution.py:331
  (13 shorter events, 0.1 us)
Async XLA Ops:
  0.0 12.9 %copy-start = (bf16[2,64,1024]{2,1,0:T(8,128)(2,1)S(1)}, bf16[2,64,1024]{2,1,0:T(8,128)(2,1)}, u32[]{:S(2)}) copy-start(bf16[2,64,1024]{2,1,0:T(8,128)(2,1)} %param.8) | copy-start | bytes 786436
  0.0 0.9 %copy-start.3 = (bf16[8,8192]{1,0:T(8,128)(2,1)S(1)}, bf16[8,8192]{1,0:T(8,128)(2,1)}, u32[]{:S(2)}) copy-start(bf16[8,8192]{1,0:T(8,128)(2,1)} %param.9) | copy-start | bytes 393220
  0.0 6.6 %copy-start.2 = (bf16[2,64,4096]{2,1,0:T(8,128)(2,1)S(1)}, bf16[2,64,4096]{2,1,0:T(8,128)(2,1)}, u32[]{:S(2)}) copy-start(bf16[2,64,4096]{2,1,0:T(8,128)(2,1)} %param.7) | copy-start | bytes 3145732
  1.0 15.2 %collective-permute-start.1 = (bf16[8,8192]{1,0:T(8,128)(2,1)S(1)}, bf16[8,8192]{1,0:T(8,128)(2,1)S(1)}, u32[]{:S(2)}, u32[]{:S(2)}) collective-permute-start(bf16[8,8192]{1,0:T(8,128)(2,1)S(1)} %copy-done.3), channel_id=1, source_target_pairs={{0,12},{1,13},{2,14},{3,15},{4,8},{5,9},{6,10},{7,11},{8,4},{9,5},... | collective-permute-start | bytes 393224 | tf_op jit(solution)/shard_map/ppermute | solution.py:276
  6.0 11.9 %collective-permute-start.3 = (bf16[8,8192]{1,0:T(8,128)(2,1)S(1)}, bf16[8,8192]{1,0:T(8,128)(2,1)S(1)}, u32[]{:S(2)}, u32[]{:S(2)}) collective-permute-start(bf16[8,8192]{1,0:T(8,128)(2,1)S(1)} %copy-done.3), channel_id=1, source_target_pairs={{0,4},{1,5},{2,6},{3,7},{4,0},{5,1},{6,2},{7,3},{8,12},{9,13},{10,... | collective-permute-start | bytes 393224 | tf_op jit(solution)/shard_map/ppermute | solution.py:276
  6.0 12.1 %collective-permute-start.8 = (bf16[8,8192]{1,0:T(8,128)(2,1)S(1)}, bf16[8,8192]{1,0:T(8,128)(2,1)S(1)}, u32[]{:S(2)}, u32[]{:S(2)}) collective-permute-start(bf16[8,8192]{1,0:T(8,128)(2,1)S(1)} %copy-done.3), channel_id=1, source_target_pairs={{0,8},{1,9},{2,10},{3,11},{4,12},{5,13},{6,14},{7,15},{8,0},{9,1},... | collective-permute-start | bytes 393224 | tf_op jit(solution)/shard_map/ppermute | solution.py:276
  6.6 3.4 %copy-start.1 = (bf16[1024,4096]{1,0:T(8,128)(2,1)S(1)}, bf16[1024,4096]{1,0:T(8,128)(2,1)}, u32[]{:S(2)}) copy-start(bf16[1024,4096]{1,0:T(8,128)(2,1)} %x_ref.1) | copy-start | bytes 25165828
  10.0 2.9 %copy-start.4 = (bf16[1024,2,1024]{2,1,0:T(2,128)(2,1)S(1)}, bf16[1024,2,1024]{2,1,0:T(2,128)(2,1)}, u32[]{:S(2)}) copy-start(bf16[1024,2,1024]{2,1,0:T(2,128)(2,1)} %param.6) | copy-start | bytes 12582916
  14.9 1.3 %collective-permute-start = (f32[40,128]{1,0:T(8,128)S(1)}, f32[40,128]{1,0:T(8,128)S(1)}, u32[]{:S(2)}, u32[]{:S(2)}) collective-permute-start(f32[40,128]{1,0:T(8,128)S(1)} %get-tuple-element.23), channel_id=1, source_target_pairs={{0,1},{1,0},{2,3},{3,2},{4,5},{5,4},{6,7},{7,6},{8,9},{9,8},{10,11... | collective-permute-start | bytes 61448 | tf_op jit(solution)/shard_map/ppermute | solution.py:276
  16.1 3.8 %collective-permute-start.2 = (f32[40,128]{1,0:T(8,128)S(1)}, f32[40,128]{1,0:T(8,128)S(1)}, u32[]{:S(2)}, u32[]{:S(2)}) collective-permute-start(f32[40,128]{1,0:T(8,128)S(1)} %add.12), channel_id=1, source_target_pairs={{0,2},{1,3},{2,0},{3,1},{4,6},{5,7},{6,4},{7,5},{8,10},{9,11},{10,... | collective-permute-start | bytes 61448 | tf_op jit(solution)/shard_map/ppermute | solution.py:276
  18.0 2.0 %collective-permute-start.4 = (bf16[16,4096]{1,0:T(8,128)(2,1)S(1)}, bf16[16,4096]{1,0:T(8,128)(2,1)S(1)}, u32[]{:S(2)}, u32[]{:S(2)}) collective-permute-start(bf16[16,4096]{1,0:T(8,128)(2,1)S(1)} %pad_maximum_fusion.2), channel_id=1, source_target_pairs={{0,1},{1,0},{2,3},{3,2},{4,5},{5,4},{6,7},{7,6},{8,9},{9,8},{10,11... | collective-permute-start | bytes 393224 | tf_op jit(solution)/shard_map/ppermute | solution.py:276
  18.1 1.9 %collective-permute-start.9 = (bf16[16,4096]{1,0:T(8,128)(2,1)S(1)}, bf16[16,4096]{1,0:T(8,128)(2,1)S(1)}, u32[]{:S(2)}, u32[]{:S(2)}) collective-permute-start(bf16[16,4096]{1,0:T(8,128)(2,1)S(1)} %pad_maximum_fusion.3), channel_id=1, source_target_pairs={{0,1},{1,0},{2,3},{3,2},{4,5},{5,4},{6,7},{7,6},{8,9},{9,8},{10,11... | collective-permute-start | bytes 393224 | tf_op jit(solution)/shard_map/ppermute | solution.py:276
  20.1 13.3 %collective-permute-start.10 = (bf16[32,4096]{1,0:T(8,128)(2,1)S(1)}, bf16[32,4096]{1,0:T(8,128)(2,1)S(1)}, u32[]{:S(2)}, u32[]{:S(2)}) collective-permute-start(bf16[32,4096]{1,0:T(8,128)(2,1)S(1)} %pad_maximum_fusion.1.refs_0_), channel_id=1, source_target_pairs={{0,2},{1,3},{2,0},{3,1},{4,6},{5,7},{6,4},{7,5},{8,10},{9,11},{10,... | collective-permute-start | bytes 786440 | tf_op jit(solution)/shard_map/ppermute | solution.py:276
  21.9 12.1 %collective-permute-start.11 = (bf16[32,4096]{1,0:T(8,128)(2,1)S(1)}, bf16[32,4096]{1,0:T(8,128)(2,1)S(1)}, u32[]{:S(2)}, u32[]{:S(2)}) collective-permute-start(bf16[32,4096]{1,0:T(8,128)(2,1)S(1)} %pad_maximum_fusion.refs_2_), channel_id=1, source_target_pairs={{0,2},{1,3},{2,0},{3,1},{4,6},{5,7},{6,4},{7,5},{8,10},{9,11},{10,... | collective-permute-start | bytes 786440 | tf_op jit(solution)/shard_map/ppermute | solution.py:276
  22.1 11.2 %collective-permute-start.7 = (f32[64,512]{1,0:T(8,128)S(1)}, f32[64,512]{1,0:T(8,128)S(1)}, u32[]{:S(2)}, u32[]{:S(2)}) collective-permute-start(f32[64,512]{1,0:T(8,128)S(1)} %get-tuple-element.28), channel_id=1, source_target_pairs={{0,1},{1,0},{2,3},{3,2},{4,5},{5,4},{6,7},{7,6},{8,9},{9,8},{10,11... | collective-permute-start | bytes 393224 | tf_op jit(solution)/shard_map/ppermute | solution.py:276
  22.1 3.8 %collective-permute-start.5 = (f32[40,128]{1,0:T(8,128)S(1)}, f32[40,128]{1,0:T(8,128)S(1)}, u32[]{:S(2)}, u32[]{:S(2)}) collective-permute-start(f32[40,128]{1,0:T(8,128)S(1)} %add.13), channel_id=1, source_target_pairs={{0,4},{1,5},{2,6},{3,7},{4,0},{5,1},{6,2},{7,3},{8,12},{9,13},{10,... | collective-permute-start | bytes 61448 | tf_op jit(solution)/shard_map/ppermute | solution.py:276
  25.9 4.8 %collective-permute-start.6 = (f32[40,128]{1,0:T(8,128)S(1)}, f32[40,128]{1,0:T(8,128)S(1)}, u32[]{:S(2)}, u32[]{:S(2)}) collective-permute-start(f32[40,128]{1,0:T(8,128)S(1)} %add.14.refs_0_), channel_id=1, source_target_pairs={{0,8},{1,9},{2,10},{3,11},{4,12},{5,13},{6,14},{7,15},{8,0},{9,1},... | collective-permute-start | bytes 61448 | tf_op jit(solution)/shard_map/ppermute | solution.py:276
  35.5 1.2 %collective-permute-start.12 = (f32[8,128]{1,0:T(8,128)S(1)}, f32[8,128]{1,0:T(8,128)S(1)}, u32[]{:S(2)}, u32[]{:S(2)}) collective-permute-start(f32[8,128]{1,0:T(8,128)S(1)} %slice.9), channel_id=1, source_target_pairs={{0,1},{1,0},{2,3},{3,2},{4,5},{5,4},{6,7},{7,6},{8,9},{9,8},{10,11... | collective-permute-start | bytes 12296 | tf_op jit(solution)/shard_map/ppermute | solution.py:276

commit v8 on v7

--- a/solution.py
+++ b/solution.py
@@ -30,14 +30,14 @@
 
 
 def token_kernel(out_ref):
-    out_ref[...] = jnp.zeros_like(out_ref)
+    out_ref[0] = lax.axis_index("dp")
 
 
 def first_token():
     return pl.pallas_call(
         token_kernel,
-        out_specs=pl.BlockSpec(memory_space=pltpu.VMEM),
-        out_shape=jax.ShapeDtypeStruct((8, 128), F32),
+        out_specs=pl.BlockSpec(memory_space=pltpu.SMEM),
+        out_shape=jax.ShapeDtypeStruct((1,), jnp.int32),
         compiler_params=pltpu.CompilerParams(vmem_limit_bytes=MIB),
         cost_estimate=pl.CostEstimate(flops=STAGE, bytes_accessed=8, transcendentals=0),
         name="first_token",

time: 37.5 us -> 38.3 us (1.021)
  Pallas kernels: 7.65 us -> 8.92 us
  local copies, waits for them, and re-layouts: 4.34 us -> 3.82 us
    pallas_call x1, Pallas kernels: 2.89 us -> 3.67 us  [project(): pl.pallas_call(project_kernel, in_specs=[pl.BlockSpec(memory_space=pl.ANY...]
    unnamed x10, local copies, waits for them, and re-layouts: 4.33 us -> 3.81 us
    pallas_call x1, Pallas kernels: 0.01 us -> 0.52 us  [first_token(): pl.pallas_call(token_kernel, out_specs=pl.BlockSpec(memory_space=pltpu.SM...]
  transfers between devices with their start and end apart: 13 -> 13, of which waited for: 6 -> 6; matrix products, arithmetic and copies ran while one was open for 4% -> 4% of each run, Pallas kernels for 16% -> 18%
where the time goes in v8:
time: 38.3 us; the launch traced here: 38.1 us
  starting transfers between devices  14.1 us (37%)
  Pallas kernels  8.92 us (23%)
  waiting for transfers between devices  8.86 us (23%)
  local copies, waits for them, and re-layouts  3.82 us (10%)
  matrix products  1.44 us (4%)
  other arithmetic  0.73 us (2%)
    ppermute x13, starting transfers between devices, exchange(): lax.ppermute(value, 'dp', [(i, i ^ distance) for i in range(lax.axis_size...  14.1 us
    ppermute x13, waiting for transfers between devices, exchange(): lax.ppermute(value, 'dp', [(i, i ^ distance) for i in range(lax.axis_size...  8.86 us
    unnamed x10, local copies, waits for them, and re-layouts  3.81 us
    pallas_call x1, Pallas kernels, project(): pl.pallas_call(project_kernel, in_specs=[pl.BlockSpec(memory_space=pl.ANY...  3.67 us
    pallas_call x1, Pallas kernels, inverse(): pl.pallas_call(functools.partial(inverse_kernel, total_tokens), in_specs=...  2.65 us
    pallas_call x1, Pallas kernels, score(): pl.pallas_call(functools.partial(scores_kernel, order), in_specs=[pl.Bloc...  1.56 us
    dot_general x1, matrix products, per_device(): jnp.einsum('tmk,mrk->tmr', out_grads, out_proj, preferred_element_type=F32)  1.44 us
  transfers between devices with their start and end apart: 13, of which 6 were waited for; matrix products, arithmetic and copies ran while one was open for 4% of the time, Pallas kernels for 18%

profile of v8, /device:TPU:0, one launch (start us, length us, event | category | flops | bytes accessed | tf_op | source)
XLA Modules:
  0.0 38.1 jit_solution(6242816156813188798)
XLA Ops:
  0.0 0.0 copy-start
  0.0 0.0 copy-start.3
  0.0 0.0 copy-start.2
  0.0 0.5 %first_token.1.token_ref = s32[1]{0:T(128)} custom-call(), custom_call_target="tpu_custom_call" | custom-call | flops 80000000000 | bytes 8 | tf_op jit(solution)/shard_map/first_token/pallas_call | solution.py:37
  0.5 0.4 %copy-done.3 = bf16[8,8192]{1,0:T(8,128)(2,1)S(1)} copy-done((bf16[8,8192]{1,0:T(8,128)(2,1)S(1)}, bf16[8,8192]{1,0:T(8,128)(2,1)}, u32[]{:S(2)}) %copy-start.3) | copy-done | bytes 131096
  1.0 5.0 %collective-permute-start.1 = (bf16[8,8192]{1,0:T(8,128)(2,1)S(1)}, bf16[8,8192]{1,0:T(8,128)(2,1)S(1)}, u32[]{:S(2)}, u32[]{:S(2)}) collective-permute-start(bf16[8,8192]{1,0:T(8,128)(2,1)S(1)} %copy-done.3), channel_id=1, source_target_pairs={{0,12},{1,13},{2,14},{3,15},{4,8},{5,9},{6,10},{7,11},{8,4},{9,5},... | collective-permute-start | bytes 393224 | tf_op jit(solution)/shard_map/ppermute | solution.py:276
  6.0 0.0 collective-permute-start.3
  6.0 0.6 %collective-permute-start.8 = (bf16[8,8192]{1,0:T(8,128)(2,1)S(1)}, bf16[8,8192]{1,0:T(8,128)(2,1)S(1)}, u32[]{:S(2)}, u32[]{:S(2)}) collective-permute-start(bf16[8,8192]{1,0:T(8,128)(2,1)S(1)} %copy-done.3), channel_id=1, source_target_pairs={{0,8},{1,9},{2,10},{3,11},{4,12},{5,13},{6,14},{7,15},{8,0},{9,1},... | collective-permute-start | bytes 393224 | tf_op jit(solution)/shard_map/ppermute | solution.py:276
  6.6 0.0 copy-done.2
  6.6 0.0 copy-start.1
  6.6 3.4 %copy-done.1 = bf16[1024,4096]{1,0:T(8,128)(2,1)S(1)} copy-done((bf16[1024,4096]{1,0:T(8,128)(2,1)S(1)}, bf16[1024,4096]{1,0:T(8,128)(2,1)}, u32[]{:S(2)}) %copy-start.1) | copy-done | bytes 8388632
  10.0 0.0 copy-start.4
  10.0 3.7 %project.1.acts_ref = bf16[128,1024]{1,0:T(8,128)(2,1)S(1)} custom-call(s32[1]{0:T(128)} %first_token.1.token_ref, bf16[1024,4096]{1,0:T(8,128)(2,1)S(1)} %copy-done.1, bf16[128,4096]{1,0:T(8,128)(2,1)S(1)} %bitcast.8), custom_call_target="tpu_custom_call" | custom-call | flops 2147483648 | bytes 8388608 | tf_op jit(solution)/shard_map/project/pallas_call | solution.py:57
  13.6 0.0 copy-done
  13.6 0.0 copy-done.4
  13.7 1.4 %fusion.2 = bf16[2,1024,64]{1,2,0:T(8,128)(2,1)S(1)} fusion(bf16[2,64,1024]{2,1,0:T(8,128)(2,1)S(1)} %copy-done, bf16[1024,2,1024]{2,1,0:T(2,128)(2,1)S(1)} %copy-done.4), kind=kOutput, calls=%fused_computation.2 | convolution fusion | flops 268566528 | bytes 4718592 | tf_op jit(solution)/shard_map/tmk,mrk->tmr/dot_general | solution.py:302
  15.1 0.5 %statistics.1 = (f32[40,128]{1,0:T(8,128)S(1)}, f32[40,128]{1,0:T(8,128)S(1)}, f32[64,512]{1,0:T(8,128)S(1)}, f32[64,512]{1,0:T(8,128)S(1)}) custom-call(s32[1]{0:T(128)} %bitcast.place_ref, bf16[128,1024]{1,0:T(8,128)(2,1)S(1)} %project.1.acts_ref, bf16[128,1024]{1,0:T(8,128)(2,1)S(1)} %bitcast.9), custom_call_target="tpu_custom_call" | custom-call | tf_op jit(solution)/shard_map/statistics/pallas_call | solution.py:126
  15.6 0.1 collective-permute-start
  15.7 1.1 %collective-permute-done = f32[40,128]{1,0:T(8,128)S(1)} collective-permute-done((f32[40,128]{1,0:T(8,128)S(1)}, f32[40,128]{1,0:T(8,128)S(1)}, u32[]{:S(2)}, u32[]{:S(2)}) %collective-permute-start) | collective-permute-done | bytes 20512 | tf_op jit(solution)/shard_map/ppermute | solution.py:276
  16.9 0.0 collective-permute-done.1
  16.9 1.8 %collective-permute-start.2 = (f32[40,128]{1,0:T(8,128)S(1)}, f32[40,128]{1,0:T(8,128)S(1)}, u32[]{:S(2)}, u32[]{:S(2)}) collective-permute-start(f32[40,128]{1,0:T(8,128)S(1)} %add.12), channel_id=1, source_target_pairs={{0,2},{1,3},{2,0},{3,1},{4,6},{5,7},{6,4},{7,5},{8,10},{9,11},{10,... | collective-permute-start | bytes 61448 | tf_op jit(solution)/shard_map/ppermute | solution.py:276
  18.7 0.0 collective-permute-done.3
  18.8 0.1 collective-permute-start.4
  18.9 0.0 collective-permute-done.8
  18.9 0.5 %collective-permute-start.9 = (bf16[16,4096]{1,0:T(8,128)(2,1)S(1)}, bf16[16,4096]{1,0:T(8,128)(2,1)S(1)}, u32[]{:S(2)}, u32[]{:S(2)}) collective-permute-start(bf16[16,4096]{1,0:T(8,128)(2,1)S(1)} %pad_maximum_fusion.3), channel_id=1, source_target_pairs={{0,1},{1,0},{2,3},{3,2},{4,5},{5,4},{6,7},{7,6},{8,9},{9,8},{10,11... | collective-permute-start | bytes 393224 | tf_op jit(solution)/shard_map/ppermute | solution.py:276
  19.5 1.3 %collective-permute-done.2 = f32[40,128]{1,0:T(8,128)S(1)} collective-permute-done((f32[40,128]{1,0:T(8,128)S(1)}, f32[40,128]{1,0:T(8,128)S(1)}, u32[]{:S(2)}, u32[]{:S(2)}) %collective-permute-start.2) | collective-permute-done | bytes 20512 | tf_op jit(solution)/shard_map/ppermute | solution.py:276
  20.8 0.0 collective-permute-done.4
  20.8 0.0 collective-permute-done.9
  20.8 1.8 %collective-permute-start.10 = (bf16[32,4096]{1,0:T(8,128)(2,1)S(1)}, bf16[32,4096]{1,0:T(8,128)(2,1)S(1)}, u32[]{:S(2)}, u32[]{:S(2)}) collective-permute-start(bf16[32,4096]{1,0:T(8,128)(2,1)S(1)} %pad_maximum_fusion.1.refs_0_), channel_id=1, source_target_pairs={{0,2},{1,3},{2,0},{3,1},{4,6},{5,7},{6,4},{7,5},{8,10},{9,11},{10,... | collective-permute-start | bytes 786440 | tf_op jit(solution)/shard_map/ppermute | solution.py:276
  22.6 0.3 collective-permute-start.11
  22.9 0.0 collective-permute-start.7
  22.9 1.5 %collective-permute-start.5 = (f32[40,128]{1,0:T(8,128)S(1)}, f32[40,128]{1,0:T(8,128)S(1)}, u32[]{:S(2)}, u32[]{:S(2)}) collective-permute-start(f32[40,128]{1,0:T(8,128)S(1)} %add.13), channel_id=1, source_target_pairs={{0,4},{1,5},{2,6},{3,7},{4,0},{5,1},{6,2},{7,3},{8,12},{9,13},{10,... | collective-permute-start | bytes 61448 | tf_op jit(solution)/shard_map/ppermute | solution.py:276
  24.4 2.3 %collective-permute-done.5 = f32[40,128]{1,0:T(8,128)S(1)} collective-permute-done((f32[40,128]{1,0:T(8,128)S(1)}, f32[40,128]{1,0:T(8,128)S(1)}, u32[]{:S(2)}, u32[]{:S(2)}) %collective-permute-start.5) | collective-permute-done | bytes 20512 | tf_op jit(solution)/shard_map/ppermute | solution.py:276
  26.7 2.4 %collective-permute-start.6 = (f32[40,128]{1,0:T(8,128)S(1)}, f32[40,128]{1,0:T(8,128)S(1)}, u32[]{:S(2)}, u32[]{:S(2)}) collective-permute-start(f32[40,128]{1,0:T(8,128)S(1)} %add.14.refs_0_), channel_id=1, source_target_pairs={{0,8},{1,9},{2,10},{3,11},{4,12},{5,13},{6,14},{7,15},{8,0},{9,1},... | collective-permute-start | bytes 61448 | tf_op jit(solution)/shard_map/ppermute | solution.py:276
  29.1 2.4 %collective-permute-done.6.refs_1_ = f32[40,128]{1,0:T(8,128)S(1)} collective-permute-done((f32[40,128]{1,0:T(8,128)S(1)}, f32[40,128]{1,0:T(8,128)S(1)}, u32[]{:S(2)}, u32[]{:S(2)}) %collective-permute-start.6) | collective-permute-done | bytes 20512 | tf_op jit(solution)/shard_map/ppermute | solution.py:276
  31.5 2.6 %inverse.1.inv_ref = f32[64,128]{1,0:T(8,128)S(1)} custom-call(f32[40,128]{1,0:T(8,128)S(1)} %add.14.refs_0_, f32[40,128]{1,0:T(8,128)S(1)} %collective-permute-done.6.refs_1_), custom_call_target="tpu_custom_call" | custom-call | tf_op jit(solution)/shard_map/inverse/pallas_call | solution.py:200
  34.1 0.0 collective-permute-done.7.recv_ref
  34.1 0.0 collective-permute-done.10.refs_1_
  34.1 0.6 %collective-permute-done.11.refs_3_ = bf16[32,4096]{1,0:T(8,128)(2,1)S(1)} collective-permute-done((bf16[32,4096]{1,0:T(8,128)(2,1)S(1)}, bf16[32,4096]{1,0:T(8,128)(2,1)S(1)}, u32[]{:S(2)}, u32[]{:S(2)}) %collective-permute-start.11) | collective-permute-done | bytes 262176 | tf_op jit(solution)/shard_map/ppermute | solution.py:276
  34.7 1.6 %scores.1 = f32[16,128]{1,0:T(8,128)S(1)} custom-call(s32[1]{0:T(128)} %bitcast.place_ref, f32[64,128]{1,0:T(8,128)S(1)} %inverse.1.inv_ref, f32[64,512]{1,0:T(8,128)S(1)} %get-tuple-element.27.keep_ref, f32[64,512]{1,0:T(8,128)S(1)} %collective-permute-done.7.recv_ref, bf16[32,4096]{1,0:T(8,128)(2,1)S(1)} %pad_maximum_fusion.1.refs_0_, ...), custom_call_target="tpu_custom_call" | custom-call | tf_op jit(solution)/shard_map/scores/pallas_call | solution.py:261
  36.3 0.0 collective-permute-start.12
  36.3 1.2 %collective-permute-done.12 = f32[8,128]{1,0:T(8,128)S(1)} collective-permute-done((f32[8,128]{1,0:T(8,128)S(1)}, f32[8,128]{1,0:T(8,128)S(1)}, u32[]{:S(2)}, u32[]{:S(2)}) %collective-permute-start.12) | collective-permute-done | bytes 4128 | tf_op jit(solution)/shard_map/ppermute | solution.py:276
  37.5 0.6 %slice_add_fusion = f32[8,128]{1,0:T(8,128)} fusion(f32[8,128]{1,0:T(8,128)S(1)} %collective-permute-done.12, f32[16,128]{1,0:T(8,128)S(1)} %scores.1), kind=kLoop, calls=%fused_computation.15 | loop fusion | flops 1024 | bytes 12288 | tf_op jit(solution)/shard_map/add | solution.py:331
  (12 shorter events, 0.1 us)
Async XLA Ops:
  0.0 13.6 %copy-start = (bf16[2,64,1024]{2,1,0:T(8,128)(2,1)S(1)}, bf16[2,64,1024]{2,1,0:T(8,128)(2,1)}, u32[]{:S(2)}) copy-start(bf16[2,64,1024]{2,1,0:T(8,128)(2,1)} %param.8) | copy-start | bytes 786436
  0.0 0.9 %copy-start.3 = (bf16[8,8192]{1,0:T(8,128)(2,1)S(1)}, bf16[8,8192]{1,0:T(8,128)(2,1)}, u32[]{:S(2)}) copy-start(bf16[8,8192]{1,0:T(8,128)(2,1)} %param.9) | copy-start | bytes 393220
  0.0 6.6 %copy-start.2 = (bf16[2,64,4096]{2,1,0:T(8,128)(2,1)S(1)}, bf16[2,64,4096]{2,1,0:T(8,128)(2,1)}, u32[]{:S(2)}) copy-start(bf16[2,64,4096]{2,1,0:T(8,128)(2,1)} %param.7) | copy-start | bytes 3145732
  1.0 15.9 %collective-permute-start.1 = (bf16[8,8192]{1,0:T(8,128)(2,1)S(1)}, bf16[8,8192]{1,0:T(8,128)(2,1)S(1)}, u32[]{:S(2)}, u32[]{:S(2)}) collective-permute-start(bf16[8,8192]{1,0:T(8,128)(2,1)S(1)} %copy-done.3), channel_id=1, source_target_pairs={{0,12},{1,13},{2,14},{3,15},{4,8},{5,9},{6,10},{7,11},{8,4},{9,5},... | collective-permute-start | bytes 393224 | tf_op jit(solution)/shard_map/ppermute | solution.py:276
  6.0 12.7 %collective-permute-start.3 = (bf16[8,8192]{1,0:T(8,128)(2,1)S(1)}, bf16[8,8192]{1,0:T(8,128)(2,1)S(1)}, u32[]{:S(2)}, u32[]{:S(2)}) collective-permute-start(bf16[8,8192]{1,0:T(8,128)(2,1)S(1)} %copy-done.3), channel_id=1, source_target_pairs={{0,4},{1,5},{2,6},{3,7},{4,0},{5,1},{6,2},{7,3},{8,12},{9,13},{10,... | collective-permute-start | bytes 393224 | tf_op jit(solution)/shard_map/ppermute | solution.py:276
  6.0 12.9 %collective-permute-start.8 = (bf16[8,8192]{1,0:T(8,128)(2,1)S(1)}, bf16[8,8192]{1,0:T(8,128)(2,1)S(1)}, u32[]{:S(2)}, u32[]{:S(2)}) collective-permute-start(bf16[8,8192]{1,0:T(8,128)(2,1)S(1)} %copy-done.3), channel_id=1, source_target_pairs={{0,8},{1,9},{2,10},{3,11},{4,12},{5,13},{6,14},{7,15},{8,0},{9,1},... | collective-permute-start | bytes 393224 | tf_op jit(solution)/shard_map/ppermute | solution.py:276
  6.6 3.4 %copy-start.1 = (bf16[1024,4096]{1,0:T(8,128)(2,1)S(1)}, bf16[1024,4096]{1,0:T(8,128)(2,1)}, u32[]{:S(2)}) copy-start(bf16[1024,4096]{1,0:T(8,128)(2,1)} %x_ref.1) | copy-start | bytes 25165828
  10.0 3.7 %copy-start.4 = (bf16[1024,2,1024]{2,1,0:T(2,128)(2,1)S(1)}, bf16[1024,2,1024]{2,1,0:T(2,128)(2,1)}, u32[]{:S(2)}) copy-start(bf16[1024,2,1024]{2,1,0:T(2,128)(2,1)} %param.6) | copy-start | bytes 12582916
  15.6 1.3 %collective-permute-start = (f32[40,128]{1,0:T(8,128)S(1)}, f32[40,128]{1,0:T(8,128)S(1)}, u32[]{:S(2)}, u32[]{:S(2)}) collective-permute-start(f32[40,128]{1,0:T(8,128)S(1)} %get-tuple-element.23), channel_id=1, source_target_pairs={{0,1},{1,0},{2,3},{3,2},{4,5},{5,4},{6,7},{7,6},{8,9},{9,8},{10,11... | collective-permute-start | bytes 61448 | tf_op jit(solution)/shard_map/ppermute | solution.py:276
  16.9 3.8 %collective-permute-start.2 = (f32[40,128]{1,0:T(8,128)S(1)}, f32[40,128]{1,0:T(8,128)S(1)}, u32[]{:S(2)}, u32[]{:S(2)}) collective-permute-start(f32[40,128]{1,0:T(8,128)S(1)} %add.12), channel_id=1, source_target_pairs={{0,2},{1,3},{2,0},{3,1},{4,6},{5,7},{6,4},{7,5},{8,10},{9,11},{10,... | collective-permute-start | bytes 61448 | tf_op jit(solution)/shard_map/ppermute | solution.py:276
  18.8 2.0 %collective-permute-start.4 = (bf16[16,4096]{1,0:T(8,128)(2,1)S(1)}, bf16[16,4096]{1,0:T(8,128)(2,1)S(1)}, u32[]{:S(2)}, u32[]{:S(2)}) collective-permute-start(bf16[16,4096]{1,0:T(8,128)(2,1)S(1)} %pad_maximum_fusion.2), channel_id=1, source_target_pairs={{0,1},{1,0},{2,3},{3,2},{4,5},{5,4},{6,7},{7,6},{8,9},{9,8},{10,11... | collective-permute-start | bytes 393224 | tf_op jit(solution)/shard_map/ppermute | solution.py:276
  18.9 1.9 %collective-permute-start.9 = (bf16[16,4096]{1,0:T(8,128)(2,1)S(1)}, bf16[16,4096]{1,0:T(8,128)(2,1)S(1)}, u32[]{:S(2)}, u32[]{:S(2)}) collective-permute-start(bf16[16,4096]{1,0:T(8,128)(2,1)S(1)} %pad_maximum_fusion.3), channel_id=1, source_target_pairs={{0,1},{1,0},{2,3},{3,2},{4,5},{5,4},{6,7},{7,6},{8,9},{9,8},{10,11... | collective-permute-start | bytes 393224 | tf_op jit(solution)/shard_map/ppermute | solution.py:276
  20.8 13.3 %collective-permute-start.10 = (bf16[32,4096]{1,0:T(8,128)(2,1)S(1)}, bf16[32,4096]{1,0:T(8,128)(2,1)S(1)}, u32[]{:S(2)}, u32[]{:S(2)}) collective-permute-start(bf16[32,4096]{1,0:T(8,128)(2,1)S(1)} %pad_maximum_fusion.1.refs_0_), channel_id=1, source_target_pairs={{0,2},{1,3},{2,0},{3,1},{4,6},{5,7},{6,4},{7,5},{8,10},{9,11},{10,... | collective-permute-start | bytes 786440 | tf_op jit(solution)/shard_map/ppermute | solution.py:276
  22.6 12.1 %collective-permute-start.11 = (bf16[32,4096]{1,0:T(8,128)(2,1)S(1)}, bf16[32,4096]{1,0:T(8,128)(2,1)S(1)}, u32[]{:S(2)}, u32[]{:S(2)}) collective-permute-start(bf16[32,4096]{1,0:T(8,128)(2,1)S(1)} %pad_maximum_fusion.refs_2_), channel_id=1, source_target_pairs={{0,2},{1,3},{2,0},{3,1},{4,6},{5,7},{6,4},{7,5},{8,10},{9,11},{10,... | collective-permute-start | bytes 786440 | tf_op jit(solution)/shard_map/ppermute | solution.py:276
  22.9 11.2 %collective-permute-start.7 = (f32[64,512]{1,0:T(8,128)S(1)}, f32[64,512]{1,0:T(8,128)S(1)}, u32[]{:S(2)}, u32[]{:S(2)}) collective-permute-start(f32[64,512]{1,0:T(8,128)S(1)} %get-tuple-element.28), channel_id=1, source_target_pairs={{0,1},{1,0},{2,3},{3,2},{4,5},{5,4},{6,7},{7,6},{8,9},{9,8},{10,11... | collective-permute-start | bytes 393224 | tf_op jit(solution)/shard_map/ppermute | solution.py:276
  22.9 3.8 %collective-permute-start.5 = (f32[40,128]{1,0:T(8,128)S(1)}, f32[40,128]{1,0:T(8,128)S(1)}, u32[]{:S(2)}, u32[]{:S(2)}) collective-permute-start(f32[40,128]{1,0:T(8,128)S(1)} %add.13), channel_id=1, source_target_pairs={{0,4},{1,5},{2,6},{3,7},{4,0},{5,1},{6,2},{7,3},{8,12},{9,13},{10,... | collective-permute-start | bytes 61448 | tf_op jit(solution)/shard_map/ppermute | solution.py:276
  26.7 4.8 %collective-permute-start.6 = (f32[40,128]{1,0:T(8,128)S(1)}, f32[40,128]{1,0:T(8,128)S(1)}, u32[]{:S(2)}, u32[]{:S(2)}) collective-permute-start(f32[40,128]{1,0:T(8,128)S(1)} %add.14.refs_0_), channel_id=1, source_target_pairs={{0,8},{1,9},{2,10},{3,11},{4,12},{5,13},{6,14},{7,15},{8,0},{9,1},... | collective-permute-start | bytes 61448 | tf_op jit(solution)/shard_map/ppermute | solution.py:276
  36.3 1.2 %collective-permute-start.12 = (f32[8,128]{1,0:T(8,128)S(1)}, f32[8,128]{1,0:T(8,128)S(1)}, u32[]{:S(2)}, u32[]{:S(2)}) collective-permute-start(f32[8,128]{1,0:T(8,128)S(1)} %slice.9), channel_id=1, source_target_pairs={{0,1},{1,0},{2,3},{3,2},{4,5},{5,4},{6,7},{7,6},{8,9},{9,8},{10,11... | collective-permute-start | bytes 12296 | tf_op jit(solution)/shard_map/ppermute | solution.py:276

commit v9 on v7

--- a/solution.py
+++ b/solution.py
@@ -44,19 +44,18 @@
     )()
 
 
-def project_kernel(token_ref, x_ref, w_ref, acts_ref):
-    del token_ref
+def project_kernel(x_ref, w_ref, acts_ref):
     tokens = x_ref.shape[0]
     for at in range(0, tokens, ROWS):
         acts_ref[:, at : at + ROWS] = dot(w_ref[...], x_ref[at : at + ROWS], NT).astype(BF16)
 
 
-def project(token, layer_input, in_flat):
+def project(layer_input, in_flat):
     tokens, width = layer_input.shape
     vmem = pl.BlockSpec(memory_space=pltpu.VMEM)
     return pl.pallas_call(
         project_kernel,
-        in_specs=[pl.BlockSpec(memory_space=pl.ANY), vmem, vmem],
+        in_specs=[vmem, vmem],
         out_specs=vmem,
         out_shape=jax.ShapeDtypeStruct((PAIR, tokens), BF16),
         compiler_params=pltpu.CompilerParams(vmem_limit_bytes=24 * MIB),
@@ -64,7 +63,7 @@
             flops=4 * tokens * width * PAIR, bytes_accessed=2 * tokens * width, transcendentals=0
         ),
         name="project",
-    )(token, layer_input, in_flat)
+    )(layer_input, in_flat)
 
 
 def fold_pair(pair):
@@ -94,7 +93,8 @@
     return jnp.where((column == row) & (lane >= R), turned[half : half + 1], pair)
 
 
-def statistics_kernel(place_ref, acts_ref, outs_ref, keep_cov, send_cov, keep_mom, send_mom):
+def statistics_kernel(token_ref, place_ref, acts_ref, outs_ref, keep_cov, send_cov, keep_mom, send_mom):
+    del token_ref
     first = place_ref[0] & 1 == 0
     acts = acts_ref[...]
     outs = outs_ref[...]
@@ -118,19 +118,19 @@
         send_mom[:, lanes] = jnp.where(first, mom1, mom0)
 
 
-def statistics(place, acts, outs):
+def statistics(token, place, acts, outs):
     seqs = acts.shape[1] // LEN
     cov = jax.ShapeDtypeStruct((R // 2 + 8, PAIR), F32)
     mom = jax.ShapeDtypeStruct((R, seqs * R), F32)
     vmem = pl.BlockSpec(memory_space=pltpu.VMEM)
     return pl.pallas_call(
         statistics_kernel,
-        in_specs=[pl.BlockSpec(memory_space=pltpu.SMEM), vmem, vmem],
+        in_specs=[pl.BlockSpec(memory_space=pl.ANY), pl.BlockSpec(memory_space=pltpu.SMEM), vmem, vmem],
         out_specs=[vmem] * 4,
         out_shape=[cov, cov, mom, mom],
         compiler_params=pltpu.CompilerParams(vmem_limit_bytes=16 * MIB),
         name="statistics",
-    )(place, acts, outs)
+    )(token, place, acts, outs)
 
 
 def solve_block(p, rows):
@@ -290,7 +290,7 @@
     near_slabs, far_slabs = [0, 2], [1, 3] + list(range(4, slabs))
     column = {slab: exchange(queries, slab * GROUP) for slab in [2, 3, 1] + list(range(4, slabs))}
     column[0] = queries
-    acts = project(token, layer_input, in_proj.reshape(PAIR, in_proj.shape[2]))
+    acts = project(layer_input, in_proj.reshape(PAIR, in_proj.shape[2]))
     acts, out_grads, column[0] = lax.optimization_barrier((acts, out_grads, column[0]))
     upper = place & 1 == 1
 
@@ -301,7 +301,7 @@
 
     outs = jnp.einsum("tmk,mrk->tmr", out_grads, out_proj, preferred_element_type=F32).astype(BF16)
     outs = outs.reshape(local_tokens, PAIR).T
-    keep_cov, send_cov, keep_mom, send_mom = statistics(place.reshape(1), acts, outs)
+    keep_cov, send_cov, keep_mom, send_mom = statistics(token, place.reshape(1), acts, outs)
     cov = keep_cov + exchange(send_cov, 1)
     moments = [keep_mom, exchange(send_mom, 1)]
     cov, column[3] = lax.optimization_barrier((cov, column[3]))

time: 37.5 us -> 37.5 us (level)
  no operation moved by 1% of the time
where the time goes in v9:
time: 37.5 us; the launch traced here: 37.3 us
  starting transfers between devices  14.1 us (38%)
  waiting for transfers between devices  8.87 us (24%)
  Pallas kernels  7.64 us (20%)
  local copies, waits for them, and re-layouts  4.34 us (12%)
  matrix products  1.44 us (4%)
  other arithmetic  0.73 us (2%)
    ppermute x13, starting transfers between devices, exchange(): lax.ppermute(value, 'dp', [(i, i ^ distance) for i in range(lax.axis_size...  14.1 us
    ppermute x13, waiting for transfers between devices, exchange(): lax.ppermute(value, 'dp', [(i, i ^ distance) for i in range(lax.axis_size...  8.87 us
    unnamed x10, local copies, waits for them, and re-layouts  4.33 us
    pallas_call x1, Pallas kernels, project(): pl.pallas_call(project_kernel, in_specs=[vmem, vmem], out_specs=vmem, out...  2.89 us
    pallas_call x1, Pallas kernels, inverse(): pl.pallas_call(functools.partial(inverse_kernel, total_tokens), in_specs=...  2.65 us
    pallas_call x1, Pallas kernels, score(): pl.pallas_call(functools.partial(scores_kernel, order), in_specs=[pl.Bloc...  1.56 us
    dot_general x1, matrix products, per_device(): jnp.einsum('tmk,mrk->tmr', out_grads, out_proj, preferred_element_type=F32)  1.44 us
  transfers between devices with their start and end apart: 13, of which 6 were waited for; matrix products, arithmetic and copies ran while one was open for 4% of the time, Pallas kernels for 16%

profile of v9, /device:TPU:0, one launch (start us, length us, event | category | flops | bytes accessed | tf_op | source)
XLA Modules:
  0.0 37.3 jit_solution(14252427335653519222)
XLA Ops:
  0.0 0.0 copy-start
  0.0 0.0 copy-start.3
  0.0 0.0 copy-start.2
  0.0 0.9 %copy-done.3 = bf16[8,8192]{1,0:T(8,128)(2,1)S(1)} copy-done((bf16[8,8192]{1,0:T(8,128)(2,1)S(1)}, bf16[8,8192]{1,0:T(8,128)(2,1)}, u32[]{:S(2)}) %copy-start.3) | copy-done | bytes 131096
  1.0 5.0 %collective-permute-start.1 = (bf16[8,8192]{1,0:T(8,128)(2,1)S(1)}, bf16[8,8192]{1,0:T(8,128)(2,1)S(1)}, u32[]{:S(2)}, u32[]{:S(2)}) collective-permute-start(bf16[8,8192]{1,0:T(8,128)(2,1)S(1)} %copy-done.3), channel_id=1, source_target_pairs={{0,12},{1,13},{2,14},{3,15},{4,8},{5,9},{6,10},{7,11},{8,4},{9,5},... | collective-permute-start | bytes 393224 | tf_op jit(solution)/shard_map/ppermute | solution.py:276
  6.0 0.0 collective-permute-start.3
  6.0 0.6 %collective-permute-start.8 = (bf16[8,8192]{1,0:T(8,128)(2,1)S(1)}, bf16[8,8192]{1,0:T(8,128)(2,1)S(1)}, u32[]{:S(2)}, u32[]{:S(2)}) collective-permute-start(bf16[8,8192]{1,0:T(8,128)(2,1)S(1)} %copy-done.3), channel_id=1, source_target_pairs={{0,8},{1,9},{2,10},{3,11},{4,12},{5,13},{6,14},{7,15},{8,0},{9,1},... | collective-permute-start | bytes 393224 | tf_op jit(solution)/shard_map/ppermute | solution.py:276
  6.6 0.0 copy-done.2
  6.6 0.0 copy-start.1
  6.6 3.4 %copy-done.1 = bf16[1024,4096]{1,0:T(8,128)(2,1)S(1)} copy-done((bf16[1024,4096]{1,0:T(8,128)(2,1)S(1)}, bf16[1024,4096]{1,0:T(8,128)(2,1)}, u32[]{:S(2)}) %copy-start.1) | copy-done | bytes 8388632
  10.0 0.0 copy-start.4
  10.0 2.9 %project.1.acts_ref = bf16[128,1024]{1,0:T(8,128)(2,1)S(1)} custom-call(bf16[1024,4096]{1,0:T(8,128)(2,1)S(1)} %copy-done.1, bf16[128,4096]{1,0:T(8,128)(2,1)S(1)} %bitcast.8), custom_call_target="tpu_custom_call" | custom-call | flops 2147483648 | bytes 8388608 | tf_op jit(solution)/shard_map/project/pallas_call | solution.py:56
  12.9 0.0 copy-done
  12.9 0.0 copy-done.4
  12.9 1.4 %fusion.2 = bf16[2,1024,64]{1,2,0:T(8,128)(2,1)S(1)} fusion(bf16[2,64,1024]{2,1,0:T(8,128)(2,1)S(1)} %copy-done, bf16[1024,2,1024]{2,1,0:T(2,128)(2,1)S(1)} %copy-done.4), kind=kOutput, calls=%fused_computation.2 | convolution fusion | flops 268566528 | bytes 4718592 | tf_op jit(solution)/shard_map/tmk,mrk->tmr/dot_general | solution.py:302
  14.3 0.5 %statistics.1 = (f32[40,128]{1,0:T(8,128)S(1)}, f32[40,128]{1,0:T(8,128)S(1)}, f32[64,512]{1,0:T(8,128)S(1)}, f32[64,512]{1,0:T(8,128)S(1)}) custom-call(f32[8,128]{1,0:T(8,128)S(1)} %first_token.1.token_ref, s32[1]{0:T(128)} %bitcast.place_ref, bf16[128,1024]{1,0:T(8,128)(2,1)S(1)} %project.1.acts_ref, bf16[128,1024]{1,0:T(8,128)(2,1)S(1)} %bitcast.9), custom_call_target="tpu_custom_call" | custom-call | tf_op jit(solution)/shard_map/statistics/pallas_call | solution.py:126
  14.9 0.1 collective-permute-start
  15.0 1.1 %collective-permute-done = f32[40,128]{1,0:T(8,128)S(1)} collective-permute-done((f32[40,128]{1,0:T(8,128)S(1)}, f32[40,128]{1,0:T(8,128)S(1)}, u32[]{:S(2)}, u32[]{:S(2)}) %collective-permute-start) | collective-permute-done | bytes 20512 | tf_op jit(solution)/shard_map/ppermute | solution.py:276
  16.1 0.0 collective-permute-done.1
  16.1 1.8 %collective-permute-start.2 = (f32[40,128]{1,0:T(8,128)S(1)}, f32[40,128]{1,0:T(8,128)S(1)}, u32[]{:S(2)}, u32[]{:S(2)}) collective-permute-start(f32[40,128]{1,0:T(8,128)S(1)} %add.12), channel_id=1, source_target_pairs={{0,2},{1,3},{2,0},{3,1},{4,6},{5,7},{6,4},{7,5},{8,10},{9,11},{10,... | collective-permute-start | bytes 61448 | tf_op jit(solution)/shard_map/ppermute | solution.py:276
  17.9 0.0 collective-permute-done.3
  18.0 0.1 collective-permute-start.4
  18.1 0.0 collective-permute-done.8
  18.1 0.5 %collective-permute-start.9 = (bf16[16,4096]{1,0:T(8,128)(2,1)S(1)}, bf16[16,4096]{1,0:T(8,128)(2,1)S(1)}, u32[]{:S(2)}, u32[]{:S(2)}) collective-permute-start(bf16[16,4096]{1,0:T(8,128)(2,1)S(1)} %pad_maximum_fusion.3), channel_id=1, source_target_pairs={{0,1},{1,0},{2,3},{3,2},{4,5},{5,4},{6,7},{7,6},{8,9},{9,8},{10,11... | collective-permute-start | bytes 393224 | tf_op jit(solution)/shard_map/ppermute | solution.py:276
  18.7 1.3 %collective-permute-done.2 = f32[40,128]{1,0:T(8,128)S(1)} collective-permute-done((f32[40,128]{1,0:T(8,128)S(1)}, f32[40,128]{1,0:T(8,128)S(1)}, u32[]{:S(2)}, u32[]{:S(2)}) %collective-permute-start.2) | collective-permute-done | bytes 20512 | tf_op jit(solution)/shard_map/ppermute | solution.py:276
  20.0 0.0 collective-permute-done.4
  20.0 0.0 collective-permute-done.9
  20.0 1.8 %collective-permute-start.10 = (bf16[32,4096]{1,0:T(8,128)(2,1)S(1)}, bf16[32,4096]{1,0:T(8,128)(2,1)S(1)}, u32[]{:S(2)}, u32[]{:S(2)}) collective-permute-start(bf16[32,4096]{1,0:T(8,128)(2,1)S(1)} %pad_maximum_fusion.1.refs_0_), channel_id=1, source_target_pairs={{0,2},{1,3},{2,0},{3,1},{4,6},{5,7},{6,4},{7,5},{8,10},{9,11},{10,... | collective-permute-start | bytes 786440 | tf_op jit(solution)/shard_map/ppermute | solution.py:276
  21.8 0.3 collective-permute-start.11
  22.1 0.0 collective-permute-start.7
  22.1 1.5 %collective-permute-start.5 = (f32[40,128]{1,0:T(8,128)S(1)}, f32[40,128]{1,0:T(8,128)S(1)}, u32[]{:S(2)}, u32[]{:S(2)}) collective-permute-start(f32[40,128]{1,0:T(8,128)S(1)} %add.13), channel_id=1, source_target_pairs={{0,4},{1,5},{2,6},{3,7},{4,0},{5,1},{6,2},{7,3},{8,12},{9,13},{10,... | collective-permute-start | bytes 61448 | tf_op jit(solution)/shard_map/ppermute | solution.py:276
  23.6 2.3 %collective-permute-done.5 = f32[40,128]{1,0:T(8,128)S(1)} collective-permute-done((f32[40,128]{1,0:T(8,128)S(1)}, f32[40,128]{1,0:T(8,128)S(1)}, u32[]{:S(2)}, u32[]{:S(2)}) %collective-permute-start.5) | collective-permute-done | bytes 20512 | tf_op jit(solution)/shard_map/ppermute | solution.py:276
  25.9 2.4 %collective-permute-start.6 = (f32[40,128]{1,0:T(8,128)S(1)}, f32[40,128]{1,0:T(8,128)S(1)}, u32[]{:S(2)}, u32[]{:S(2)}) collective-permute-start(f32[40,128]{1,0:T(8,128)S(1)} %add.14.refs_0_), channel_id=1, source_target_pairs={{0,8},{1,9},{2,10},{3,11},{4,12},{5,13},{6,14},{7,15},{8,0},{9,1},... | collective-permute-start | bytes 61448 | tf_op jit(solution)/shard_map/ppermute | solution.py:276
  28.3 2.4 %collective-permute-done.6.refs_1_ = f32[40,128]{1,0:T(8,128)S(1)} collective-permute-done((f32[40,128]{1,0:T(8,128)S(1)}, f32[40,128]{1,0:T(8,128)S(1)}, u32[]{:S(2)}, u32[]{:S(2)}) %collective-permute-start.6) | collective-permute-done | bytes 20512 | tf_op jit(solution)/shard_map/ppermute | solution.py:276
  30.7 2.6 %inverse.1.inv_ref = f32[64,128]{1,0:T(8,128)S(1)} custom-call(f32[40,128]{1,0:T(8,128)S(1)} %add.14.refs_0_, f32[40,128]{1,0:T(8,128)S(1)} %collective-permute-done.6.refs_1_), custom_call_target="tpu_custom_call" | custom-call | tf_op jit(solution)/shard_map/inverse/pallas_call | solution.py:200
  33.3 0.0 collective-permute-done.7.recv_ref
  33.4 0.0 collective-permute-done.10.refs_1_
  33.4 0.6 %collective-permute-done.11.refs_3_ = bf16[32,4096]{1,0:T(8,128)(2,1)S(1)} collective-permute-done((bf16[32,4096]{1,0:T(8,128)(2,1)S(1)}, bf16[32,4096]{1,0:T(8,128)(2,1)S(1)}, u32[]{:S(2)}, u32[]{:S(2)}) %collective-permute-start.11) | collective-permute-done | bytes 262176 | tf_op jit(solution)/shard_map/ppermute | solution.py:276
  33.9 1.6 %scores.1 = f32[16,128]{1,0:T(8,128)S(1)} custom-call(s32[1]{0:T(128)} %bitcast.place_ref, f32[64,128]{1,0:T(8,128)S(1)} %inverse.1.inv_ref, f32[64,512]{1,0:T(8,128)S(1)} %get-tuple-element.27.keep_ref, f32[64,512]{1,0:T(8,128)S(1)} %collective-permute-done.7.recv_ref, bf16[32,4096]{1,0:T(8,128)(2,1)S(1)} %pad_maximum_fusion.1.refs_0_, ...), custom_call_target="tpu_custom_call" | custom-call | tf_op jit(solution)/shard_map/scores/pallas_call | solution.py:261
  35.5 0.0 collective-permute-start.12
  35.6 1.2 %collective-permute-done.12 = f32[8,128]{1,0:T(8,128)S(1)} collective-permute-done((f32[8,128]{1,0:T(8,128)S(1)}, f32[8,128]{1,0:T(8,128)S(1)}, u32[]{:S(2)}, u32[]{:S(2)}) %collective-permute-start.12) | collective-permute-done | bytes 4128 | tf_op jit(solution)/shard_map/ppermute | solution.py:276
  36.7 0.6 %slice_add_fusion = f32[8,128]{1,0:T(8,128)} fusion(f32[8,128]{1,0:T(8,128)S(1)} %collective-permute-done.12, f32[16,128]{1,0:T(8,128)S(1)} %scores.1), kind=kLoop, calls=%fused_computation.15 | loop fusion | flops 1024 | bytes 12288 | tf_op jit(solution)/shard_map/add | solution.py:331
  (13 shorter events, 0.1 us)
Async XLA Ops:
  0.0 12.9 %copy-start = (bf16[2,64,1024]{2,1,0:T(8,128)(2,1)S(1)}, bf16[2,64,1024]{2,1,0:T(8,128)(2,1)}, u32[]{:S(2)}) copy-start(bf16[2,64,1024]{2,1,0:T(8,128)(2,1)} %param.8) | copy-start | bytes 786436
  0.0 0.9 %copy-start.3 = (bf16[8,8192]{1,0:T(8,128)(2,1)S(1)}, bf16[8,8192]{1,0:T(8,128)(2,1)}, u32[]{:S(2)}) copy-start(bf16[8,8192]{1,0:T(8,128)(2,1)} %param.9) | copy-start | bytes 393220
  0.0 6.6 %copy-start.2 = (bf16[2,64,4096]{2,1,0:T(8,128)(2,1)S(1)}, bf16[2,64,4096]{2,1,0:T(8,128)(2,1)}, u32[]{:S(2)}) copy-start(bf16[2,64,4096]{2,1,0:T(8,128)(2,1)} %param.7) | copy-start | bytes 3145732
  1.0 15.2 %collective-permute-start.1 = (bf16[8,8192]{1,0:T(8,128)(2,1)S(1)}, bf16[8,8192]{1,0:T(8,128)(2,1)S(1)}, u32[]{:S(2)}, u32[]{:S(2)}) collective-permute-start(bf16[8,8192]{1,0:T(8,128)(2,1)S(1)} %copy-done.3), channel_id=1, source_target_pairs={{0,12},{1,13},{2,14},{3,15},{4,8},{5,9},{6,10},{7,11},{8,4},{9,5},... | collective-permute-start | bytes 393224 | tf_op jit(solution)/shard_map/ppermute | solution.py:276
  6.0 11.9 %collective-permute-start.3 = (bf16[8,8192]{1,0:T(8,128)(2,1)S(1)}, bf16[8,8192]{1,0:T(8,128)(2,1)S(1)}, u32[]{:S(2)}, u32[]{:S(2)}) collective-permute-start(bf16[8,8192]{1,0:T(8,128)(2,1)S(1)} %copy-done.3), channel_id=1, source_target_pairs={{0,4},{1,5},{2,6},{3,7},{4,0},{5,1},{6,2},{7,3},{8,12},{9,13},{10,... | collective-permute-start | bytes 393224 | tf_op jit(solution)/shard_map/ppermute | solution.py:276
  6.0 12.1 %collective-permute-start.8 = (bf16[8,8192]{1,0:T(8,128)(2,1)S(1)}, bf16[8,8192]{1,0:T(8,128)(2,1)S(1)}, u32[]{:S(2)}, u32[]{:S(2)}) collective-permute-start(bf16[8,8192]{1,0:T(8,128)(2,1)S(1)} %copy-done.3), channel_id=1, source_target_pairs={{0,8},{1,9},{2,10},{3,11},{4,12},{5,13},{6,14},{7,15},{8,0},{9,1},... | collective-permute-start | bytes 393224 | tf_op jit(solution)/shard_map/ppermute | solution.py:276
  6.6 3.4 %copy-start.1 = (bf16[1024,4096]{1,0:T(8,128)(2,1)S(1)}, bf16[1024,4096]{1,0:T(8,128)(2,1)}, u32[]{:S(2)}) copy-start(bf16[1024,4096]{1,0:T(8,128)(2,1)} %x_ref.1) | copy-start | bytes 25165828
  10.0 2.9 %copy-start.4 = (bf16[1024,2,1024]{2,1,0:T(2,128)(2,1)S(1)}, bf16[1024,2,1024]{2,1,0:T(2,128)(2,1)}, u32[]{:S(2)}) copy-start(bf16[1024,2,1024]{2,1,0:T(2,128)(2,1)} %param.6) | copy-start | bytes 12582916
  14.9 1.3 %collective-permute-start = (f32[40,128]{1,0:T(8,128)S(1)}, f32[40,128]{1,0:T(8,128)S(1)}, u32[]{:S(2)}, u32[]{:S(2)}) collective-permute-start(f32[40,128]{1,0:T(8,128)S(1)} %get-tuple-element.23), channel_id=1, source_target_pairs={{0,1},{1,0},{2,3},{3,2},{4,5},{5,4},{6,7},{7,6},{8,9},{9,8},{10,11... | collective-permute-start | bytes 61448 | tf_op jit(solution)/shard_map/ppermute | solution.py:276
  16.1 3.8 %collective-permute-start.2 = (f32[40,128]{1,0:T(8,128)S(1)}, f32[40,128]{1,0:T(8,128)S(1)}, u32[]{:S(2)}, u32[]{:S(2)}) collective-permute-start(f32[40,128]{1,0:T(8,128)S(1)} %add.12), channel_id=1, source_target_pairs={{0,2},{1,3},{2,0},{3,1},{4,6},{5,7},{6,4},{7,5},{8,10},{9,11},{10,... | collective-permute-start | bytes 61448 | tf_op jit(solution)/shard_map/ppermute | solution.py:276
  18.0 2.0 %collective-permute-start.4 = (bf16[16,4096]{1,0:T(8,128)(2,1)S(1)}, bf16[16,4096]{1,0:T(8,128)(2,1)S(1)}, u32[]{:S(2)}, u32[]{:S(2)}) collective-permute-start(bf16[16,4096]{1,0:T(8,128)(2,1)S(1)} %pad_maximum_fusion.2), channel_id=1, source_target_pairs={{0,1},{1,0},{2,3},{3,2},{4,5},{5,4},{6,7},{7,6},{8,9},{9,8},{10,11... | collective-permute-start | bytes 393224 | tf_op jit(solution)/shard_map/ppermute | solution.py:276
  18.1 1.9 %collective-permute-start.9 = (bf16[16,4096]{1,0:T(8,128)(2,1)S(1)}, bf16[16,4096]{1,0:T(8,128)(2,1)S(1)}, u32[]{:S(2)}, u32[]{:S(2)}) collective-permute-start(bf16[16,4096]{1,0:T(8,128)(2,1)S(1)} %pad_maximum_fusion.3), channel_id=1, source_target_pairs={{0,1},{1,0},{2,3},{3,2},{4,5},{5,4},{6,7},{7,6},{8,9},{9,8},{10,11... | collective-permute-start | bytes 393224 | tf_op jit(solution)/shard_map/ppermute | solution.py:276
  20.0 13.3 %collective-permute-start.10 = (bf16[32,4096]{1,0:T(8,128)(2,1)S(1)}, bf16[32,4096]{1,0:T(8,128)(2,1)S(1)}, u32[]{:S(2)}, u32[]{:S(2)}) collective-permute-start(bf16[32,4096]{1,0:T(8,128)(2,1)S(1)} %pad_maximum_fusion.1.refs_0_), channel_id=1, source_target_pairs={{0,2},{1,3},{2,0},{3,1},{4,6},{5,7},{6,4},{7,5},{8,10},{9,11},{10,... | collective-permute-start | bytes 786440 | tf_op jit(solution)/shard_map/ppermute | solution.py:276
  21.8 12.1 %collective-permute-start.11 = (bf16[32,4096]{1,0:T(8,128)(2,1)S(1)}, bf16[32,4096]{1,0:T(8,128)(2,1)S(1)}, u32[]{:S(2)}, u32[]{:S(2)}) collective-permute-start(bf16[32,4096]{1,0:T(8,128)(2,1)S(1)} %pad_maximum_fusion.refs_2_), channel_id=1, source_target_pairs={{0,2},{1,3},{2,0},{3,1},{4,6},{5,7},{6,4},{7,5},{8,10},{9,11},{10,... | collective-permute-start | bytes 786440 | tf_op jit(solution)/shard_map/ppermute | solution.py:276
  22.1 11.2 %collective-permute-start.7 = (f32[64,512]{1,0:T(8,128)S(1)}, f32[64,512]{1,0:T(8,128)S(1)}, u32[]{:S(2)}, u32[]{:S(2)}) collective-permute-start(f32[64,512]{1,0:T(8,128)S(1)} %get-tuple-element.28), channel_id=1, source_target_pairs={{0,1},{1,0},{2,3},{3,2},{4,5},{5,4},{6,7},{7,6},{8,9},{9,8},{10,11... | collective-permute-start | bytes 393224 | tf_op jit(solution)/shard_map/ppermute | solution.py:276
  22.1 3.8 %collective-permute-start.5 = (f32[40,128]{1,0:T(8,128)S(1)}, f32[40,128]{1,0:T(8,128)S(1)}, u32[]{:S(2)}, u32[]{:S(2)}) collective-permute-start(f32[40,128]{1,0:T(8,128)S(1)} %add.13), channel_id=1, source_target_pairs={{0,4},{1,5},{2,6},{3,7},{4,0},{5,1},{6,2},{7,3},{8,12},{9,13},{10,... | collective-permute-start | bytes 61448 | tf_op jit(solution)/shard_map/ppermute | solution.py:276
  25.9 4.8 %collective-permute-start.6 = (f32[40,128]{1,0:T(8,128)S(1)}, f32[40,128]{1,0:T(8,128)S(1)}, u32[]{:S(2)}, u32[]{:S(2)}) collective-permute-start(f32[40,128]{1,0:T(8,128)S(1)} %add.14.refs_0_), channel_id=1, source_target_pairs={{0,8},{1,9},{2,10},{3,11},{4,12},{5,13},{6,14},{7,15},{8,0},{9,1},... | collective-permute-start | bytes 61448 | tf_op jit(solution)/shard_map/ppermute | solution.py:276
  35.5 1.2 %collective-permute-start.12 = (f32[8,128]{1,0:T(8,128)S(1)}, f32[8,128]{1,0:T(8,128)S(1)}, u32[]{:S(2)}, u32[]{:S(2)}) collective-permute-start(f32[8,128]{1,0:T(8,128)S(1)} %slice.9), channel_id=1, source_target_pairs={{0,1},{1,0},{2,3},{3,2},{4,5},{5,4},{6,7},{7,6},{8,9},{9,8},{10,11... | collective-permute-start | bytes 12296 | tf_op jit(solution)/shard_map/ppermute | solution.py:276

commit v10 on v8

--- a/solution.py
+++ b/solution.py
@@ -29,34 +29,33 @@
 NT = ((1,), (1,))
 
 
-def token_kernel(out_ref):
+def place_kernel(out_ref):
     out_ref[0] = lax.axis_index("dp")
 
 
-def first_token():
-    return pl.pallas_call(
-        token_kernel,
+def own_place():
+    return pl.pallas_call(
+        place_kernel,
         out_specs=pl.BlockSpec(memory_space=pltpu.SMEM),
         out_shape=jax.ShapeDtypeStruct((1,), jnp.int32),
         compiler_params=pltpu.CompilerParams(vmem_limit_bytes=MIB),
         cost_estimate=pl.CostEstimate(flops=STAGE, bytes_accessed=8, transcendentals=0),
-        name="first_token",
+        name="own_place",
     )()
 
 
-def project_kernel(token_ref, x_ref, w_ref, acts_ref):
-    del token_ref
+def project_kernel(x_ref, w_ref, acts_ref):
     tokens = x_ref.shape[0]
     for at in range(0, tokens, ROWS):
         acts_ref[:, at : at + ROWS] = dot(w_ref[...], x_ref[at : at + ROWS], NT).astype(BF16)
 
 
-def project(token, layer_input, in_flat):
+def project(layer_input, in_flat):
     tokens, width = layer_input.shape
     vmem = pl.BlockSpec(memory_space=pltpu.VMEM)
     return pl.pallas_call(
         project_kernel,
-        in_specs=[pl.BlockSpec(memory_space=pl.ANY), vmem, vmem],
+        in_specs=[vmem, vmem],
         out_specs=vmem,
         out_shape=jax.ShapeDtypeStruct((PAIR, tokens), BF16),
         compiler_params=pltpu.CompilerParams(vmem_limit_bytes=24 * MIB),
@@ -64,7 +63,7 @@
             flops=4 * tokens * width * PAIR, bytes_accessed=2 * tokens * width, transcendentals=0
         ),
         name="project",
-    )(token, layer_input, in_flat)
+    )(layer_input, in_flat)
 
 
 def fold_pair(pair):
@@ -286,13 +285,13 @@
     devices = lax.axis_size("dp")
     slabs = devices // GROUP
     place = lax.axis_index("dp").astype(jnp.int32)
-    token, queries = lax.optimization_barrier((first_token(), queries))
+    device, queries = lax.optimization_barrier((own_place(), queries))
     near_slabs, far_slabs = [0, 2], [1, 3] + list(range(4, slabs))
     column = {slab: exchange(queries, slab * GROUP) for slab in [2, 3, 1] + list(range(4, slabs))}
     column[0] = queries
-    acts = project(token, layer_input, in_proj.reshape(PAIR, in_proj.shape[2]))
+    acts = project(layer_input, in_proj.reshape(PAIR, in_proj.shape[2]))
     acts, out_grads, column[0] = lax.optimization_barrier((acts, out_grads, column[0]))
-    upper = place & 1 == 1
+    upper = device[0] & 1 == 1
 
     def fold(picked):
         keep, send = zip(*(halves(column[slab], upper) for slab in picked))

time: 38.3 us -> 37.5 us (0.979)
  Pallas kernels: 8.92 us -> 8.15 us
  between operations: 0.19 us -> 0.81 us
  waiting for transfers between devices: 8.86 us -> 8.25 us
    pallas_call x2, Pallas kernels: 4.18 us -> 3.41 us  [the longest x1 2.89 us: project(): pl.pallas_call(project_kernel, in_specs=[vmem, vmem], out_specs=vmem, out...]
    ppermute x13, waiting for transfers between devices: 8.86 us -> 8.25 us  [exchange(): lax.ppermute(value, 'dp', [(i, i ^ distance) for i in range(lax.axis_size...]
  transfers between devices with their start and end apart: 13 -> 13, of which waited for: 6 -> 6; matrix products, arithmetic and copies ran while one was open for 4% -> 4% of each run, Pallas kernels for 18% -> 16%
where the time goes in v10:
time: 37.5 us; the launch traced here: 37.3 us
  starting transfers between devices  14.1 us (38%)
  waiting for transfers between devices  8.25 us (22%)
  Pallas kernels  8.15 us (22%)
  local copies, waits for them, and re-layouts  3.82 us (10%)
  matrix products  1.44 us (4%)
  between operations  0.81 us (2%)
  other arithmetic  0.73 us (2%)
    ppermute x13, starting transfers between devices, exchange(): lax.ppermute(value, 'dp', [(i, i ^ distance) for i in range(lax.axis_size...  14.1 us
    ppermute x13, waiting for transfers between devices, exchange(): lax.ppermute(value, 'dp', [(i, i ^ distance) for i in range(lax.axis_size...  8.25 us
    unnamed x10, local copies, waits for them, and re-layouts  3.81 us
    pallas_call x1, Pallas kernels, project(): pl.pallas_call(project_kernel, in_specs=[vmem, vmem], out_specs=vmem, out...  2.89 us
    pallas_call x1, Pallas kernels, inverse(): pl.pallas_call(functools.partial(inverse_kernel, total_tokens), in_specs=...  2.65 us
    pallas_call x1, Pallas kernels, score(): pl.pallas_call(functools.partial(scores_kernel, order), in_specs=[pl.Bloc...  1.56 us
    dot_general x1, matrix products, per_device(): jnp.einsum('tmk,mrk->tmr', out_grads, out_proj, preferred_element_type=F32)  1.44 us
  transfers between devices with their start and end apart: 13, of which 6 were waited for; matrix products, arithmetic and copies ran while one was open for 4% of the time, Pallas kernels for 16%

profile of v10, /device:TPU:0, one launch (start us, length us, event | category | flops | bytes accessed | tf_op | source)
XLA Modules:
  0.0 37.3 jit_solution(1842113426804125591)
XLA Ops:
  0.0 0.0 copy-start
  0.0 0.0 copy-start.3
  0.0 0.0 copy-start.2
  0.0 0.5 %own_place.1 = s32[1]{0:T(128)} custom-call(), custom_call_target="tpu_custom_call" | custom-call | flops 80000000000 | bytes 8 | tf_op jit(solution)/shard_map/own_place/pallas_call | solution.py:37
  0.5 0.4 %copy-done.3 = bf16[8,8192]{1,0:T(8,128)(2,1)S(1)} copy-done((bf16[8,8192]{1,0:T(8,128)(2,1)S(1)}, bf16[8,8192]{1,0:T(8,128)(2,1)}, u32[]{:S(2)}) %copy-start.3) | copy-done | bytes 131096
  1.0 5.0 %collective-permute-start.1 = (bf16[8,8192]{1,0:T(8,128)(2,1)S(1)}, bf16[8,8192]{1,0:T(8,128)(2,1)S(1)}, u32[]{:S(2)}, u32[]{:S(2)}) collective-permute-start(bf16[8,8192]{1,0:T(8,128)(2,1)S(1)} %copy-done.3), channel_id=1, source_target_pairs={{0,12},{1,13},{2,14},{3,15},{4,8},{5,9},{6,10},{7,11},{8,4},{9,5},... | collective-permute-start | bytes 393224 | tf_op jit(solution)/shard_map/ppermute | solution.py:275
  6.0 0.0 collective-permute-start.3
  6.0 0.6 %collective-permute-start.8 = (bf16[8,8192]{1,0:T(8,128)(2,1)S(1)}, bf16[8,8192]{1,0:T(8,128)(2,1)S(1)}, u32[]{:S(2)}, u32[]{:S(2)}) collective-permute-start(bf16[8,8192]{1,0:T(8,128)(2,1)S(1)} %copy-done.3), channel_id=1, source_target_pairs={{0,8},{1,9},{2,10},{3,11},{4,12},{5,13},{6,14},{7,15},{8,0},{9,1},... | collective-permute-start | bytes 393224 | tf_op jit(solution)/shard_map/ppermute | solution.py:275
  6.6 0.0 copy-done.2
  6.6 0.0 copy-start.1
  6.6 3.4 %copy-done.1 = bf16[1024,4096]{1,0:T(8,128)(2,1)S(1)} copy-done((bf16[1024,4096]{1,0:T(8,128)(2,1)S(1)}, bf16[1024,4096]{1,0:T(8,128)(2,1)}, u32[]{:S(2)}) %copy-start.1) | copy-done | bytes 8388632
  10.0 0.0 copy-start.4
  10.0 2.9 %project.1.acts_ref = bf16[128,1024]{1,0:T(8,128)(2,1)S(1)} custom-call(bf16[1024,4096]{1,0:T(8,128)(2,1)S(1)} %copy-done.1, bf16[128,4096]{1,0:T(8,128)(2,1)S(1)} %bitcast.9), custom_call_target="tpu_custom_call" | custom-call | flops 2147483648 | bytes 8388608 | tf_op jit(solution)/shard_map/project/pallas_call | solution.py:56
  12.9 0.0 copy-done
  12.9 0.0 copy-done.4
  12.9 1.4 %fusion.2 = bf16[2,1024,64]{1,2,0:T(8,128)(2,1)S(1)} fusion(bf16[2,64,1024]{2,1,0:T(8,128)(2,1)S(1)} %copy-done, bf16[1024,2,1024]{2,1,0:T(2,128)(2,1)S(1)} %copy-done.4), kind=kOutput, calls=%fused_computation.2 | convolution fusion | flops 268566528 | bytes 4718592 | tf_op jit(solution)/shard_map/tmk,mrk->tmr/dot_general | solution.py:301
  14.3 0.5 %statistics.1 = (f32[40,128]{1,0:T(8,128)S(1)}, f32[40,128]{1,0:T(8,128)S(1)}, f32[64,512]{1,0:T(8,128)S(1)}, f32[64,512]{1,0:T(8,128)S(1)}) custom-call(s32[1]{0:T(128)} %bitcast.place_ref, bf16[128,1024]{1,0:T(8,128)(2,1)S(1)} %project.1.acts_ref, bf16[128,1024]{1,0:T(8,128)(2,1)S(1)} %bitcast.10), custom_call_target="tpu_custom_call" | custom-call | tf_op jit(solution)/shard_map/statistics/pallas_call | solution.py:125
  14.9 0.1 collective-permute-start
  15.6 0.5 %collective-permute-done = f32[40,128]{1,0:T(8,128)S(1)} collective-permute-done((f32[40,128]{1,0:T(8,128)S(1)}, f32[40,128]{1,0:T(8,128)S(1)}, u32[]{:S(2)}, u32[]{:S(2)}) %collective-permute-start) | collective-permute-done | bytes 20512 | tf_op jit(solution)/shard_map/ppermute | solution.py:275
  16.1 0.0 collective-permute-done.1
  16.1 1.8 %collective-permute-start.2 = (f32[40,128]{1,0:T(8,128)S(1)}, f32[40,128]{1,0:T(8,128)S(1)}, u32[]{:S(2)}, u32[]{:S(2)}) collective-permute-start(f32[40,128]{1,0:T(8,128)S(1)} %add.12), channel_id=1, source_target_pairs={{0,2},{1,3},{2,0},{3,1},{4,6},{5,7},{6,4},{7,5},{8,10},{9,11},{10,... | collective-permute-start | bytes 61448 | tf_op jit(solution)/shard_map/ppermute | solution.py:275
  17.9 0.0 collective-permute-done.3
  18.0 0.1 collective-permute-start.4
  18.1 0.0 collective-permute-done.8
  18.1 0.5 %collective-permute-start.9 = (bf16[16,4096]{1,0:T(8,128)(2,1)S(1)}, bf16[16,4096]{1,0:T(8,128)(2,1)S(1)}, u32[]{:S(2)}, u32[]{:S(2)}) collective-permute-start(bf16[16,4096]{1,0:T(8,128)(2,1)S(1)} %pad_maximum_fusion.3), channel_id=1, source_target_pairs={{0,1},{1,0},{2,3},{3,2},{4,5},{5,4},{6,7},{7,6},{8,9},{9,8},{10,11... | collective-permute-start | bytes 393224 | tf_op jit(solution)/shard_map/ppermute | solution.py:275
  18.7 1.3 %collective-permute-done.2 = f32[40,128]{1,0:T(8,128)S(1)} collective-permute-done((f32[40,128]{1,0:T(8,128)S(1)}, f32[40,128]{1,0:T(8,128)S(1)}, u32[]{:S(2)}, u32[]{:S(2)}) %collective-permute-start.2) | collective-permute-done | bytes 20512 | tf_op jit(solution)/shard_map/ppermute | solution.py:275
  20.0 0.0 collective-permute-done.4
  20.0 0.0 collective-permute-done.9
  20.0 1.8 %collective-permute-start.10 = (bf16[32,4096]{1,0:T(8,128)(2,1)S(1)}, bf16[32,4096]{1,0:T(8,128)(2,1)S(1)}, u32[]{:S(2)}, u32[]{:S(2)}) collective-permute-start(bf16[32,4096]{1,0:T(8,128)(2,1)S(1)} %pad_maximum_fusion.1.refs_0_), channel_id=1, source_target_pairs={{0,2},{1,3},{2,0},{3,1},{4,6},{5,7},{6,4},{7,5},{8,10},{9,11},{10,... | collective-permute-start | bytes 786440 | tf_op jit(solution)/shard_map/ppermute | solution.py:275
  21.8 0.3 collective-permute-start.11
  22.1 0.0 collective-permute-start.7
  22.1 1.5 %collective-permute-start.5 = (f32[40,128]{1,0:T(8,128)S(1)}, f32[40,128]{1,0:T(8,128)S(1)}, u32[]{:S(2)}, u32[]{:S(2)}) collective-permute-start(f32[40,128]{1,0:T(8,128)S(1)} %add.13), channel_id=1, source_target_pairs={{0,4},{1,5},{2,6},{3,7},{4,0},{5,1},{6,2},{7,3},{8,12},{9,13},{10,... | collective-permute-start | bytes 61448 | tf_op jit(solution)/shard_map/ppermute | solution.py:275
  23.6 2.3 %collective-permute-done.5 = f32[40,128]{1,0:T(8,128)S(1)} collective-permute-done((f32[40,128]{1,0:T(8,128)S(1)}, f32[40,128]{1,0:T(8,128)S(1)}, u32[]{:S(2)}, u32[]{:S(2)}) %collective-permute-start.5) | collective-permute-done | bytes 20512 | tf_op jit(solution)/shard_map/ppermute | solution.py:275
  25.9 2.4 %collective-permute-start.6 = (f32[40,128]{1,0:T(8,128)S(1)}, f32[40,128]{1,0:T(8,128)S(1)}, u32[]{:S(2)}, u32[]{:S(2)}) collective-permute-start(f32[40,128]{1,0:T(8,128)S(1)} %add.14.refs_0_), channel_id=1, source_target_pairs={{0,8},{1,9},{2,10},{3,11},{4,12},{5,13},{6,14},{7,15},{8,0},{9,1},... | collective-permute-start | bytes 61448 | tf_op jit(solution)/shard_map/ppermute | solution.py:275
  28.3 2.4 %collective-permute-done.6.refs_1_ = f32[40,128]{1,0:T(8,128)S(1)} collective-permute-done((f32[40,128]{1,0:T(8,128)S(1)}, f32[40,128]{1,0:T(8,128)S(1)}, u32[]{:S(2)}, u32[]{:S(2)}) %collective-permute-start.6) | collective-permute-done | bytes 20512 | tf_op jit(solution)/shard_map/ppermute | solution.py:275
  30.7 2.6 %inverse.1.inv_ref = f32[64,128]{1,0:T(8,128)S(1)} custom-call(f32[40,128]{1,0:T(8,128)S(1)} %add.14.refs_0_, f32[40,128]{1,0:T(8,128)S(1)} %collective-permute-done.6.refs_1_), custom_call_target="tpu_custom_call" | custom-call | tf_op jit(solution)/shard_map/inverse/pallas_call | solution.py:199
  33.3 0.0 collective-permute-done.7.recv_ref
  33.4 0.0 collective-permute-done.10.refs_1_
  33.4 0.6 %collective-permute-done.11.refs_3_ = bf16[32,4096]{1,0:T(8,128)(2,1)S(1)} collective-permute-done((bf16[32,4096]{1,0:T(8,128)(2,1)S(1)}, bf16[32,4096]{1,0:T(8,128)(2,1)S(1)}, u32[]{:S(2)}, u32[]{:S(2)}) %collective-permute-start.11) | collective-permute-done | bytes 262176 | tf_op jit(solution)/shard_map/ppermute | solution.py:275
  33.9 1.6 %scores.1 = f32[16,128]{1,0:T(8,128)S(1)} custom-call(s32[1]{0:T(128)} %bitcast.place_ref, f32[64,128]{1,0:T(8,128)S(1)} %inverse.1.inv_ref, f32[64,512]{1,0:T(8,128)S(1)} %get-tuple-element.27.keep_ref, f32[64,512]{1,0:T(8,128)S(1)} %collective-permute-done.7.recv_ref, bf16[32,4096]{1,0:T(8,128)(2,1)S(1)} %pad_maximum_fusion.1.refs_0_, ...), custom_call_target="tpu_custom_call" | custom-call | tf_op jit(solution)/shard_map/scores/pallas_call | solution.py:260
  35.5 0.0 collective-permute-start.12
  35.6 1.2 %collective-permute-done.12 = f32[8,128]{1,0:T(8,128)S(1)} collective-permute-done((f32[8,128]{1,0:T(8,128)S(1)}, f32[8,128]{1,0:T(8,128)S(1)}, u32[]{:S(2)}, u32[]{:S(2)}) %collective-permute-start.12) | collective-permute-done | bytes 4128 | tf_op jit(solution)/shard_map/ppermute | solution.py:275
  36.7 0.6 %slice_add_fusion = f32[8,128]{1,0:T(8,128)} fusion(f32[8,128]{1,0:T(8,128)S(1)} %collective-permute-done.12, f32[16,128]{1,0:T(8,128)S(1)} %scores.1), kind=kLoop, calls=%fused_computation.15 | loop fusion | flops 1024 | bytes 12288 | tf_op jit(solution)/shard_map/add | solution.py:330
  (12 shorter events, 0.1 us)
Async XLA Ops:
  0.0 12.9 %copy-start = (bf16[2,64,1024]{2,1,0:T(8,128)(2,1)S(1)}, bf16[2,64,1024]{2,1,0:T(8,128)(2,1)}, u32[]{:S(2)}) copy-start(bf16[2,64,1024]{2,1,0:T(8,128)(2,1)} %param.8) | copy-start | bytes 786436
  0.0 0.9 %copy-start.3 = (bf16[8,8192]{1,0:T(8,128)(2,1)S(1)}, bf16[8,8192]{1,0:T(8,128)(2,1)}, u32[]{:S(2)}) copy-start(bf16[8,8192]{1,0:T(8,128)(2,1)} %param.9) | copy-start | bytes 393220
  0.0 6.6 %copy-start.2 = (bf16[2,64,4096]{2,1,0:T(8,128)(2,1)S(1)}, bf16[2,64,4096]{2,1,0:T(8,128)(2,1)}, u32[]{:S(2)}) copy-start(bf16[2,64,4096]{2,1,0:T(8,128)(2,1)} %param.7) | copy-start | bytes 3145732
  1.0 15.2 %collective-permute-start.1 = (bf16[8,8192]{1,0:T(8,128)(2,1)S(1)}, bf16[8,8192]{1,0:T(8,128)(2,1)S(1)}, u32[]{:S(2)}, u32[]{:S(2)}) collective-permute-start(bf16[8,8192]{1,0:T(8,128)(2,1)S(1)} %copy-done.3), channel_id=1, source_target_pairs={{0,12},{1,13},{2,14},{3,15},{4,8},{5,9},{6,10},{7,11},{8,4},{9,5},... | collective-permute-start | bytes 393224 | tf_op jit(solution)/shard_map/ppermute | solution.py:275
  6.0 11.9 %collective-permute-start.3 = (bf16[8,8192]{1,0:T(8,128)(2,1)S(1)}, bf16[8,8192]{1,0:T(8,128)(2,1)S(1)}, u32[]{:S(2)}, u32[]{:S(2)}) collective-permute-start(bf16[8,8192]{1,0:T(8,128)(2,1)S(1)} %copy-done.3), channel_id=1, source_target_pairs={{0,4},{1,5},{2,6},{3,7},{4,0},{5,1},{6,2},{7,3},{8,12},{9,13},{10,... | collective-permute-start | bytes 393224 | tf_op jit(solution)/shard_map/ppermute | solution.py:275
  6.0 12.1 %collective-permute-start.8 = (bf16[8,8192]{1,0:T(8,128)(2,1)S(1)}, bf16[8,8192]{1,0:T(8,128)(2,1)S(1)}, u32[]{:S(2)}, u32[]{:S(2)}) collective-permute-start(bf16[8,8192]{1,0:T(8,128)(2,1)S(1)} %copy-done.3), channel_id=1, source_target_pairs={{0,8},{1,9},{2,10},{3,11},{4,12},{5,13},{6,14},{7,15},{8,0},{9,1},... | collective-permute-start | bytes 393224 | tf_op jit(solution)/shard_map/ppermute | solution.py:275
  6.6 3.4 %copy-start.1 = (bf16[1024,4096]{1,0:T(8,128)(2,1)S(1)}, bf16[1024,4096]{1,0:T(8,128)(2,1)}, u32[]{:S(2)}) copy-start(bf16[1024,4096]{1,0:T(8,128)(2,1)} %x_ref.1) | copy-start | bytes 25165828
  10.0 2.9 %copy-start.4 = (bf16[1024,2,1024]{2,1,0:T(2,128)(2,1)S(1)}, bf16[1024,2,1024]{2,1,0:T(2,128)(2,1)}, u32[]{:S(2)}) copy-start(bf16[1024,2,1024]{2,1,0:T(2,128)(2,1)} %param.6) | copy-start | bytes 12582916
  14.9 1.3 %collective-permute-start = (f32[40,128]{1,0:T(8,128)S(1)}, f32[40,128]{1,0:T(8,128)S(1)}, u32[]{:S(2)}, u32[]{:S(2)}) collective-permute-start(f32[40,128]{1,0:T(8,128)S(1)} %get-tuple-element.22), channel_id=1, source_target_pairs={{0,1},{1,0},{2,3},{3,2},{4,5},{5,4},{6,7},{7,6},{8,9},{9,8},{10,11... | collective-permute-start | bytes 61448 | tf_op jit(solution)/shard_map/ppermute | solution.py:275
  16.1 3.8 %collective-permute-start.2 = (f32[40,128]{1,0:T(8,128)S(1)}, f32[40,128]{1,0:T(8,128)S(1)}, u32[]{:S(2)}, u32[]{:S(2)}) collective-permute-start(f32[40,128]{1,0:T(8,128)S(1)} %add.12), channel_id=1, source_target_pairs={{0,2},{1,3},{2,0},{3,1},{4,6},{5,7},{6,4},{7,5},{8,10},{9,11},{10,... | collective-permute-start | bytes 61448 | tf_op jit(solution)/shard_map/ppermute | solution.py:275
  18.0 2.0 %collective-permute-start.4 = (bf16[16,4096]{1,0:T(8,128)(2,1)S(1)}, bf16[16,4096]{1,0:T(8,128)(2,1)S(1)}, u32[]{:S(2)}, u32[]{:S(2)}) collective-permute-start(bf16[16,4096]{1,0:T(8,128)(2,1)S(1)} %pad_maximum_fusion.2), channel_id=1, source_target_pairs={{0,1},{1,0},{2,3},{3,2},{4,5},{5,4},{6,7},{7,6},{8,9},{9,8},{10,11... | collective-permute-start | bytes 393224 | tf_op jit(solution)/shard_map/ppermute | solution.py:275
  18.1 1.9 %collective-permute-start.9 = (bf16[16,4096]{1,0:T(8,128)(2,1)S(1)}, bf16[16,4096]{1,0:T(8,128)(2,1)S(1)}, u32[]{:S(2)}, u32[]{:S(2)}) collective-permute-start(bf16[16,4096]{1,0:T(8,128)(2,1)S(1)} %pad_maximum_fusion.3), channel_id=1, source_target_pairs={{0,1},{1,0},{2,3},{3,2},{4,5},{5,4},{6,7},{7,6},{8,9},{9,8},{10,11... | collective-permute-start | bytes 393224 | tf_op jit(solution)/shard_map/ppermute | solution.py:275
  20.0 13.3 %collective-permute-start.10 = (bf16[32,4096]{1,0:T(8,128)(2,1)S(1)}, bf16[32,4096]{1,0:T(8,128)(2,1)S(1)}, u32[]{:S(2)}, u32[]{:S(2)}) collective-permute-start(bf16[32,4096]{1,0:T(8,128)(2,1)S(1)} %pad_maximum_fusion.1.refs_0_), channel_id=1, source_target_pairs={{0,2},{1,3},{2,0},{3,1},{4,6},{5,7},{6,4},{7,5},{8,10},{9,11},{10,... | collective-permute-start | bytes 786440 | tf_op jit(solution)/shard_map/ppermute | solution.py:275
  21.8 12.1 %collective-permute-start.11 = (bf16[32,4096]{1,0:T(8,128)(2,1)S(1)}, bf16[32,4096]{1,0:T(8,128)(2,1)S(1)}, u32[]{:S(2)}, u32[]{:S(2)}) collective-permute-start(bf16[32,4096]{1,0:T(8,128)(2,1)S(1)} %pad_maximum_fusion.refs_2_), channel_id=1, source_target_pairs={{0,2},{1,3},{2,0},{3,1},{4,6},{5,7},{6,4},{7,5},{8,10},{9,11},{10,... | collective-permute-start | bytes 786440 | tf_op jit(solution)/shard_map/ppermute | solution.py:275
  22.1 11.2 %collective-permute-start.7 = (f32[64,512]{1,0:T(8,128)S(1)}, f32[64,512]{1,0:T(8,128)S(1)}, u32[]{:S(2)}, u32[]{:S(2)}) collective-permute-start(f32[64,512]{1,0:T(8,128)S(1)} %get-tuple-element.28), channel_id=1, source_target_pairs={{0,1},{1,0},{2,3},{3,2},{4,5},{5,4},{6,7},{7,6},{8,9},{9,8},{10,11... | collective-permute-start | bytes 393224 | tf_op jit(solution)/shard_map/ppermute | solution.py:275
  22.1 3.8 %collective-permute-start.5 = (f32[40,128]{1,0:T(8,128)S(1)}, f32[40,128]{1,0:T(8,128)S(1)}, u32[]{:S(2)}, u32[]{:S(2)}) collective-permute-start(f32[40,128]{1,0:T(8,128)S(1)} %add.13), channel_id=1, source_target_pairs={{0,4},{1,5},{2,6},{3,7},{4,0},{5,1},{6,2},{7,3},{8,12},{9,13},{10,... | collective-permute-start | bytes 61448 | tf_op jit(solution)/shard_map/ppermute | solution.py:275
  25.9 4.8 %collective-permute-start.6 = (f32[40,128]{1,0:T(8,128)S(1)}, f32[40,128]{1,0:T(8,128)S(1)}, u32[]{:S(2)}, u32[]{:S(2)}) collective-permute-start(f32[40,128]{1,0:T(8,128)S(1)} %add.14.refs_0_), channel_id=1, source_target_pairs={{0,8},{1,9},{2,10},{3,11},{4,12},{5,13},{6,14},{7,15},{8,0},{9,1},... | collective-permute-start | bytes 61448 | tf_op jit(solution)/shard_map/ppermute | solution.py:275
  35.5 1.2 %collective-permute-start.12 = (f32[8,128]{1,0:T(8,128)S(1)}, f32[8,128]{1,0:T(8,128)S(1)}, u32[]{:S(2)}, u32[]{:S(2)}) collective-permute-start(f32[8,128]{1,0:T(8,128)S(1)} %slice.9), channel_id=1, source_target_pairs={{0,1},{1,0},{2,3},{3,2},{4,5},{5,4},{6,7},{7,6},{8,9},{9,8},{10,11... | collective-permute-start | bytes 12296 | tf_op jit(solution)/shard_map/ppermute | solution.py:275

commit v11 on v10

--- a/solution.py
+++ b/solution.py
@@ -93,8 +93,8 @@
     return jnp.where((column == row) & (lane >= R), turned[half : half + 1], pair)
 
 
-def statistics_kernel(place_ref, acts_ref, outs_ref, keep_cov, send_cov, keep_mom, send_mom):
-    first = place_ref[0] & 1 == 0
+def statistics_kernel(acts_ref, outs_ref, keep_cov, send_cov, keep_mom, send_mom):
+    first = lax.axis_index("dp") & 1 == 0
     acts = acts_ref[...]
     outs = outs_ref[...]
     low = lax.broadcasted_iota(jnp.int32, (R, PAIR), 1) < R
@@ -117,19 +117,19 @@
         send_mom[:, lanes] = jnp.where(first, mom1, mom0)
 
 
-def statistics(place, acts, outs):
+def statistics(acts, outs):
     seqs = acts.shape[1] // LEN
     cov = jax.ShapeDtypeStruct((R // 2 + 8, PAIR), F32)
     mom = jax.ShapeDtypeStruct((R, seqs * R), F32)
     vmem = pl.BlockSpec(memory_space=pltpu.VMEM)
     return pl.pallas_call(
         statistics_kernel,
-        in_specs=[pl.BlockSpec(memory_space=pltpu.SMEM), vmem, vmem],
+        in_specs=[vmem, vmem],
         out_specs=[vmem] * 4,
         out_shape=[cov, cov, mom, mom],
         compiler_params=pltpu.CompilerParams(vmem_limit_bytes=16 * MIB),
         name="statistics",
-    )(place, acts, outs)
+    )(acts, outs)
 
 
 def solve_block(p, rows):
@@ -206,9 +206,9 @@
     )(*covs)
 
 
-def scores_kernel(order, place_ref, inv_ref, keep_ref, recv_ref, *refs):
+def scores_kernel(order, inv_ref, keep_ref, recv_ref, *refs):
     query_refs, (out_ref, flat_ref, part_ref) = refs[:-3], refs[-3:]
-    place = place_ref[0]
+    place = lax.axis_index("dp")
     low = lax.broadcasted_iota(jnp.int32, (R, PAIR), 1) < R
     inv = inv_ref[...]
     tiles = R // 2
@@ -253,13 +253,13 @@
     out_ref[...] = part_ref[...].reshape(part.shape).T
 
 
-def score(place, inv, moments, queries, order):
+def score(inv, moments, queries, order):
     seqs = sum(part.shape[1] for part in moments) // R
     count = sum(part.shape[0] for part in queries)
     vmem = pl.BlockSpec(memory_space=pltpu.VMEM)
     return pl.pallas_call(
         functools.partial(scores_kernel, order),
-        in_specs=[pl.BlockSpec(memory_space=pltpu.SMEM)] + [vmem] * (1 + len(moments) + len(queries)),
+        in_specs=[vmem] * (1 + len(moments) + len(queries)),
         out_specs=vmem,
         out_shape=jax.ShapeDtypeStruct((seqs, count), F32),
         scratch_shapes=[
@@ -268,7 +268,7 @@
         ],
         compiler_params=pltpu.CompilerParams(vmem_limit_bytes=16 * MIB),
         name="scores",
-    )(place, inv, *moments, *queries)
+    )(inv, *moments, *queries)
 
 
 def exchange(value, distance):
@@ -284,7 +284,6 @@
     local_tokens = layer_input.shape[0]
     devices = lax.axis_size("dp")
     slabs = devices // GROUP
-    place = lax.axis_index("dp").astype(jnp.int32)
     device, queries = lax.optimization_barrier((own_place(), queries))
     near_slabs, far_slabs = [0, 2], [1, 3] + list(range(4, slabs))
     column = {slab: exchange(queries, slab * GROUP) for slab in [2, 3, 1] + list(range(4, slabs))}
@@ -300,7 +299,7 @@
 
     outs = jnp.einsum("tmk,mrk->tmr", out_grads, out_proj, preferred_element_type=F32).astype(BF16)
     outs = outs.reshape(local_tokens, PAIR).T
-    keep_cov, send_cov, keep_mom, send_mom = statistics(place.reshape(1), acts, outs)
+    keep_cov, send_cov, keep_mom, send_mom = statistics(acts, outs)
     cov = keep_cov + exchange(send_cov, 1)
     moments = [keep_mom, exchange(send_mom, 1)]
     cov, column[3] = lax.optimization_barrier((cov, column[3]))
@@ -325,7 +324,7 @@
         for core in range(2)
         for slab in part
     ]
-    partial = score(place.reshape(1), inv, moments, gathered, order)
+    partial = score(inv, moments, gathered, order)
     seqs = local_tokens // LEN
     return partial[:seqs] + exchange(partial[seqs:], 1)
 

time: 37.5 us -> 36.1 us (0.963)
  waiting for transfers between devices: 8.25 us -> 13.5 us
  local copies, waits for them, and re-layouts: 3.82 us -> 0.43 us
  starting transfers between devices: 14.1 us -> 10.8 us
    ppermute x13, waiting for transfers between devices: 8.25 us -> 13.5 us  [exchange(): lax.ppermute(value, 'dp', [(i, i ^ distance) for i in range(lax.axis_size...]
    unnamed x10, local copies, waits for them, and re-layouts: 3.81 us -> 0.42 us
    ppermute x13, starting transfers between devices: 14.1 us -> 10.8 us  [exchange(): lax.ppermute(value, 'dp', [(i, i ^ distance) for i in range(lax.axis_size...]
  transfers between devices with their start and end apart: 13 -> 13, of which waited for: 6 -> 7; matrix products, arithmetic and copies ran while one was open for 4% -> 4% of each run, Pallas kernels for 16% -> 17%
where the time goes in v11:
time: 36.1 us; the launch traced here: 36 us
  waiting for transfers between devices  13.5 us (37%)
  starting transfers between devices  10.8 us (30%)
  Pallas kernels  8.16 us (23%)
  matrix products  1.44 us (4%)
  between operations  0.84 us (2%)
  other arithmetic  0.73 us (2%)
  local copies, waits for them, and re-layouts  0.43 us (1%)
    ppermute x13, waiting for transfers between devices, exchange(): lax.ppermute(value, 'dp', [(i, i ^ distance) for i in range(lax.axis_size...  13.5 us
    ppermute x13, starting transfers between devices, exchange(): lax.ppermute(value, 'dp', [(i, i ^ distance) for i in range(lax.axis_size...  10.8 us
    pallas_call x1, Pallas kernels, project(): pl.pallas_call(project_kernel, in_specs=[vmem, vmem], out_specs=vmem, out...  2.89 us
    pallas_call x1, Pallas kernels, inverse(): pl.pallas_call(functools.partial(inverse_kernel, total_tokens), in_specs=...  2.65 us
    pallas_call x1, Pallas kernels, score(): pl.pallas_call(functools.partial(scores_kernel, order), in_specs=[vmem] *...  1.56 us
    dot_general x1, matrix products, per_device(): jnp.einsum('tmk,mrk->tmr', out_grads, out_proj, preferred_element_type=F32)  1.44 us
  transfers between devices with their start and end apart: 13, of which 7 were waited for; matrix products, arithmetic and copies ran while one was open for 4% of the time, Pallas kernels for 17%

profile of v11, /device:TPU:0, one launch (start us, length us, event | category | flops | bytes accessed | tf_op | source)
XLA Modules:
  0.0 36.0 jit_solution(9783553240741393529)
XLA Ops:
  0.0 0.0 copy-start
  0.0 0.0 copy-start.3
  0.0 0.0 copy-start.1
  0.0 0.0 copy-start.2
  0.0 0.5 %own_place.1 = s32[1]{0:T(128)} custom-call(), custom_call_target="tpu_custom_call" | custom-call | flops 80000000000 | bytes 8 | tf_op jit(solution)/shard_map/own_place/pallas_call | solution.py:37
  0.5 0.4 %copy-done.3 = bf16[8,8192]{1,0:T(8,128)(2,1)S(1)} copy-done((bf16[8,8192]{1,0:T(8,128)(2,1)S(1)}, bf16[8,8192]{1,0:T(8,128)(2,1)}, u32[]{:S(2)}) %copy-start.3) | copy-done | bytes 131096
  1.0 5.0 %collective-permute-start.1 = (bf16[8,8192]{1,0:T(8,128)(2,1)S(1)}, bf16[8,8192]{1,0:T(8,128)(2,1)S(1)}, u32[]{:S(2)}, u32[]{:S(2)}) collective-permute-start(bf16[8,8192]{1,0:T(8,128)(2,1)S(1)} %copy-done.3), channel_id=1, source_target_pairs={{0,12},{1,13},{2,14},{3,15},{4,8},{5,9},{6,10},{7,11},{8,4},{9,5},... | collective-permute-start | bytes 393224 | tf_op jit(solution)/shard_map/ppermute | solution.py:275
  6.0 0.0 collective-permute-start.3
  6.0 0.6 %collective-permute-start.8 = (bf16[8,8192]{1,0:T(8,128)(2,1)S(1)}, bf16[8,8192]{1,0:T(8,128)(2,1)S(1)}, u32[]{:S(2)}, u32[]{:S(2)}) collective-permute-start(bf16[8,8192]{1,0:T(8,128)(2,1)S(1)} %copy-done.3), channel_id=1, source_target_pairs={{0,8},{1,9},{2,10},{3,11},{4,12},{5,13},{6,14},{7,15},{8,0},{9,1},... | collective-permute-start | bytes 393224 | tf_op jit(solution)/shard_map/ppermute | solution.py:275
  6.6 0.0 copy-done.1
  6.6 0.0 copy-done.2
  6.6 0.0 copy-start.4
  6.6 2.9 %project.1.acts_ref = bf16[128,1024]{1,0:T(8,128)(2,1)S(1)} custom-call(bf16[1024,4096]{1,0:T(8,128)(2,1)S(1)} %copy-done.1, bf16[128,4096]{1,0:T(8,128)(2,1)S(1)} %bitcast.8), custom_call_target="tpu_custom_call" | custom-call | flops 2147483648 | bytes 8388608 | tf_op jit(solution)/shard_map/project/pallas_call | solution.py:56
  9.5 0.0 copy-done
  9.5 0.0 copy-done.4
  9.5 1.4 %fusion.2 = bf16[2,1024,64]{1,2,0:T(8,128)(2,1)S(1)} fusion(bf16[2,64,1024]{2,1,0:T(8,128)(2,1)S(1)} %copy-done, bf16[1024,2,1024]{2,1,0:T(2,128)(2,1)S(1)} %copy-done.4), kind=kOutput, calls=%fused_computation.2 | convolution fusion | flops 268566528 | bytes 4718592 | tf_op jit(solution)/shard_map/tmk,mrk->tmr/dot_general | solution.py:300
  10.9 0.5 %statistics.1 = (f32[40,128]{1,0:T(8,128)S(1)}, f32[40,128]{1,0:T(8,128)S(1)}, f32[64,512]{1,0:T(8,128)S(1)}, f32[64,512]{1,0:T(8,128)S(1)}) custom-call(bf16[128,1024]{1,0:T(8,128)(2,1)S(1)} %project.1.acts_ref, bf16[128,1024]{1,0:T(8,128)(2,1)S(1)} %bitcast.9), custom_call_target="tpu_custom_call" | custom-call | tf_op jit(solution)/shard_map/statistics/pallas_call | solution.py:125
  11.5 0.1 collective-permute-start
  12.2 0.5 %collective-permute-done = f32[40,128]{1,0:T(8,128)S(1)} collective-permute-done((f32[40,128]{1,0:T(8,128)S(1)}, f32[40,128]{1,0:T(8,128)S(1)}, u32[]{:S(2)}, u32[]{:S(2)}) %collective-permute-start) | collective-permute-done | bytes 20512 | tf_op jit(solution)/shard_map/ppermute | solution.py:275
  12.7 0.0 collective-permute-done.1
  12.7 1.8 %collective-permute-start.2 = (f32[40,128]{1,0:T(8,128)S(1)}, f32[40,128]{1,0:T(8,128)S(1)}, u32[]{:S(2)}, u32[]{:S(2)}) collective-permute-start(f32[40,128]{1,0:T(8,128)S(1)} %add.12), channel_id=1, source_target_pairs={{0,2},{1,3},{2,0},{3,1},{4,6},{5,7},{6,4},{7,5},{8,10},{9,11},{10,... | collective-permute-start | bytes 61448 | tf_op jit(solution)/shard_map/ppermute | solution.py:275
  14.6 0.0 collective-permute-done.3
  14.6 0.1 collective-permute-start.4
  14.7 2.4 %collective-permute-done.8 = bf16[8,8192]{1,0:T(8,128)(2,1)S(1)} collective-permute-done((bf16[8,8192]{1,0:T(8,128)(2,1)S(1)}, bf16[8,8192]{1,0:T(8,128)(2,1)S(1)}, u32[]{:S(2)}, u32[]{:S(2)}) %collective-permute-start.8) | collective-permute-done | bytes 131104 | tf_op jit(solution)/shard_map/ppermute | solution.py:275
  17.1 0.1 collective-permute-start.9
  17.2 0.0 collective-permute-done.2
  17.2 0.0 collective-permute-done.4
  17.3 1.3 %collective-permute-done.9 = bf16[16,4096]{1,0:T(8,128)(2,1)S(1)} collective-permute-done((bf16[16,4096]{1,0:T(8,128)(2,1)S(1)}, bf16[16,4096]{1,0:T(8,128)(2,1)S(1)}, u32[]{:S(2)}, u32[]{:S(2)}) %collective-permute-start.9) | collective-permute-done | bytes 131104 | tf_op jit(solution)/shard_map/ppermute | solution.py:275
  18.5 1.6 %collective-permute-start.10 = (bf16[32,4096]{1,0:T(8,128)(2,1)S(1)}, bf16[32,4096]{1,0:T(8,128)(2,1)S(1)}, u32[]{:S(2)}, u32[]{:S(2)}) collective-permute-start(bf16[32,4096]{1,0:T(8,128)(2,1)S(1)} %pad_maximum_fusion.1.refs_0_), channel_id=1, source_target_pairs={{0,2},{1,3},{2,0},{3,1},{4,6},{5,7},{6,4},{7,5},{8,10},{9,11},{10,... | collective-permute-start | bytes 786440 | tf_op jit(solution)/shard_map/ppermute | solution.py:275
  20.1 0.5 %collective-permute-start.11 = (bf16[32,4096]{1,0:T(8,128)(2,1)S(1)}, bf16[32,4096]{1,0:T(8,128)(2,1)S(1)}, u32[]{:S(2)}, u32[]{:S(2)}) collective-permute-start(bf16[32,4096]{1,0:T(8,128)(2,1)S(1)} %pad_maximum_fusion.refs_2_), channel_id=1, source_target_pairs={{0,2},{1,3},{2,0},{3,1},{4,6},{5,7},{6,4},{7,5},{8,10},{9,11},{10,... | collective-permute-start | bytes 786440 | tf_op jit(solution)/shard_map/ppermute | solution.py:275
  20.6 0.0 collective-permute-start.7
  20.6 0.0 collective-permute-start.5
  20.6 3.8 %collective-permute-done.5 = f32[40,128]{1,0:T(8,128)S(1)} collective-permute-done((f32[40,128]{1,0:T(8,128)S(1)}, f32[40,128]{1,0:T(8,128)S(1)}, u32[]{:S(2)}, u32[]{:S(2)}) %collective-permute-start.5) | collective-permute-done | bytes 20512 | tf_op jit(solution)/shard_map/ppermute | solution.py:275
  24.4 1.1 %collective-permute-start.6 = (f32[40,128]{1,0:T(8,128)S(1)}, f32[40,128]{1,0:T(8,128)S(1)}, u32[]{:S(2)}, u32[]{:S(2)}) collective-permute-start(f32[40,128]{1,0:T(8,128)S(1)} %add.14.refs_0_), channel_id=1, source_target_pairs={{0,8},{1,9},{2,10},{3,11},{4,12},{5,13},{6,14},{7,15},{8,0},{9,1},... | collective-permute-start | bytes 61448 | tf_op jit(solution)/shard_map/ppermute | solution.py:275
  25.5 3.6 %collective-permute-done.6.refs_1_ = f32[40,128]{1,0:T(8,128)S(1)} collective-permute-done((f32[40,128]{1,0:T(8,128)S(1)}, f32[40,128]{1,0:T(8,128)S(1)}, u32[]{:S(2)}, u32[]{:S(2)}) %collective-permute-start.6) | collective-permute-done | bytes 20512 | tf_op jit(solution)/shard_map/ppermute | solution.py:275
  29.1 2.6 %inverse.1.inv_ref = f32[64,128]{1,0:T(8,128)S(1)} custom-call(f32[40,128]{1,0:T(8,128)S(1)} %add.14.refs_0_, f32[40,128]{1,0:T(8,128)S(1)} %collective-permute-done.6.refs_1_), custom_call_target="tpu_custom_call" | custom-call | tf_op jit(solution)/shard_map/inverse/pallas_call | solution.py:199
  31.8 0.0 collective-permute-done.7.recv_ref
  31.8 0.0 collective-permute-done.10.refs_1_
  31.8 0.8 %collective-permute-done.11.refs_3_ = bf16[32,4096]{1,0:T(8,128)(2,1)S(1)} collective-permute-done((bf16[32,4096]{1,0:T(8,128)(2,1)S(1)}, bf16[32,4096]{1,0:T(8,128)(2,1)S(1)}, u32[]{:S(2)}, u32[]{:S(2)}) %collective-permute-start.11) | collective-permute-done | bytes 262176 | tf_op jit(solution)/shard_map/ppermute | solution.py:275
  32.6 1.6 %scores.1 = f32[16,128]{1,0:T(8,128)S(1)} custom-call(f32[64,128]{1,0:T(8,128)S(1)} %inverse.1.inv_ref, f32[64,512]{1,0:T(8,128)S(1)} %get-tuple-element.27.keep_ref, f32[64,512]{1,0:T(8,128)S(1)} %collective-permute-done.7.recv_ref, bf16[32,4096]{1,0:T(8,128)(2,1)S(1)} %pad_maximum_fusion.1.refs_0_, bf16[32,4096]{1,0:T(8,128)(2,1)S(1)} %collective-permute-done.10.refs_1_, ...), custom_call_target="tpu_custom_call" | custom-call | tf_op jit(solution)/shard_map/scores/pallas_call | solution.py:260
  34.2 0.0 collective-permute-start.12
  34.2 1.2 %collective-permute-done.12 = f32[8,128]{1,0:T(8,128)S(1)} collective-permute-done((f32[8,128]{1,0:T(8,128)S(1)}, f32[8,128]{1,0:T(8,128)S(1)}, u32[]{:S(2)}, u32[]{:S(2)}) %collective-permute-start.12) | collective-permute-done | bytes 4128 | tf_op jit(solution)/shard_map/ppermute | solution.py:275
  35.4 0.6 %slice_add_fusion = f32[8,128]{1,0:T(8,128)} fusion(f32[8,128]{1,0:T(8,128)S(1)} %collective-permute-done.12, f32[16,128]{1,0:T(8,128)S(1)} %scores.1), kind=kLoop, calls=%fused_computation.15 | loop fusion | flops 1024 | bytes 12288 | tf_op jit(solution)/shard_map/add | solution.py:329
  (12 shorter events, 0.1 us)
Async XLA Ops:
  0.0 9.5 %copy-start = (bf16[2,64,1024]{2,1,0:T(8,128)(2,1)S(1)}, bf16[2,64,1024]{2,1,0:T(8,128)(2,1)}, u32[]{:S(2)}) copy-start(bf16[2,64,1024]{2,1,0:T(8,128)(2,1)} %param.8) | copy-start | bytes 786436
  0.0 0.9 %copy-start.3 = (bf16[8,8192]{1,0:T(8,128)(2,1)S(1)}, bf16[8,8192]{1,0:T(8,128)(2,1)}, u32[]{:S(2)}) copy-start(bf16[8,8192]{1,0:T(8,128)(2,1)} %param.9) | copy-start | bytes 393220
  0.0 6.6 %copy-start.1 = (bf16[1024,4096]{1,0:T(8,128)(2,1)S(1)}, bf16[1024,4096]{1,0:T(8,128)(2,1)}, u32[]{:S(2)}) copy-start(bf16[1024,4096]{1,0:T(8,128)(2,1)} %x_ref.1) | copy-start | bytes 25165828
  0.0 6.6 %copy-start.2 = (bf16[2,64,4096]{2,1,0:T(8,128)(2,1)S(1)}, bf16[2,64,4096]{2,1,0:T(8,128)(2,1)}, u32[]{:S(2)}) copy-start(bf16[2,64,4096]{2,1,0:T(8,128)(2,1)} %param.7) | copy-start | bytes 3145732
  1.0 11.8 %collective-permute-start.1 = (bf16[8,8192]{1,0:T(8,128)(2,1)S(1)}, bf16[8,8192]{1,0:T(8,128)(2,1)S(1)}, u32[]{:S(2)}, u32[]{:S(2)}) collective-permute-start(bf16[8,8192]{1,0:T(8,128)(2,1)S(1)} %copy-done.3), channel_id=1, source_target_pairs={{0,12},{1,13},{2,14},{3,15},{4,8},{5,9},{6,10},{7,11},{8,4},{9,5},... | collective-permute-start | bytes 393224 | tf_op jit(solution)/shard_map/ppermute | solution.py:275
  6.0 8.6 %collective-permute-start.3 = (bf16[8,8192]{1,0:T(8,128)(2,1)S(1)}, bf16[8,8192]{1,0:T(8,128)(2,1)S(1)}, u32[]{:S(2)}, u32[]{:S(2)}) collective-permute-start(bf16[8,8192]{1,0:T(8,128)(2,1)S(1)} %copy-done.3), channel_id=1, source_target_pairs={{0,4},{1,5},{2,6},{3,7},{4,0},{5,1},{6,2},{7,3},{8,12},{9,13},{10,... | collective-permute-start | bytes 393224 | tf_op jit(solution)/shard_map/ppermute | solution.py:275
  6.0 11.1 %collective-permute-start.8 = (bf16[8,8192]{1,0:T(8,128)(2,1)S(1)}, bf16[8,8192]{1,0:T(8,128)(2,1)S(1)}, u32[]{:S(2)}, u32[]{:S(2)}) collective-permute-start(bf16[8,8192]{1,0:T(8,128)(2,1)S(1)} %copy-done.3), channel_id=1, source_target_pairs={{0,8},{1,9},{2,10},{3,11},{4,12},{5,13},{6,14},{7,15},{8,0},{9,1},... | collective-permute-start | bytes 393224 | tf_op jit(solution)/shard_map/ppermute | solution.py:275
  6.6 2.9 %copy-start.4 = (bf16[1024,2,1024]{2,1,0:T(2,128)(2,1)S(1)}, bf16[1024,2,1024]{2,1,0:T(2,128)(2,1)}, u32[]{:S(2)}) copy-start(bf16[1024,2,1024]{2,1,0:T(2,128)(2,1)} %param.6) | copy-start | bytes 12582916
  11.5 1.3 %collective-permute-start = (f32[40,128]{1,0:T(8,128)S(1)}, f32[40,128]{1,0:T(8,128)S(1)}, u32[]{:S(2)}, u32[]{:S(2)}) collective-permute-start(f32[40,128]{1,0:T(8,128)S(1)} %get-tuple-element.22), channel_id=1, source_target_pairs={{0,1},{1,0},{2,3},{3,2},{4,5},{5,4},{6,7},{7,6},{8,9},{9,8},{10,11... | collective-permute-start | bytes 61448 | tf_op jit(solution)/shard_map/ppermute | solution.py:275
  12.7 4.5 %collective-permute-start.2 = (f32[40,128]{1,0:T(8,128)S(1)}, f32[40,128]{1,0:T(8,128)S(1)}, u32[]{:S(2)}, u32[]{:S(2)}) collective-permute-start(f32[40,128]{1,0:T(8,128)S(1)} %add.12), channel_id=1, source_target_pairs={{0,2},{1,3},{2,0},{3,1},{4,6},{5,7},{6,4},{7,5},{8,10},{9,11},{10,... | collective-permute-start | bytes 61448 | tf_op jit(solution)/shard_map/ppermute | solution.py:275
  14.6 2.6 %collective-permute-start.4 = (bf16[16,4096]{1,0:T(8,128)(2,1)S(1)}, bf16[16,4096]{1,0:T(8,128)(2,1)S(1)}, u32[]{:S(2)}, u32[]{:S(2)}) collective-permute-start(bf16[16,4096]{1,0:T(8,128)(2,1)S(1)} %pad_maximum_fusion.2), channel_id=1, source_target_pairs={{0,1},{1,0},{2,3},{3,2},{4,5},{5,4},{6,7},{7,6},{8,9},{9,8},{10,11... | collective-permute-start | bytes 393224 | tf_op jit(solution)/shard_map/ppermute | solution.py:275
  17.1 1.4 %collective-permute-start.9 = (bf16[16,4096]{1,0:T(8,128)(2,1)S(1)}, bf16[16,4096]{1,0:T(8,128)(2,1)S(1)}, u32[]{:S(2)}, u32[]{:S(2)}) collective-permute-start(bf16[16,4096]{1,0:T(8,128)(2,1)S(1)} %pad_maximum_fusion.3), channel_id=1, source_target_pairs={{0,1},{1,0},{2,3},{3,2},{4,5},{5,4},{6,7},{7,6},{8,9},{9,8},{10,11... | collective-permute-start | bytes 393224 | tf_op jit(solution)/shard_map/ppermute | solution.py:275
  18.5 13.2 %collective-permute-start.10 = (bf16[32,4096]{1,0:T(8,128)(2,1)S(1)}, bf16[32,4096]{1,0:T(8,128)(2,1)S(1)}, u32[]{:S(2)}, u32[]{:S(2)}) collective-permute-start(bf16[32,4096]{1,0:T(8,128)(2,1)S(1)} %pad_maximum_fusion.1.refs_0_), channel_id=1, source_target_pairs={{0,2},{1,3},{2,0},{3,1},{4,6},{5,7},{6,4},{7,5},{8,10},{9,11},{10,... | collective-permute-start | bytes 786440 | tf_op jit(solution)/shard_map/ppermute | solution.py:275
  20.1 12.4 %collective-permute-start.11 = (bf16[32,4096]{1,0:T(8,128)(2,1)S(1)}, bf16[32,4096]{1,0:T(8,128)(2,1)S(1)}, u32[]{:S(2)}, u32[]{:S(2)}) collective-permute-start(bf16[32,4096]{1,0:T(8,128)(2,1)S(1)} %pad_maximum_fusion.refs_2_), channel_id=1, source_target_pairs={{0,2},{1,3},{2,0},{3,1},{4,6},{5,7},{6,4},{7,5},{8,10},{9,11},{10,... | collective-permute-start | bytes 786440 | tf_op jit(solution)/shard_map/ppermute | solution.py:275
  20.6 11.1 %collective-permute-start.7 = (f32[64,512]{1,0:T(8,128)S(1)}, f32[64,512]{1,0:T(8,128)S(1)}, u32[]{:S(2)}, u32[]{:S(2)}) collective-permute-start(f32[64,512]{1,0:T(8,128)S(1)} %get-tuple-element.28), channel_id=1, source_target_pairs={{0,1},{1,0},{2,3},{3,2},{4,5},{5,4},{6,7},{7,6},{8,9},{9,8},{10,11... | collective-permute-start | bytes 393224 | tf_op jit(solution)/shard_map/ppermute | solution.py:275
  20.6 3.8 %collective-permute-start.5 = (f32[40,128]{1,0:T(8,128)S(1)}, f32[40,128]{1,0:T(8,128)S(1)}, u32[]{:S(2)}, u32[]{:S(2)}) collective-permute-start(f32[40,128]{1,0:T(8,128)S(1)} %add.13), channel_id=1, source_target_pairs={{0,4},{1,5},{2,6},{3,7},{4,0},{5,1},{6,2},{7,3},{8,12},{9,13},{10,... | collective-permute-start | bytes 61448 | tf_op jit(solution)/shard_map/ppermute | solution.py:275
  24.4 4.7 %collective-permute-start.6 = (f32[40,128]{1,0:T(8,128)S(1)}, f32[40,128]{1,0:T(8,128)S(1)}, u32[]{:S(2)}, u32[]{:S(2)}) collective-permute-start(f32[40,128]{1,0:T(8,128)S(1)} %add.14.refs_0_), channel_id=1, source_target_pairs={{0,8},{1,9},{2,10},{3,11},{4,12},{5,13},{6,14},{7,15},{8,0},{9,1},... | collective-permute-start | bytes 61448 | tf_op jit(solution)/shard_map/ppermute | solution.py:275
  34.2 1.2 %collective-permute-start.12 = (f32[8,128]{1,0:T(8,128)S(1)}, f32[8,128]{1,0:T(8,128)S(1)}, u32[]{:S(2)}, u32[]{:S(2)}) collective-permute-start(f32[8,128]{1,0:T(8,128)S(1)} %slice.9), channel_id=1, source_target_pairs={{0,1},{1,0},{2,3},{3,2},{4,5},{5,4},{6,7},{7,6},{8,9},{9,8},{10,11... | collective-permute-start | bytes 12296 | tf_op jit(solution)/shard_map/ppermute | solution.py:275

commit v12 on v11

--- a/solution.py
+++ b/solution.py
@@ -206,9 +206,7 @@
     )(*covs)
 
 
-def scores_kernel(order, inv_ref, keep_ref, recv_ref, *refs):
-    query_refs, (out_ref, flat_ref, part_ref) = refs[:-3], refs[-3:]
-    place = lax.axis_index("dp")
+def precondition_kernel(inv_ref, keep_ref, recv_ref, out_ref, flat_ref):
     low = lax.broadcasted_iota(jnp.int32, (R, PAIR), 1) < R
     inv = inv_ref[...]
     tiles = R // 2
@@ -243,32 +241,47 @@
         rows = done[j * tiles : (j + 1) * tiles]
         flat_ref[(2 * j) * tiles : (2 * j + 1) * tiles, :] = rows[:, :PAIR]
         flat_ref[(2 * j + 1) * tiles : (2 * j + 2) * tiles, :] = rows[:, PAIR:]
-    flat = jnp.concatenate(
-        [flat_ref[pl.ds(k, 2 * pairs, stride=tiles), :].astype(BF16) for k in range(tiles)], axis=1
-    )
-    part = dot(jnp.concatenate([ref[...] for ref in query_refs], axis=0), flat, NT)
+    for k in range(tiles):
+        out_ref[:, k * PAIR : (k + 1) * PAIR] = flat_ref[pl.ds(k, 2 * pairs, stride=tiles), :].astype(BF16)
+
+
+def precondition(inv, moments):
+    seqs = sum(part.shape[1] for part in moments) // R
+    vmem = pl.BlockSpec(memory_space=pltpu.VMEM)
+    return pl.pallas_call(
+        precondition_kernel,
+        in_specs=[vmem] * (1 + len(moments)),
+        out_specs=vmem,
+        out_shape=jax.ShapeDtypeStruct((seqs, R * R), BF16),
+        scratch_shapes=[pltpu.VMEM((seqs * R // 2, PAIR), F32)],
+        compiler_params=pltpu.CompilerParams(vmem_limit_bytes=16 * MIB),
+        name="precondition",
+    )(inv, *moments)
+
+
+def scores_kernel(order, flat_ref, *refs):
+    query_refs, (out_ref, part_ref) = refs[:-2], refs[-2:]
+    place = lax.axis_index("dp")
+    part = dot(jnp.concatenate([ref[...] for ref in query_refs], axis=0), flat_ref[...], NT)
     group = part_ref.shape[1]
     for at, distance in enumerate(order):
         part_ref[place ^ distance] = part[at * group : (at + 1) * group]
     out_ref[...] = part_ref[...].reshape(part.shape).T
 
 
-def score(inv, moments, queries, order):
-    seqs = sum(part.shape[1] for part in moments) // R
+def score(flat, queries, order):
+    seqs = flat.shape[0]
     count = sum(part.shape[0] for part in queries)
     vmem = pl.BlockSpec(memory_space=pltpu.VMEM)
     return pl.pallas_call(
         functools.partial(scores_kernel, order),
-        in_specs=[vmem] * (1 + len(moments) + len(queries)),
+        in_specs=[vmem] * (1 + len(queries)),
         out_specs=vmem,
         out_shape=jax.ShapeDtypeStruct((seqs, count), F32),
-        scratch_shapes=[
-            pltpu.VMEM((seqs * R // 2, PAIR), F32),
-            pltpu.VMEM((len(order), count // len(order), seqs), F32),
-        ],
+        scratch_shapes=[pltpu.VMEM((len(order), count // len(order), seqs), F32)],
         compiler_params=pltpu.CompilerParams(vmem_limit_bytes=16 * MIB),
         name="scores",
-    )(inv, *moments, *queries)
+    )(flat, *queries)
 
 
 def exchange(value, distance):
@@ -285,8 +298,8 @@
     devices = lax.axis_size("dp")
     slabs = devices // GROUP
     device, queries = lax.optimization_barrier((own_place(), queries))
-    near_slabs, far_slabs = [0, 2], [1, 3] + list(range(4, slabs))
-    column = {slab: exchange(queries, slab * GROUP) for slab in [2, 3, 1] + list(range(4, slabs))}
+    near_slabs, far_slabs = [0, 1], [2, 3] + list(range(4, slabs))
+    column = {slab: exchange(queries, slab * GROUP) for slab in [1, 2, 3] + list(range(4, slabs))}
     column[0] = queries
     acts = project(layer_input, in_proj.reshape(PAIR, in_proj.shape[2]))
     acts, out_grads, column[0] = lax.optimization_barrier((acts, out_grads, column[0]))
@@ -305,17 +318,12 @@
     cov, column[3] = lax.optimization_barrier((cov, column[3]))
     cov = cov + exchange(cov, 2)
     far = fold(far_slabs)
-    cov, far = lax.optimization_barrier((cov, far))
-    cov = cov + exchange(cov, GROUP)
+    cov, far, moments = lax.optimization_barrier((cov, far, moments))
     near = fold(near_slabs)
     across = exchange(near, 2)
-    distance = 2 * GROUP
-    while distance < devices:
-        last = exchange(cov, distance)
-        if 2 * distance < devices:
-            cov = cov + last
-        distance *= 2
-    inv = inverse([cov, last], local_tokens * devices)
+    covs = [cov] + [exchange(cov, slab * GROUP) for slab in range(1, slabs)]
+    covs, across = lax.optimization_barrier((covs, across))
+    inv = inverse(covs, local_tokens * devices)
     gathered = [near, across, far, exchange(far, 2)]
     order = [
         slab * GROUP + 2 * over + core
@@ -324,7 +332,7 @@
         for core in range(2)
         for slab in part
     ]
-    partial = score(inv, moments, gathered, order)
+    partial = score(precondition(inv, moments), gathered, order)
     seqs = local_tokens // LEN
     return partial[:seqs] + exchange(partial[seqs:], 1)
 

time: 36.1 us -> 34.8 us (0.964)
  waiting for transfers between devices: 13.5 us -> 7.81 us
  starting transfers between devices: 10.8 us -> 15.4 us
    ppermute x13 -> x14, waiting for transfers between devices: 13.5 us -> 7.81 us  [exchange(): lax.ppermute(value, 'dp', [(i, i ^ distance) for i in range(lax.axis_size...]
    ppermute x13 -> x14, starting transfers between devices: 10.8 us -> 15.4 us  [exchange(): lax.ppermute(value, 'dp', [(i, i ^ distance) for i in range(lax.axis_size...]
    pallas_call x1, Pallas kernels: 1.56 us -> 0.47 us  [score(): pl.pallas_call(functools.partial(scores_kernel, order), in_specs=[vmem] *...]
    pallas_call x0 -> x1, Pallas kernels: none -> 0.83 us  [precondition(): pl.pallas_call(precondition_kernel, in_specs=[vmem] * (1 + len(moments)),...]
  transfers between devices with their start and end apart: 13 -> 14, of which waited for: 7 -> 4; matrix products, arithmetic and copies ran while one was open for 4% -> 5% of each run, Pallas kernels for 17% -> 20%
where the time goes in v12:
time: 34.8 us; the launch traced here: 34.6 us
  starting transfers between devices  15.4 us (44%)
  Pallas kernels  7.89 us (23%)
  waiting for transfers between devices  7.81 us (22%)
  matrix products  1.44 us (4%)
  between operations  0.87 us (2%)
  other arithmetic  0.72 us (2%)
  local copies, waits for them, and re-layouts  0.43 us (1%)
    ppermute x14, starting transfers between devices, exchange(): lax.ppermute(value, 'dp', [(i, i ^ distance) for i in range(lax.axis_size...  15.4 us
    ppermute x14, waiting for transfers between devices, exchange(): lax.ppermute(value, 'dp', [(i, i ^ distance) for i in range(lax.axis_size...  7.81 us
    pallas_call x1, Pallas kernels, project(): pl.pallas_call(project_kernel, in_specs=[vmem, vmem], out_specs=vmem, out...  2.89 us
    pallas_call x1, Pallas kernels, inverse(): pl.pallas_call(functools.partial(inverse_kernel, total_tokens), in_specs=...  2.65 us
    dot_general x1, matrix products, per_device(): jnp.einsum('tmk,mrk->tmr', out_grads, out_proj, preferred_element_type=F32)  1.44 us
    pallas_call x1, Pallas kernels, precondition(): pl.pallas_call(precondition_kernel, in_specs=[vmem] * (1 + len(moments)),...  0.83 us
  transfers between devices with their start and end apart: 14, of which 4 were waited for; matrix products, arithmetic and copies ran while one was open for 5% of the time, Pallas kernels for 20%

profile of v12, /device:TPU:0, one launch (start us, length us, event | category | flops | bytes accessed | tf_op | source)
XLA Modules:
  0.0 34.6 jit_solution(7638049187353214202)
XLA Ops:
  0.0 0.0 copy-start
  0.0 0.0 copy-start.3
  0.0 0.0 copy-start.2
  0.0 0.0 copy-start.1
  0.0 0.5 %own_place.1 = s32[1]{0:T(128)} custom-call(), custom_call_target="tpu_custom_call" | custom-call | flops 80000000000 | bytes 8 | tf_op jit(solution)/shard_map/own_place/pallas_call | solution.py:37
  0.5 0.4 %copy-done.3 = bf16[8,8192]{1,0:T(8,128)(2,1)S(1)} copy-done((bf16[8,8192]{1,0:T(8,128)(2,1)S(1)}, bf16[8,8192]{1,0:T(8,128)(2,1)}, u32[]{:S(2)}) %copy-start.3) | copy-done | bytes 131096
  1.0 5.0 %collective-permute-start.1 = (bf16[8,8192]{1,0:T(8,128)(2,1)S(1)}, bf16[8,8192]{1,0:T(8,128)(2,1)S(1)}, u32[]{:S(2)}, u32[]{:S(2)}) collective-permute-start(bf16[8,8192]{1,0:T(8,128)(2,1)S(1)} %copy-done.3), channel_id=1, source_target_pairs={{0,12},{1,13},{2,14},{3,15},{4,8},{5,9},{6,10},{7,11},{8,4},{9,5},... | collective-permute-start | bytes 393224 | tf_op jit(solution)/shard_map/ppermute | solution.py:288
  6.0 0.0 collective-permute-start.3
  6.0 0.6 %collective-permute-start.9 = (bf16[8,8192]{1,0:T(8,128)(2,1)S(1)}, bf16[8,8192]{1,0:T(8,128)(2,1)S(1)}, u32[]{:S(2)}, u32[]{:S(2)}) collective-permute-start(bf16[8,8192]{1,0:T(8,128)(2,1)S(1)} %copy-done.3), channel_id=1, source_target_pairs={{0,4},{1,5},{2,6},{3,7},{4,0},{5,1},{6,2},{7,3},{8,12},{9,13},{10,... | collective-permute-start | bytes 393224 | tf_op jit(solution)/shard_map/ppermute | solution.py:288
  6.6 0.0 copy-done.2
  6.6 0.0 copy-done.1
  6.6 0.0 copy-start.4
  6.6 2.9 %project.1.acts_ref = bf16[128,1024]{1,0:T(8,128)(2,1)S(1)} custom-call(bf16[1024,4096]{1,0:T(8,128)(2,1)S(1)} %copy-done.1, bf16[128,4096]{1,0:T(8,128)(2,1)S(1)} %bitcast.8), custom_call_target="tpu_custom_call" | custom-call | flops 2147483648 | bytes 8388608 | tf_op jit(solution)/shard_map/project/pallas_call | solution.py:56
  9.5 0.0 copy-done
  9.5 0.0 copy-done.4
  9.5 1.4 %fusion.2 = bf16[2,1024,64]{1,2,0:T(8,128)(2,1)S(1)} fusion(bf16[2,64,1024]{2,1,0:T(8,128)(2,1)S(1)} %copy-done, bf16[1024,2,1024]{2,1,0:T(2,128)(2,1)S(1)} %copy-done.4), kind=kOutput, calls=%fused_computation.2 | convolution fusion | flops 268566528 | bytes 4718592 | tf_op jit(solution)/shard_map/tmk,mrk->tmr/dot_general | solution.py:313
  10.9 0.5 %statistics.1 = (f32[40,128]{1,0:T(8,128)S(1)}, f32[40,128]{1,0:T(8,128)S(1)}, f32[64,512]{1,0:T(8,128)S(1)}, f32[64,512]{1,0:T(8,128)S(1)}) custom-call(bf16[128,1024]{1,0:T(8,128)(2,1)S(1)} %project.1.acts_ref, bf16[128,1024]{1,0:T(8,128)(2,1)S(1)} %bitcast.9), custom_call_target="tpu_custom_call" | custom-call | tf_op jit(solution)/shard_map/statistics/pallas_call | solution.py:125
  11.5 0.1 collective-permute-start
  11.6 0.5 %collective-permute-start.5 = (f32[64,512]{1,0:T(8,128)S(1)}, f32[64,512]{1,0:T(8,128)S(1)}, u32[]{:S(2)}, u32[]{:S(2)}) collective-permute-start(f32[64,512]{1,0:T(8,128)S(1)} %get-tuple-element.34), channel_id=1, source_target_pairs={{0,1},{1,0},{2,3},{3,2},{4,5},{5,4},{6,7},{7,6},{8,9},{9,8},{10,11... | collective-permute-start | bytes 393224 | tf_op jit(solution)/shard_map/ppermute | solution.py:288
  12.7 0.0 collective-permute-done
  12.8 0.0 collective-permute-done.1
  12.8 1.8 %collective-permute-start.2 = (f32[40,128]{1,0:T(8,128)S(1)}, f32[40,128]{1,0:T(8,128)S(1)}, u32[]{:S(2)}, u32[]{:S(2)}) collective-permute-start(f32[40,128]{1,0:T(8,128)S(1)} %add.9), channel_id=1, source_target_pairs={{0,2},{1,3},{2,0},{3,1},{4,6},{5,7},{6,4},{7,5},{8,10},{9,11},{10,... | collective-permute-start | bytes 61448 | tf_op jit(solution)/shard_map/ppermute | solution.py:288
  14.6 0.0 collective-permute-done.9
  14.6 0.1 collective-permute-start.10
  14.7 2.4 %collective-permute-done.3 = bf16[8,8192]{1,0:T(8,128)(2,1)S(1)} collective-permute-done((bf16[8,8192]{1,0:T(8,128)(2,1)S(1)}, bf16[8,8192]{1,0:T(8,128)(2,1)S(1)}, u32[]{:S(2)}, u32[]{:S(2)}) %collective-permute-start.3) | collective-permute-done | bytes 131104 | tf_op jit(solution)/shard_map/ppermute | solution.py:288
  17.1 0.1 collective-permute-start.4
  17.2 0.0 collective-permute-done.2
  17.2 0.0 collective-permute-done.10
  17.3 1.6 %collective-permute-start.11 = (bf16[32,4096]{1,0:T(8,128)(2,1)S(1)}, bf16[32,4096]{1,0:T(8,128)(2,1)S(1)}, u32[]{:S(2)}, u32[]{:S(2)}) collective-permute-start(bf16[32,4096]{1,0:T(8,128)(2,1)S(1)} %pad_maximum_fusion.1.refs_0_), channel_id=1, source_target_pairs={{0,2},{1,3},{2,0},{3,1},{4,6},{5,7},{6,4},{7,5},{8,10},{9,11},{10,... | collective-permute-start | bytes 786440 | tf_op jit(solution)/shard_map/ppermute | solution.py:288
  18.8 0.0 collective-permute-done.4
  18.9 0.0 collective-permute-done.5.recv_ref
  18.9 1.3 %collective-permute-start.12 = (bf16[32,4096]{1,0:T(8,128)(2,1)S(1)}, bf16[32,4096]{1,0:T(8,128)(2,1)S(1)}, u32[]{:S(2)}, u32[]{:S(2)}) collective-permute-start(bf16[32,4096]{1,0:T(8,128)(2,1)S(1)} %pad_maximum_fusion.refs_2_), channel_id=1, source_target_pairs={{0,2},{1,3},{2,0},{3,1},{4,6},{5,7},{6,4},{7,5},{8,10},{9,11},{10,... | collective-permute-start | bytes 786440 | tf_op jit(solution)/shard_map/ppermute | solution.py:288
  20.1 1.7 %collective-permute-start.6 = (f32[40,128]{1,0:T(8,128)S(1)}, f32[40,128]{1,0:T(8,128)S(1)}, u32[]{:S(2)}, u32[]{:S(2)}) collective-permute-start(f32[40,128]{1,0:T(8,128)S(1)} %add.10.refs_0_), channel_id=1, source_target_pairs={{0,4},{1,5},{2,6},{3,7},{4,0},{5,1},{6,2},{7,3},{8,12},{9,13},{10,... | collective-permute-start | bytes 61448 | tf_op jit(solution)/shard_map/ppermute | solution.py:288
  21.9 1.4 %collective-permute-start.7 = (f32[40,128]{1,0:T(8,128)S(1)}, f32[40,128]{1,0:T(8,128)S(1)}, u32[]{:S(2)}, u32[]{:S(2)}) collective-permute-start(f32[40,128]{1,0:T(8,128)S(1)} %add.10.refs_0_), channel_id=1, source_target_pairs={{0,8},{1,9},{2,10},{3,11},{4,12},{5,13},{6,14},{7,15},{8,0},{9,1},... | collective-permute-start | bytes 61448 | tf_op jit(solution)/shard_map/ppermute | solution.py:288
  23.2 1.3 %collective-permute-start.8 = (f32[40,128]{1,0:T(8,128)S(1)}, f32[40,128]{1,0:T(8,128)S(1)}, u32[]{:S(2)}, u32[]{:S(2)}) collective-permute-start(f32[40,128]{1,0:T(8,128)S(1)} %add.10.refs_0_), channel_id=1, source_target_pairs={{0,12},{1,13},{2,14},{3,15},{4,8},{5,9},{6,10},{7,11},{8,4},{9,5},... | collective-permute-start | bytes 61448 | tf_op jit(solution)/shard_map/ppermute | solution.py:288
  24.6 0.0 collective-permute-done.6.refs_1_
  24.6 2.2 %collective-permute-done.7.refs_2_ = f32[40,128]{1,0:T(8,128)S(1)} collective-permute-done((f32[40,128]{1,0:T(8,128)S(1)}, f32[40,128]{1,0:T(8,128)S(1)}, u32[]{:S(2)}, u32[]{:S(2)}) %collective-permute-start.7) | collective-permute-done | bytes 20512 | tf_op jit(solution)/shard_map/ppermute | solution.py:288
  26.7 2.1 %collective-permute-done.8.refs_3_ = f32[40,128]{1,0:T(8,128)S(1)} collective-permute-done((f32[40,128]{1,0:T(8,128)S(1)}, f32[40,128]{1,0:T(8,128)S(1)}, u32[]{:S(2)}, u32[]{:S(2)}) %collective-permute-start.8) | collective-permute-done | bytes 20512 | tf_op jit(solution)/shard_map/ppermute | solution.py:288
  28.8 0.0 collective-permute-done.11.refs_1_
  28.8 2.7 %inverse.1.inv_ref = f32[64,128]{1,0:T(8,128)S(1)} custom-call(f32[40,128]{1,0:T(8,128)S(1)} %add.10.refs_0_, f32[40,128]{1,0:T(8,128)S(1)} %collective-permute-done.6.refs_1_, f32[40,128]{1,0:T(8,128)S(1)} %collective-permute-done.7.refs_2_, f32[40,128]{1,0:T(8,128)S(1)} %collective-permute-done.8.refs_3_), custom_call_target="tpu_custom_call" | custom-call | tf_op jit(solution)/shard_map/inverse/pallas_call | solution.py:199
  31.5 0.8 %precondition.1.flat_ref = bf16[16,4096]{1,0:T(8,128)(2,1)S(1)} custom-call(f32[64,128]{1,0:T(8,128)S(1)} %inverse.1.inv_ref, f32[64,512]{1,0:T(8,128)S(1)} %get-tuple-element.41.keep_ref, f32[64,512]{1,0:T(8,128)S(1)} %collective-permute-done.5.recv_ref), custom_call_target="tpu_custom_call" | custom-call | tf_op jit(solution)/shard_map/precondition/pallas_call | solution.py:251
  32.3 0.0 collective-permute-done.12.refs_3_
  32.3 0.5 %scores.1 = f32[16,128]{1,0:T(8,128)S(1)} custom-call(bf16[16,4096]{1,0:T(8,128)(2,1)S(1)} %precondition.1.flat_ref, bf16[32,4096]{1,0:T(8,128)(2,1)S(1)} %pad_maximum_fusion.1.refs_0_, bf16[32,4096]{1,0:T(8,128)(2,1)S(1)} %collective-permute-done.11.refs_1_, bf16[32,4096]{1,0:T(8,128)(2,1)S(1)} %pad_maximum_fusion.refs_2_, ...), custom_call_target="tpu_custom_call" | custom-call | tf_op jit(solution)/shard_map/scores/pallas_call | solution.py:276
  32.8 0.0 collective-permute-start.13
  32.9 1.2 %collective-permute-done.13 = f32[8,128]{1,0:T(8,128)S(1)} collective-permute-done((f32[8,128]{1,0:T(8,128)S(1)}, f32[8,128]{1,0:T(8,128)S(1)}, u32[]{:S(2)}, u32[]{:S(2)}) %collective-permute-start.13) | collective-permute-done | bytes 4128 | tf_op jit(solution)/shard_map/ppermute | solution.py:288
  34.0 0.6 %slice_add_fusion = f32[8,128]{1,0:T(8,128)} fusion(f32[8,128]{1,0:T(8,128)S(1)} %collective-permute-done.13, f32[16,128]{1,0:T(8,128)S(1)} %scores.1), kind=kLoop, calls=%fused_computation.15 | loop fusion | flops 1024 | bytes 12288 | tf_op jit(solution)/shard_map/add | solution.py:337
  (11 shorter events, 0.1 us)
Async XLA Ops:
  0.0 9.5 %copy-start = (bf16[2,64,1024]{2,1,0:T(8,128)(2,1)S(1)}, bf16[2,64,1024]{2,1,0:T(8,128)(2,1)}, u32[]{:S(2)}) copy-start(bf16[2,64,1024]{2,1,0:T(8,128)(2,1)} %param.8) | copy-start | bytes 786436
  0.0 0.9 %copy-start.3 = (bf16[8,8192]{1,0:T(8,128)(2,1)S(1)}, bf16[8,8192]{1,0:T(8,128)(2,1)}, u32[]{:S(2)}) copy-start(bf16[8,8192]{1,0:T(8,128)(2,1)} %param.9) | copy-start | bytes 393220
  0.0 6.6 %copy-start.2 = (bf16[2,64,4096]{2,1,0:T(8,128)(2,1)S(1)}, bf16[2,64,4096]{2,1,0:T(8,128)(2,1)}, u32[]{:S(2)}) copy-start(bf16[2,64,4096]{2,1,0:T(8,128)(2,1)} %param.7) | copy-start | bytes 3145732
  0.0 6.6 %copy-start.1 = (bf16[1024,4096]{1,0:T(8,128)(2,1)S(1)}, bf16[1024,4096]{1,0:T(8,128)(2,1)}, u32[]{:S(2)}) copy-start(bf16[1024,4096]{1,0:T(8,128)(2,1)} %x_ref.1) | copy-start | bytes 25165828
  1.0 11.8 %collective-permute-start.1 = (bf16[8,8192]{1,0:T(8,128)(2,1)S(1)}, bf16[8,8192]{1,0:T(8,128)(2,1)S(1)}, u32[]{:S(2)}, u32[]{:S(2)}) collective-permute-start(bf16[8,8192]{1,0:T(8,128)(2,1)S(1)} %copy-done.3), channel_id=1, source_target_pairs={{0,12},{1,13},{2,14},{3,15},{4,8},{5,9},{6,10},{7,11},{8,4},{9,5},... | collective-permute-start | bytes 393224 | tf_op jit(solution)/shard_map/ppermute | solution.py:288
  6.0 11.1 %collective-permute-start.3 = (bf16[8,8192]{1,0:T(8,128)(2,1)S(1)}, bf16[8,8192]{1,0:T(8,128)(2,1)S(1)}, u32[]{:S(2)}, u32[]{:S(2)}) collective-permute-start(bf16[8,8192]{1,0:T(8,128)(2,1)S(1)} %copy-done.3), channel_id=1, source_target_pairs={{0,8},{1,9},{2,10},{3,11},{4,12},{5,13},{6,14},{7,15},{8,0},{9,1},... | collective-permute-start | bytes 393224 | tf_op jit(solution)/shard_map/ppermute | solution.py:288
  6.0 8.6 %collective-permute-start.9 = (bf16[8,8192]{1,0:T(8,128)(2,1)S(1)}, bf16[8,8192]{1,0:T(8,128)(2,1)S(1)}, u32[]{:S(2)}, u32[]{:S(2)}) collective-permute-start(bf16[8,8192]{1,0:T(8,128)(2,1)S(1)} %copy-done.3), channel_id=1, source_target_pairs={{0,4},{1,5},{2,6},{3,7},{4,0},{5,1},{6,2},{7,3},{8,12},{9,13},{10,... | collective-permute-start | bytes 393224 | tf_op jit(solution)/shard_map/ppermute | solution.py:288
  6.6 2.9 %copy-start.4 = (bf16[1024,2,1024]{2,1,0:T(2,128)(2,1)S(1)}, bf16[1024,2,1024]{2,1,0:T(2,128)(2,1)}, u32[]{:S(2)}) copy-start(bf16[1024,2,1024]{2,1,0:T(2,128)(2,1)} %param.6) | copy-start | bytes 12582916
  11.5 1.3 %collective-permute-start = (f32[40,128]{1,0:T(8,128)S(1)}, f32[40,128]{1,0:T(8,128)S(1)}, u32[]{:S(2)}, u32[]{:S(2)}) collective-permute-start(f32[40,128]{1,0:T(8,128)S(1)} %get-tuple-element.29), channel_id=1, source_target_pairs={{0,1},{1,0},{2,3},{3,2},{4,5},{5,4},{6,7},{7,6},{8,9},{9,8},{10,11... | collective-permute-start | bytes 61448 | tf_op jit(solution)/shard_map/ppermute | solution.py:288
  11.6 7.3 %collective-permute-start.5 = (f32[64,512]{1,0:T(8,128)S(1)}, f32[64,512]{1,0:T(8,128)S(1)}, u32[]{:S(2)}, u32[]{:S(2)}) collective-permute-start(f32[64,512]{1,0:T(8,128)S(1)} %get-tuple-element.34), channel_id=1, source_target_pairs={{0,1},{1,0},{2,3},{3,2},{4,5},{5,4},{6,7},{7,6},{8,9},{9,8},{10,11... | collective-permute-start | bytes 393224 | tf_op jit(solution)/shard_map/ppermute | solution.py:288
  12.8 4.4 %collective-permute-start.2 = (f32[40,128]{1,0:T(8,128)S(1)}, f32[40,128]{1,0:T(8,128)S(1)}, u32[]{:S(2)}, u32[]{:S(2)}) collective-permute-start(f32[40,128]{1,0:T(8,128)S(1)} %add.9), channel_id=1, source_target_pairs={{0,2},{1,3},{2,0},{3,1},{4,6},{5,7},{6,4},{7,5},{8,10},{9,11},{10,... | collective-permute-start | bytes 61448 | tf_op jit(solution)/shard_map/ppermute | solution.py:288
  14.6 2.6 %collective-permute-start.10 = (bf16[16,4096]{1,0:T(8,128)(2,1)S(1)}, bf16[16,4096]{1,0:T(8,128)(2,1)S(1)}, u32[]{:S(2)}, u32[]{:S(2)}) collective-permute-start(bf16[16,4096]{1,0:T(8,128)(2,1)S(1)} %pad_maximum_fusion.3), channel_id=1, source_target_pairs={{0,1},{1,0},{2,3},{3,2},{4,5},{5,4},{6,7},{7,6},{8,9},{9,8},{10,11... | collective-permute-start | bytes 393224 | tf_op jit(solution)/shard_map/ppermute | solution.py:288
  17.1 1.7 %collective-permute-start.4 = (bf16[16,4096]{1,0:T(8,128)(2,1)S(1)}, bf16[16,4096]{1,0:T(8,128)(2,1)S(1)}, u32[]{:S(2)}, u32[]{:S(2)}) collective-permute-start(bf16[16,4096]{1,0:T(8,128)(2,1)S(1)} %pad_maximum_fusion.2), channel_id=1, source_target_pairs={{0,1},{1,0},{2,3},{3,2},{4,5},{5,4},{6,7},{7,6},{8,9},{9,8},{10,11... | collective-permute-start | bytes 393224 | tf_op jit(solution)/shard_map/ppermute | solution.py:288
  17.3 11.6 %collective-permute-start.11 = (bf16[32,4096]{1,0:T(8,128)(2,1)S(1)}, bf16[32,4096]{1,0:T(8,128)(2,1)S(1)}, u32[]{:S(2)}, u32[]{:S(2)}) collective-permute-start(bf16[32,4096]{1,0:T(8,128)(2,1)S(1)} %pad_maximum_fusion.1.refs_0_), channel_id=1, source_target_pairs={{0,2},{1,3},{2,0},{3,1},{4,6},{5,7},{6,4},{7,5},{8,10},{9,11},{10,... | collective-permute-start | bytes 786440 | tf_op jit(solution)/shard_map/ppermute | solution.py:288
  18.9 13.4 %collective-permute-start.12 = (bf16[32,4096]{1,0:T(8,128)(2,1)S(1)}, bf16[32,4096]{1,0:T(8,128)(2,1)S(1)}, u32[]{:S(2)}, u32[]{:S(2)}) collective-permute-start(bf16[32,4096]{1,0:T(8,128)(2,1)S(1)} %pad_maximum_fusion.refs_2_), channel_id=1, source_target_pairs={{0,2},{1,3},{2,0},{3,1},{4,6},{5,7},{6,4},{7,5},{8,10},{9,11},{10,... | collective-permute-start | bytes 786440 | tf_op jit(solution)/shard_map/ppermute | solution.py:288
  20.1 4.4 %collective-permute-start.6 = (f32[40,128]{1,0:T(8,128)S(1)}, f32[40,128]{1,0:T(8,128)S(1)}, u32[]{:S(2)}, u32[]{:S(2)}) collective-permute-start(f32[40,128]{1,0:T(8,128)S(1)} %add.10.refs_0_), channel_id=1, source_target_pairs={{0,4},{1,5},{2,6},{3,7},{4,0},{5,1},{6,2},{7,3},{8,12},{9,13},{10,... | collective-permute-start | bytes 61448 | tf_op jit(solution)/shard_map/ppermute | solution.py:288
  21.9 4.9 %collective-permute-start.7 = (f32[40,128]{1,0:T(8,128)S(1)}, f32[40,128]{1,0:T(8,128)S(1)}, u32[]{:S(2)}, u32[]{:S(2)}) collective-permute-start(f32[40,128]{1,0:T(8,128)S(1)} %add.10.refs_0_), channel_id=1, source_target_pairs={{0,8},{1,9},{2,10},{3,11},{4,12},{5,13},{6,14},{7,15},{8,0},{9,1},... | collective-permute-start | bytes 61448 | tf_op jit(solution)/shard_map/ppermute | solution.py:288
  23.2 5.6 %collective-permute-start.8 = (f32[40,128]{1,0:T(8,128)S(1)}, f32[40,128]{1,0:T(8,128)S(1)}, u32[]{:S(2)}, u32[]{:S(2)}) collective-permute-start(f32[40,128]{1,0:T(8,128)S(1)} %add.10.refs_0_), channel_id=1, source_target_pairs={{0,12},{1,13},{2,14},{3,15},{4,8},{5,9},{6,10},{7,11},{8,4},{9,5},... | collective-permute-start | bytes 61448 | tf_op jit(solution)/shard_map/ppermute | solution.py:288
  32.8 1.2 %collective-permute-start.13 = (f32[8,128]{1,0:T(8,128)S(1)}, f32[8,128]{1,0:T(8,128)S(1)}, u32[]{:S(2)}, u32[]{:S(2)}) collective-permute-start(f32[8,128]{1,0:T(8,128)S(1)} %slice.9), channel_id=1, source_target_pairs={{0,1},{1,0},{2,3},{3,2},{4,5},{5,4},{6,7},{7,6},{8,9},{9,8},{10,11... | collective-permute-start | bytes 12296 | tf_op jit(solution)/shard_map/ppermute | solution.py:288

commit v13 on v12

--- a/solution.py
+++ b/solution.py
@@ -320,15 +320,15 @@
     far = fold(far_slabs)
     cov, far, moments = lax.optimization_barrier((cov, far, moments))
     near = fold(near_slabs)
-    across = exchange(near, 2)
-    covs = [cov] + [exchange(cov, slab * GROUP) for slab in range(1, slabs)]
-    covs, across = lax.optimization_barrier((covs, across))
+    mine = jnp.concatenate([near, far], axis=0)
+    across = exchange(mine, 2)
+    covs = [cov] + [exchange(cov, slab * GROUP) for slab in reversed(range(1, slabs))]
     inv = inverse(covs, local_tokens * devices)
-    gathered = [near, across, far, exchange(far, 2)]
+    gathered = [mine, across]
     order = [
         slab * GROUP + 2 * over + core
+        for over in range(2)
         for part in (near_slabs, far_slabs)
-        for over in range(2)
         for core in range(2)
         for slab in part
     ]

time: 34.8 us -> 35.5 us (1.020)
  waiting for transfers between devices: 7.81 us -> 9.38 us
  starting transfers between devices: 15.4 us -> 14.6 us
    ppermute x14 -> x13, waiting for transfers between devices: 7.81 us -> 9.38 us  [exchange(): lax.ppermute(value, 'dp', [(i, i ^ distance) for i in range(lax.axis_size...]
    ppermute x14 -> x13, starting transfers between devices: 15.4 us -> 14.6 us  [exchange(): lax.ppermute(value, 'dp', [(i, i ^ distance) for i in range(lax.axis_size...]
  transfers between devices with their start and end apart: 14 -> 13, of which waited for: 4 -> 7; matrix products, arithmetic and copies ran while one was open for 5% -> 4% of each run, Pallas kernels for 20% -> 20%
where the time goes in v13:
time: 35.5 us; the launch traced here: 35.3 us
  starting transfers between devices  14.6 us (41%)
  waiting for transfers between devices  9.38 us (26%)
  Pallas kernels  7.9 us (22%)
  matrix products  1.44 us (4%)
  between operations  0.83 us (2%)
  other arithmetic  0.74 us (2%)
  local copies, waits for them, and re-layouts  0.43 us (1%)
    ppermute x13, starting transfers between devices, exchange(): lax.ppermute(value, 'dp', [(i, i ^ distance) for i in range(lax.axis_size...  14.6 us
    ppermute x13, waiting for transfers between devices, exchange(): lax.ppermute(value, 'dp', [(i, i ^ distance) for i in range(lax.axis_size...  9.38 us
    pallas_call x1, Pallas kernels, project(): pl.pallas_call(project_kernel, in_specs=[vmem, vmem], out_specs=vmem, out...  2.89 us
    pallas_call x1, Pallas kernels, inverse(): pl.pallas_call(functools.partial(inverse_kernel, total_tokens), in_specs=...  2.65 us
    dot_general x1, matrix products, per_device(): jnp.einsum('tmk,mrk->tmr', out_grads, out_proj, preferred_element_type=F32)  1.44 us
    pallas_call x1, Pallas kernels, precondition(): pl.pallas_call(precondition_kernel, in_specs=[vmem] * (1 + len(moments)),...  0.83 us
  transfers between devices with their start and end apart: 13, of which 7 were waited for; matrix products, arithmetic and copies ran while one was open for 4% of the time, Pallas kernels for 20%

profile of v13, /device:TPU:0, one launch (start us, length us, event | category | flops | bytes accessed | tf_op | source)
XLA Modules:
  0.0 35.3 jit_solution(17910667159862839067)
XLA Ops:
  0.0 0.0 copy-start
  0.0 0.0 copy-start.3
  0.0 0.0 copy-start.1
  0.0 0.0 copy-start.2
  0.0 0.5 %own_place.1 = s32[1]{0:T(128)} custom-call(), custom_call_target="tpu_custom_call" | custom-call | flops 80000000000 | bytes 8 | tf_op jit(solution)/shard_map/own_place/pallas_call | solution.py:37
  0.5 0.4 %copy-done.3 = bf16[8,8192]{1,0:T(8,128)(2,1)S(1)} copy-done((bf16[8,8192]{1,0:T(8,128)(2,1)S(1)}, bf16[8,8192]{1,0:T(8,128)(2,1)}, u32[]{:S(2)}) %copy-start.3) | copy-done | bytes 131096
  1.0 5.0 %collective-permute-start.1 = (bf16[8,8192]{1,0:T(8,128)(2,1)S(1)}, bf16[8,8192]{1,0:T(8,128)(2,1)S(1)}, u32[]{:S(2)}, u32[]{:S(2)}) collective-permute-start(bf16[8,8192]{1,0:T(8,128)(2,1)S(1)} %copy-done.3), channel_id=1, source_target_pairs={{0,12},{1,13},{2,14},{3,15},{4,8},{5,9},{6,10},{7,11},{8,4},{9,5},... | collective-permute-start | bytes 393224 | tf_op jit(solution)/shard_map/ppermute | solution.py:288
  6.0 0.0 collective-permute-start.3
  6.0 0.6 %collective-permute-start.9 = (bf16[8,8192]{1,0:T(8,128)(2,1)S(1)}, bf16[8,8192]{1,0:T(8,128)(2,1)S(1)}, u32[]{:S(2)}, u32[]{:S(2)}) collective-permute-start(bf16[8,8192]{1,0:T(8,128)(2,1)S(1)} %copy-done.3), channel_id=1, source_target_pairs={{0,4},{1,5},{2,6},{3,7},{4,0},{5,1},{6,2},{7,3},{8,12},{9,13},{10,... | collective-permute-start | bytes 393224 | tf_op jit(solution)/shard_map/ppermute | solution.py:288
  6.6 0.0 copy-done.1
  6.6 0.0 copy-done.2
  6.6 0.0 copy-start.4
  6.6 2.9 %project.1.acts_ref = bf16[128,1024]{1,0:T(8,128)(2,1)S(1)} custom-call(bf16[1024,4096]{1,0:T(8,128)(2,1)S(1)} %copy-done.1, bf16[128,4096]{1,0:T(8,128)(2,1)S(1)} %bitcast.8), custom_call_target="tpu_custom_call" | custom-call | flops 2147483648 | bytes 8388608 | tf_op jit(solution)/shard_map/project/pallas_call | solution.py:56
  9.5 0.0 copy-done
  9.5 0.0 copy-done.4
  9.5 1.4 %fusion.2 = bf16[2,1024,64]{1,2,0:T(8,128)(2,1)S(1)} fusion(bf16[2,64,1024]{2,1,0:T(8,128)(2,1)S(1)} %copy-done, bf16[1024,2,1024]{2,1,0:T(2,128)(2,1)S(1)} %copy-done.4), kind=kOutput, calls=%fused_computation.2 | convolution fusion | flops 268566528 | bytes 4718592 | tf_op jit(solution)/shard_map/tmk,mrk->tmr/dot_general | solution.py:313
  10.9 0.5 %statistics.1 = (f32[40,128]{1,0:T(8,128)S(1)}, f32[40,128]{1,0:T(8,128)S(1)}, f32[64,512]{1,0:T(8,128)S(1)}, f32[64,512]{1,0:T(8,128)S(1)}) custom-call(bf16[128,1024]{1,0:T(8,128)(2,1)S(1)} %project.1.acts_ref, bf16[128,1024]{1,0:T(8,128)(2,1)S(1)} %bitcast.9), custom_call_target="tpu_custom_call" | custom-call | tf_op jit(solution)/shard_map/statistics/pallas_call | solution.py:125
  11.5 0.1 collective-permute-start
  11.6 0.5 %collective-permute-start.5 = (f32[64,512]{1,0:T(8,128)S(1)}, f32[64,512]{1,0:T(8,128)S(1)}, u32[]{:S(2)}, u32[]{:S(2)}) collective-permute-start(f32[64,512]{1,0:T(8,128)S(1)} %get-tuple-element.29), channel_id=1, source_target_pairs={{0,1},{1,0},{2,3},{3,2},{4,5},{5,4},{6,7},{7,6},{8,9},{9,8},{10,11... | collective-permute-start | bytes 393224 | tf_op jit(solution)/shard_map/ppermute | solution.py:288
  12.7 0.0 collective-permute-done
  12.8 0.0 collective-permute-done.1
  12.8 1.8 %collective-permute-start.2 = (f32[40,128]{1,0:T(8,128)S(1)}, f32[40,128]{1,0:T(8,128)S(1)}, u32[]{:S(2)}, u32[]{:S(2)}) collective-permute-start(f32[40,128]{1,0:T(8,128)S(1)} %add.9), channel_id=1, source_target_pairs={{0,2},{1,3},{2,0},{3,1},{4,6},{5,7},{6,4},{7,5},{8,10},{9,11},{10,... | collective-permute-start | bytes 61448 | tf_op jit(solution)/shard_map/ppermute | solution.py:288
  14.6 2.5 %collective-permute-done.3 = bf16[8,8192]{1,0:T(8,128)(2,1)S(1)} collective-permute-done((bf16[8,8192]{1,0:T(8,128)(2,1)S(1)}, bf16[8,8192]{1,0:T(8,128)(2,1)S(1)}, u32[]{:S(2)}, u32[]{:S(2)}) %collective-permute-start.3) | collective-permute-done | bytes 131104 | tf_op jit(solution)/shard_map/ppermute | solution.py:288
  17.1 0.1 collective-permute-start.4
  17.2 0.0 collective-permute-done.9
  17.2 0.5 %collective-permute-start.10 = (bf16[16,4096]{1,0:T(8,128)(2,1)S(1)}, bf16[16,4096]{1,0:T(8,128)(2,1)S(1)}, u32[]{:S(2)}, u32[]{:S(2)}) collective-permute-start(bf16[16,4096]{1,0:T(8,128)(2,1)S(1)} %pad_maximum_fusion.3), channel_id=1, source_target_pairs={{0,1},{1,0},{2,3},{3,2},{4,5},{5,4},{6,7},{7,6},{8,9},{9,8},{10,11... | collective-permute-start | bytes 393224 | tf_op jit(solution)/shard_map/ppermute | solution.py:288
  17.8 0.0 collective-permute-done.2
  17.8 0.7 %collective-permute-done.4 = bf16[16,4096]{1,0:T(8,128)(2,1)S(1)} collective-permute-done((bf16[16,4096]{1,0:T(8,128)(2,1)S(1)}, bf16[16,4096]{1,0:T(8,128)(2,1)S(1)}, u32[]{:S(2)}, u32[]{:S(2)}) %collective-permute-start.4) | collective-permute-done | bytes 131104 | tf_op jit(solution)/shard_map/ppermute | solution.py:288
  18.5 0.0 collective-permute-done.5.recv_ref
  18.6 0.2 collective-permute-done.10
  18.8 1.6 %collective-permute-start.11 = (bf16[64,4096]{1,0:T(8,128)(2,1)S(1)}, bf16[64,4096]{1,0:T(8,128)(2,1)S(1)}, u32[]{:S(2)}, u32[]{:S(2)}) collective-permute-start(bf16[64,4096]{1,0:T(8,128)(2,1)S(1)} %pad_maximum_fusion.refs_0_), channel_id=1, source_target_pairs={{0,2},{1,3},{2,0},{3,1},{4,6},{5,7},{6,4},{7,5},{8,10},{9,11},{10,... | collective-permute-start | bytes 1572872 | tf_op jit(solution)/shard_map/ppermute | solution.py:288
  20.4 2.5 %collective-permute-start.6 = (f32[40,128]{1,0:T(8,128)S(1)}, f32[40,128]{1,0:T(8,128)S(1)}, u32[]{:S(2)}, u32[]{:S(2)}) collective-permute-start(f32[40,128]{1,0:T(8,128)S(1)} %add.10.refs_0_), channel_id=1, source_target_pairs={{0,12},{1,13},{2,14},{3,15},{4,8},{5,9},{6,10},{7,11},{8,4},{9,5},... | collective-permute-start | bytes 61448 | tf_op jit(solution)/shard_map/ppermute | solution.py:288
  22.9 0.0 collective-permute-start.7
  22.9 1.9 %collective-permute-start.8 = (f32[40,128]{1,0:T(8,128)S(1)}, f32[40,128]{1,0:T(8,128)S(1)}, u32[]{:S(2)}, u32[]{:S(2)}) collective-permute-start(f32[40,128]{1,0:T(8,128)S(1)} %add.10.refs_0_), channel_id=1, source_target_pairs={{0,4},{1,5},{2,6},{3,7},{4,0},{5,1},{6,2},{7,3},{8,12},{9,13},{10,... | collective-permute-start | bytes 61448 | tf_op jit(solution)/shard_map/ppermute | solution.py:288
  24.8 1.2 %collective-permute-done.6.refs_1_ = f32[40,128]{1,0:T(8,128)S(1)} collective-permute-done((f32[40,128]{1,0:T(8,128)S(1)}, f32[40,128]{1,0:T(8,128)S(1)}, u32[]{:S(2)}, u32[]{:S(2)}) %collective-permute-start.6) | collective-permute-done | bytes 20512 | tf_op jit(solution)/shard_map/ppermute | solution.py:288
  26.0 1.6 %collective-permute-done.7.refs_2_ = f32[40,128]{1,0:T(8,128)S(1)} collective-permute-done((f32[40,128]{1,0:T(8,128)S(1)}, f32[40,128]{1,0:T(8,128)S(1)}, u32[]{:S(2)}, u32[]{:S(2)}) %collective-permute-start.7) | collective-permute-done | bytes 20512 | tf_op jit(solution)/shard_map/ppermute | solution.py:288
  27.6 0.0 collective-permute-done.8.refs_3_
  27.6 2.7 %inverse.1.inv_ref = f32[64,128]{1,0:T(8,128)S(1)} custom-call(f32[40,128]{1,0:T(8,128)S(1)} %add.10.refs_0_, f32[40,128]{1,0:T(8,128)S(1)} %collective-permute-done.6.refs_1_, f32[40,128]{1,0:T(8,128)S(1)} %collective-permute-done.7.refs_2_, f32[40,128]{1,0:T(8,128)S(1)} %collective-permute-done.8.refs_3_), custom_call_target="tpu_custom_call" | custom-call | tf_op jit(solution)/shard_map/inverse/pallas_call | solution.py:199
  30.2 0.8 %precondition.1.flat_ref = bf16[16,4096]{1,0:T(8,128)(2,1)S(1)} custom-call(f32[64,128]{1,0:T(8,128)S(1)} %inverse.1.inv_ref, f32[64,512]{1,0:T(8,128)S(1)} %get-tuple-element.31.keep_ref, f32[64,512]{1,0:T(8,128)S(1)} %collective-permute-done.5.recv_ref), custom_call_target="tpu_custom_call" | custom-call | tf_op jit(solution)/shard_map/precondition/pallas_call | solution.py:251
  31.1 2.0 %collective-permute-done.11.refs_1_ = bf16[64,4096]{1,0:T(8,128)(2,1)S(1)} collective-permute-done((bf16[64,4096]{1,0:T(8,128)(2,1)S(1)}, bf16[64,4096]{1,0:T(8,128)(2,1)S(1)}, u32[]{:S(2)}, u32[]{:S(2)}) %collective-permute-start.11) | collective-permute-done | bytes 524320 | tf_op jit(solution)/shard_map/ppermute | solution.py:288
  33.1 0.5 %scores.1 = f32[16,128]{1,0:T(8,128)S(1)} custom-call(bf16[16,4096]{1,0:T(8,128)(2,1)S(1)} %precondition.1.flat_ref, bf16[64,4096]{1,0:T(8,128)(2,1)S(1)} %pad_maximum_fusion.refs_0_, bf16[64,4096]{1,0:T(8,128)(2,1)S(1)} %collective-permute-done.11.refs_1_), custom_call_target="tpu_custom_call" | custom-call | tf_op jit(solution)/shard_map/scores/pallas_call | solution.py:276
  33.5 0.0 collective-permute-start.12
  33.6 1.2 %collective-permute-done.12 = f32[8,128]{1,0:T(8,128)S(1)} collective-permute-done((f32[8,128]{1,0:T(8,128)S(1)}, f32[8,128]{1,0:T(8,128)S(1)}, u32[]{:S(2)}, u32[]{:S(2)}) %collective-permute-start.12) | collective-permute-done | bytes 4128 | tf_op jit(solution)/shard_map/ppermute | solution.py:288
  34.8 0.6 %slice_add_fusion = f32[8,128]{1,0:T(8,128)} fusion(f32[8,128]{1,0:T(8,128)S(1)} %collective-permute-done.12, f32[16,128]{1,0:T(8,128)S(1)} %scores.1), kind=kLoop, calls=%fused_computation.15 | loop fusion | flops 1024 | bytes 12288 | tf_op jit(solution)/shard_map/add | solution.py:337
  (11 shorter events, 0.2 us)
Async XLA Ops:
  0.0 9.5 %copy-start = (bf16[2,64,1024]{2,1,0:T(8,128)(2,1)S(1)}, bf16[2,64,1024]{2,1,0:T(8,128)(2,1)}, u32[]{:S(2)}) copy-start(bf16[2,64,1024]{2,1,0:T(8,128)(2,1)} %param.8) | copy-start | bytes 786436
  0.0 0.9 %copy-start.3 = (bf16[8,8192]{1,0:T(8,128)(2,1)S(1)}, bf16[8,8192]{1,0:T(8,128)(2,1)}, u32[]{:S(2)}) copy-start(bf16[8,8192]{1,0:T(8,128)(2,1)} %param.9) | copy-start | bytes 393220
  0.0 6.6 %copy-start.1 = (bf16[1024,4096]{1,0:T(8,128)(2,1)S(1)}, bf16[1024,4096]{1,0:T(8,128)(2,1)}, u32[]{:S(2)}) copy-start(bf16[1024,4096]{1,0:T(8,128)(2,1)} %x_ref.1) | copy-start | bytes 25165828
  0.0 6.6 %copy-start.2 = (bf16[2,64,4096]{2,1,0:T(8,128)(2,1)S(1)}, bf16[2,64,4096]{2,1,0:T(8,128)(2,1)}, u32[]{:S(2)}) copy-start(bf16[2,64,4096]{2,1,0:T(8,128)(2,1)} %param.7) | copy-start | bytes 3145732
  1.0 11.8 %collective-permute-start.1 = (bf16[8,8192]{1,0:T(8,128)(2,1)S(1)}, bf16[8,8192]{1,0:T(8,128)(2,1)S(1)}, u32[]{:S(2)}, u32[]{:S(2)}) collective-permute-start(bf16[8,8192]{1,0:T(8,128)(2,1)S(1)} %copy-done.3), channel_id=1, source_target_pairs={{0,12},{1,13},{2,14},{3,15},{4,8},{5,9},{6,10},{7,11},{8,4},{9,5},... | collective-permute-start | bytes 393224 | tf_op jit(solution)/shard_map/ppermute | solution.py:288
  6.0 11.1 %collective-permute-start.3 = (bf16[8,8192]{1,0:T(8,128)(2,1)S(1)}, bf16[8,8192]{1,0:T(8,128)(2,1)S(1)}, u32[]{:S(2)}, u32[]{:S(2)}) collective-permute-start(bf16[8,8192]{1,0:T(8,128)(2,1)S(1)} %copy-done.3), channel_id=1, source_target_pairs={{0,8},{1,9},{2,10},{3,11},{4,12},{5,13},{6,14},{7,15},{8,0},{9,1},... | collective-permute-start | bytes 393224 | tf_op jit(solution)/shard_map/ppermute | solution.py:288
  6.0 11.2 %collective-permute-start.9 = (bf16[8,8192]{1,0:T(8,128)(2,1)S(1)}, bf16[8,8192]{1,0:T(8,128)(2,1)S(1)}, u32[]{:S(2)}, u32[]{:S(2)}) collective-permute-start(bf16[8,8192]{1,0:T(8,128)(2,1)S(1)} %copy-done.3), channel_id=1, source_target_pairs={{0,4},{1,5},{2,6},{3,7},{4,0},{5,1},{6,2},{7,3},{8,12},{9,13},{10,... | collective-permute-start | bytes 393224 | tf_op jit(solution)/shard_map/ppermute | solution.py:288
  6.6 2.9 %copy-start.4 = (bf16[1024,2,1024]{2,1,0:T(2,128)(2,1)S(1)}, bf16[1024,2,1024]{2,1,0:T(2,128)(2,1)}, u32[]{:S(2)}) copy-start(bf16[1024,2,1024]{2,1,0:T(2,128)(2,1)} %param.6) | copy-start | bytes 12582916
  11.5 1.3 %collective-permute-start = (f32[40,128]{1,0:T(8,128)S(1)}, f32[40,128]{1,0:T(8,128)S(1)}, u32[]{:S(2)}, u32[]{:S(2)}) collective-permute-start(f32[40,128]{1,0:T(8,128)S(1)} %get-tuple-element.24), channel_id=1, source_target_pairs={{0,1},{1,0},{2,3},{3,2},{4,5},{5,4},{6,7},{7,6},{8,9},{9,8},{10,11... | collective-permute-start | bytes 61448 | tf_op jit(solution)/shard_map/ppermute | solution.py:288
  11.6 7.0 %collective-permute-start.5 = (f32[64,512]{1,0:T(8,128)S(1)}, f32[64,512]{1,0:T(8,128)S(1)}, u32[]{:S(2)}, u32[]{:S(2)}) collective-permute-start(f32[64,512]{1,0:T(8,128)S(1)} %get-tuple-element.29), channel_id=1, source_target_pairs={{0,1},{1,0},{2,3},{3,2},{4,5},{5,4},{6,7},{7,6},{8,9},{9,8},{10,11... | collective-permute-start | bytes 393224 | tf_op jit(solution)/shard_map/ppermute | solution.py:288
  12.8 5.0 %collective-permute-start.2 = (f32[40,128]{1,0:T(8,128)S(1)}, f32[40,128]{1,0:T(8,128)S(1)}, u32[]{:S(2)}, u32[]{:S(2)}) collective-permute-start(f32[40,128]{1,0:T(8,128)S(1)} %add.9), channel_id=1, source_target_pairs={{0,2},{1,3},{2,0},{3,1},{4,6},{5,7},{6,4},{7,5},{8,10},{9,11},{10,... | collective-permute-start | bytes 61448 | tf_op jit(solution)/shard_map/ppermute | solution.py:288
  17.1 1.4 %collective-permute-start.4 = (bf16[16,4096]{1,0:T(8,128)(2,1)S(1)}, bf16[16,4096]{1,0:T(8,128)(2,1)S(1)}, u32[]{:S(2)}, u32[]{:S(2)}) collective-permute-start(bf16[16,4096]{1,0:T(8,128)(2,1)S(1)} %pad_maximum_fusion.2), channel_id=1, source_target_pairs={{0,1},{1,0},{2,3},{3,2},{4,5},{5,4},{6,7},{7,6},{8,9},{9,8},{10,11... | collective-permute-start | bytes 393224 | tf_op jit(solution)/shard_map/ppermute | solution.py:288
  17.2 1.5 %collective-permute-start.10 = (bf16[16,4096]{1,0:T(8,128)(2,1)S(1)}, bf16[16,4096]{1,0:T(8,128)(2,1)S(1)}, u32[]{:S(2)}, u32[]{:S(2)}) collective-permute-start(bf16[16,4096]{1,0:T(8,128)(2,1)S(1)} %pad_maximum_fusion.3), channel_id=1, source_target_pairs={{0,1},{1,0},{2,3},{3,2},{4,5},{5,4},{6,7},{7,6},{8,9},{9,8},{10,11... | collective-permute-start | bytes 393224 | tf_op jit(solution)/shard_map/ppermute | solution.py:288
  18.8 14.3 %collective-permute-start.11 = (bf16[64,4096]{1,0:T(8,128)(2,1)S(1)}, bf16[64,4096]{1,0:T(8,128)(2,1)S(1)}, u32[]{:S(2)}, u32[]{:S(2)}) collective-permute-start(bf16[64,4096]{1,0:T(8,128)(2,1)S(1)} %pad_maximum_fusion.refs_0_), channel_id=1, source_target_pairs={{0,2},{1,3},{2,0},{3,1},{4,6},{5,7},{6,4},{7,5},{8,10},{9,11},{10,... | collective-permute-start | bytes 1572872 | tf_op jit(solution)/shard_map/ppermute | solution.py:288
  20.4 5.6 %collective-permute-start.6 = (f32[40,128]{1,0:T(8,128)S(1)}, f32[40,128]{1,0:T(8,128)S(1)}, u32[]{:S(2)}, u32[]{:S(2)}) collective-permute-start(f32[40,128]{1,0:T(8,128)S(1)} %add.10.refs_0_), channel_id=1, source_target_pairs={{0,12},{1,13},{2,14},{3,15},{4,8},{5,9},{6,10},{7,11},{8,4},{9,5},... | collective-permute-start | bytes 61448 | tf_op jit(solution)/shard_map/ppermute | solution.py:288
  22.9 4.7 %collective-permute-start.7 = (f32[40,128]{1,0:T(8,128)S(1)}, f32[40,128]{1,0:T(8,128)S(1)}, u32[]{:S(2)}, u32[]{:S(2)}) collective-permute-start(f32[40,128]{1,0:T(8,128)S(1)} %add.10.refs_0_), channel_id=1, source_target_pairs={{0,8},{1,9},{2,10},{3,11},{4,12},{5,13},{6,14},{7,15},{8,0},{9,1},... | collective-permute-start | bytes 61448 | tf_op jit(solution)/shard_map/ppermute | solution.py:288
  22.9 4.7 %collective-permute-start.8 = (f32[40,128]{1,0:T(8,128)S(1)}, f32[40,128]{1,0:T(8,128)S(1)}, u32[]{:S(2)}, u32[]{:S(2)}) collective-permute-start(f32[40,128]{1,0:T(8,128)S(1)} %add.10.refs_0_), channel_id=1, source_target_pairs={{0,4},{1,5},{2,6},{3,7},{4,0},{5,1},{6,2},{7,3},{8,12},{9,13},{10,... | collective-permute-start | bytes 61448 | tf_op jit(solution)/shard_map/ppermute | solution.py:288
  33.5 1.2 %collective-permute-start.12 = (f32[8,128]{1,0:T(8,128)S(1)}, f32[8,128]{1,0:T(8,128)S(1)}, u32[]{:S(2)}, u32[]{:S(2)}) collective-permute-start(f32[8,128]{1,0:T(8,128)S(1)} %slice.9), channel_id=1, source_target_pairs={{0,1},{1,0},{2,3},{3,2},{4,5},{5,4},{6,7},{7,6},{8,9},{9,8},{10,11... | collective-permute-start | bytes 12296 | tf_op jit(solution)/shard_map/ppermute | solution.py:288

commit v14 on v12

--- a/solution.py
+++ b/solution.py
@@ -321,7 +321,7 @@
     cov, far, moments = lax.optimization_barrier((cov, far, moments))
     near = fold(near_slabs)
     across = exchange(near, 2)
-    covs = [cov] + [exchange(cov, slab * GROUP) for slab in range(1, slabs)]
+    covs = [cov] + [exchange(cov, slab * GROUP) for slab in reversed(range(1, slabs))]
     covs, across = lax.optimization_barrier((covs, across))
     inv = inverse(covs, local_tokens * devices)
     gathered = [near, across, far, exchange(far, 2)]

time: 34.8 us -> 34 us (0.977)
  waiting for transfers between devices: 7.81 us -> 7.14 us
    ppermute x14, waiting for transfers between devices: 7.81 us -> 7.14 us  [exchange(): lax.ppermute(value, 'dp', [(i, i ^ distance) for i in range(lax.axis_size...]
  transfers between devices with their start and end apart: 14 -> 14, of which waited for: 4 -> 5; matrix products, arithmetic and copies ran while one was open for 5% -> 5% of each run, Pallas kernels for 20% -> 20%
where the time goes in v14:
time: 34 us; the launch traced here: 33.9 us
  starting transfers between devices  15.4 us (45%)
  Pallas kernels  7.89 us (23%)
  waiting for transfers between devices  7.14 us (21%)
  matrix products  1.44 us (4%)
  between operations  0.86 us (3%)
  other arithmetic  0.72 us (2%)
  local copies, waits for them, and re-layouts  0.43 us (1%)
    ppermute x14, starting transfers between devices, exchange(): lax.ppermute(value, 'dp', [(i, i ^ distance) for i in range(lax.axis_size...  15.4 us
    ppermute x14, waiting for transfers between devices, exchange(): lax.ppermute(value, 'dp', [(i, i ^ distance) for i in range(lax.axis_size...  7.14 us
    pallas_call x1, Pallas kernels, project(): pl.pallas_call(project_kernel, in_specs=[vmem, vmem], out_specs=vmem, out...  2.89 us
    pallas_call x1, Pallas kernels, inverse(): pl.pallas_call(functools.partial(inverse_kernel, total_tokens), in_specs=...  2.65 us
    dot_general x1, matrix products, per_device(): jnp.einsum('tmk,mrk->tmr', out_grads, out_proj, preferred_element_type=F32)  1.44 us
    pallas_call x1, Pallas kernels, precondition(): pl.pallas_call(precondition_kernel, in_specs=[vmem] * (1 + len(moments)),...  0.83 us
  transfers between devices with their start and end apart: 14, of which 5 were waited for; matrix products, arithmetic and copies ran while one was open for 5% of the time, Pallas kernels for 20%

profile of v14, /device:TPU:0, one launch (start us, length us, event | category | flops | bytes accessed | tf_op | source)
XLA Modules:
  0.0 33.9 jit_solution(9826520724706943091)
XLA Ops:
  0.0 0.0 copy-start
  0.0 0.0 copy-start.3
  0.0 0.0 copy-start.2
  0.0 0.0 copy-start.1
  0.0 0.5 %own_place.1 = s32[1]{0:T(128)} custom-call(), custom_call_target="tpu_custom_call" | custom-call | flops 80000000000 | bytes 8 | tf_op jit(solution)/shard_map/own_place/pallas_call | solution.py:37
  0.5 0.4 %copy-done.3 = bf16[8,8192]{1,0:T(8,128)(2,1)S(1)} copy-done((bf16[8,8192]{1,0:T(8,128)(2,1)S(1)}, bf16[8,8192]{1,0:T(8,128)(2,1)}, u32[]{:S(2)}) %copy-start.3) | copy-done | bytes 131096
  1.0 5.0 %collective-permute-start.1 = (bf16[8,8192]{1,0:T(8,128)(2,1)S(1)}, bf16[8,8192]{1,0:T(8,128)(2,1)S(1)}, u32[]{:S(2)}, u32[]{:S(2)}) collective-permute-start(bf16[8,8192]{1,0:T(8,128)(2,1)S(1)} %copy-done.3), channel_id=1, source_target_pairs={{0,12},{1,13},{2,14},{3,15},{4,8},{5,9},{6,10},{7,11},{8,4},{9,5},... | collective-permute-start | bytes 393224 | tf_op jit(solution)/shard_map/ppermute | solution.py:288
  6.0 0.0 collective-permute-start.3
  6.0 0.6 %collective-permute-start.9 = (bf16[8,8192]{1,0:T(8,128)(2,1)S(1)}, bf16[8,8192]{1,0:T(8,128)(2,1)S(1)}, u32[]{:S(2)}, u32[]{:S(2)}) collective-permute-start(bf16[8,8192]{1,0:T(8,128)(2,1)S(1)} %copy-done.3), channel_id=1, source_target_pairs={{0,4},{1,5},{2,6},{3,7},{4,0},{5,1},{6,2},{7,3},{8,12},{9,13},{10,... | collective-permute-start | bytes 393224 | tf_op jit(solution)/shard_map/ppermute | solution.py:288
  6.6 0.0 copy-done.2
  6.6 0.0 copy-done.1
  6.6 0.0 copy-start.4
  6.6 2.9 %project.1.acts_ref = bf16[128,1024]{1,0:T(8,128)(2,1)S(1)} custom-call(bf16[1024,4096]{1,0:T(8,128)(2,1)S(1)} %copy-done.1, bf16[128,4096]{1,0:T(8,128)(2,1)S(1)} %bitcast.8), custom_call_target="tpu_custom_call" | custom-call | flops 2147483648 | bytes 8388608 | tf_op jit(solution)/shard_map/project/pallas_call | solution.py:56
  9.5 0.0 copy-done
  9.5 0.0 copy-done.4
  9.5 1.4 %fusion.2 = bf16[2,1024,64]{1,2,0:T(8,128)(2,1)S(1)} fusion(bf16[2,64,1024]{2,1,0:T(8,128)(2,1)S(1)} %copy-done, bf16[1024,2,1024]{2,1,0:T(2,128)(2,1)S(1)} %copy-done.4), kind=kOutput, calls=%fused_computation.2 | convolution fusion | flops 268566528 | bytes 4718592 | tf_op jit(solution)/shard_map/tmk,mrk->tmr/dot_general | solution.py:313
  10.9 0.5 %statistics.1 = (f32[40,128]{1,0:T(8,128)S(1)}, f32[40,128]{1,0:T(8,128)S(1)}, f32[64,512]{1,0:T(8,128)S(1)}, f32[64,512]{1,0:T(8,128)S(1)}) custom-call(bf16[128,1024]{1,0:T(8,128)(2,1)S(1)} %project.1.acts_ref, bf16[128,1024]{1,0:T(8,128)(2,1)S(1)} %bitcast.9), custom_call_target="tpu_custom_call" | custom-call | tf_op jit(solution)/shard_map/statistics/pallas_call | solution.py:125
  11.5 0.1 collective-permute-start
  11.6 0.5 %collective-permute-start.5 = (f32[64,512]{1,0:T(8,128)S(1)}, f32[64,512]{1,0:T(8,128)S(1)}, u32[]{:S(2)}, u32[]{:S(2)}) collective-permute-start(f32[64,512]{1,0:T(8,128)S(1)} %get-tuple-element.34), channel_id=1, source_target_pairs={{0,1},{1,0},{2,3},{3,2},{4,5},{5,4},{6,7},{7,6},{8,9},{9,8},{10,11... | collective-permute-start | bytes 393224 | tf_op jit(solution)/shard_map/ppermute | solution.py:288
  12.7 0.0 collective-permute-done
  12.8 0.0 collective-permute-done.1
  12.8 1.8 %collective-permute-start.2 = (f32[40,128]{1,0:T(8,128)S(1)}, f32[40,128]{1,0:T(8,128)S(1)}, u32[]{:S(2)}, u32[]{:S(2)}) collective-permute-start(f32[40,128]{1,0:T(8,128)S(1)} %add.9), channel_id=1, source_target_pairs={{0,2},{1,3},{2,0},{3,1},{4,6},{5,7},{6,4},{7,5},{8,10},{9,11},{10,... | collective-permute-start | bytes 61448 | tf_op jit(solution)/shard_map/ppermute | solution.py:288
  14.6 0.0 collective-permute-done.9
  14.6 0.1 collective-permute-start.10
  14.7 2.4 %collective-permute-done.3 = bf16[8,8192]{1,0:T(8,128)(2,1)S(1)} collective-permute-done((bf16[8,8192]{1,0:T(8,128)(2,1)S(1)}, bf16[8,8192]{1,0:T(8,128)(2,1)S(1)}, u32[]{:S(2)}, u32[]{:S(2)}) %collective-permute-start.3) | collective-permute-done | bytes 131104 | tf_op jit(solution)/shard_map/ppermute | solution.py:288
  17.1 0.1 collective-permute-start.4
  17.2 0.0 collective-permute-done.2
  17.2 0.0 collective-permute-done.10
  17.3 1.6 %collective-permute-start.11 = (bf16[32,4096]{1,0:T(8,128)(2,1)S(1)}, bf16[32,4096]{1,0:T(8,128)(2,1)S(1)}, u32[]{:S(2)}, u32[]{:S(2)}) collective-permute-start(bf16[32,4096]{1,0:T(8,128)(2,1)S(1)} %pad_maximum_fusion.1.refs_0_), channel_id=1, source_target_pairs={{0,2},{1,3},{2,0},{3,1},{4,6},{5,7},{6,4},{7,5},{8,10},{9,11},{10,... | collective-permute-start | bytes 786440 | tf_op jit(solution)/shard_map/ppermute | solution.py:288
  18.8 0.0 collective-permute-done.4
  18.9 0.0 collective-permute-done.5.recv_ref
  18.9 1.3 %collective-permute-start.12 = (bf16[32,4096]{1,0:T(8,128)(2,1)S(1)}, bf16[32,4096]{1,0:T(8,128)(2,1)S(1)}, u32[]{:S(2)}, u32[]{:S(2)}) collective-permute-start(bf16[32,4096]{1,0:T(8,128)(2,1)S(1)} %pad_maximum_fusion.refs_2_), channel_id=1, source_target_pairs={{0,2},{1,3},{2,0},{3,1},{4,6},{5,7},{6,4},{7,5},{8,10},{9,11},{10,... | collective-permute-start | bytes 786440 | tf_op jit(solution)/shard_map/ppermute | solution.py:288
  20.1 2.5 %collective-permute-start.6 = (f32[40,128]{1,0:T(8,128)S(1)}, f32[40,128]{1,0:T(8,128)S(1)}, u32[]{:S(2)}, u32[]{:S(2)}) collective-permute-start(f32[40,128]{1,0:T(8,128)S(1)} %add.10.refs_0_), channel_id=1, source_target_pairs={{0,12},{1,13},{2,14},{3,15},{4,8},{5,9},{6,10},{7,11},{8,4},{9,5},... | collective-permute-start | bytes 61448 | tf_op jit(solution)/shard_map/ppermute | solution.py:288
  22.7 0.7 %collective-permute-start.7 = (f32[40,128]{1,0:T(8,128)S(1)}, f32[40,128]{1,0:T(8,128)S(1)}, u32[]{:S(2)}, u32[]{:S(2)}) collective-permute-start(f32[40,128]{1,0:T(8,128)S(1)} %add.10.refs_0_), channel_id=1, source_target_pairs={{0,8},{1,9},{2,10},{3,11},{4,12},{5,13},{6,14},{7,15},{8,0},{9,1},... | collective-permute-start | bytes 61448 | tf_op jit(solution)/shard_map/ppermute | solution.py:288
  23.4 1.2 %collective-permute-start.8 = (f32[40,128]{1,0:T(8,128)S(1)}, f32[40,128]{1,0:T(8,128)S(1)}, u32[]{:S(2)}, u32[]{:S(2)}) collective-permute-start(f32[40,128]{1,0:T(8,128)S(1)} %add.10.refs_0_), channel_id=1, source_target_pairs={{0,4},{1,5},{2,6},{3,7},{4,0},{5,1},{6,2},{7,3},{8,12},{9,13},{10,... | collective-permute-start | bytes 61448 | tf_op jit(solution)/shard_map/ppermute | solution.py:288
  24.5 1.2 %collective-permute-done.6.refs_1_ = f32[40,128]{1,0:T(8,128)S(1)} collective-permute-done((f32[40,128]{1,0:T(8,128)S(1)}, f32[40,128]{1,0:T(8,128)S(1)}, u32[]{:S(2)}, u32[]{:S(2)}) %collective-permute-start.6) | collective-permute-done | bytes 20512 | tf_op jit(solution)/shard_map/ppermute | solution.py:288
  25.7 1.6 %collective-permute-done.7.refs_2_ = f32[40,128]{1,0:T(8,128)S(1)} collective-permute-done((f32[40,128]{1,0:T(8,128)S(1)}, f32[40,128]{1,0:T(8,128)S(1)}, u32[]{:S(2)}, u32[]{:S(2)}) %collective-permute-start.7) | collective-permute-done | bytes 20512 | tf_op jit(solution)/shard_map/ppermute | solution.py:288
  27.4 0.0 collective-permute-done.8.refs_3_
  27.4 0.0 collective-permute-done.11.refs_1_
  27.4 2.7 %inverse.1.inv_ref = f32[64,128]{1,0:T(8,128)S(1)} custom-call(f32[40,128]{1,0:T(8,128)S(1)} %add.10.refs_0_, f32[40,128]{1,0:T(8,128)S(1)} %collective-permute-done.6.refs_1_, f32[40,128]{1,0:T(8,128)S(1)} %collective-permute-done.7.refs_2_, f32[40,128]{1,0:T(8,128)S(1)} %collective-permute-done.8.refs_3_), custom_call_target="tpu_custom_call" | custom-call | tf_op jit(solution)/shard_map/inverse/pallas_call | solution.py:199
  30.0 0.8 %precondition.1.flat_ref = bf16[16,4096]{1,0:T(8,128)(2,1)S(1)} custom-call(f32[64,128]{1,0:T(8,128)S(1)} %inverse.1.inv_ref, f32[64,512]{1,0:T(8,128)S(1)} %get-tuple-element.41.keep_ref, f32[64,512]{1,0:T(8,128)S(1)} %collective-permute-done.5.recv_ref), custom_call_target="tpu_custom_call" | custom-call | tf_op jit(solution)/shard_map/precondition/pallas_call | solution.py:251
  30.9 0.8 %collective-permute-done.12.refs_3_ = bf16[32,4096]{1,0:T(8,128)(2,1)S(1)} collective-permute-done((bf16[32,4096]{1,0:T(8,128)(2,1)S(1)}, bf16[32,4096]{1,0:T(8,128)(2,1)S(1)}, u32[]{:S(2)}, u32[]{:S(2)}) %collective-permute-start.12) | collective-permute-done | bytes 262176 | tf_op jit(solution)/shard_map/ppermute | solution.py:288
  31.6 0.5 %scores.1 = f32[16,128]{1,0:T(8,128)S(1)} custom-call(bf16[16,4096]{1,0:T(8,128)(2,1)S(1)} %precondition.1.flat_ref, bf16[32,4096]{1,0:T(8,128)(2,1)S(1)} %pad_maximum_fusion.1.refs_0_, bf16[32,4096]{1,0:T(8,128)(2,1)S(1)} %collective-permute-done.11.refs_1_, bf16[32,4096]{1,0:T(8,128)(2,1)S(1)} %pad_maximum_fusion.refs_2_, ...), custom_call_target="tpu_custom_call" | custom-call | tf_op jit(solution)/shard_map/scores/pallas_call | solution.py:276
  32.1 0.0 collective-permute-start.13
  32.2 1.2 %collective-permute-done.13 = f32[8,128]{1,0:T(8,128)S(1)} collective-permute-done((f32[8,128]{1,0:T(8,128)S(1)}, f32[8,128]{1,0:T(8,128)S(1)}, u32[]{:S(2)}, u32[]{:S(2)}) %collective-permute-start.13) | collective-permute-done | bytes 4128 | tf_op jit(solution)/shard_map/ppermute | solution.py:288
  33.3 0.6 %slice_add_fusion = f32[8,128]{1,0:T(8,128)} fusion(f32[8,128]{1,0:T(8,128)S(1)} %collective-permute-done.13, f32[16,128]{1,0:T(8,128)S(1)} %scores.1), kind=kLoop, calls=%fused_computation.15 | loop fusion | flops 1024 | bytes 12288 | tf_op jit(solution)/shard_map/add | solution.py:337
  (11 shorter events, 0.1 us)
Async XLA Ops:
  0.0 9.5 %copy-start = (bf16[2,64,1024]{2,1,0:T(8,128)(2,1)S(1)}, bf16[2,64,1024]{2,1,0:T(8,128)(2,1)}, u32[]{:S(2)}) copy-start(bf16[2,64,1024]{2,1,0:T(8,128)(2,1)} %param.8) | copy-start | bytes 786436
  0.0 0.9 %copy-start.3 = (bf16[8,8192]{1,0:T(8,128)(2,1)S(1)}, bf16[8,8192]{1,0:T(8,128)(2,1)}, u32[]{:S(2)}) copy-start(bf16[8,8192]{1,0:T(8,128)(2,1)} %param.9) | copy-start | bytes 393220
  0.0 6.6 %copy-start.2 = (bf16[2,64,4096]{2,1,0:T(8,128)(2,1)S(1)}, bf16[2,64,4096]{2,1,0:T(8,128)(2,1)}, u32[]{:S(2)}) copy-start(bf16[2,64,4096]{2,1,0:T(8,128)(2,1)} %param.7) | copy-start | bytes 3145732
  0.0 6.6 %copy-start.1 = (bf16[1024,4096]{1,0:T(8,128)(2,1)S(1)}, bf16[1024,4096]{1,0:T(8,128)(2,1)}, u32[]{:S(2)}) copy-start(bf16[1024,4096]{1,0:T(8,128)(2,1)} %x_ref.1) | copy-start | bytes 25165828
  1.0 11.8 %collective-permute-start.1 = (bf16[8,8192]{1,0:T(8,128)(2,1)S(1)}, bf16[8,8192]{1,0:T(8,128)(2,1)S(1)}, u32[]{:S(2)}, u32[]{:S(2)}) collective-permute-start(bf16[8,8192]{1,0:T(8,128)(2,1)S(1)} %copy-done.3), channel_id=1, source_target_pairs={{0,12},{1,13},{2,14},{3,15},{4,8},{5,9},{6,10},{7,11},{8,4},{9,5},... | collective-permute-start | bytes 393224 | tf_op jit(solution)/shard_map/ppermute | solution.py:288
  6.0 11.1 %collective-permute-start.3 = (bf16[8,8192]{1,0:T(8,128)(2,1)S(1)}, bf16[8,8192]{1,0:T(8,128)(2,1)S(1)}, u32[]{:S(2)}, u32[]{:S(2)}) collective-permute-start(bf16[8,8192]{1,0:T(8,128)(2,1)S(1)} %copy-done.3), channel_id=1, source_target_pairs={{0,8},{1,9},{2,10},{3,11},{4,12},{5,13},{6,14},{7,15},{8,0},{9,1},... | collective-permute-start | bytes 393224 | tf_op jit(solution)/shard_map/ppermute | solution.py:288
  6.0 8.6 %collective-permute-start.9 = (bf16[8,8192]{1,0:T(8,128)(2,1)S(1)}, bf16[8,8192]{1,0:T(8,128)(2,1)S(1)}, u32[]{:S(2)}, u32[]{:S(2)}) collective-permute-start(bf16[8,8192]{1,0:T(8,128)(2,1)S(1)} %copy-done.3), channel_id=1, source_target_pairs={{0,4},{1,5},{2,6},{3,7},{4,0},{5,1},{6,2},{7,3},{8,12},{9,13},{10,... | collective-permute-start | bytes 393224 | tf_op jit(solution)/shard_map/ppermute | solution.py:288
  6.6 2.9 %copy-start.4 = (bf16[1024,2,1024]{2,1,0:T(2,128)(2,1)S(1)}, bf16[1024,2,1024]{2,1,0:T(2,128)(2,1)}, u32[]{:S(2)}) copy-start(bf16[1024,2,1024]{2,1,0:T(2,128)(2,1)} %param.6) | copy-start | bytes 12582916
  11.5 1.3 %collective-permute-start = (f32[40,128]{1,0:T(8,128)S(1)}, f32[40,128]{1,0:T(8,128)S(1)}, u32[]{:S(2)}, u32[]{:S(2)}) collective-permute-start(f32[40,128]{1,0:T(8,128)S(1)} %get-tuple-element.29), channel_id=1, source_target_pairs={{0,1},{1,0},{2,3},{3,2},{4,5},{5,4},{6,7},{7,6},{8,9},{9,8},{10,11... | collective-permute-start | bytes 61448 | tf_op jit(solution)/shard_map/ppermute | solution.py:288
  11.6 7.3 %collective-permute-start.5 = (f32[64,512]{1,0:T(8,128)S(1)}, f32[64,512]{1,0:T(8,128)S(1)}, u32[]{:S(2)}, u32[]{:S(2)}) collective-permute-start(f32[64,512]{1,0:T(8,128)S(1)} %get-tuple-element.34), channel_id=1, source_target_pairs={{0,1},{1,0},{2,3},{3,2},{4,5},{5,4},{6,7},{7,6},{8,9},{9,8},{10,11... | collective-permute-start | bytes 393224 | tf_op jit(solution)/shard_map/ppermute | solution.py:288
  12.8 4.4 %collective-permute-start.2 = (f32[40,128]{1,0:T(8,128)S(1)}, f32[40,128]{1,0:T(8,128)S(1)}, u32[]{:S(2)}, u32[]{:S(2)}) collective-permute-start(f32[40,128]{1,0:T(8,128)S(1)} %add.9), channel_id=1, source_target_pairs={{0,2},{1,3},{2,0},{3,1},{4,6},{5,7},{6,4},{7,5},{8,10},{9,11},{10,... | collective-permute-start | bytes 61448 | tf_op jit(solution)/shard_map/ppermute | solution.py:288
  14.6 2.6 %collective-permute-start.10 = (bf16[16,4096]{1,0:T(8,128)(2,1)S(1)}, bf16[16,4096]{1,0:T(8,128)(2,1)S(1)}, u32[]{:S(2)}, u32[]{:S(2)}) collective-permute-start(bf16[16,4096]{1,0:T(8,128)(2,1)S(1)} %pad_maximum_fusion.3), channel_id=1, source_target_pairs={{0,1},{1,0},{2,3},{3,2},{4,5},{5,4},{6,7},{7,6},{8,9},{9,8},{10,11... | collective-permute-start | bytes 393224 | tf_op jit(solution)/shard_map/ppermute | solution.py:288
  17.1 1.7 %collective-permute-start.4 = (bf16[16,4096]{1,0:T(8,128)(2,1)S(1)}, bf16[16,4096]{1,0:T(8,128)(2,1)S(1)}, u32[]{:S(2)}, u32[]{:S(2)}) collective-permute-start(bf16[16,4096]{1,0:T(8,128)(2,1)S(1)} %pad_maximum_fusion.2), channel_id=1, source_target_pairs={{0,1},{1,0},{2,3},{3,2},{4,5},{5,4},{6,7},{7,6},{8,9},{9,8},{10,11... | collective-permute-start | bytes 393224 | tf_op jit(solution)/shard_map/ppermute | solution.py:288
  17.3 10.1 %collective-permute-start.11 = (bf16[32,4096]{1,0:T(8,128)(2,1)S(1)}, bf16[32,4096]{1,0:T(8,128)(2,1)S(1)}, u32[]{:S(2)}, u32[]{:S(2)}) collective-permute-start(bf16[32,4096]{1,0:T(8,128)(2,1)S(1)} %pad_maximum_fusion.1.refs_0_), channel_id=1, source_target_pairs={{0,2},{1,3},{2,0},{3,1},{4,6},{5,7},{6,4},{7,5},{8,10},{9,11},{10,... | collective-permute-start | bytes 786440 | tf_op jit(solution)/shard_map/ppermute | solution.py:288
  18.9 12.7 %collective-permute-start.12 = (bf16[32,4096]{1,0:T(8,128)(2,1)S(1)}, bf16[32,4096]{1,0:T(8,128)(2,1)S(1)}, u32[]{:S(2)}, u32[]{:S(2)}) collective-permute-start(bf16[32,4096]{1,0:T(8,128)(2,1)S(1)} %pad_maximum_fusion.refs_2_), channel_id=1, source_target_pairs={{0,2},{1,3},{2,0},{3,1},{4,6},{5,7},{6,4},{7,5},{8,10},{9,11},{10,... | collective-permute-start | bytes 786440 | tf_op jit(solution)/shard_map/ppermute | solution.py:288
  20.1 5.6 %collective-permute-start.6 = (f32[40,128]{1,0:T(8,128)S(1)}, f32[40,128]{1,0:T(8,128)S(1)}, u32[]{:S(2)}, u32[]{:S(2)}) collective-permute-start(f32[40,128]{1,0:T(8,128)S(1)} %add.10.refs_0_), channel_id=1, source_target_pairs={{0,12},{1,13},{2,14},{3,15},{4,8},{5,9},{6,10},{7,11},{8,4},{9,5},... | collective-permute-start | bytes 61448 | tf_op jit(solution)/shard_map/ppermute | solution.py:288
  22.7 4.7 %collective-permute-start.7 = (f32[40,128]{1,0:T(8,128)S(1)}, f32[40,128]{1,0:T(8,128)S(1)}, u32[]{:S(2)}, u32[]{:S(2)}) collective-permute-start(f32[40,128]{1,0:T(8,128)S(1)} %add.10.refs_0_), channel_id=1, source_target_pairs={{0,8},{1,9},{2,10},{3,11},{4,12},{5,13},{6,14},{7,15},{8,0},{9,1},... | collective-permute-start | bytes 61448 | tf_op jit(solution)/shard_map/ppermute | solution.py:288
  23.4 4.0 %collective-permute-start.8 = (f32[40,128]{1,0:T(8,128)S(1)}, f32[40,128]{1,0:T(8,128)S(1)}, u32[]{:S(2)}, u32[]{:S(2)}) collective-permute-start(f32[40,128]{1,0:T(8,128)S(1)} %add.10.refs_0_), channel_id=1, source_target_pairs={{0,4},{1,5},{2,6},{3,7},{4,0},{5,1},{6,2},{7,3},{8,12},{9,13},{10,... | collective-permute-start | bytes 61448 | tf_op jit(solution)/shard_map/ppermute | solution.py:288
  32.1 1.2 %collective-permute-start.13 = (f32[8,128]{1,0:T(8,128)S(1)}, f32[8,128]{1,0:T(8,128)S(1)}, u32[]{:S(2)}, u32[]{:S(2)}) collective-permute-start(f32[8,128]{1,0:T(8,128)S(1)} %slice.9), channel_id=1, source_target_pairs={{0,1},{1,0},{2,3},{3,2},{4,5},{5,4},{6,7},{7,6},{8,9},{9,8},{10,11... | collective-permute-start | bytes 12296 | tf_op jit(solution)/shard_map/ppermute | solution.py:288

commit v15 on v14

--- a/solution.py
+++ b/solution.py
@@ -301,6 +301,7 @@
     near_slabs, far_slabs = [0, 1], [2, 3] + list(range(4, slabs))
     column = {slab: exchange(queries, slab * GROUP) for slab in [1, 2, 3] + list(range(4, slabs))}
     column[0] = queries
+    beside = exchange(queries, 2)
     acts = project(layer_input, in_proj.reshape(PAIR, in_proj.shape[2]))
     acts, out_grads, column[0] = lax.optimization_barrier((acts, out_grads, column[0]))
     upper = device[0] & 1 == 1
@@ -319,15 +320,17 @@
     cov = cov + exchange(cov, 2)
     far = fold(far_slabs)
     cov, far, moments = lax.optimization_barrier((cov, far, moments))
-    near = fold(near_slabs)
+    column[-1] = beside
+    local = fold([0, -1])
+    near = fold([1])
     across = exchange(near, 2)
     covs = [cov] + [exchange(cov, slab * GROUP) for slab in reversed(range(1, slabs))]
     covs, across = lax.optimization_barrier((covs, across))
     inv = inverse(covs, local_tokens * devices)
-    gathered = [near, across, far, exchange(far, 2)]
-    order = [
+    gathered = [local, near, across, far, exchange(far, 2)]
+    order = [0, 2, 1, 3] + [
         slab * GROUP + 2 * over + core
-        for part in (near_slabs, far_slabs)
+        for part in ([1], far_slabs)
         for over in range(2)
         for core in range(2)
         for slab in part

time: 34 us -> 34.6 us (1.018)
  waiting for transfers between devices: 7.14 us -> 7.92 us
    ppermute x14 -> x16, waiting for transfers between devices: 7.14 us -> 7.92 us  [exchange(): lax.ppermute(value, 'dp', [(i, i ^ distance) for i in range(lax.axis_size...]
    ppermute x14 -> x16, starting transfers between devices: 15.4 us -> 15.2 us  [exchange(): lax.ppermute(value, 'dp', [(i, i ^ distance) for i in range(lax.axis_size...]
  transfers between devices with their start and end apart: 14 -> 16, of which waited for: 5 -> 8; matrix products, arithmetic and copies ran while one was open for 5% -> 5% of each run, Pallas kernels for 20% -> 20%
where the time goes in v15:
time: 34.6 us; the launch traced here: 34.5 us
  starting transfers between devices  15.2 us (44%)
  waiting for transfers between devices  7.92 us (23%)
  Pallas kernels  7.9 us (23%)
  matrix products  1.44 us (4%)
  between operations  0.82 us (2%)
  other arithmetic  0.74 us (2%)
  local copies, waits for them, and re-layouts  0.43 us (1%)
    ppermute x16, starting transfers between devices, exchange(): lax.ppermute(value, 'dp', [(i, i ^ distance) for i in range(lax.axis_size...  15.2 us
    ppermute x16, waiting for transfers between devices, exchange(): lax.ppermute(value, 'dp', [(i, i ^ distance) for i in range(lax.axis_size...  7.92 us
    pallas_call x1, Pallas kernels, project(): pl.pallas_call(project_kernel, in_specs=[vmem, vmem], out_specs=vmem, out...  2.89 us
    pallas_call x1, Pallas kernels, inverse(): pl.pallas_call(functools.partial(inverse_kernel, total_tokens), in_specs=...  2.65 us
    dot_general x1, matrix products, per_device(): jnp.einsum('tmk,mrk->tmr', out_grads, out_proj, preferred_element_type=F32)  1.44 us
    pallas_call x1, Pallas kernels, precondition(): pl.pallas_call(precondition_kernel, in_specs=[vmem] * (1 + len(moments)),...  0.84 us
  transfers between devices with their start and end apart: 16, of which 8 were waited for; matrix products, arithmetic and copies ran while one was open for 5% of the time, Pallas kernels for 20%

profile of v15, /device:TPU:0, one launch (start us, length us, event | category | flops | bytes accessed | tf_op | source)
XLA Modules:
  0.0 34.5 jit_solution(11696479088673712790)
XLA Ops:
  0.0 0.0 copy-start
  0.0 0.0 copy-start.3
  0.0 0.0 copy-start.1
  0.0 0.5 %own_place.1 = s32[1]{0:T(128)} custom-call(), custom_call_target="tpu_custom_call" | custom-call | flops 80000000000 | bytes 8 | tf_op jit(solution)/shard_map/own_place/pallas_call | solution.py:37
  0.5 0.4 %copy-done.3 = bf16[8,8192]{1,0:T(8,128)(2,1)S(1)} copy-done((bf16[8,8192]{1,0:T(8,128)(2,1)S(1)}, bf16[8,8192]{1,0:T(8,128)(2,1)}, u32[]{:S(2)}) %copy-start.3) | copy-done | bytes 131096
  1.0 5.0 %collective-permute-start.1 = (bf16[8,8192]{1,0:T(8,128)(2,1)S(1)}, bf16[8,8192]{1,0:T(8,128)(2,1)S(1)}, u32[]{:S(2)}, u32[]{:S(2)}) collective-permute-start(bf16[8,8192]{1,0:T(8,128)(2,1)S(1)} %copy-done.3), channel_id=1, source_target_pairs={{0,12},{1,13},{2,14},{3,15},{4,8},{5,9},{6,10},{7,11},{8,4},{9,5},... | collective-permute-start | bytes 393224 | tf_op jit(solution)/shard_map/ppermute | solution.py:288
  6.0 0.0 collective-permute-start.3
  6.0 0.6 %collective-permute-start.9 = (bf16[8,8192]{1,0:T(8,128)(2,1)S(1)}, bf16[8,8192]{1,0:T(8,128)(2,1)S(1)}, u32[]{:S(2)}, u32[]{:S(2)}) collective-permute-start(bf16[8,8192]{1,0:T(8,128)(2,1)S(1)} %copy-done.3), channel_id=1, source_target_pairs={{0,4},{1,5},{2,6},{3,7},{4,0},{5,1},{6,2},{7,3},{8,12},{9,13},{10,... | collective-permute-start | bytes 393224 | tf_op jit(solution)/shard_map/ppermute | solution.py:288
  6.6 1.7 %collective-permute-start.12 = (bf16[8,8192]{1,0:T(8,128)(2,1)S(1)}, bf16[8,8192]{1,0:T(8,128)(2,1)S(1)}, u32[]{:S(2)}, u32[]{:S(2)}) collective-permute-start(bf16[8,8192]{1,0:T(8,128)(2,1)S(1)} %copy-done.3), channel_id=1, source_target_pairs={{0,2},{1,3},{2,0},{3,1},{4,6},{5,7},{6,4},{7,5},{8,10},{9,11},{10,... | collective-permute-start | bytes 393224 | tf_op jit(solution)/shard_map/ppermute | solution.py:288
  8.3 0.0 copy-done.1
  8.3 0.0 copy-done.2
  8.3 2.9 %project.1.acts_ref = bf16[128,1024]{1,0:T(8,128)(2,1)S(1)} custom-call(bf16[1024,4096]{1,0:T(8,128)(2,1)S(1)} %copy-done.1, bf16[128,4096]{1,0:T(8,128)(2,1)S(1)} %bitcast.8), custom_call_target="tpu_custom_call" | custom-call | flops 2147483648 | bytes 8388608 | tf_op jit(solution)/shard_map/project/pallas_call | solution.py:56
  11.2 0.0 copy-done
  11.2 0.0 copy-done.4
  11.2 1.4 %fusion.2 = bf16[2,1024,64]{1,2,0:T(8,128)(2,1)S(1)} fusion(bf16[2,64,1024]{2,1,0:T(8,128)(2,1)S(1)} %copy-done, bf16[1024,2,1024]{2,1,0:T(2,128)(2,1)S(1)} %copy-done.4), kind=kOutput, calls=%fused_computation.2 | convolution fusion | flops 268566528 | bytes 4718592 | tf_op jit(solution)/shard_map/tmk,mrk->tmr/dot_general | solution.py:314
  12.7 0.5 %statistics.1 = (f32[40,128]{1,0:T(8,128)S(1)}, f32[40,128]{1,0:T(8,128)S(1)}, f32[64,512]{1,0:T(8,128)S(1)}, f32[64,512]{1,0:T(8,128)S(1)}) custom-call(bf16[128,1024]{1,0:T(8,128)(2,1)S(1)} %project.1.acts_ref, bf16[128,1024]{1,0:T(8,128)(2,1)S(1)} %bitcast.9), custom_call_target="tpu_custom_call" | custom-call | tf_op jit(solution)/shard_map/statistics/pallas_call | solution.py:125
  13.2 0.1 collective-permute-start
  14.0 0.5 %collective-permute-done = f32[40,128]{1,0:T(8,128)S(1)} collective-permute-done((f32[40,128]{1,0:T(8,128)S(1)}, f32[40,128]{1,0:T(8,128)S(1)}, u32[]{:S(2)}, u32[]{:S(2)}) %collective-permute-start) | collective-permute-done | bytes 20512 | tf_op jit(solution)/shard_map/ppermute | solution.py:288
  14.5 0.2 collective-permute-start.5
  14.6 0.0 collective-permute-done.1
  14.6 0.3 %collective-permute-start.2 = (f32[40,128]{1,0:T(8,128)S(1)}, f32[40,128]{1,0:T(8,128)S(1)}, u32[]{:S(2)}, u32[]{:S(2)}) collective-permute-start(f32[40,128]{1,0:T(8,128)S(1)} %add.9), channel_id=1, source_target_pairs={{0,2},{1,3},{2,0},{3,1},{4,6},{5,7},{6,4},{7,5},{8,10},{9,11},{10,... | collective-permute-start | bytes 61448 | tf_op jit(solution)/shard_map/ppermute | solution.py:288
  15.0 2.1 %collective-permute-done.3 = bf16[8,8192]{1,0:T(8,128)(2,1)S(1)} collective-permute-done((bf16[8,8192]{1,0:T(8,128)(2,1)S(1)}, bf16[8,8192]{1,0:T(8,128)(2,1)S(1)}, u32[]{:S(2)}, u32[]{:S(2)}) %collective-permute-start.3) | collective-permute-done | bytes 131104 | tf_op jit(solution)/shard_map/ppermute | solution.py:288
  17.1 0.1 collective-permute-start.4
  17.2 0.0 collective-permute-done.9
  17.2 0.5 %collective-permute-start.10 = (bf16[8,4096]{1,0:T(8,128)(2,1)S(1)}, bf16[8,4096]{1,0:T(8,128)(2,1)S(1)}, u32[]{:S(2)}, u32[]{:S(2)}) collective-permute-start(bf16[8,4096]{1,0:T(8,128)(2,1)S(1)} %get-tuple-element.50), channel_id=1, source_target_pairs={{0,1},{1,0},{2,3},{3,2},{4,5},{5,4},{6,7},{7,6},{8,9},{9,8},{10,11... | collective-permute-start | bytes 196616 | tf_op jit(solution)/shard_map/ppermute | solution.py:288
  17.8 0.0 collective-permute-done.12
  17.8 0.1 collective-permute-start.13
  17.9 0.6 %collective-permute-done.2 = f32[40,128]{1,0:T(8,128)S(1)} collective-permute-done((f32[40,128]{1,0:T(8,128)S(1)}, f32[40,128]{1,0:T(8,128)S(1)}, u32[]{:S(2)}, u32[]{:S(2)}) %collective-permute-start.2) | collective-permute-done | bytes 20512 | tf_op jit(solution)/shard_map/ppermute | solution.py:288
  18.5 0.2 collective-permute-done.10
  18.7 1.6 %collective-permute-start.11 = (bf16[16,4096]{1,0:T(8,128)(2,1)S(1)}, bf16[16,4096]{1,0:T(8,128)(2,1)S(1)}, u32[]{:S(2)}, u32[]{:S(2)}) collective-permute-start(bf16[16,4096]{1,0:T(8,128)(2,1)S(1)} %pad_maximum_fusion.3.refs_1_), channel_id=1, source_target_pairs={{0,2},{1,3},{2,0},{3,1},{4,6},{5,7},{6,4},{7,5},{8,10},{9,11},{10,... | collective-permute-start | bytes 393224 | tf_op jit(solution)/shard_map/ppermute | solution.py:288
  20.3 0.0 collective-permute-done.4
  20.3 0.0 collective-permute-done.5.recv_ref
  20.3 2.5 %collective-permute-start.6 = (f32[40,128]{1,0:T(8,128)S(1)}, f32[40,128]{1,0:T(8,128)S(1)}, u32[]{:S(2)}, u32[]{:S(2)}) collective-permute-start(f32[40,128]{1,0:T(8,128)S(1)} %add.10.refs_0_), channel_id=1, source_target_pairs={{0,12},{1,13},{2,14},{3,15},{4,8},{5,9},{6,10},{7,11},{8,4},{9,5},... | collective-permute-start | bytes 61448 | tf_op jit(solution)/shard_map/ppermute | solution.py:288
  22.9 0.0 collective-permute-start.7
  22.9 1.9 %collective-permute-start.8 = (f32[40,128]{1,0:T(8,128)S(1)}, f32[40,128]{1,0:T(8,128)S(1)}, u32[]{:S(2)}, u32[]{:S(2)}) collective-permute-start(f32[40,128]{1,0:T(8,128)S(1)} %add.10.refs_0_), channel_id=1, source_target_pairs={{0,4},{1,5},{2,6},{3,7},{4,0},{5,1},{6,2},{7,3},{8,12},{9,13},{10,... | collective-permute-start | bytes 61448 | tf_op jit(solution)/shard_map/ppermute | solution.py:288
  24.8 0.0 collective-permute-done.13
  24.8 0.5 %collective-permute-start.14 = (bf16[32,4096]{1,0:T(8,128)(2,1)S(1)}, bf16[32,4096]{1,0:T(8,128)(2,1)S(1)}, u32[]{:S(2)}, u32[]{:S(2)}) collective-permute-start(bf16[32,4096]{1,0:T(8,128)(2,1)S(1)} %pad_maximum_fusion.refs_3_), channel_id=1, source_target_pairs={{0,2},{1,3},{2,0},{3,1},{4,6},{5,7},{6,4},{7,5},{8,10},{9,11},{10,... | collective-permute-start | bytes 786440 | tf_op jit(solution)/shard_map/ppermute | solution.py:288
  25.3 0.7 %collective-permute-done.6.refs_1_ = f32[40,128]{1,0:T(8,128)S(1)} collective-permute-done((f32[40,128]{1,0:T(8,128)S(1)}, f32[40,128]{1,0:T(8,128)S(1)}, u32[]{:S(2)}, u32[]{:S(2)}) %collective-permute-start.6) | collective-permute-done | bytes 20512 | tf_op jit(solution)/shard_map/ppermute | solution.py:288
  26.0 1.6 %collective-permute-done.7.refs_2_ = f32[40,128]{1,0:T(8,128)S(1)} collective-permute-done((f32[40,128]{1,0:T(8,128)S(1)}, f32[40,128]{1,0:T(8,128)S(1)}, u32[]{:S(2)}, u32[]{:S(2)}) %collective-permute-start.7) | collective-permute-done | bytes 20512 | tf_op jit(solution)/shard_map/ppermute | solution.py:288
  27.5 0.0 collective-permute-done.8.refs_3_
  27.5 0.0 collective-permute-done.11.refs_2_
  27.5 2.7 %inverse.1.inv_ref = f32[64,128]{1,0:T(8,128)S(1)} custom-call(f32[40,128]{1,0:T(8,128)S(1)} %add.10.refs_0_, f32[40,128]{1,0:T(8,128)S(1)} %collective-permute-done.6.refs_1_, f32[40,128]{1,0:T(8,128)S(1)} %collective-permute-done.7.refs_2_, f32[40,128]{1,0:T(8,128)S(1)} %collective-permute-done.8.refs_3_), custom_call_target="tpu_custom_call" | custom-call | tf_op jit(solution)/shard_map/inverse/pallas_call | solution.py:199
  30.2 0.8 %precondition.1.flat_ref = bf16[16,4096]{1,0:T(8,128)(2,1)S(1)} custom-call(f32[64,128]{1,0:T(8,128)S(1)} %inverse.1.inv_ref, f32[64,512]{1,0:T(8,128)S(1)} %get-tuple-element.40.keep_ref, f32[64,512]{1,0:T(8,128)S(1)} %collective-permute-done.5.recv_ref), custom_call_target="tpu_custom_call" | custom-call | tf_op jit(solution)/shard_map/precondition/pallas_call | solution.py:251
  31.1 1.2 %collective-permute-done.14.refs_4_ = bf16[32,4096]{1,0:T(8,128)(2,1)S(1)} collective-permute-done((bf16[32,4096]{1,0:T(8,128)(2,1)S(1)}, bf16[32,4096]{1,0:T(8,128)(2,1)S(1)}, u32[]{:S(2)}, u32[]{:S(2)}) %collective-permute-start.14) | collective-permute-done | bytes 262176 | tf_op jit(solution)/shard_map/ppermute | solution.py:288
  32.2 0.5 %scores.1 = f32[16,128]{1,0:T(8,128)S(1)} custom-call(bf16[16,4096]{1,0:T(8,128)(2,1)S(1)} %precondition.1.flat_ref, bf16[32,4096]{1,0:T(8,128)(2,1)S(1)} %pad_maximum_fusion.1.refs_0_, bf16[16,4096]{1,0:T(8,128)(2,1)S(1)} %pad_maximum_fusion.3.refs_1_, bf16[16,4096]{1,0:T(8,128)(2,1)S(1)} %collective-permute-done.11.refs_2_, ...), custom_call_target="tpu_custom_call" | custom-call | tf_op jit(solution)/shard_map/scores/pallas_call | solution.py:276
  32.7 0.0 collective-permute-start.15
  32.7 1.2 %collective-permute-done.15 = f32[8,128]{1,0:T(8,128)S(1)} collective-permute-done((f32[8,128]{1,0:T(8,128)S(1)}, f32[8,128]{1,0:T(8,128)S(1)}, u32[]{:S(2)}, u32[]{:S(2)}) %collective-permute-start.15) | collective-permute-done | bytes 4128 | tf_op jit(solution)/shard_map/ppermute | solution.py:288
  33.9 0.6 %slice_add_fusion = f32[8,128]{1,0:T(8,128)} fusion(f32[8,128]{1,0:T(8,128)S(1)} %collective-permute-done.15, f32[16,128]{1,0:T(8,128)S(1)} %scores.1), kind=kLoop, calls=%fused_computation.18 | loop fusion | flops 1024 | bytes 12288 | tf_op jit(solution)/shard_map/add | solution.py:340
  (15 shorter events, 0.2 us)
Async XLA Ops:
  0.0 11.2 %copy-start = (bf16[2,64,1024]{2,1,0:T(8,128)(2,1)S(1)}, bf16[2,64,1024]{2,1,0:T(8,128)(2,1)}, u32[]{:S(2)}) copy-start(bf16[2,64,1024]{2,1,0:T(8,128)(2,1)} %param.8) | copy-start | bytes 786436
  0.0 0.9 %copy-start.3 = (bf16[8,8192]{1,0:T(8,128)(2,1)S(1)}, bf16[8,8192]{1,0:T(8,128)(2,1)}, u32[]{:S(2)}) copy-start(bf16[8,8192]{1,0:T(8,128)(2,1)} %param.9) | copy-start | bytes 393220
  0.0 8.3 %copy-start.1 = (bf16[1024,4096]{1,0:T(8,128)(2,1)S(1)}, bf16[1024,4096]{1,0:T(8,128)(2,1)}, u32[]{:S(2)}) copy-start(bf16[1024,4096]{1,0:T(8,128)(2,1)} %x_ref.1) | copy-start | bytes 25165828
  0.0 8.3 %copy-start.2 = (bf16[2,64,4096]{2,1,0:T(8,128)(2,1)S(1)}, bf16[2,64,4096]{2,1,0:T(8,128)(2,1)}, u32[]{:S(2)}) copy-start(bf16[2,64,4096]{2,1,0:T(8,128)(2,1)} %param.7) | copy-start | bytes 3145732
  1.0 13.7 %collective-permute-start.1 = (bf16[8,8192]{1,0:T(8,128)(2,1)S(1)}, bf16[8,8192]{1,0:T(8,128)(2,1)S(1)}, u32[]{:S(2)}, u32[]{:S(2)}) collective-permute-start(bf16[8,8192]{1,0:T(8,128)(2,1)S(1)} %copy-done.3), channel_id=1, source_target_pairs={{0,12},{1,13},{2,14},{3,15},{4,8},{5,9},{6,10},{7,11},{8,4},{9,5},... | collective-permute-start | bytes 393224 | tf_op jit(solution)/shard_map/ppermute | solution.py:288
  6.0 11.1 %collective-permute-start.3 = (bf16[8,8192]{1,0:T(8,128)(2,1)S(1)}, bf16[8,8192]{1,0:T(8,128)(2,1)S(1)}, u32[]{:S(2)}, u32[]{:S(2)}) collective-permute-start(bf16[8,8192]{1,0:T(8,128)(2,1)S(1)} %copy-done.3), channel_id=1, source_target_pairs={{0,8},{1,9},{2,10},{3,11},{4,12},{5,13},{6,14},{7,15},{8,0},{9,1},... | collective-permute-start | bytes 393224 | tf_op jit(solution)/shard_map/ppermute | solution.py:288
  6.0 11.2 %collective-permute-start.9 = (bf16[8,8192]{1,0:T(8,128)(2,1)S(1)}, bf16[8,8192]{1,0:T(8,128)(2,1)S(1)}, u32[]{:S(2)}, u32[]{:S(2)}) collective-permute-start(bf16[8,8192]{1,0:T(8,128)(2,1)S(1)} %copy-done.3), channel_id=1, source_target_pairs={{0,4},{1,5},{2,6},{3,7},{4,0},{5,1},{6,2},{7,3},{8,12},{9,13},{10,... | collective-permute-start | bytes 393224 | tf_op jit(solution)/shard_map/ppermute | solution.py:288
  6.6 11.2 %collective-permute-start.12 = (bf16[8,8192]{1,0:T(8,128)(2,1)S(1)}, bf16[8,8192]{1,0:T(8,128)(2,1)S(1)}, u32[]{:S(2)}, u32[]{:S(2)}) collective-permute-start(bf16[8,8192]{1,0:T(8,128)(2,1)S(1)} %copy-done.3), channel_id=1, source_target_pairs={{0,2},{1,3},{2,0},{3,1},{4,6},{5,7},{6,4},{7,5},{8,10},{9,11},{10,... | collective-permute-start | bytes 393224 | tf_op jit(solution)/shard_map/ppermute | solution.py:288
  8.3 2.9 %copy-start.4 = (bf16[1024,2,1024]{2,1,0:T(2,128)(2,1)S(1)}, bf16[1024,2,1024]{2,1,0:T(2,128)(2,1)}, u32[]{:S(2)}) copy-start(bf16[1024,2,1024]{2,1,0:T(2,128)(2,1)} %param.6) | copy-start | bytes 12582916
  13.2 1.3 %collective-permute-start = (f32[40,128]{1,0:T(8,128)S(1)}, f32[40,128]{1,0:T(8,128)S(1)}, u32[]{:S(2)}, u32[]{:S(2)}) collective-permute-start(f32[40,128]{1,0:T(8,128)S(1)} %get-tuple-element.29), channel_id=1, source_target_pairs={{0,1},{1,0},{2,3},{3,2},{4,5},{5,4},{6,7},{7,6},{8,9},{9,8},{10,11... | collective-permute-start | bytes 61448 | tf_op jit(solution)/shard_map/ppermute | solution.py:288
  14.5 5.8 %collective-permute-start.5 = (f32[64,512]{1,0:T(8,128)S(1)}, f32[64,512]{1,0:T(8,128)S(1)}, u32[]{:S(2)}, u32[]{:S(2)}) collective-permute-start(f32[64,512]{1,0:T(8,128)S(1)} %get-tuple-element.34), channel_id=1, source_target_pairs={{0,1},{1,0},{2,3},{3,2},{4,5},{5,4},{6,7},{7,6},{8,9},{9,8},{10,11... | collective-permute-start | bytes 393224 | tf_op jit(solution)/shard_map/ppermute | solution.py:288
  14.6 3.8 %collective-permute-start.2 = (f32[40,128]{1,0:T(8,128)S(1)}, f32[40,128]{1,0:T(8,128)S(1)}, u32[]{:S(2)}, u32[]{:S(2)}) collective-permute-start(f32[40,128]{1,0:T(8,128)S(1)} %add.9), channel_id=1, source_target_pairs={{0,2},{1,3},{2,0},{3,1},{4,6},{5,7},{6,4},{7,5},{8,10},{9,11},{10,... | collective-permute-start | bytes 61448 | tf_op jit(solution)/shard_map/ppermute | solution.py:288
  17.1 3.2 %collective-permute-start.4 = (bf16[16,4096]{1,0:T(8,128)(2,1)S(1)}, bf16[16,4096]{1,0:T(8,128)(2,1)S(1)}, u32[]{:S(2)}, u32[]{:S(2)}) collective-permute-start(bf16[16,4096]{1,0:T(8,128)(2,1)S(1)} %pad_maximum_fusion.2), channel_id=1, source_target_pairs={{0,1},{1,0},{2,3},{3,2},{4,5},{5,4},{6,7},{7,6},{8,9},{9,8},{10,11... | collective-permute-start | bytes 393224 | tf_op jit(solution)/shard_map/ppermute | solution.py:288
  17.2 1.5 %collective-permute-start.10 = (bf16[8,4096]{1,0:T(8,128)(2,1)S(1)}, bf16[8,4096]{1,0:T(8,128)(2,1)S(1)}, u32[]{:S(2)}, u32[]{:S(2)}) collective-permute-start(bf16[8,4096]{1,0:T(8,128)(2,1)S(1)} %get-tuple-element.50), channel_id=1, source_target_pairs={{0,1},{1,0},{2,3},{3,2},{4,5},{5,4},{6,7},{7,6},{8,9},{9,8},{10,11... | collective-permute-start | bytes 196616 | tf_op jit(solution)/shard_map/ppermute | solution.py:288
  17.8 7.0 %collective-permute-start.13 = (bf16[16,4096]{1,0:T(8,128)(2,1)S(1)}, bf16[16,4096]{1,0:T(8,128)(2,1)S(1)}, u32[]{:S(2)}, u32[]{:S(2)}) collective-permute-start(bf16[16,4096]{1,0:T(8,128)(2,1)S(1)} %pad_maximum_fusion.4), channel_id=1, source_target_pairs={{0,1},{1,0},{2,3},{3,2},{4,5},{5,4},{6,7},{7,6},{8,9},{9,8},{10,11... | collective-permute-start | bytes 393224 | tf_op jit(solution)/shard_map/ppermute | solution.py:288
  18.7 8.9 %collective-permute-start.11 = (bf16[16,4096]{1,0:T(8,128)(2,1)S(1)}, bf16[16,4096]{1,0:T(8,128)(2,1)S(1)}, u32[]{:S(2)}, u32[]{:S(2)}) collective-permute-start(bf16[16,4096]{1,0:T(8,128)(2,1)S(1)} %pad_maximum_fusion.3.refs_1_), channel_id=1, source_target_pairs={{0,2},{1,3},{2,0},{3,1},{4,6},{5,7},{6,4},{7,5},{8,10},{9,11},{10,... | collective-permute-start | bytes 393224 | tf_op jit(solution)/shard_map/ppermute | solution.py:288
  20.3 5.6 %collective-permute-start.6 = (f32[40,128]{1,0:T(8,128)S(1)}, f32[40,128]{1,0:T(8,128)S(1)}, u32[]{:S(2)}, u32[]{:S(2)}) collective-permute-start(f32[40,128]{1,0:T(8,128)S(1)} %add.10.refs_0_), channel_id=1, source_target_pairs={{0,12},{1,13},{2,14},{3,15},{4,8},{5,9},{6,10},{7,11},{8,4},{9,5},... | collective-permute-start | bytes 61448 | tf_op jit(solution)/shard_map/ppermute | solution.py:288
  22.9 4.7 %collective-permute-start.7 = (f32[40,128]{1,0:T(8,128)S(1)}, f32[40,128]{1,0:T(8,128)S(1)}, u32[]{:S(2)}, u32[]{:S(2)}) collective-permute-start(f32[40,128]{1,0:T(8,128)S(1)} %add.10.refs_0_), channel_id=1, source_target_pairs={{0,8},{1,9},{2,10},{3,11},{4,12},{5,13},{6,14},{7,15},{8,0},{9,1},... | collective-permute-start | bytes 61448 | tf_op jit(solution)/shard_map/ppermute | solution.py:288
  22.9 4.7 %collective-permute-start.8 = (f32[40,128]{1,0:T(8,128)S(1)}, f32[40,128]{1,0:T(8,128)S(1)}, u32[]{:S(2)}, u32[]{:S(2)}) collective-permute-start(f32[40,128]{1,0:T(8,128)S(1)} %add.10.refs_0_), channel_id=1, source_target_pairs={{0,4},{1,5},{2,6},{3,7},{4,0},{5,1},{6,2},{7,3},{8,12},{9,13},{10,... | collective-permute-start | bytes 61448 | tf_op jit(solution)/shard_map/ppermute | solution.py:288
  24.8 7.4 %collective-permute-start.14 = (bf16[32,4096]{1,0:T(8,128)(2,1)S(1)}, bf16[32,4096]{1,0:T(8,128)(2,1)S(1)}, u32[]{:S(2)}, u32[]{:S(2)}) collective-permute-start(bf16[32,4096]{1,0:T(8,128)(2,1)S(1)} %pad_maximum_fusion.refs_3_), channel_id=1, source_target_pairs={{0,2},{1,3},{2,0},{3,1},{4,6},{5,7},{6,4},{7,5},{8,10},{9,11},{10,... | collective-permute-start | bytes 786440 | tf_op jit(solution)/shard_map/ppermute | solution.py:288
  32.7 1.2 %collective-permute-start.15 = (f32[8,128]{1,0:T(8,128)S(1)}, f32[8,128]{1,0:T(8,128)S(1)}, u32[]{:S(2)}, u32[]{:S(2)}) collective-permute-start(f32[8,128]{1,0:T(8,128)S(1)} %slice.9), channel_id=1, source_target_pairs={{0,1},{1,0},{2,3},{3,2},{4,5},{5,4},{6,7},{7,6},{8,9},{9,8},{10,11... | collective-permute-start | bytes 12296 | tf_op jit(solution)/shard_map/ppermute | solution.py:288

commit v16 on v15

--- a/solution.py
+++ b/solution.py
@@ -323,15 +323,15 @@
     column[-1] = beside
     local = fold([0, -1])
     near = fold([1])
-    across = exchange(near, 2)
+    mine = jnp.concatenate([near, far], axis=0)
+    across = exchange(mine, 2)
     covs = [cov] + [exchange(cov, slab * GROUP) for slab in reversed(range(1, slabs))]
-    covs, across = lax.optimization_barrier((covs, across))
     inv = inverse(covs, local_tokens * devices)
-    gathered = [local, near, across, far, exchange(far, 2)]
+    gathered = [local, mine, across]
     order = [0, 2, 1, 3] + [
         slab * GROUP + 2 * over + core
+        for over in range(2)
         for part in ([1], far_slabs)
-        for over in range(2)
         for core in range(2)
         for slab in part
     ]

time: 34.6 us -> 35.9 us (1.038)
  waiting for transfers between devices: 7.92 us -> 9.65 us
  starting transfers between devices: 15.2 us -> 14.7 us
    ppermute x16 -> x15, waiting for transfers between devices: 7.92 us -> 9.65 us  [exchange(): lax.ppermute(value, 'dp', [(i, i ^ distance) for i in range(lax.axis_size...]
    ppermute x16 -> x15, starting transfers between devices: 15.2 us -> 14.7 us  [exchange(): lax.ppermute(value, 'dp', [(i, i ^ distance) for i in range(lax.axis_size...]
  transfers between devices with their start and end apart: 16 -> 15, of which waited for: 8 -> 6; matrix products, arithmetic and copies ran while one was open for 5% -> 5% of each run, Pallas kernels for 20% -> 19%
where the time goes in v16:
time: 35.9 us; the launch traced here: 35.7 us
  starting transfers between devices  14.7 us (41%)
  waiting for transfers between devices  9.65 us (27%)
  Pallas kernels  7.88 us (22%)
  matrix products  1.44 us (4%)
  between operations  0.82 us (2%)
  other arithmetic  0.77 us (2%)
  local copies, waits for them, and re-layouts  0.43 us (1%)
    ppermute x15, starting transfers between devices, exchange(): lax.ppermute(value, 'dp', [(i, i ^ distance) for i in range(lax.axis_size...  14.7 us
    ppermute x15, waiting for transfers between devices, exchange(): lax.ppermute(value, 'dp', [(i, i ^ distance) for i in range(lax.axis_size...  9.65 us
    pallas_call x1, Pallas kernels, project(): pl.pallas_call(project_kernel, in_specs=[vmem, vmem], out_specs=vmem, out...  2.89 us
    pallas_call x1, Pallas kernels, inverse(): pl.pallas_call(functools.partial(inverse_kernel, total_tokens), in_specs=...  2.65 us
    dot_general x1, matrix products, per_device(): jnp.einsum('tmk,mrk->tmr', out_grads, out_proj, preferred_element_type=F32)  1.44 us
    pallas_call x1, Pallas kernels, precondition(): pl.pallas_call(precondition_kernel, in_specs=[vmem] * (1 + len(moments)),...  0.83 us
  transfers between devices with their start and end apart: 15, of which 6 were waited for; matrix products, arithmetic and copies ran while one was open for 5% of the time, Pallas kernels for 19%

profile of v16, /device:TPU:0, one launch (start us, length us, event | category | flops | bytes accessed | tf_op | source)
XLA Modules:
  0.0 35.7 jit_solution(11374474962966457873)
XLA Ops:
  0.0 0.0 copy-start
  0.0 0.0 copy-start.3
  0.0 0.0 copy-start.1
  0.0 0.0 copy-start.2
  0.0 0.5 %own_place.1 = s32[1]{0:T(128)} custom-call(), custom_call_target="tpu_custom_call" | custom-call | flops 80000000000 | bytes 8 | tf_op jit(solution)/shard_map/own_place/pallas_call | solution.py:37
  0.5 0.4 %copy-done.3 = bf16[8,8192]{1,0:T(8,128)(2,1)S(1)} copy-done((bf16[8,8192]{1,0:T(8,128)(2,1)S(1)}, bf16[8,8192]{1,0:T(8,128)(2,1)}, u32[]{:S(2)}) %copy-start.3) | copy-done | bytes 131096
  1.0 5.0 %collective-permute-start.1 = (bf16[8,8192]{1,0:T(8,128)(2,1)S(1)}, bf16[8,8192]{1,0:T(8,128)(2,1)S(1)}, u32[]{:S(2)}, u32[]{:S(2)}) collective-permute-start(bf16[8,8192]{1,0:T(8,128)(2,1)S(1)} %copy-done.3), channel_id=1, source_target_pairs={{0,12},{1,13},{2,14},{3,15},{4,8},{5,9},{6,10},{7,11},{8,4},{9,5},... | collective-permute-start | bytes 393224 | tf_op jit(solution)/shard_map/ppermute | solution.py:288
  6.0 0.0 collective-permute-start.3
  6.0 1.5 %collective-permute-start.9 = (bf16[8,8192]{1,0:T(8,128)(2,1)S(1)}, bf16[8,8192]{1,0:T(8,128)(2,1)S(1)}, u32[]{:S(2)}, u32[]{:S(2)}) collective-permute-start(bf16[8,8192]{1,0:T(8,128)(2,1)S(1)} %copy-done.3), channel_id=1, source_target_pairs={{0,2},{1,3},{2,0},{3,1},{4,6},{5,7},{6,4},{7,5},{8,10},{9,11},{10,... | collective-permute-start | bytes 393224 | tf_op jit(solution)/shard_map/ppermute | solution.py:288
  7.5 0.8 %collective-permute-start.11 = (bf16[8,8192]{1,0:T(8,128)(2,1)S(1)}, bf16[8,8192]{1,0:T(8,128)(2,1)S(1)}, u32[]{:S(2)}, u32[]{:S(2)}) collective-permute-start(bf16[8,8192]{1,0:T(8,128)(2,1)S(1)} %copy-done.3), channel_id=1, source_target_pairs={{0,4},{1,5},{2,6},{3,7},{4,0},{5,1},{6,2},{7,3},{8,12},{9,13},{10,... | collective-permute-start | bytes 393224 | tf_op jit(solution)/shard_map/ppermute | solution.py:288
  8.3 0.0 copy-done.1
  8.3 0.0 copy-done.2
  8.3 0.0 copy-start.4
  8.3 2.9 %project.1.acts_ref = bf16[128,1024]{1,0:T(8,128)(2,1)S(1)} custom-call(bf16[1024,4096]{1,0:T(8,128)(2,1)S(1)} %copy-done.1, bf16[128,4096]{1,0:T(8,128)(2,1)S(1)} %bitcast.8), custom_call_target="tpu_custom_call" | custom-call | flops 2147483648 | bytes 8388608 | tf_op jit(solution)/shard_map/project/pallas_call | solution.py:56
  11.2 0.0 copy-done
  11.2 0.0 copy-done.4
  11.2 1.4 %fusion.2 = bf16[2,1024,64]{1,2,0:T(8,128)(2,1)S(1)} fusion(bf16[2,64,1024]{2,1,0:T(8,128)(2,1)S(1)} %copy-done, bf16[1024,2,1024]{2,1,0:T(2,128)(2,1)S(1)} %copy-done.4), kind=kOutput, calls=%fused_computation.2 | convolution fusion | flops 268566528 | bytes 4718592 | tf_op jit(solution)/shard_map/tmk,mrk->tmr/dot_general | solution.py:314
  12.7 0.5 %statistics.1 = (f32[40,128]{1,0:T(8,128)S(1)}, f32[40,128]{1,0:T(8,128)S(1)}, f32[64,512]{1,0:T(8,128)S(1)}, f32[64,512]{1,0:T(8,128)S(1)}) custom-call(bf16[128,1024]{1,0:T(8,128)(2,1)S(1)} %project.1.acts_ref, bf16[128,1024]{1,0:T(8,128)(2,1)S(1)} %bitcast.9), custom_call_target="tpu_custom_call" | custom-call | tf_op jit(solution)/shard_map/statistics/pallas_call | solution.py:125
  13.2 0.1 collective-permute-start
  14.0 0.5 %collective-permute-done = f32[40,128]{1,0:T(8,128)S(1)} collective-permute-done((f32[40,128]{1,0:T(8,128)S(1)}, f32[40,128]{1,0:T(8,128)S(1)}, u32[]{:S(2)}, u32[]{:S(2)}) %collective-permute-start) | collective-permute-done | bytes 20512 | tf_op jit(solution)/shard_map/ppermute | solution.py:288
  14.5 0.2 collective-permute-start.5
  14.6 0.0 collective-permute-done.1
  14.6 0.3 collective-permute-start.2
  15.0 2.1 %collective-permute-done.3 = bf16[8,8192]{1,0:T(8,128)(2,1)S(1)} collective-permute-done((bf16[8,8192]{1,0:T(8,128)(2,1)S(1)}, bf16[8,8192]{1,0:T(8,128)(2,1)S(1)}, u32[]{:S(2)}, u32[]{:S(2)}) %collective-permute-start.3) | collective-permute-done | bytes 131104 | tf_op jit(solution)/shard_map/ppermute | solution.py:288
  17.1 0.1 collective-permute-start.4
  17.2 0.0 collective-permute-done.9
  17.2 0.5 %collective-permute-start.10 = (bf16[16,4096]{1,0:T(8,128)(2,1)S(1)}, bf16[16,4096]{1,0:T(8,128)(2,1)S(1)}, u32[]{:S(2)}, u32[]{:S(2)}) collective-permute-start(bf16[16,4096]{1,0:T(8,128)(2,1)S(1)} %pad_maximum_fusion.4), channel_id=1, source_target_pairs={{0,1},{1,0},{2,3},{3,2},{4,5},{5,4},{6,7},{7,6},{8,9},{9,8},{10,11... | collective-permute-start | bytes 393224 | tf_op jit(solution)/shard_map/ppermute | solution.py:288
  17.8 0.0 collective-permute-done.11
  17.8 0.1 collective-permute-start.12
  17.9 0.6 %collective-permute-done.2 = f32[40,128]{1,0:T(8,128)S(1)} collective-permute-done((f32[40,128]{1,0:T(8,128)S(1)}, f32[40,128]{1,0:T(8,128)S(1)}, u32[]{:S(2)}, u32[]{:S(2)}) %collective-permute-start.2) | collective-permute-done | bytes 20512 | tf_op jit(solution)/shard_map/ppermute | solution.py:288
  18.5 0.0 collective-permute-done.4
  18.6 0.0 collective-permute-done.5.recv_ref
  18.6 3.6 %collective-permute-start.6 = (f32[40,128]{1,0:T(8,128)S(1)}, f32[40,128]{1,0:T(8,128)S(1)}, u32[]{:S(2)}, u32[]{:S(2)}) collective-permute-start(f32[40,128]{1,0:T(8,128)S(1)} %add.10.refs_0_), channel_id=1, source_target_pairs={{0,12},{1,13},{2,14},{3,15},{4,8},{5,9},{6,10},{7,11},{8,4},{9,5},... | collective-permute-start | bytes 61448 | tf_op jit(solution)/shard_map/ppermute | solution.py:288
  22.2 0.0 collective-permute-start.7
  22.2 0.8 %collective-permute-start.8 = (f32[40,128]{1,0:T(8,128)S(1)}, f32[40,128]{1,0:T(8,128)S(1)}, u32[]{:S(2)}, u32[]{:S(2)}) collective-permute-start(f32[40,128]{1,0:T(8,128)S(1)} %add.10.refs_0_), channel_id=1, source_target_pairs={{0,4},{1,5},{2,6},{3,7},{4,0},{5,1},{6,2},{7,3},{8,12},{9,13},{10,... | collective-permute-start | bytes 61448 | tf_op jit(solution)/shard_map/ppermute | solution.py:288
  23.0 0.0 collective-permute-done.12
  23.1 1.6 %collective-permute-start.13 = (bf16[48,4096]{1,0:T(8,128)(2,1)S(1)}, bf16[48,4096]{1,0:T(8,128)(2,1)S(1)}, u32[]{:S(2)}, u32[]{:S(2)}) collective-permute-start(bf16[48,4096]{1,0:T(8,128)(2,1)S(1)} %pad_maximum_fusion.refs_1_), channel_id=1, source_target_pairs={{0,2},{1,3},{2,0},{3,1},{4,6},{5,7},{6,4},{7,5},{8,10},{9,11},{10,... | collective-permute-start | bytes 1179656 | tf_op jit(solution)/shard_map/ppermute | solution.py:288
  24.6 0.0 collective-permute-done.10
  24.7 0.0 collective-permute-done.6.refs_1_
  24.7 2.2 %collective-permute-done.7.refs_2_ = f32[40,128]{1,0:T(8,128)S(1)} collective-permute-done((f32[40,128]{1,0:T(8,128)S(1)}, f32[40,128]{1,0:T(8,128)S(1)}, u32[]{:S(2)}, u32[]{:S(2)}) %collective-permute-start.7) | collective-permute-done | bytes 20512 | tf_op jit(solution)/shard_map/ppermute | solution.py:288
  26.9 0.0 collective-permute-done.8.refs_3_
  26.9 2.7 %inverse.1.inv_ref = f32[64,128]{1,0:T(8,128)S(1)} custom-call(f32[40,128]{1,0:T(8,128)S(1)} %add.10.refs_0_, f32[40,128]{1,0:T(8,128)S(1)} %collective-permute-done.6.refs_1_, f32[40,128]{1,0:T(8,128)S(1)} %collective-permute-done.7.refs_2_, f32[40,128]{1,0:T(8,128)S(1)} %collective-permute-done.8.refs_3_), custom_call_target="tpu_custom_call" | custom-call | tf_op jit(solution)/shard_map/inverse/pallas_call | solution.py:199
  29.5 0.8 %precondition.1.flat_ref = bf16[16,4096]{1,0:T(8,128)(2,1)S(1)} custom-call(f32[64,128]{1,0:T(8,128)S(1)} %inverse.1.inv_ref, f32[64,512]{1,0:T(8,128)S(1)} %get-tuple-element.31.keep_ref, f32[64,512]{1,0:T(8,128)S(1)} %collective-permute-done.5.recv_ref), custom_call_target="tpu_custom_call" | custom-call | tf_op jit(solution)/shard_map/precondition/pallas_call | solution.py:251
  30.4 3.1 %collective-permute-done.13.refs_2_ = bf16[48,4096]{1,0:T(8,128)(2,1)S(1)} collective-permute-done((bf16[48,4096]{1,0:T(8,128)(2,1)S(1)}, bf16[48,4096]{1,0:T(8,128)(2,1)S(1)}, u32[]{:S(2)}, u32[]{:S(2)}) %collective-permute-start.13) | collective-permute-done | bytes 393248 | tf_op jit(solution)/shard_map/ppermute | solution.py:288
  33.4 0.5 %scores.1 = f32[16,128]{1,0:T(8,128)S(1)} custom-call(bf16[16,4096]{1,0:T(8,128)(2,1)S(1)} %precondition.1.flat_ref, bf16[32,4096]{1,0:T(8,128)(2,1)S(1)} %pad_maximum_fusion.2.refs_0_, bf16[48,4096]{1,0:T(8,128)(2,1)S(1)} %pad_maximum_fusion.refs_1_, bf16[48,4096]{1,0:T(8,128)(2,1)S(1)} %collective-permute-done.13.refs_2_), custom_call_target="tpu_custom_call" | custom-call | tf_op jit(solution)/shard_map/scores/pallas_call | solution.py:276
  33.9 0.0 collective-permute-start.14
  34.0 1.2 %collective-permute-done.14 = f32[8,128]{1,0:T(8,128)S(1)} collective-permute-done((f32[8,128]{1,0:T(8,128)S(1)}, f32[8,128]{1,0:T(8,128)S(1)}, u32[]{:S(2)}, u32[]{:S(2)}) %collective-permute-start.14) | collective-permute-done | bytes 4128 | tf_op jit(solution)/shard_map/ppermute | solution.py:288
  35.1 0.6 %slice_add_fusion = f32[8,128]{1,0:T(8,128)} fusion(f32[8,128]{1,0:T(8,128)S(1)} %collective-permute-done.14, f32[16,128]{1,0:T(8,128)S(1)} %scores.1), kind=kLoop, calls=%fused_computation.18 | loop fusion | flops 1024 | bytes 12288 | tf_op jit(solution)/shard_map/add | solution.py:340
  (13 shorter events, 0.2 us)
Async XLA Ops:
  0.0 11.2 %copy-start = (bf16[2,64,1024]{2,1,0:T(8,128)(2,1)S(1)}, bf16[2,64,1024]{2,1,0:T(8,128)(2,1)}, u32[]{:S(2)}) copy-start(bf16[2,64,1024]{2,1,0:T(8,128)(2,1)} %param.8) | copy-start | bytes 786436
  0.0 0.9 %copy-start.3 = (bf16[8,8192]{1,0:T(8,128)(2,1)S(1)}, bf16[8,8192]{1,0:T(8,128)(2,1)}, u32[]{:S(2)}) copy-start(bf16[8,8192]{1,0:T(8,128)(2,1)} %param.9) | copy-start | bytes 393220
  0.0 8.3 %copy-start.1 = (bf16[1024,4096]{1,0:T(8,128)(2,1)S(1)}, bf16[1024,4096]{1,0:T(8,128)(2,1)}, u32[]{:S(2)}) copy-start(bf16[1024,4096]{1,0:T(8,128)(2,1)} %x_ref.1) | copy-start | bytes 25165828
  0.0 8.3 %copy-start.2 = (bf16[2,64,4096]{2,1,0:T(8,128)(2,1)S(1)}, bf16[2,64,4096]{2,1,0:T(8,128)(2,1)}, u32[]{:S(2)}) copy-start(bf16[2,64,4096]{2,1,0:T(8,128)(2,1)} %param.7) | copy-start | bytes 3145732
  1.0 13.7 %collective-permute-start.1 = (bf16[8,8192]{1,0:T(8,128)(2,1)S(1)}, bf16[8,8192]{1,0:T(8,128)(2,1)S(1)}, u32[]{:S(2)}, u32[]{:S(2)}) collective-permute-start(bf16[8,8192]{1,0:T(8,128)(2,1)S(1)} %copy-done.3), channel_id=1, source_target_pairs={{0,12},{1,13},{2,14},{3,15},{4,8},{5,9},{6,10},{7,11},{8,4},{9,5},... | collective-permute-start | bytes 393224 | tf_op jit(solution)/shard_map/ppermute | solution.py:288
  6.0 11.1 %collective-permute-start.3 = (bf16[8,8192]{1,0:T(8,128)(2,1)S(1)}, bf16[8,8192]{1,0:T(8,128)(2,1)S(1)}, u32[]{:S(2)}, u32[]{:S(2)}) collective-permute-start(bf16[8,8192]{1,0:T(8,128)(2,1)S(1)} %copy-done.3), channel_id=1, source_target_pairs={{0,8},{1,9},{2,10},{3,11},{4,12},{5,13},{6,14},{7,15},{8,0},{9,1},... | collective-permute-start | bytes 393224 | tf_op jit(solution)/shard_map/ppermute | solution.py:288
  6.0 11.2 %collective-permute-start.9 = (bf16[8,8192]{1,0:T(8,128)(2,1)S(1)}, bf16[8,8192]{1,0:T(8,128)(2,1)S(1)}, u32[]{:S(2)}, u32[]{:S(2)}) collective-permute-start(bf16[8,8192]{1,0:T(8,128)(2,1)S(1)} %copy-done.3), channel_id=1, source_target_pairs={{0,2},{1,3},{2,0},{3,1},{4,6},{5,7},{6,4},{7,5},{8,10},{9,11},{10,... | collective-permute-start | bytes 393224 | tf_op jit(solution)/shard_map/ppermute | solution.py:288
  7.5 10.3 %collective-permute-start.11 = (bf16[8,8192]{1,0:T(8,128)(2,1)S(1)}, bf16[8,8192]{1,0:T(8,128)(2,1)S(1)}, u32[]{:S(2)}, u32[]{:S(2)}) collective-permute-start(bf16[8,8192]{1,0:T(8,128)(2,1)S(1)} %copy-done.3), channel_id=1, source_target_pairs={{0,4},{1,5},{2,6},{3,7},{4,0},{5,1},{6,2},{7,3},{8,12},{9,13},{10,... | collective-permute-start | bytes 393224 | tf_op jit(solution)/shard_map/ppermute | solution.py:288
  8.3 2.9 %copy-start.4 = (bf16[1024,2,1024]{2,1,0:T(2,128)(2,1)S(1)}, bf16[1024,2,1024]{2,1,0:T(2,128)(2,1)}, u32[]{:S(2)}) copy-start(bf16[1024,2,1024]{2,1,0:T(2,128)(2,1)} %param.6) | copy-start | bytes 12582916
  13.2 1.3 %collective-permute-start = (f32[40,128]{1,0:T(8,128)S(1)}, f32[40,128]{1,0:T(8,128)S(1)}, u32[]{:S(2)}, u32[]{:S(2)}) collective-permute-start(f32[40,128]{1,0:T(8,128)S(1)} %get-tuple-element.24), channel_id=1, source_target_pairs={{0,1},{1,0},{2,3},{3,2},{4,5},{5,4},{6,7},{7,6},{8,9},{9,8},{10,11... | collective-permute-start | bytes 61448 | tf_op jit(solution)/shard_map/ppermute | solution.py:288
  14.5 4.1 %collective-permute-start.5 = (f32[64,512]{1,0:T(8,128)S(1)}, f32[64,512]{1,0:T(8,128)S(1)}, u32[]{:S(2)}, u32[]{:S(2)}) collective-permute-start(f32[64,512]{1,0:T(8,128)S(1)} %get-tuple-element.29), channel_id=1, source_target_pairs={{0,1},{1,0},{2,3},{3,2},{4,5},{5,4},{6,7},{7,6},{8,9},{9,8},{10,11... | collective-permute-start | bytes 393224 | tf_op jit(solution)/shard_map/ppermute | solution.py:288
  14.6 3.8 %collective-permute-start.2 = (f32[40,128]{1,0:T(8,128)S(1)}, f32[40,128]{1,0:T(8,128)S(1)}, u32[]{:S(2)}, u32[]{:S(2)}) collective-permute-start(f32[40,128]{1,0:T(8,128)S(1)} %add.9), channel_id=1, source_target_pairs={{0,2},{1,3},{2,0},{3,1},{4,6},{5,7},{6,4},{7,5},{8,10},{9,11},{10,... | collective-permute-start | bytes 61448 | tf_op jit(solution)/shard_map/ppermute | solution.py:288
  17.1 1.4 %collective-permute-start.4 = (bf16[16,4096]{1,0:T(8,128)(2,1)S(1)}, bf16[16,4096]{1,0:T(8,128)(2,1)S(1)}, u32[]{:S(2)}, u32[]{:S(2)}) collective-permute-start(bf16[16,4096]{1,0:T(8,128)(2,1)S(1)} %pad_maximum_fusion.3), channel_id=1, source_target_pairs={{0,1},{1,0},{2,3},{3,2},{4,5},{5,4},{6,7},{7,6},{8,9},{9,8},{10,11... | collective-permute-start | bytes 393224 | tf_op jit(solution)/shard_map/ppermute | solution.py:288
  17.2 7.4 %collective-permute-start.10 = (bf16[16,4096]{1,0:T(8,128)(2,1)S(1)}, bf16[16,4096]{1,0:T(8,128)(2,1)S(1)}, u32[]{:S(2)}, u32[]{:S(2)}) collective-permute-start(bf16[16,4096]{1,0:T(8,128)(2,1)S(1)} %pad_maximum_fusion.4), channel_id=1, source_target_pairs={{0,1},{1,0},{2,3},{3,2},{4,5},{5,4},{6,7},{7,6},{8,9},{9,8},{10,11... | collective-permute-start | bytes 393224 | tf_op jit(solution)/shard_map/ppermute | solution.py:288
  17.8 5.2 %collective-permute-start.12 = (bf16[8,4096]{1,0:T(8,128)(2,1)S(1)}, bf16[8,4096]{1,0:T(8,128)(2,1)S(1)}, u32[]{:S(2)}, u32[]{:S(2)}) collective-permute-start(bf16[8,4096]{1,0:T(8,128)(2,1)S(1)} %get-tuple-element.36), channel_id=1, source_target_pairs={{0,1},{1,0},{2,3},{3,2},{4,5},{5,4},{6,7},{7,6},{8,9},{9,8},{10,11... | collective-permute-start | bytes 196616 | tf_op jit(solution)/shard_map/ppermute | solution.py:288
  18.6 6.1 %collective-permute-start.6 = (f32[40,128]{1,0:T(8,128)S(1)}, f32[40,128]{1,0:T(8,128)S(1)}, u32[]{:S(2)}, u32[]{:S(2)}) collective-permute-start(f32[40,128]{1,0:T(8,128)S(1)} %add.10.refs_0_), channel_id=1, source_target_pairs={{0,12},{1,13},{2,14},{3,15},{4,8},{5,9},{6,10},{7,11},{8,4},{9,5},... | collective-permute-start | bytes 61448 | tf_op jit(solution)/shard_map/ppermute | solution.py:288
  22.2 4.7 %collective-permute-start.7 = (f32[40,128]{1,0:T(8,128)S(1)}, f32[40,128]{1,0:T(8,128)S(1)}, u32[]{:S(2)}, u32[]{:S(2)}) collective-permute-start(f32[40,128]{1,0:T(8,128)S(1)} %add.10.refs_0_), channel_id=1, source_target_pairs={{0,8},{1,9},{2,10},{3,11},{4,12},{5,13},{6,14},{7,15},{8,0},{9,1},... | collective-permute-start | bytes 61448 | tf_op jit(solution)/shard_map/ppermute | solution.py:288
  22.2 4.7 %collective-permute-start.8 = (f32[40,128]{1,0:T(8,128)S(1)}, f32[40,128]{1,0:T(8,128)S(1)}, u32[]{:S(2)}, u32[]{:S(2)}) collective-permute-start(f32[40,128]{1,0:T(8,128)S(1)} %add.10.refs_0_), channel_id=1, source_target_pairs={{0,4},{1,5},{2,6},{3,7},{4,0},{5,1},{6,2},{7,3},{8,12},{9,13},{10,... | collective-permute-start | bytes 61448 | tf_op jit(solution)/shard_map/ppermute | solution.py:288
  23.1 10.4 %collective-permute-start.13 = (bf16[48,4096]{1,0:T(8,128)(2,1)S(1)}, bf16[48,4096]{1,0:T(8,128)(2,1)S(1)}, u32[]{:S(2)}, u32[]{:S(2)}) collective-permute-start(bf16[48,4096]{1,0:T(8,128)(2,1)S(1)} %pad_maximum_fusion.refs_1_), channel_id=1, source_target_pairs={{0,2},{1,3},{2,0},{3,1},{4,6},{5,7},{6,4},{7,5},{8,10},{9,11},{10,... | collective-permute-start | bytes 1179656 | tf_op jit(solution)/shard_map/ppermute | solution.py:288
  33.9 1.2 %collective-permute-start.14 = (f32[8,128]{1,0:T(8,128)S(1)}, f32[8,128]{1,0:T(8,128)S(1)}, u32[]{:S(2)}, u32[]{:S(2)}) collective-permute-start(f32[8,128]{1,0:T(8,128)S(1)} %slice.9), channel_id=1, source_target_pairs={{0,1},{1,0},{2,3},{3,2},{4,5},{5,4},{6,7},{7,6},{8,9},{9,8},{10,11... | collective-permute-start | bytes 12296 | tf_op jit(solution)/shard_map/ppermute | solution.py:288

commit v17 on v15

--- a/solution.py
+++ b/solution.py
@@ -298,7 +298,7 @@
     devices = lax.axis_size("dp")
     slabs = devices // GROUP
     device, queries = lax.optimization_barrier((own_place(), queries))
-    near_slabs, far_slabs = [0, 1], [2, 3] + list(range(4, slabs))
+    near_slabs, far_slabs = [1, 2], list(range(3, slabs))
     column = {slab: exchange(queries, slab * GROUP) for slab in [1, 2, 3] + list(range(4, slabs))}
     column[0] = queries
     beside = exchange(queries, 2)
@@ -322,7 +322,7 @@
     cov, far, moments = lax.optimization_barrier((cov, far, moments))
     column[-1] = beside
     local = fold([0, -1])
-    near = fold([1])
+    near = fold(near_slabs)
     across = exchange(near, 2)
     covs = [cov] + [exchange(cov, slab * GROUP) for slab in reversed(range(1, slabs))]
     covs, across = lax.optimization_barrier((covs, across))
@@ -330,7 +330,7 @@
     gathered = [local, near, across, far, exchange(far, 2)]
     order = [0, 2, 1, 3] + [
         slab * GROUP + 2 * over + core
-        for part in ([1], far_slabs)
+        for part in (near_slabs, far_slabs)
         for over in range(2)
         for core in range(2)
         for slab in part

time: 34.6 us -> 39.1 us (1.13)
  waiting for transfers between devices: 7.92 us -> 12.4 us
    ppermute x16, waiting for transfers between devices: 7.92 us -> 12.4 us  [exchange(): lax.ppermute(value, 'dp', [(i, i ^ distance) for i in range(lax.axis_size...]
  transfers between devices with their start and end apart: 16 -> 16, of which waited for: 8 -> 6; matrix products, arithmetic and copies ran while one was open for 5% -> 4% of each run, Pallas kernels for 20% -> 18%
where the time goes in v17:
time: 39.1 us; the launch traced here: 38.9 us
  starting transfers between devices  15.2 us (39%)
  waiting for transfers between devices  12.4 us (32%)
  Pallas kernels  7.89 us (20%)
  matrix products  1.44 us (4%)
  between operations  0.83 us (2%)
  other arithmetic  0.76 us (2%)
  local copies, waits for them, and re-layouts  0.43 us (1%)
    ppermute x16, starting transfers between devices, exchange(): lax.ppermute(value, 'dp', [(i, i ^ distance) for i in range(lax.axis_size...  15.2 us
    ppermute x16, waiting for transfers between devices, exchange(): lax.ppermute(value, 'dp', [(i, i ^ distance) for i in range(lax.axis_size...  12.4 us
    pallas_call x1, Pallas kernels, project(): pl.pallas_call(project_kernel, in_specs=[vmem, vmem], out_specs=vmem, out...  2.89 us
    pallas_call x1, Pallas kernels, inverse(): pl.pallas_call(functools.partial(inverse_kernel, total_tokens), in_specs=...  2.65 us
    dot_general x1, matrix products, per_device(): jnp.einsum('tmk,mrk->tmr', out_grads, out_proj, preferred_element_type=F32)  1.44 us
    pallas_call x1, Pallas kernels, precondition(): pl.pallas_call(precondition_kernel, in_specs=[vmem] * (1 + len(moments)),...  0.83 us
  transfers between devices with their start and end apart: 16, of which 6 were waited for; matrix products, arithmetic and copies ran while one was open for 4% of the time, Pallas kernels for 18%

profile of v17, /device:TPU:0, one launch (start us, length us, event | category | flops | bytes accessed | tf_op | source)
XLA Modules:
  0.0 38.9 jit_solution(16667414549446696363)
XLA Ops:
  0.0 0.0 copy-start
  0.0 0.0 copy-start.3
  0.0 0.0 copy-start.1
  0.0 0.5 %own_place.1 = s32[1]{0:T(128)} custom-call(), custom_call_target="tpu_custom_call" | custom-call | flops 80000000000 | bytes 8 | tf_op jit(solution)/shard_map/own_place/pallas_call | solution.py:37
  0.5 0.4 %copy-done.3 = bf16[8,8192]{1,0:T(8,128)(2,1)S(1)} copy-done((bf16[8,8192]{1,0:T(8,128)(2,1)S(1)}, bf16[8,8192]{1,0:T(8,128)(2,1)}, u32[]{:S(2)}) %copy-start.3) | copy-done | bytes 131096
  1.0 5.0 %collective-permute-start.1 = (bf16[8,8192]{1,0:T(8,128)(2,1)S(1)}, bf16[8,8192]{1,0:T(8,128)(2,1)S(1)}, u32[]{:S(2)}, u32[]{:S(2)}) collective-permute-start(bf16[8,8192]{1,0:T(8,128)(2,1)S(1)} %copy-done.3), channel_id=1, source_target_pairs={{0,12},{1,13},{2,14},{3,15},{4,8},{5,9},{6,10},{7,11},{8,4},{9,5},... | collective-permute-start | bytes 393224 | tf_op jit(solution)/shard_map/ppermute | solution.py:288
  6.0 0.0 collective-permute-start.9
  6.0 0.6 %collective-permute-start.8 = (bf16[8,8192]{1,0:T(8,128)(2,1)S(1)}, bf16[8,8192]{1,0:T(8,128)(2,1)S(1)}, u32[]{:S(2)}, u32[]{:S(2)}) collective-permute-start(bf16[8,8192]{1,0:T(8,128)(2,1)S(1)} %copy-done.3), channel_id=1, source_target_pairs={{0,4},{1,5},{2,6},{3,7},{4,0},{5,1},{6,2},{7,3},{8,12},{9,13},{10,... | collective-permute-start | bytes 393224 | tf_op jit(solution)/shard_map/ppermute | solution.py:288
  6.6 1.7 %collective-permute-start.12 = (bf16[8,8192]{1,0:T(8,128)(2,1)S(1)}, bf16[8,8192]{1,0:T(8,128)(2,1)S(1)}, u32[]{:S(2)}, u32[]{:S(2)}) collective-permute-start(bf16[8,8192]{1,0:T(8,128)(2,1)S(1)} %copy-done.3), channel_id=1, source_target_pairs={{0,2},{1,3},{2,0},{3,1},{4,6},{5,7},{6,4},{7,5},{8,10},{9,11},{10,... | collective-permute-start | bytes 393224 | tf_op jit(solution)/shard_map/ppermute | solution.py:288
  8.3 0.0 copy-done.1
  8.3 0.0 copy-done.2
  8.3 2.9 %project.1.acts_ref = bf16[128,1024]{1,0:T(8,128)(2,1)S(1)} custom-call(bf16[1024,4096]{1,0:T(8,128)(2,1)S(1)} %copy-done.1, bf16[128,4096]{1,0:T(8,128)(2,1)S(1)} %bitcast.8), custom_call_target="tpu_custom_call" | custom-call | flops 2147483648 | bytes 8388608 | tf_op jit(solution)/shard_map/project/pallas_call | solution.py:56
  11.2 0.0 copy-done
  11.2 0.0 copy-done.4
  11.2 1.4 %fusion.2 = bf16[2,1024,64]{1,2,0:T(8,128)(2,1)S(1)} fusion(bf16[2,64,1024]{2,1,0:T(8,128)(2,1)S(1)} %copy-done, bf16[1024,2,1024]{2,1,0:T(2,128)(2,1)S(1)} %copy-done.4), kind=kOutput, calls=%fused_computation.2 | convolution fusion | flops 268566528 | bytes 4718592 | tf_op jit(solution)/shard_map/tmk,mrk->tmr/dot_general | solution.py:314
  12.7 0.5 %statistics.1 = (f32[40,128]{1,0:T(8,128)S(1)}, f32[40,128]{1,0:T(8,128)S(1)}, f32[64,512]{1,0:T(8,128)S(1)}, f32[64,512]{1,0:T(8,128)S(1)}) custom-call(bf16[128,1024]{1,0:T(8,128)(2,1)S(1)} %project.1.acts_ref, bf16[128,1024]{1,0:T(8,128)(2,1)S(1)} %bitcast.9), custom_call_target="tpu_custom_call" | custom-call | tf_op jit(solution)/shard_map/statistics/pallas_call | solution.py:125
  13.2 0.1 collective-permute-start
  14.0 0.5 %collective-permute-done = f32[40,128]{1,0:T(8,128)S(1)} collective-permute-done((f32[40,128]{1,0:T(8,128)S(1)}, f32[40,128]{1,0:T(8,128)S(1)}, u32[]{:S(2)}, u32[]{:S(2)}) %collective-permute-start) | collective-permute-done | bytes 20512 | tf_op jit(solution)/shard_map/ppermute | solution.py:288
  14.5 0.2 collective-permute-start.4
  14.6 0.0 collective-permute-done.1
  14.6 0.3 collective-permute-start.2
  15.0 2.1 %collective-permute-done.9 = bf16[8,8192]{1,0:T(8,128)(2,1)S(1)} collective-permute-done((bf16[8,8192]{1,0:T(8,128)(2,1)S(1)}, bf16[8,8192]{1,0:T(8,128)(2,1)S(1)}, u32[]{:S(2)}, u32[]{:S(2)}) %collective-permute-start.9) | collective-permute-done | bytes 131104 | tf_op jit(solution)/shard_map/ppermute | solution.py:288
  17.1 0.0 collective-permute-start.3
  17.1 0.0 collective-permute-done.8
  17.1 0.6 %collective-permute-start.10 = (bf16[16,4096]{1,0:T(8,128)(2,1)S(1)}, bf16[16,4096]{1,0:T(8,128)(2,1)S(1)}, u32[]{:S(2)}, u32[]{:S(2)}) collective-permute-start(bf16[16,4096]{1,0:T(8,128)(2,1)S(1)} %pad_maximum_fusion.3), channel_id=1, source_target_pairs={{0,1},{1,0},{2,3},{3,2},{4,5},{5,4},{6,7},{7,6},{8,9},{9,8},{10,11... | collective-permute-start | bytes 393224 | tf_op jit(solution)/shard_map/ppermute | solution.py:288
  17.7 0.0 collective-permute-done.12
  17.8 0.1 collective-permute-start.13
  17.9 0.6 %collective-permute-done.2 = f32[40,128]{1,0:T(8,128)S(1)} collective-permute-done((f32[40,128]{1,0:T(8,128)S(1)}, f32[40,128]{1,0:T(8,128)S(1)}, u32[]{:S(2)}, u32[]{:S(2)}) %collective-permute-start.2) | collective-permute-done | bytes 20512 | tf_op jit(solution)/shard_map/ppermute | solution.py:288
  18.5 0.0 collective-permute-done.3
  18.5 0.0 collective-permute-done.4.recv_ref
  18.5 3.7 %collective-permute-start.5 = (f32[40,128]{1,0:T(8,128)S(1)}, f32[40,128]{1,0:T(8,128)S(1)}, u32[]{:S(2)}, u32[]{:S(2)}) collective-permute-start(f32[40,128]{1,0:T(8,128)S(1)} %add.10.refs_0_), channel_id=1, source_target_pairs={{0,12},{1,13},{2,14},{3,15},{4,8},{5,9},{6,10},{7,11},{8,4},{9,5},... | collective-permute-start | bytes 61448 | tf_op jit(solution)/shard_map/ppermute | solution.py:288
  22.2 0.0 collective-permute-start.6
  22.2 0.8 %collective-permute-start.7 = (f32[40,128]{1,0:T(8,128)S(1)}, f32[40,128]{1,0:T(8,128)S(1)}, u32[]{:S(2)}, u32[]{:S(2)}) collective-permute-start(f32[40,128]{1,0:T(8,128)S(1)} %add.10.refs_0_), channel_id=1, source_target_pairs={{0,4},{1,5},{2,6},{3,7},{4,0},{5,1},{6,2},{7,3},{8,12},{9,13},{10,... | collective-permute-start | bytes 61448 | tf_op jit(solution)/shard_map/ppermute | solution.py:288
  23.0 0.0 collective-permute-done.10
  23.0 1.4 %collective-permute-start.14 = (bf16[16,4096]{1,0:T(8,128)(2,1)S(1)}, bf16[16,4096]{1,0:T(8,128)(2,1)S(1)}, u32[]{:S(2)}, u32[]{:S(2)}) collective-permute-start(bf16[16,4096]{1,0:T(8,128)(2,1)S(1)} %pad_maximum_fusion.2.refs_3_), channel_id=1, source_target_pairs={{0,2},{1,3},{2,0},{3,1},{4,6},{5,7},{6,4},{7,5},{8,10},{9,11},{10,... | collective-permute-start | bytes 393224 | tf_op jit(solution)/shard_map/ppermute | solution.py:288
  24.4 0.0 collective-permute-done.13
  24.4 0.7 %collective-permute-start.11 = (bf16[32,4096]{1,0:T(8,128)(2,1)S(1)}, bf16[32,4096]{1,0:T(8,128)(2,1)S(1)}, u32[]{:S(2)}, u32[]{:S(2)}) collective-permute-start(bf16[32,4096]{1,0:T(8,128)(2,1)S(1)} %pad_maximum_fusion.refs_1_), channel_id=1, source_target_pairs={{0,2},{1,3},{2,0},{3,1},{4,6},{5,7},{6,4},{7,5},{8,10},{9,11},{10,... | collective-permute-start | bytes 786440 | tf_op jit(solution)/shard_map/ppermute | solution.py:288
  25.1 0.0 collective-permute-done.5.refs_1_
  25.1 1.7 %collective-permute-done.6.refs_2_ = f32[40,128]{1,0:T(8,128)S(1)} collective-permute-done((f32[40,128]{1,0:T(8,128)S(1)}, f32[40,128]{1,0:T(8,128)S(1)}, u32[]{:S(2)}, u32[]{:S(2)}) %collective-permute-start.6) | collective-permute-done | bytes 20512 | tf_op jit(solution)/shard_map/ppermute | solution.py:288
  26.9 0.0 collective-permute-done.7.refs_3_
  26.9 6.3 %collective-permute-done.11.refs_2_ = bf16[32,4096]{1,0:T(8,128)(2,1)S(1)} collective-permute-done((bf16[32,4096]{1,0:T(8,128)(2,1)S(1)}, bf16[32,4096]{1,0:T(8,128)(2,1)S(1)}, u32[]{:S(2)}, u32[]{:S(2)}) %collective-permute-start.11) | collective-permute-done | bytes 262176 | tf_op jit(solution)/shard_map/ppermute | solution.py:288
  33.2 2.7 %inverse.1.inv_ref = f32[64,128]{1,0:T(8,128)S(1)} custom-call(f32[40,128]{1,0:T(8,128)S(1)} %add.10.refs_0_, f32[40,128]{1,0:T(8,128)S(1)} %collective-permute-done.5.refs_1_, f32[40,128]{1,0:T(8,128)S(1)} %collective-permute-done.6.refs_2_, f32[40,128]{1,0:T(8,128)S(1)} %collective-permute-done.7.refs_3_), custom_call_target="tpu_custom_call" | custom-call | tf_op jit(solution)/shard_map/inverse/pallas_call | solution.py:199
  35.8 0.8 %precondition.1.flat_ref = bf16[16,4096]{1,0:T(8,128)(2,1)S(1)} custom-call(f32[64,128]{1,0:T(8,128)S(1)} %inverse.1.inv_ref, f32[64,512]{1,0:T(8,128)S(1)} %get-tuple-element.40.keep_ref, f32[64,512]{1,0:T(8,128)S(1)} %collective-permute-done.4.recv_ref), custom_call_target="tpu_custom_call" | custom-call | tf_op jit(solution)/shard_map/precondition/pallas_call | solution.py:251
  36.6 0.0 collective-permute-done.14.refs_4_
  36.7 0.5 %scores.1 = f32[16,128]{1,0:T(8,128)S(1)} custom-call(bf16[16,4096]{1,0:T(8,128)(2,1)S(1)} %precondition.1.flat_ref, bf16[32,4096]{1,0:T(8,128)(2,1)S(1)} %pad_maximum_fusion.1.refs_0_, bf16[32,4096]{1,0:T(8,128)(2,1)S(1)} %pad_maximum_fusion.refs_1_, bf16[32,4096]{1,0:T(8,128)(2,1)S(1)} %collective-permute-done.11.refs_2_, ...), custom_call_target="tpu_custom_call" | custom-call | tf_op jit(solution)/shard_map/scores/pallas_call | solution.py:276
  37.1 0.0 collective-permute-start.15
  37.2 1.2 %collective-permute-done.15 = f32[8,128]{1,0:T(8,128)S(1)} collective-permute-done((f32[8,128]{1,0:T(8,128)S(1)}, f32[8,128]{1,0:T(8,128)S(1)}, u32[]{:S(2)}, u32[]{:S(2)}) %collective-permute-start.15) | collective-permute-done | bytes 4128 | tf_op jit(solution)/shard_map/ppermute | solution.py:288
  38.3 0.6 %slice_add_fusion = f32[8,128]{1,0:T(8,128)} fusion(f32[8,128]{1,0:T(8,128)S(1)} %collective-permute-done.15, f32[16,128]{1,0:T(8,128)S(1)} %scores.1), kind=kLoop, calls=%fused_computation.18 | loop fusion | flops 1024 | bytes 12288 | tf_op jit(solution)/shard_map/add | solution.py:340
  (15 shorter events, 0.2 us)
Async XLA Ops:
  0.0 11.2 %copy-start = (bf16[2,64,1024]{2,1,0:T(8,128)(2,1)S(1)}, bf16[2,64,1024]{2,1,0:T(8,128)(2,1)}, u32[]{:S(2)}) copy-start(bf16[2,64,1024]{2,1,0:T(8,128)(2,1)} %param.8) | copy-start | bytes 786436
  0.0 0.9 %copy-start.3 = (bf16[8,8192]{1,0:T(8,128)(2,1)S(1)}, bf16[8,8192]{1,0:T(8,128)(2,1)}, u32[]{:S(2)}) copy-start(bf16[8,8192]{1,0:T(8,128)(2,1)} %param.9) | copy-start | bytes 393220
  0.0 8.3 %copy-start.1 = (bf16[1024,4096]{1,0:T(8,128)(2,1)S(1)}, bf16[1024,4096]{1,0:T(8,128)(2,1)}, u32[]{:S(2)}) copy-start(bf16[1024,4096]{1,0:T(8,128)(2,1)} %x_ref.1) | copy-start | bytes 25165828
  0.0 8.3 %copy-start.2 = (bf16[2,64,4096]{2,1,0:T(8,128)(2,1)S(1)}, bf16[2,64,4096]{2,1,0:T(8,128)(2,1)}, u32[]{:S(2)}) copy-start(bf16[2,64,4096]{2,1,0:T(8,128)(2,1)} %param.7) | copy-start | bytes 3145732
  1.0 13.7 %collective-permute-start.1 = (bf16[8,8192]{1,0:T(8,128)(2,1)S(1)}, bf16[8,8192]{1,0:T(8,128)(2,1)S(1)}, u32[]{:S(2)}, u32[]{:S(2)}) collective-permute-start(bf16[8,8192]{1,0:T(8,128)(2,1)S(1)} %copy-done.3), channel_id=1, source_target_pairs={{0,12},{1,13},{2,14},{3,15},{4,8},{5,9},{6,10},{7,11},{8,4},{9,5},... | collective-permute-start | bytes 393224 | tf_op jit(solution)/shard_map/ppermute | solution.py:288
  6.0 11.1 %collective-permute-start.9 = (bf16[8,8192]{1,0:T(8,128)(2,1)S(1)}, bf16[8,8192]{1,0:T(8,128)(2,1)S(1)}, u32[]{:S(2)}, u32[]{:S(2)}) collective-permute-start(bf16[8,8192]{1,0:T(8,128)(2,1)S(1)} %copy-done.3), channel_id=1, source_target_pairs={{0,8},{1,9},{2,10},{3,11},{4,12},{5,13},{6,14},{7,15},{8,0},{9,1},... | collective-permute-start | bytes 393224 | tf_op jit(solution)/shard_map/ppermute | solution.py:288
  6.0 11.1 %collective-permute-start.8 = (bf16[8,8192]{1,0:T(8,128)(2,1)S(1)}, bf16[8,8192]{1,0:T(8,128)(2,1)S(1)}, u32[]{:S(2)}, u32[]{:S(2)}) collective-permute-start(bf16[8,8192]{1,0:T(8,128)(2,1)S(1)} %copy-done.3), channel_id=1, source_target_pairs={{0,4},{1,5},{2,6},{3,7},{4,0},{5,1},{6,2},{7,3},{8,12},{9,13},{10,... | collective-permute-start | bytes 393224 | tf_op jit(solution)/shard_map/ppermute | solution.py:288
  6.6 11.2 %collective-permute-start.12 = (bf16[8,8192]{1,0:T(8,128)(2,1)S(1)}, bf16[8,8192]{1,0:T(8,128)(2,1)S(1)}, u32[]{:S(2)}, u32[]{:S(2)}) collective-permute-start(bf16[8,8192]{1,0:T(8,128)(2,1)S(1)} %copy-done.3), channel_id=1, source_target_pairs={{0,2},{1,3},{2,0},{3,1},{4,6},{5,7},{6,4},{7,5},{8,10},{9,11},{10,... | collective-permute-start | bytes 393224 | tf_op jit(solution)/shard_map/ppermute | solution.py:288
  8.3 2.9 %copy-start.4 = (bf16[1024,2,1024]{2,1,0:T(2,128)(2,1)S(1)}, bf16[1024,2,1024]{2,1,0:T(2,128)(2,1)}, u32[]{:S(2)}) copy-start(bf16[1024,2,1024]{2,1,0:T(2,128)(2,1)} %param.6) | copy-start | bytes 12582916
  13.2 1.3 %collective-permute-start = (f32[40,128]{1,0:T(8,128)S(1)}, f32[40,128]{1,0:T(8,128)S(1)}, u32[]{:S(2)}, u32[]{:S(2)}) collective-permute-start(f32[40,128]{1,0:T(8,128)S(1)} %get-tuple-element.29), channel_id=1, source_target_pairs={{0,1},{1,0},{2,3},{3,2},{4,5},{5,4},{6,7},{7,6},{8,9},{9,8},{10,11... | collective-permute-start | bytes 61448 | tf_op jit(solution)/shard_map/ppermute | solution.py:288
  14.5 4.0 %collective-permute-start.4 = (f32[64,512]{1,0:T(8,128)S(1)}, f32[64,512]{1,0:T(8,128)S(1)}, u32[]{:S(2)}, u32[]{:S(2)}) collective-permute-start(f32[64,512]{1,0:T(8,128)S(1)} %get-tuple-element.34), channel_id=1, source_target_pairs={{0,1},{1,0},{2,3},{3,2},{4,5},{5,4},{6,7},{7,6},{8,9},{9,8},{10,11... | collective-permute-start | bytes 393224 | tf_op jit(solution)/shard_map/ppermute | solution.py:288
  14.6 3.8 %collective-permute-start.2 = (f32[40,128]{1,0:T(8,128)S(1)}, f32[40,128]{1,0:T(8,128)S(1)}, u32[]{:S(2)}, u32[]{:S(2)}) collective-permute-start(f32[40,128]{1,0:T(8,128)S(1)} %add.9), channel_id=1, source_target_pairs={{0,2},{1,3},{2,0},{3,1},{4,6},{5,7},{6,4},{7,5},{8,10},{9,11},{10,... | collective-permute-start | bytes 61448 | tf_op jit(solution)/shard_map/ppermute | solution.py:288
  17.1 1.4 %collective-permute-start.3 = (bf16[8,4096]{1,0:T(8,128)(2,1)S(1)}, bf16[8,4096]{1,0:T(8,128)(2,1)S(1)}, u32[]{:S(2)}, u32[]{:S(2)}) collective-permute-start(bf16[8,4096]{1,0:T(8,128)(2,1)S(1)} %get-tuple-element.54), channel_id=1, source_target_pairs={{0,1},{1,0},{2,3},{3,2},{4,5},{5,4},{6,7},{7,6},{8,9},{9,8},{10,11... | collective-permute-start | bytes 196616 | tf_op jit(solution)/shard_map/ppermute | solution.py:288
  17.1 5.8 %collective-permute-start.10 = (bf16[16,4096]{1,0:T(8,128)(2,1)S(1)}, bf16[16,4096]{1,0:T(8,128)(2,1)S(1)}, u32[]{:S(2)}, u32[]{:S(2)}) collective-permute-start(bf16[16,4096]{1,0:T(8,128)(2,1)S(1)} %pad_maximum_fusion.3), channel_id=1, source_target_pairs={{0,1},{1,0},{2,3},{3,2},{4,5},{5,4},{6,7},{7,6},{8,9},{9,8},{10,11... | collective-permute-start | bytes 393224 | tf_op jit(solution)/shard_map/ppermute | solution.py:288
  17.8 6.6 %collective-permute-start.13 = (bf16[16,4096]{1,0:T(8,128)(2,1)S(1)}, bf16[16,4096]{1,0:T(8,128)(2,1)S(1)}, u32[]{:S(2)}, u32[]{:S(2)}) collective-permute-start(bf16[16,4096]{1,0:T(8,128)(2,1)S(1)} %pad_maximum_fusion.4), channel_id=1, source_target_pairs={{0,1},{1,0},{2,3},{3,2},{4,5},{5,4},{6,7},{7,6},{8,9},{9,8},{10,11... | collective-permute-start | bytes 393224 | tf_op jit(solution)/shard_map/ppermute | solution.py:288
  18.5 6.6 %collective-permute-start.5 = (f32[40,128]{1,0:T(8,128)S(1)}, f32[40,128]{1,0:T(8,128)S(1)}, u32[]{:S(2)}, u32[]{:S(2)}) collective-permute-start(f32[40,128]{1,0:T(8,128)S(1)} %add.10.refs_0_), channel_id=1, source_target_pairs={{0,12},{1,13},{2,14},{3,15},{4,8},{5,9},{6,10},{7,11},{8,4},{9,5},... | collective-permute-start | bytes 61448 | tf_op jit(solution)/shard_map/ppermute | solution.py:288
  22.2 4.7 %collective-permute-start.6 = (f32[40,128]{1,0:T(8,128)S(1)}, f32[40,128]{1,0:T(8,128)S(1)}, u32[]{:S(2)}, u32[]{:S(2)}) collective-permute-start(f32[40,128]{1,0:T(8,128)S(1)} %add.10.refs_0_), channel_id=1, source_target_pairs={{0,8},{1,9},{2,10},{3,11},{4,12},{5,13},{6,14},{7,15},{8,0},{9,1},... | collective-permute-start | bytes 61448 | tf_op jit(solution)/shard_map/ppermute | solution.py:288
  22.2 4.7 %collective-permute-start.7 = (f32[40,128]{1,0:T(8,128)S(1)}, f32[40,128]{1,0:T(8,128)S(1)}, u32[]{:S(2)}, u32[]{:S(2)}) collective-permute-start(f32[40,128]{1,0:T(8,128)S(1)} %add.10.refs_0_), channel_id=1, source_target_pairs={{0,4},{1,5},{2,6},{3,7},{4,0},{5,1},{6,2},{7,3},{8,12},{9,13},{10,... | collective-permute-start | bytes 61448 | tf_op jit(solution)/shard_map/ppermute | solution.py:288
  23.0 13.7 %collective-permute-start.14 = (bf16[16,4096]{1,0:T(8,128)(2,1)S(1)}, bf16[16,4096]{1,0:T(8,128)(2,1)S(1)}, u32[]{:S(2)}, u32[]{:S(2)}) collective-permute-start(bf16[16,4096]{1,0:T(8,128)(2,1)S(1)} %pad_maximum_fusion.2.refs_3_), channel_id=1, source_target_pairs={{0,2},{1,3},{2,0},{3,1},{4,6},{5,7},{6,4},{7,5},{8,10},{9,11},{10,... | collective-permute-start | bytes 393224 | tf_op jit(solution)/shard_map/ppermute | solution.py:288
  24.4 8.8 %collective-permute-start.11 = (bf16[32,4096]{1,0:T(8,128)(2,1)S(1)}, bf16[32,4096]{1,0:T(8,128)(2,1)S(1)}, u32[]{:S(2)}, u32[]{:S(2)}) collective-permute-start(bf16[32,4096]{1,0:T(8,128)(2,1)S(1)} %pad_maximum_fusion.refs_1_), channel_id=1, source_target_pairs={{0,2},{1,3},{2,0},{3,1},{4,6},{5,7},{6,4},{7,5},{8,10},{9,11},{10,... | collective-permute-start | bytes 786440 | tf_op jit(solution)/shard_map/ppermute | solution.py:288
  37.1 1.2 %collective-permute-start.15 = (f32[8,128]{1,0:T(8,128)S(1)}, f32[8,128]{1,0:T(8,128)S(1)}, u32[]{:S(2)}, u32[]{:S(2)}) collective-permute-start(f32[8,128]{1,0:T(8,128)S(1)} %slice.9), channel_id=1, source_target_pairs={{0,1},{1,0},{2,3},{3,2},{4,5},{5,4},{6,7},{7,6},{8,9},{9,8},{10,11... | collective-permute-start | bytes 12296 | tf_op jit(solution)/shard_map/ppermute | solution.py:288
